TPU v7x, 32 devices: a whole 2x2x4 slice. The times are simulated.
32 devices in a mesh: prow: 4 (over y, core), pcol: 8 (over z, x).
Axes of the slice: x: 2, y: 2, z: 4, core: 2. Of those that a mesh axis runs over, the one named last changes fastest.
Arguments:
- right_sides: bfloat16 [16384, 128], P(('prow', 'pcol')), may hold values from -6 to 6
- factor: bfloat16 [16, 8, 32, 4, 128, 128], P(None, 'pcol', None, 'prow'), may hold values from -0.0625 to 0.0625
- pattern: int32 [16, 8, 32, 4], P(None, 'pcol', None, 'prow'), may hold values 0 or 1
- lower_inverse: bfloat16 [16, 8, 128, 128], P(None, 'pcol'), may hold values from -0.5 to 0.5
- upper_inverse: bfloat16 [16, 8, 128, 128], P(None, 'pcol'), may hold values from -0.5 to 0.5
Outputs:
- solution: bfloat16 [16384, 128], P(('prow', 'pcol'))
All inputs are finite; a program needn't handle non-finite values. No bound on the sum of `pattern` on one device may be relied on, other than what follows from the above.
Results may differ from a plain program's by a relative error of at most 0.02.
Values may be sent and summed in bfloat16 or wider, within the bound.
No kernel may reach another device: no remote copies, remote signals or barrier semaphores. Data moves between devices by JAX's collectives and lax.ppermute only.
A program may use at most 128 MiB of HBM per device.

v0:
```python
import jax
import jax.numpy as jnp
from jax import lax
from jax.sharding import PartitionSpec as P


def level_index(index_vals, node_count):
    bounds = (node_count // 2, 3 * node_count // 4, 7 * node_count // 8)
    result = jnp.zeros(index_vals.shape, jnp.int32)
    for edge_val in bounds:
        result = result + (index_vals >= edge_val).astype(jnp.int32)
    return result


def level_sums(
    blocks,
    pattern_loc,
    col_levels,
    solved_all,
    row_id,
    prow_n,
    row_start,
    row_end,
    col_start,
    col_end,
    level_id,
    upward,
):
    if col_end <= col_start:
        return None
    block_size = blocks.shape[2]
    rhs_count = solved_all.shape[2]
    grouped = solved_all.reshape(-1, prow_n, block_size, rhs_count)
    column_vals = lax.dynamic_index_in_dim(grouped, row_id, 1, keepdims=False)[col_start:col_end]
    levels_here = col_levels[col_start:col_end]
    if upward:
        order_mask = levels_here > level_id
    else:
        order_mask = levels_here < level_id
    keep_mask = (pattern_loc[row_start:row_end, col_start:col_end] > 0) & order_mask[None, :]
    masked = jnp.where(
        keep_mask[:, :, None, None],
        blocks[row_start:row_end, col_start:col_end],
        jnp.zeros((), jnp.bfloat16),
    )
    return jnp.einsum("ijab,jbn->ian", masked, column_vals, preferred_element_type=jnp.float32)


def finish_level(partial_value, base_rows, inverse_rows, pcol_n):
    row_count = base_rows.shape[0]
    block_size = base_rows.shape[1]
    rhs_count = base_rows.shape[2]
    if partial_value is None:
        remainder = base_rows
    else:
        summed = lax.psum(partial_value.astype(jnp.bfloat16), "prow").astype(jnp.float32)
        remainder = (base_rows.astype(jnp.float32) - summed).astype(jnp.bfloat16)
    solved = jnp.einsum(
        "iab,ibn->ian", inverse_rows, remainder, preferred_element_type=jnp.float32
    ).astype(jnp.bfloat16)
    gathered = lax.all_gather(solved[:, None], "pcol", axis=1, tiled=True)
    return gathered.reshape(row_count * pcol_n, block_size, rhs_count)


def on_device(right_sides, factor, pattern, lower_inverse, upper_inverse):
    prow_n = lax.axis_size("prow")
    pcol_n = lax.axis_size("pcol")
    row_id = lax.axis_index("prow")
    col_id = lax.axis_index("pcol")
    blocks = factor[:, 0, :, 0]
    pattern_loc = pattern[:, 0, :, 0]
    lower_rows = lower_inverse[:, 0]
    upper_rows = upper_inverse[:, 0]
    row_blocks = blocks.shape[0]
    col_blocks = blocks.shape[1]
    block_size = blocks.shape[2]
    rhs_count = right_sides.shape[1]
    node_count = row_blocks * pcol_n
    per_device = right_sides.shape[0] // block_size
    local_rows = right_sides.reshape(1, per_device, block_size, rhs_count)
    group_rows = lax.all_gather(local_rows, "pcol", axis=0, tiled=True)
    group_rows = group_rows.reshape(per_device, pcol_n, block_size, rhs_count)
    picked = lax.dynamic_index_in_dim(group_rows, col_id, 1, keepdims=False)
    mine_right = lax.all_gather(picked, "prow", axis=0, tiled=True)
    col_levels = level_index(jnp.arange(col_blocks, dtype=jnp.int32) * prow_n + row_id, node_count)
    bounds = (0, row_blocks // 2, 3 * row_blocks // 4, 7 * row_blocks // 8, row_blocks)
    forward_vals = jnp.zeros((node_count, block_size, rhs_count), jnp.bfloat16)
    for level_id in range(4):
        row_start, row_end = (bounds[level_id], bounds[level_id + 1])
        col_end = min(col_blocks, -(-(row_start * pcol_n) // prow_n))
        partial_value = level_sums(
            blocks,
            pattern_loc,
            col_levels,
            forward_vals,
            row_id,
            prow_n,
            row_start,
            row_end,
            0,
            col_end,
            level_id,
            False,
        )
        solved = finish_level(
            partial_value, mine_right[row_start:row_end], lower_rows[row_start:row_end], pcol_n
        )
        forward_vals = lax.dynamic_update_slice_in_dim(forward_vals, solved, row_start * pcol_n, 0)
    forward_mine = lax.dynamic_index_in_dim(
        forward_vals.reshape(row_blocks, pcol_n, block_size, rhs_count), col_id, 1, keepdims=False
    )
    backward_vals = jnp.zeros((node_count, block_size, rhs_count), jnp.bfloat16)
    for level_id in (3, 2, 1, 0):
        row_start, row_end = (bounds[level_id], bounds[level_id + 1])
        col_start = row_end * pcol_n // prow_n
        partial_value = level_sums(
            blocks,
            pattern_loc,
            col_levels,
            backward_vals,
            row_id,
            prow_n,
            row_start,
            row_end,
            col_start,
            col_blocks,
            level_id,
            True,
        )
        solved = finish_level(
            partial_value, forward_mine[row_start:row_end], upper_rows[row_start:row_end], pcol_n
        )
        backward_vals = lax.dynamic_update_slice_in_dim(
            backward_vals, solved, row_start * pcol_n, 0
        )
    out_rows = right_sides.shape[0]
    device_id = row_id * pcol_n + col_id
    flat = backward_vals.reshape(node_count * block_size, rhs_count)
    return lax.dynamic_slice_in_dim(flat, device_id * out_rows, out_rows, 0)


def solution(mesh):
    placed = (
        P(("prow", "pcol"), None),
        P(None, "pcol", None, "prow", None, None),
        P(None, "pcol", None, "prow"),
        P(None, "pcol", None, None),
        P(None, "pcol", None, None),
    )
    return jax.shard_map(
        on_device, mesh=mesh, in_specs=placed, out_specs=P(("prow", "pcol"), None), check_vma=False
    )
```

profile of v0, /device:TPU:0, one launch (start us, length us, event | category | flops | bytes accessed | tf_op | source)
XLA Modules:
  0.0 588.2 jit_solution(5344179804150050705)
XLA Ops:
  7.3 45.1 %all-gather.15.cloned.1.call-done = bf16[8,4,128,128]{3,2,1,0:T(8,128)(2,1)} async-done(((bf16[1,4,128,128]{3,2,1,0:T(8,128)(2,1)}), bf16[8,4,128,128]{3,2,1,0:T(8,128)(2,1)}) %all-gather.15.cloned.1.call-update) | async-done | bytes 1048592 | tf_op jit(solution)/shard_map/all_gather | solution.py:81
  52.4 0.9 constant_dynamic-slice_fusion.4
  53.3 7.2 %all-gather = bf16[16,1,128,128]{3,2,1,0:T(8,128)(2,1)S(1)} all-gather(bf16[4,1,128,128]{3,2,1,0:T(8,128)(2,1)S(1)} %constant_dynamic-slice_fusion.4), channel_id=2, replica_groups=mesh['prow'=4,'pcol'=8] {'prow'}, dimensions={0}, use_global_device_ids=true | all-gather | bytes 655360 | tf_op jit(solution)/shard_map/all_gather | solution.py:84
  60.4 2.0 fusion.11
  63.3 48.5 %all-gather.17.cloned.1.call-done = bf16[8,1024,128]{1,2,0:T(8,128)(2,1)} async-done(((bf16[8,128,128]{1,2,0:T(8,128)(2,1)}), bf16[8,1024,128]{1,2,0:T(8,128)(2,1)}) %all-gather.17.cloned.1.call-update) | async-done | bytes 2097168 | tf_op jit(solution)/shard_map/all_gather | solution.py:61
  111.8 3.0 copy.61
  115.7 1.9 copy-done
  117.6 3.0 fusion.15
  120.6 29.7 %all-reduce.9.cloned.1.call-done = bf16[4,128,128]{2,1,0:T(8,128)(2,1)} async-done(((bf16[4,128,128]{2,1,0:T(8,128)(2,1)}), bf16[4,128,128]{2,1,0:T(8,128)(2,1)}) %all-reduce.9.cloned.1.call-update) | async-done | bytes 131088 | tf_op jit(solution)/shard_map/psum | solution.py:56
  150.4 1.8 fusion.17
  152.4 39.6 %all-gather.19.cloned.1.call-done = bf16[4,1024,128]{1,2,0:T(8,128)(2,1)} async-done(((bf16[4,128,128]{1,2,0:T(8,128)(2,1)}), bf16[4,1024,128]{1,2,0:T(8,128)(2,1)}) %all-gather.19.cloned.1.call-update) | async-done | bytes 1048592 | tf_op jit(solution)/shard_map/all_gather | solution.py:61
  192.0 1.6 copy.66
  193.6 1.0 constant_dynamic-update-slice_fusion.5
  194.7 2.9 fusion.22
  197.7 30.0 %all-reduce.11.cloned.1.call-done = bf16[2,128,128]{2,1,0:T(8,128)(2,1)} async-done(((bf16[2,128,128]{2,1,0:T(8,128)(2,1)}), bf16[2,128,128]{2,1,0:T(8,128)(2,1)}) %all-reduce.11.cloned.1.call-update) | async-done | bytes 65552 | tf_op jit(solution)/shard_map/psum | solution.py:56
  227.7 1.0 fusion.23
  228.7 27.8 %all-gather.3 = bf16[2,1024,128]{1,2,0:T(8,128)(2,1)S(1)} all-gather(bf16[2,128,128]{1,2,0:T(8,128)(2,1)S(1)} %fusion.23), channel_id=5, replica_groups=mesh['prow'=4,'pcol'=8] {'pcol'}, dimensions={1}, use_global_device_ids=true | all-gather | bytes 589824 | tf_op jit(solution)/shard_map/all_gather | solution.py:61
  256.8 0.8 constant_dynamic-update-slice_fusion.4
  257.6 3.1 fusion.20
  260.9 28.6 %all-reduce.13.cloned.1.call-done = bf16[2,128,128]{2,1,0:T(8,128)(2,1)} async-done(((bf16[2,128,128]{2,1,0:T(8,128)(2,1)}), bf16[2,128,128]{2,1,0:T(8,128)(2,1)}) %all-reduce.13.cloned.1.call-update) | async-done | bytes 65552 | tf_op jit(solution)/shard_map/psum | solution.py:56
  289.5 1.0 fusion.24
  290.6 27.8 %all-gather.4 = bf16[2,1024,128]{1,2,0:T(8,128)(2,1)S(1)} all-gather(bf16[2,128,128]{1,2,0:T(8,128)(2,1)S(1)} %fusion.24), channel_id=6, replica_groups=mesh['prow'=4,'pcol'=8] {'pcol'}, dimensions={1}, use_global_device_ids=true | all-gather | bytes 589824 | tf_op jit(solution)/shard_map/all_gather | solution.py:61
  318.7 0.8 constant_dynamic-update-slice_fusion.3
  319.5 1.0 fusion.25
  320.5 27.1 %all-gather.5 = bf16[2,1024,128]{1,2,0:T(8,128)(2,1)S(1)} all-gather(bf16[2,128,128]{1,2,0:T(8,128)(2,1)S(1)} %fusion.25), channel_id=7, replica_groups=mesh['prow'=4,'pcol'=8] {'pcol'}, dimensions={1}, use_global_device_ids=true | all-gather | bytes 589824 | tf_op jit(solution)/shard_map/all_gather | solution.py:61
  347.9 1.0 dynamic_update_slice.28
  348.9 2.0 copy-done.1
  350.9 1.9 fusion.21
  352.8 0.9 constant_dynamic-slice_fusion.1
  353.8 26.9 %all-reduce.15.cloned.1.call-done = bf16[2,128,128]{1,2,0:T(8,128)(2,1)} async-done(((bf16[2,128,128]{1,2,0:T(8,128)(2,1)}), bf16[2,128,128]{1,2,0:T(8,128)(2,1)}) %all-reduce.15.cloned.1.call-update) | async-done | bytes 65552 | tf_op jit(solution)/shard_map/psum | solution.py:56
  380.7 1.0 fusion.26
  381.7 27.8 %all-gather.6 = bf16[2,1024,128]{1,2,0:T(8,128)(2,1)S(1)} all-gather(bf16[2,128,128]{1,2,0:T(8,128)(2,1)S(1)} %fusion.26), channel_id=8, replica_groups=mesh['prow'=4,'pcol'=8] {'pcol'}, dimensions={1}, use_global_device_ids=true | all-gather | bytes 589824 | tf_op jit(solution)/shard_map/all_gather | solution.py:61
  409.8 0.8 constant_dynamic-update-slice_fusion.2
  410.7 2.5 fusion.14
  413.2 0.9 constant_dynamic-slice_fusion
  414.3 28.0 %all-reduce.17.cloned.1.call-done = bf16[4,128,128]{1,2,0:T(8,128)(2,1)} async-done(((bf16[4,128,128]{1,2,0:T(8,128)(2,1)}), bf16[4,128,128]{1,2,0:T(8,128)(2,1)}) %all-reduce.17.cloned.1.call-update) | async-done | bytes 131088 | tf_op jit(solution)/shard_map/psum | solution.py:56
  442.3 1.8 fusion.18
  444.2 39.9 %all-gather.21.cloned.1.call-done = bf16[4,1024,128]{1,2,0:T(8,128)(2,1)} async-done(((bf16[4,128,128]{1,2,0:T(8,128)(2,1)}), bf16[4,1024,128]{1,2,0:T(8,128)(2,1)}) %all-gather.21.cloned.1.call-update) | async-done | bytes 1048592 | tf_op jit(solution)/shard_map/all_gather | solution.py:61
  484.1 1.6 copy.87
  485.7 1.1 constant_dynamic-update-slice_fusion.1
  486.7 4.6 fusion.10
  491.4 1.0 constant_dynamic-slice_fusion.3
  492.6 29.8 %all-reduce.19.cloned.1.call-done = bf16[8,128,128]{1,2,0:T(8,128)(2,1)} async-done(((bf16[8,128,128]{1,2,0:T(8,128)(2,1)}), bf16[8,128,128]{1,2,0:T(8,128)(2,1)}) %all-reduce.19.cloned.1.call-update) | async-done | bytes 262160 | tf_op jit(solution)/shard_map/psum | solution.py:56
  522.4 1.9 fusion.12
  524.4 51.2 %all-gather.23.cloned.1.call-done = bf16[8,1024,128]{1,2,0:T(8,128)(2,1)} async-done(((bf16[8,128,128]{1,2,0:T(8,128)(2,1)}), bf16[8,1024,128]{1,2,0:T(8,128)(2,1)}) %all-gather.23.cloned.1.call-update) | async-done | bytes 2097168 | tf_op jit(solution)/shard_map/all_gather | solution.py:61
  575.6 3.0 copy.91
  578.6 1.5 constant_dynamic-update-slice_fusion
  580.1 1.6 constant_dynamic-slice_fusion.2
  (50 shorter events, 4.8 us)
Async XLA Ops:
  6.5 45.8 %all-gather.15.cloned.1.call-start = ((), (), s32[]{:S(2)}) async-start(), calls=%async_computation | async-start | bytes 1179648 | tf_op jit(solution)/shard_map/all_gather | solution.py:81
  7.3 104.6 %all-gather.17.cloned.1.call-start = ((), (), s32[]{:S(2)}) async-start(), calls=%async_computation.7 | async-start | bytes 2359296 | tf_op jit(solution)/shard_map/all_gather | solution.py:61
  62.4 87.9 %all-reduce.9.cloned.1.call-start = ((), (), s32[]{:S(2)}) async-start(), calls=%async_computation.1 | async-start | bytes 262144 | tf_op jit(solution)/shard_map/psum | solution.py:56
  115.6 1.9 copy-start
  115.6 34.7 %copy-start.2 = (bf16[16,1,128,128]{3,2,1,0:T(8,128)(2,1)S(1)}, bf16[16,1,128,128]{3,2,1,0:T(8,128)(2,1)}, u32[]{:S(2)}) copy-start(bf16[16,1,128,128]{3,2,1,0:T(8,128)(2,1)} %param.8) | copy-start | bytes 1572868
  115.6 36.7 %copy-start.4 = (s32[16,1,32,1]{2,3,1,0:T(1,128)S(1)}, s32[16,1,32,1]{2,3,1,0:T(1,128)}, u32[]{:S(2)}) copy-start(s32[16,1,32,1]{2,3,1,0:T(1,128)} %param.7) | copy-start | bytes 6148
  120.6 71.4 %all-gather.19.cloned.1.call-start = ((), (), s32[]{:S(2)}) async-start(), calls=%async_computation.8 | async-start | bytes 1179648 | tf_op jit(solution)/shard_map/all_gather | solution.py:61
  152.2 75.5 %all-reduce.11.cloned.1.call-start = ((), (), s32[]{:S(2)}) async-start(), calls=%async_computation.2 | async-start | bytes 131072 | tf_op jit(solution)/shard_map/psum | solution.py:56
  197.6 91.9 %all-reduce.13.cloned.1.call-start = ((), (), s32[]{:S(2)}) async-start(), calls=%async_computation.3 | async-start | bytes 131072 | tf_op jit(solution)/shard_map/psum | solution.py:56
  257.6 61.9 %copy-start.3 = (bf16[16,1,128,128]{3,2,1,0:T(8,128)(2,1)S(1)}, bf16[16,1,128,128]{3,2,1,0:T(8,128)(2,1)}, u32[]{:S(2)}) copy-start(bf16[16,1,128,128]{3,2,1,0:T(8,128)(2,1)} %param.9) | copy-start | bytes 1572868
  260.8 120.0 %all-reduce.15.cloned.1.call-start = ((), (), s32[]{:S(2)}) async-start(), calls=%async_computation.4 | async-start | bytes 131072 | tf_op jit(solution)/shard_map/psum | solution.py:56
  348.9 2.0 copy-start.1
  352.8 89.5 %all-reduce.17.cloned.1.call-start = ((), (), s32[]{:S(2)}) async-start(), calls=%async_computation.5 | async-start | bytes 262144 | tf_op jit(solution)/shard_map/psum | solution.py:56
  413.2 70.9 %all-gather.21.cloned.1.call-start = ((), (), s32[]{:S(2)}) async-start(), calls=%async_computation.9 | async-start | bytes 1179648 | tf_op jit(solution)/shard_map/all_gather | solution.py:61
  444.1 78.3 %all-reduce.19.cloned.1.call-start = ((), (), s32[]{:S(2)}) async-start(), calls=%async_computation.6 | async-start | bytes 524288 | tf_op jit(solution)/shard_map/psum | solution.py:56
  491.4 84.2 %all-gather.23.cloned.1.call-start = ((), (), s32[]{:S(2)}) async-start(), calls=%async_computation.10 | async-start | bytes 2359296 | tf_op jit(solution)/shard_map/all_gather | solution.py:61
Sparse Core Ops, SparseCore 0:
  9.5 42.8 all-gather.14
  62.6 49.2 all-gather.16
  120.7 29.5 all-reduce.8
  152.4 39.5 all-gather.18
  197.7 29.9 all-reduce.10
  260.9 28.5 all-reduce.12
  352.9 27.7 all-reduce.14
  413.3 28.9 all-reduce.16
  444.5 39.5 all-gather.20
  491.5 30.8 all-reduce.18
  524.5 51.0 all-gather.22
where the time goes:
time: 589 us; the launch traced here: 588 us
  waiting for transfers between devices  398 us (68%)
  blocking collectives  118 us (20%)
  matrix products  29.5 us (5%)
  local copies, waits for them, and re-layouts  27.8 us (5%)
  between operations  13.4 us (2%)
    all_gather x4, waiting for transfers between devices, finish_level(): gathered = lax.all_gather(solved[:, None], 'pcol', axis=1, tiled=True)  179 us
    psum x6, waiting for transfers between devices, finish_level(): lax.psum(partial_value.astype(jnp.bfloat16), 'prow').astype(jnp.float32)  173 us
    all_gather x4, blocking collectives, finish_level(): gathered = lax.all_gather(solved[:, None], 'pcol', axis=1, tiled=True)  111 us
    all_gather x1, waiting for transfers between devices, on_device(): group_rows = lax.all_gather(local_rows, 'pcol', axis=0, tiled=True)  45.1 us
    dot_general x6, matrix products, level_sums(): jnp.einsum('ijab,jbn->ian', masked, column_vals, preferred_element_type=j...  17.9 us
  transfers between devices with their start and end apart: 11, of which 11 were waited for; matrix products, arithmetic and copies ran while one was open for 1% of the time, Pallas kernels for 0%

commit v1 on v0

v1 whole, which is shorter than its diff:
```python
import functools

import jax
import jax.numpy as jnp
from jax import lax
from jax.experimental import pallas as pl
from jax.experimental.pallas import tpu as pltpu
from jax.sharding import Mesh
from jax.sharding import PartitionSpec as P

ROW_AXES = ("hi", "lo")
COL_AXES = ("q", "s")
ALL_AXES = ROW_AXES + COL_AXES
VMEM_LIMIT = 40 * 1024 * 1024


def params():
    return pltpu.CompilerParams(vmem_limit_bytes=VMEM_LIMIT)


def block_sums(scalars, pattern, factor, pieces, row_start, row_count, col_start, col_count, acc, base, negate):
    size = factor.shape[-1]
    rhs = pieces[0][0].shape[-1]
    piece_count = len(pieces)

    def first_row(scal):
        return row_start if isinstance(row_start, int) else scal[row_start[0]]

    def kernel(scal, pat, factor_ref, *refs):
        piece_refs = refs[:piece_count]
        rest = list(refs[piece_count:])
        acc_ref = rest.pop(0) if acc is not None else None
        base_ref = rest.pop(0) if base is not None else None
        out_ref = rest.pop(0)
        row = first_row(scal) + pl.program_id(0)
        total = acc_ref[0] if acc is not None else jnp.zeros((size, rhs), jnp.float32)
        for (_, pairs), ref in zip(pieces, piece_refs):
            for start, columns in pairs(scal):
                tiles = []
                for column in columns:
                    tile = factor_ref[0, 0, column - col_start, 0]
                    tiles.append(jnp.where(pat[row, column] > 0, tile, jnp.zeros_like(tile)))
                left = jnp.concatenate(tiles, axis=1)
                right = ref[start : start + len(columns)].reshape(len(columns) * size, rhs)
                total = total + jnp.dot(left, right, preferred_element_type=jnp.float32)
        if negate:
            total = -total if base is None else base_ref[0].astype(jnp.float32) - total
        out_ref[0] = total.astype(out_ref.dtype)

    in_specs = [
        pl.BlockSpec(
            (1, 1, col_count, 1, size, size),
            lambda g, scal, pat: (first_row(scal) + g, 0, col_start // col_count, 0, 0, 0),
        )
    ]
    operands = [factor]
    for blocks, _ in pieces:
        in_specs.append(pl.BlockSpec(blocks.shape, lambda g, scal, pat: (0, 0, 0)))
        operands.append(blocks)
    for extra in (acc, base):
        if extra is not None:
            array, offset = extra
            if isinstance(offset, int):
                index = lambda g, scal, pat, offset=offset: (g + offset, 0, 0)
            else:
                index = lambda g, scal, pat, offset=offset: (g + scal[offset[0]], 0, 0)
            in_specs.append(pl.BlockSpec((1, size, rhs), index))
            operands.append(array)
    out_dtype = jnp.bfloat16 if negate else jnp.float32
    return pl.pallas_call(
        kernel,
        grid_spec=pltpu.PrefetchScalarGridSpec(
            num_scalar_prefetch=2,
            grid=(row_count,),
            in_specs=in_specs,
            out_specs=pl.BlockSpec((1, size, rhs), lambda g, scal, pat: (g, 0, 0)),
        ),
        out_shape=jax.ShapeDtypeStruct((row_count, size, rhs), out_dtype),
        compiler_params=params(),
        cost_estimate=pl.CostEstimate(
            flops=2 * row_count * col_count * size * size * rhs,
            bytes_accessed=2 * row_count * col_count * size * size,
            transcendentals=0,
        ),
        name="block_sums",
    )(scalars, pattern, *operands)


def sum_and_solve(gathered, base, inverses, row_start):
    parts, rows, size, rhs = gathered.shape

    def kernel(gathered_ref, *refs):
        refs = list(refs)
        base_ref = refs.pop(0) if base is not None else None
        out_ref = refs.pop()
        for i in range(rows):
            value = gathered_ref[0, i].astype(jnp.float32)
            for part in range(1, parts):
                value = value + gathered_ref[part, i].astype(jnp.float32)
            if base is not None:
                value = value + base_ref[i].astype(jnp.float32)
            value = value.astype(jnp.bfloat16)
            for inverse_ref in refs:
                value = jnp.dot(inverse_ref[i, 0], value, preferred_element_type=jnp.float32).astype(jnp.bfloat16)
            out_ref[i] = value

    operands = [gathered]
    in_specs = [pl.BlockSpec(gathered.shape, lambda g: (0, 0, 0, 0))]
    if base is not None:
        operands.append(base)
        in_specs.append(pl.BlockSpec(base.shape, lambda g: (0, 0, 0)))
    for inverse in inverses:
        operands.append(inverse)
        in_specs.append(pl.BlockSpec((rows, 1, size, size), lambda g: (row_start // rows, 0, 0, 0)))
    return pl.pallas_call(
        kernel,
        grid=(1,),
        in_specs=in_specs,
        out_specs=pl.BlockSpec((rows, size, rhs), lambda g: (0, 0, 0)),
        out_shape=jax.ShapeDtypeStruct((rows, size, rhs), jnp.bfloat16),
        compiler_params=params(),
        cost_estimate=pl.CostEstimate(
            flops=2 * rows * size * size * rhs, bytes_accessed=2 * (parts + 2) * rows * size * rhs, transcendentals=0
        ),
        name="sum_and_solve",
    )(*operands)


def solve_copies(inverse, values, copies):
    count, size, rhs = values.shape

    def kernel(inverse_ref, value_ref, out_ref):
        for i in range(count):
            solved = jnp.dot(inverse_ref[i], value_ref[i], preferred_element_type=jnp.float32).astype(jnp.bfloat16)
            for copy in range(copies):
                out_ref[copy, i] = solved

    return pl.pallas_call(
        kernel,
        grid=(1,),
        in_specs=[
            pl.BlockSpec((count, size, size), lambda g: (0, 0, 0)),
            pl.BlockSpec((count, size, rhs), lambda g: (0, 0, 0)),
        ],
        out_specs=pl.BlockSpec((copies, count, size, rhs), lambda g: (0, 0, 0, 0)),
        out_shape=jax.ShapeDtypeStruct((copies, count, size, rhs), jnp.bfloat16),
        compiler_params=params(),
        name="solve_copies",
    )(inverse, values)


def last_solve(scalars, start_index, own, other, inverse, solved, copies):
    count, size, rhs = own.shape

    def kernel(scal, own_ref, other_ref, inverse_ref, solved_ref, out_ref):
        for h in range(count):
            value = (own_ref[h] + other_ref[h].astype(jnp.float32)).astype(jnp.bfloat16)
            value = jnp.dot(inverse_ref[h, 0], value, preferred_element_type=jnp.float32).astype(jnp.bfloat16)
            value = jnp.where(scal[start_index + 1] > 0, value, solved_ref[h])
            for copy in range(copies):
                out_ref[h * copies + copy] = value

    full = lambda g, scal: (0, 0, 0)
    return pl.pallas_call(
        kernel,
        grid_spec=pltpu.PrefetchScalarGridSpec(
            num_scalar_prefetch=1,
            grid=(1,),
            in_specs=[
                pl.BlockSpec(own.shape, full),
                pl.BlockSpec(other.shape, full),
                pl.BlockSpec((count, 1, size, size), lambda g, scal: (scal[start_index], 0, 0, 0)),
                pl.BlockSpec((count, size, rhs), lambda g, scal: (scal[start_index + 2], 0, 0)),
            ],
            out_specs=pl.BlockSpec((count * copies, size, rhs), full),
        ),
        out_shape=jax.ShapeDtypeStruct((count * copies, size, rhs), jnp.bfloat16),
        compiler_params=params(),
        name="last_solve",
    )(scalars, own, other, inverse, solved)


def on_device(right_sides, factor, pattern, lower_inverse, upper_inverse):
    lo_n = lax.axis_size("lo")
    prow_n = lax.axis_size("hi") * lo_n
    q_n = lax.axis_size("q")
    pcol_n = q_n * lax.axis_size("s")
    row_id = lax.axis_index("hi") * lo_n + lax.axis_index("lo")
    q_id = lax.axis_index("q")
    s_id = lax.axis_index("s")
    col_id = q_id * prow_n + s_id
    row_blocks, _, col_blocks, _, size, _ = factor.shape
    rhs = right_sides.shape[1]
    per = right_sides.shape[0] // size
    spread_n = pcol_n // per
    half = row_blocks // 2
    bounds = (0, half, 3 * row_blocks // 4, 7 * row_blocks // 8, row_blocks)
    cols = tuple(q_n * b for b in bounds)
    device = lambda r, c: r * pcol_n + c
    everyone = [(r, c) for r in range(prow_n) for c in range(pcol_n)]

    is_low = row_id < prow_n // 2
    lo_id = lax.axis_index("lo")
    entries = [q_id] + [per * lax.rem(lo_id + t, lo_n) for t in range(lo_n)]
    last_index = len(entries)
    entries += [lo_id, is_low.astype(jnp.int32), jnp.where(is_low, 0, lo_id)]
    scalars = jnp.stack([jnp.asarray(v, jnp.int32) for v in entries])
    pattern = pattern.reshape(row_blocks, col_blocks)
    sums = functools.partial(block_sums, scalars, pattern, factor)

    def spread(values):
        return [
            lax.ppermute(
                values,
                ALL_AXES,
                [
                    (device(r, c), device(c % prow_n, (c // prow_n + t) % q_n * prow_n + r))
                    for r, c in everyone
                ],
            )
            for t in range(q_n)
        ]

    def spread_pieces(received, first):
        result = []
        for t, blocks in enumerate(received):

            def pairs(scal, t=t, count=blocks.shape[0]):
                q = lax.rem(scal[0] + (q_n - t), q_n)
                return [(m, [q_n * (first + m + n) + q for n in range(2)]) for m in range(0, count, 2)]

            result.append((blocks, pairs))
        return result

    def gather(partial):
        return lax.all_gather(partial, ROW_AXES, axis=0)

    if per == prow_n:
        blocks = lax.all_to_all(right_sides.reshape(per, size, rhs), ROW_AXES, 0, 0, tiled=True)
        there = [(device(r, c), device(c % prow_n, r * q_n + c // prow_n)) for r, c in everyone]
        back = [(target, source) for source, target in there]
        inverse_rows = lax.dynamic_index_in_dim(
            lower_inverse[:half].reshape(half // per, per, size, size), row_id, 1, keepdims=False
        )
        inverse_rows = lax.ppermute(inverse_rows, ALL_AXES, there)
        first_half = half // per
        copies = solve_copies(inverse_rows, blocks[:first_half], pcol_n)
        zero_vals = lax.all_to_all(copies, COL_AXES, 0, 0, tiled=True)
        flat = zero_vals.reshape(pcol_n * first_half, size, rhs)

        def zero_pairs(scal):
            result = []
            for c in range(pcol_n):
                for r in range(0, first_half, 2):
                    result.append((c * first_half + r, [pcol_n * (r + n) + c for n in range(2)]))
            return result

        zero_pieces = [(flat, zero_pairs)]
        rest = lax.ppermute(blocks[first_half:], ALL_AXES, back)
        owned = (jnp.arange(per) == row_id)[None, :, None, None]
        base_rest = jnp.where(owned, rest[:, None], jnp.zeros((), jnp.bfloat16)).reshape(row_blocks - half, size, rhs)
        own_zero = lax.dynamic_index_in_dim(
            zero_vals.reshape(per, q_n, first_half, size, rhs), q_id, 1, keepdims=False
        )
        base_zero = jnp.where(row_id == s_id, jnp.swapaxes(own_zero, 0, 1), jnp.zeros((), jnp.bfloat16))
        base_zero = base_zero.reshape(half, size, rhs)
    else:
        group_rows = lax.all_gather(right_sides.reshape(per, size, rhs), COL_AXES, axis=0, tiled=True)
        picked = lax.dynamic_index_in_dim(group_rows.reshape(per, pcol_n, size, rhs), col_id, 1, keepdims=False)
        mine = lax.all_gather(picked, ROW_AXES, axis=0, tiled=True)
        zero_rows = sum_and_solve(mine[None, :half], None, [lower_inverse], 0)
        zero_pieces = spread_pieces(spread(zero_rows), 0)
        base_rest = jnp.where(row_id == 0, mine[half:], jnp.zeros((), jnp.bfloat16))
        base_zero = jnp.where(row_id == 0, zero_rows, jnp.zeros((), jnp.bfloat16))

    def count(level):
        return bounds[level + 1] - bounds[level]

    def width(first, last):
        return cols[last + 1] - cols[first]

    partial = sums(zero_pieces, bounds[1], count(1), 0, cols[1], None, (base_rest, 0), True)
    one_rows = sum_and_solve(gather(partial), None, [lower_inverse], bounds[1])
    one_pieces = spread_pieces(spread(one_rows), bounds[1])
    late = sums(zero_pieces, bounds[2], count(2) + count(3), 0, cols[1], None, None, False)
    partial = sums(
        one_pieces, bounds[2], count(2), cols[1], width(1, 1), (late, 0), (base_rest, bounds[2] - half), True
    )
    two_rows = sum_and_solve(gather(partial), None, [lower_inverse], bounds[2])
    two_pieces = spread_pieces(spread(two_rows), bounds[2])
    late = sums(one_pieces, bounds[3], count(3), cols[1], width(1, 1), (late, count(2)), None, False)
    partial = sums(
        two_pieces, bounds[3], count(3), cols[2], width(2, 2), (late, 0), (base_rest, bounds[3] - half), True
    )
    three_solved = sum_and_solve(gather(partial), None, [lower_inverse, upper_inverse], bounds[3])
    three_pieces = spread_pieces(spread(three_solved), bounds[3])
    partial = sums(three_pieces, bounds[2], count(2), cols[3], width(3, 3), None, None, True)
    two_solved = sum_and_solve(gather(partial), two_rows, [upper_inverse], bounds[2])
    two_pieces = spread_pieces(spread(two_solved), bounds[2])
    late = sums(three_pieces, bounds[1], count(1), cols[3], width(3, 3), None, None, False)
    partial = sums(two_pieces, bounds[1], count(1), cols[2], width(2, 2), (late, 0), None, True)
    one_solved = sum_and_solve(gather(partial), one_rows, [upper_inverse], bounds[1])
    one_pieces = spread_pieces(spread(one_solved), bounds[1])
    upper = sums(two_pieces + three_pieces, 0, half, cols[2], width(2, 3), None, None, False)
    chunks = []
    for t in range(1, lo_n):
        chunks.append(
            sums(one_pieces, (1 + t,), per, cols[1], width(1, 1), (upper, (1 + t,)), (base_zero, (1 + t,)), True)
        )
    own = sums(one_pieces, (1,), per, cols[1], width(1, 1), (upper, (1,)), (base_zero, (1,)), True)
    own = own.astype(jnp.float32)
    for t in range(1, lo_n):
        pairs = [((lo, (lo + t) % lo_n)) for lo in range(lo_n)]
        own = own + lax.ppermute(chunks[t - 1], "lo", pairs).astype(jnp.float32)
    other = lax.ppermute(own.astype(jnp.bfloat16), "hi", [(0, 1), (1, 0)])
    solved = jnp.concatenate([one_solved, two_solved, three_solved], axis=0)
    slots = last_solve(scalars, last_index, own, other, upper_inverse, solved, spread_n)
    received = lax.all_to_all(slots, COL_AXES, 0, 0, tiled=True)
    mine = lax.dynamic_slice_in_dim(received, lax.rem(col_id, spread_n) * per, per, 0)
    return mine.reshape(per * size, rhs)


def solution(mesh):
    prow_n, pcol_n = mesh.shape["prow"], mesh.shape["pcol"]
    fine = Mesh(mesh.devices.reshape(2, prow_n // 2, pcol_n // prow_n, prow_n), ALL_AXES)
    placed = (
        P(ALL_AXES, None),
        P(None, COL_AXES, None, ROW_AXES, None, None),
        P(None, COL_AXES, None, ROW_AXES),
        P(None, COL_AXES, None, None),
        P(None, COL_AXES, None, None),
    )
    return jax.shard_map(on_device, mesh=fine, in_specs=placed, out_specs=P(ALL_AXES, None), check_vma=False)
```

time: 589 us -> 171 us (0.29)
  waiting for transfers between devices: 398 us -> 49.1 us
  blocking collectives: 118 us -> 49 us
  Pallas kernels: 0 us -> 37.7 us
  starting transfers between devices: 0.42 us -> 31.4 us
  matrix products: 29.5 us -> 0 us
  local copies, waits for them, and re-layouts: 27.8 us -> 2.54 us
  between operations: 13.4 us -> 0.3 us
    all_gather x5 -> x0, waiting for transfers between devices: 224 us -> none  [the longest x4 179 us: finish_level(): gathered = lax.all_gather(solved[:, None], 'pcol', axis=1, tiled=True)]
    psum x6 -> x0, waiting for transfers between devices: 173 us -> none  [finish_level(): lax.psum(partial_value.astype(jnp.bfloat16), 'prow').astype(jnp.float32)]
    all_gather x5, blocking collectives: 118 us -> 49 us  [gather(): return lax.all_gather(partial, ROW_AXES, axis=0)]
    pallas_call x0 -> x18, Pallas kernels: none -> 37.7 us  [the longest x11 34.2 us: block_sums(): pl.pallas_call(kernel, grid_spec=pltpu.PrefetchScalarGridSpec(num_scalar_...]
    dot_general x14 -> x0, matrix products: 29.5 us -> none  [the longest x6 17.9 us: level_sums(): jnp.einsum('ijab,jbn->ian', masked, column_vals, preferred_element_type=j...]
    all_to_all x0 -> x3, waiting for transfers between devices: none -> 28.1 us  [the longest x1 16.3 us: on_device(): zero_vals = lax.all_to_all(copies, COL_AXES, 0, 0, tiled=True)]
    ppermute x0 -> x14, waiting for transfers between devices: none -> 21.1 us  [the longest x10 16.9 us: spread(): lax.ppermute(values, ALL_AXES, [(device(r, c), device(c % prow_n, (c // p...]
    all_to_all x0 -> x3, starting transfers between devices: none -> 20.3 us  [the longest x1 10.4 us: on_device(): zero_vals = lax.all_to_all(copies, COL_AXES, 0, 0, tiled=True)]
  transfers between devices with their start and end apart: 11 -> 17, of which waited for: 11 -> 9; matrix products, arithmetic and copies ran while one was open for 1% -> 1% of each run, Pallas kernels for 0% -> 11%
where the time goes in v1:
time: 171 us; the launch traced here: 170 us
  waiting for transfers between devices  49.1 us (29%)
  blocking collectives  49 us (29%)
  Pallas kernels  37.7 us (22%)
  starting transfers between devices  31.4 us (18%)
  local copies, waits for them, and re-layouts  2.54 us (1%)
    all_gather x5, blocking collectives, gather(): return lax.all_gather(partial, ROW_AXES, axis=0)  49 us
    pallas_call x11, Pallas kernels, block_sums(): pl.pallas_call(kernel, grid_spec=pltpu.PrefetchScalarGridSpec(num_scalar_...  34.2 us
    ppermute x10, waiting for transfers between devices, spread(): lax.ppermute(values, ALL_AXES, [(device(r, c), device(c % prow_n, (c // p...  16.9 us
    all_to_all x1, waiting for transfers between devices, on_device(): zero_vals = lax.all_to_all(copies, COL_AXES, 0, 0, tiled=True)  16.3 us
    all_to_all x1, starting transfers between devices, on_device(): zero_vals = lax.all_to_all(copies, COL_AXES, 0, 0, tiled=True)  10.4 us
    all_to_all x1, waiting for transfers between devices, on_device(): received = lax.all_to_all(slots, COL_AXES, 0, 0, tiled=True)  8.8 us
    all_to_all x1, starting transfers between devices, on_device(): received = lax.all_to_all(slots, COL_AXES, 0, 0, tiled=True)  5.45 us
    ppermute x10, starting transfers between devices, spread(): lax.ppermute(values, ALL_AXES, [(device(r, c), device(c % prow_n, (c // p...  5.22 us
  transfers between devices with their start and end apart: 17, of which 9 were waited for; matrix products, arithmetic and copies ran while one was open for 1% of the time, Pallas kernels for 11%

profile of v1, /device:TPU:0, one launch (start us, length us, event | category | flops | bytes accessed | tf_op | source)
XLA Modules:
  0.0 170.3 jit_solution(17038314094005447731)
XLA Ops:
  0.0 4.4 %all-to-all-start = ((bf16[4,128,128]{2,1,0:T(8,128)(2,1)}), bf16[4,128,128]{2,1,0:T(8,128)(2,1)S(1)}, u32[]{:S(2)}, u32[]{:S(2)}) async-start(bf16[4,128,128]{2,1,0:T(8,128)(2,1)} %bitcast.50), calls=%async_computation | async-start | bytes 262144 | tf_op jit(solution)/shard_map/all_to_all | solution.py:239
  4.4 1.0 slice.9
  5.4 0.7 collective-permute-start
  6.0 3.0 %all-to-all-done = bf16[4,128,128]{2,1,0:T(8,128)(2,1)S(1)} async-done(((bf16[4,128,128]{2,1,0:T(8,128)(2,1)}), bf16[4,128,128]{2,1,0:T(8,128)(2,1)S(1)}, u32[]{:S(2)}, u32[]{:S(2)}) %all-to-all-start) | async-done | bytes 131104 | tf_op jit(solution)/shard_map/all_to_all | solution.py:239
  9.0 1.0 solve_copies.1
  10.0 10.4 %all-to-all-start.1 = ((bf16[8,2,128,128]{3,2,1,0:T(8,128)(2,1)}), bf16[8,2,128,128]{3,2,1,0:T(8,128)(2,1)S(1)}, u32[]{:S(2)}, u32[]{:S(2)}) async-start(bf16[8,2,128,128]{3,2,1,0:T(8,128)(2,1)} %solve_copies.1), calls=%async_computation.1 | async-start | bytes 1048576 | tf_op jit(solution)/shard_map/all_to_all | solution.py:248
  20.5 0.7 collective-permute-start.1
  21.4 16.3 %all-to-all-done.1 = bf16[8,2,128,128]{3,2,1,0:T(8,128)(2,1)S(1)} async-done(((bf16[8,2,128,128]{3,2,1,0:T(8,128)(2,1)}), bf16[8,2,128,128]{3,2,1,0:T(8,128)(2,1)S(1)}, u32[]{:S(2)}, u32[]{:S(2)}) %all-to-all-start.1) | async-done | bytes 524320 | tf_op jit(solution)/shard_map/all_to_all | solution.py:248
  37.8 0.7 copy-done.2
  38.4 3.7 %block_sums.11 = bf16[4,128,128]{2,1,0:T(8,128)(2,1)S(1)} custom-call(s32[6]{0:T(128)S(1)} %stack.31.scal, s32[16,32]{1,0:T(8,128)S(1)} %bitcast.38, bf16[16,1,32,1,128,128]{5,4,3,2,1,0:T(8,128)(2,1)} %factor_ref.21, bf16[16,128,128]{2,1,0:T(8,128)(2,1)S(1)} %bitcast.28, bf16[8,128,128]{2,1,0:T(8,128)(2,1)S(1)} %bitcast_select_fusion.refs_1_.refs_3_), custom_call_target="tpu_custom_call" | custom-call | flops 268435456 | bytes 2097152 | tf_op jit(solution)/shard_map/block_sums/pallas_call | solution.py:70
  42.2 8.2 %all-gather = bf16[16,128,128]{2,1,0:T(8,128)(2,1)S(1)} all-gather(bf16[4,128,128]{2,1,0:T(8,128)(2,1)S(1)} %block_sums.11), channel_id=2, replica_groups=mesh['hi'=2,'lo'=2,'q'=2,'s'=4] {'hi','lo'}, dimensions={0}, use_global_device_ids=true | all-gather | bytes 655360 | tf_op jit(solution)/shard_map/all_gather | solution.py:236
  50.4 0.2 sum_and_solve.5.refs_0_
  50.7 0.7 collective-permute-start.2
  51.4 3.7 %block_sums.12.refs_2_ = f32[4,128,128]{2,1,0:T(8,128)S(1)} custom-call(s32[6]{0:T(128)S(1)} %stack.31.scal, s32[16,32]{1,0:T(8,128)S(1)} %bitcast.39, bf16[16,1,32,1,128,128]{5,4,3,2,1,0:T(8,128)(2,1)} %factor_ref.21, bf16[16,128,128]{2,1,0:T(8,128)(2,1)S(1)} %bitcast.29), custom_call_target="tpu_custom_call" | custom-call | flops 268435456 | bytes 2097152 | tf_op jit(solution)/shard_map/block_sums/pallas_call | solution.py:70
  55.1 5.6 %collective-permute-done.3.refs_1_ = bf16[4,128,128]{2,1,0:T(8,128)(2,1)S(1)} collective-permute-done((bf16[4,128,128]{2,1,0:T(8,128)(2,1)S(1)}, bf16[4,128,128]{2,1,0:T(8,128)(2,1)S(1)}, u32[]{:S(2)}, u32[]{:S(2)}) %collective-permute-start.3) | collective-permute-done | bytes 131104 | tf_op jit(solution)/shard_map/ppermute | solution.py:213
  60.8 2.1 %block_sums.13 = bf16[2,128,128]{2,1,0:T(8,128)(2,1)S(1)} custom-call(s32[6]{0:T(128)S(1)} %stack.31.scal, s32[16,32]{1,0:T(8,128)S(1)} %bitcast.40, bf16[16,1,32,1,128,128]{5,4,3,2,1,0:T(8,128)(2,1)} %factor_ref.21, bf16[4,128,128]{2,1,0:T(8,128)(2,1)S(1)} %collective-permute-done.2.refs_0_, bf16[4,128,128]{2,1,0:T(8,128)(2,1)S(1)} %collective-permute-done.3.refs_1_, ...), custom_call_target="tpu_custom_call" | custom-call | flops 67108864 | bytes 524288 | tf_op jit(solution)/shard_map/block_sums/pallas_call | solution.py:70
  62.9 8.4 %all-gather.1 = bf16[8,128,128]{2,1,0:T(8,128)(2,1)S(1)} all-gather(bf16[2,128,128]{2,1,0:T(8,128)(2,1)S(1)} %block_sums.13), channel_id=3, replica_groups=mesh['hi'=2,'lo'=2,'q'=2,'s'=4] {'hi','lo'}, dimensions={0}, use_global_device_ids=true | all-gather | bytes 327680 | tf_op jit(solution)/shard_map/all_gather | solution.py:236
  71.6 0.8 collective-permute-start.4
  72.4 2.1 %block_sums.14.refs_2_ = f32[2,128,128]{2,1,0:T(8,128)S(1)} custom-call(s32[6]{0:T(128)S(1)} %stack.31.scal, s32[16,32]{1,0:T(8,128)S(1)} %bitcast.41, bf16[16,1,32,1,128,128]{5,4,3,2,1,0:T(8,128)(2,1)} %factor_ref.21, bf16[4,128,128]{2,1,0:T(8,128)(2,1)S(1)} %collective-permute-done.2.refs_0_, bf16[4,128,128]{2,1,0:T(8,128)(2,1)S(1)} %collective-permute-done.3.refs_1_, ...), custom_call_target="tpu_custom_call" | custom-call | flops 67108864 | bytes 524288 | tf_op jit(solution)/shard_map/block_sums/pallas_call | solution.py:70
  74.5 2.6 %collective-permute-done.5.refs_1_ = bf16[2,128,128]{2,1,0:T(8,128)(2,1)S(1)} collective-permute-done((bf16[2,128,128]{2,1,0:T(8,128)(2,1)S(1)}, bf16[2,128,128]{2,1,0:T(8,128)(2,1)S(1)}, u32[]{:S(2)}, u32[]{:S(2)}) %collective-permute-start.5) | collective-permute-done | bytes 65568 | tf_op jit(solution)/shard_map/ppermute | solution.py:213
  77.2 2.0 %block_sums.15 = bf16[2,128,128]{2,1,0:T(8,128)(2,1)S(1)} custom-call(s32[6]{0:T(128)S(1)} %stack.31.scal, s32[16,32]{1,0:T(8,128)S(1)} %bitcast.42, bf16[16,1,32,1,128,128]{5,4,3,2,1,0:T(8,128)(2,1)} %factor_ref.21, bf16[2,128,128]{2,1,0:T(8,128)(2,1)S(1)} %collective-permute-done.4.refs_0_, bf16[2,128,128]{2,1,0:T(8,128)(2,1)S(1)} %collective-permute-done.5.refs_1_, ...), custom_call_target="tpu_custom_call" | custom-call | flops 33554432 | bytes 262144 | tf_op jit(solution)/shard_map/block_sums/pallas_call | solution.py:70
  79.1 9.8 %all-gather.2 = bf16[8,128,128]{2,1,0:T(8,128)(2,1)S(1)} all-gather(bf16[2,128,128]{2,1,0:T(8,128)(2,1)S(1)} %block_sums.15), channel_id=4, replica_groups=mesh['hi'=2,'lo'=2,'q'=2,'s'=4] {'hi','lo'}, dimensions={0}, use_global_device_ids=true | all-gather | bytes 327680 | tf_op jit(solution)/shard_map/all_gather | solution.py:236
  89.0 0.3 sum_and_solve.7
  89.3 0.3 collective-permute-start.7
  89.6 0.7 collective-permute-start.6
  90.2 4.7 %collective-permute-done.7.refs_1_.refs_3_ = bf16[2,128,128]{2,1,0:T(8,128)(2,1)S(1)} collective-permute-done((bf16[2,128,128]{2,1,0:T(8,128)(2,1)S(1)}, bf16[2,128,128]{2,1,0:T(8,128)(2,1)S(1)}, u32[]{:S(2)}, u32[]{:S(2)}) %collective-permute-start.7) | collective-permute-done | bytes 65568 | tf_op jit(solution)/shard_map/ppermute | solution.py:213
  95.0 2.0 %block_sums.16 = bf16[2,128,128]{2,1,0:T(8,128)(2,1)S(1)} custom-call(s32[6]{0:T(128)S(1)} %stack.31.scal, s32[16,32]{1,0:T(8,128)S(1)} %bitcast.43, bf16[16,1,32,1,128,128]{5,4,3,2,1,0:T(8,128)(2,1)} %factor_ref.21, bf16[2,128,128]{2,1,0:T(8,128)(2,1)S(1)} %collective-permute-done.6.refs_0_.refs_2_, ...), custom_call_target="tpu_custom_call" | custom-call | flops 33554432 | bytes 262144 | tf_op jit(solution)/shard_map/block_sums/pallas_call | solution.py:70
  97.0 10.9 %all-gather.3 = bf16[8,128,128]{2,1,0:T(8,128)(2,1)S(1)} all-gather(bf16[2,128,128]{2,1,0:T(8,128)(2,1)S(1)} %block_sums.16), channel_id=5, replica_groups=mesh['hi'=2,'lo'=2,'q'=2,'s'=4] {'hi','lo'}, dimensions={0}, use_global_device_ids=true | all-gather | bytes 327680 | tf_op jit(solution)/shard_map/all_gather | solution.py:236
  107.9 0.2 sum_and_solve.8
  108.1 0.7 collective-permute-start.8
  108.8 3.1 %block_sums.17.refs_2_ = f32[4,128,128]{2,1,0:T(8,128)S(1)} custom-call(s32[6]{0:T(128)S(1)} %stack.31.scal, s32[16,32]{1,0:T(8,128)S(1)} %bitcast.44, bf16[16,1,32,1,128,128]{5,4,3,2,1,0:T(8,128)(2,1)} %factor_ref.21, bf16[2,128,128]{2,1,0:T(8,128)(2,1)S(1)} %collective-permute-done.6.refs_0_.refs_2_, ...), custom_call_target="tpu_custom_call" | custom-call | flops 67108864 | bytes 524288 | tf_op jit(solution)/shard_map/block_sums/pallas_call | solution.py:70
  111.9 1.6 collective-permute-done.9.refs_1_
  113.5 3.1 %block_sums.18 = bf16[4,128,128]{2,1,0:T(8,128)(2,1)S(1)} custom-call(s32[6]{0:T(128)S(1)} %stack.31.scal, s32[16,32]{1,0:T(8,128)S(1)} %bitcast.45, bf16[16,1,32,1,128,128]{5,4,3,2,1,0:T(8,128)(2,1)} %factor_ref.21, bf16[2,128,128]{2,1,0:T(8,128)(2,1)S(1)} %collective-permute-done.8.refs_0_, bf16[2,128,128]{2,1,0:T(8,128)(2,1)S(1)} %collective-permute-done.9.refs_1_, ...), custom_call_target="tpu_custom_call" | custom-call | flops 67108864 | bytes 524288 | tf_op jit(solution)/shard_map/block_sums/pallas_call | solution.py:70
  116.6 11.6 %all-gather.4 = bf16[16,128,128]{2,1,0:T(8,128)(2,1)S(1)} all-gather(bf16[4,128,128]{2,1,0:T(8,128)(2,1)S(1)} %block_sums.18), channel_id=6, replica_groups=mesh['hi'=2,'lo'=2,'q'=2,'s'=4] {'hi','lo'}, dimensions={0}, use_global_device_ids=true | all-gather | bytes 655360 | tf_op jit(solution)/shard_map/all_gather | solution.py:236
  128.2 0.2 sum_and_solve.9
  128.5 1.2 collective-permute-start.11
  129.7 0.7 collective-permute-start.10
  130.5 5.7 %block_sums.19.refs_2_ = f32[8,128,128]{2,1,0:T(8,128)S(1)} custom-call(s32[6]{0:T(128)S(1)} %stack.31.scal, s32[16,32]{1,0:T(8,128)S(1)} %bitcast.46, bf16[16,1,32,1,128,128]{5,4,3,2,1,0:T(8,128)(2,1)} %factor_ref.21, bf16[2,128,128]{2,1,0:T(8,128)(2,1)S(1)} %collective-permute-done.8.refs_0_, bf16[2,128,128]{2,1,0:T(8,128)(2,1)S(1)} %collective-permute-done.9.refs_1_, ...), custom_call_target="tpu_custom_call" | custom-call | flops 268435456 | bytes 2097152 | tf_op jit(solution)/shard_map/block_sums/pallas_call | solution.py:70
  136.2 2.3 %collective-permute-done.11.refs_1_ = bf16[4,128,128]{2,1,0:T(8,128)(2,1)S(1)} collective-permute-done((bf16[4,128,128]{2,1,0:T(8,128)(2,1)S(1)}, bf16[4,128,128]{2,1,0:T(8,128)(2,1)S(1)}, u32[]{:S(2)}, u32[]{:S(2)}) %collective-permute-start.11) | collective-permute-done | bytes 131104 | tf_op jit(solution)/shard_map/ppermute | solution.py:213
  138.4 3.3 %block_sums.21 = bf16[4,128,128]{2,1,0:T(8,128)(2,1)S(1)} custom-call(s32[6]{0:T(128)S(1)} %stack.31.scal, s32[16,32]{1,0:T(8,128)S(1)} %bitcast.47, bf16[16,1,32,1,128,128]{5,4,3,2,1,0:T(8,128)(2,1)} %factor_ref.21, bf16[4,128,128]{2,1,0:T(8,128)(2,1)S(1)} %collective-permute-done.10.refs_0_, bf16[4,128,128]{2,1,0:T(8,128)(2,1)S(1)} %collective-permute-done.11.refs_1_, ...), custom_call_target="tpu_custom_call" | custom-call | flops 134217728 | bytes 1048576 | tf_op jit(solution)/shard_map/block_sums/pallas_call | solution.py:70
  141.8 2.1 %collective-permute-start.12 = (bf16[4,128,128]{2,1,0:T(8,128)(2,1)S(1)}, bf16[4,128,128]{2,1,0:T(8,128)(2,1)S(1)}, u32[]{:S(2)}, u32[]{:S(2)}) collective-permute-start(bf16[4,128,128]{2,1,0:T(8,128)(2,1)S(1)} %block_sums.21), channel_id=1, source_target_pairs={{0,8},{8,0},{1,9},{9,1},{2,10},{10,2},{3,11},{11,3},{4,12},{12,4},... | collective-permute-start | bytes 393224 | tf_op jit(solution)/shard_map/ppermute | solution.py:314
  143.9 3.3 %block_sums.20 = bf16[4,128,128]{2,1,0:T(8,128)(2,1)S(1)} custom-call(s32[6]{0:T(128)S(1)} %stack.31.scal, s32[16,32]{1,0:T(8,128)S(1)} %bitcast.48, bf16[16,1,32,1,128,128]{5,4,3,2,1,0:T(8,128)(2,1)} %factor_ref.21, bf16[4,128,128]{2,1,0:T(8,128)(2,1)S(1)} %collective-permute-done.10.refs_0_, bf16[4,128,128]{2,1,0:T(8,128)(2,1)S(1)} %collective-permute-done.11.refs_1_, ...), custom_call_target="tpu_custom_call" | custom-call | flops 134217728 | bytes 1048576 | tf_op jit(solution)/shard_map/block_sums/pallas_call | solution.py:70
  147.3 2.5 %collective-permute-start.13 = (bf16[4,128,128]{2,1,0:T(8,128)(2,1)S(1)}, bf16[4,128,128]{2,1,0:T(8,128)(2,1)S(1)}, u32[]{:S(2)}, u32[]{:S(2)}) collective-permute-start(bf16[4,128,128]{2,1,0:T(8,128)(2,1)S(1)} %get-tuple-element.5), channel_id=1, source_target_pairs={{0,16},{16,0},{1,17},{17,1},{2,18},{18,2},{3,19},{19,3},{4,20},{20... | collective-permute-start | bytes 393224 | tf_op jit(solution)/shard_map/ppermute | solution.py:315
  149.8 4.1 %collective-permute-done.13.other_ref = bf16[4,128,128]{2,1,0:T(8,128)(2,1)S(1)} collective-permute-done((bf16[4,128,128]{2,1,0:T(8,128)(2,1)S(1)}, bf16[4,128,128]{2,1,0:T(8,128)(2,1)S(1)}, u32[]{:S(2)}, u32[]{:S(2)}) %collective-permute-start.13) | collective-permute-done | bytes 131104 | tf_op jit(solution)/shard_map/ppermute | solution.py:315
  154.0 1.4 last_solve.1
  155.4 5.4 %all-to-all-start.2 = ((bf16[8,128,128]{2,1,0:T(8,128)(2,1)}), bf16[8,128,128]{2,1,0:T(8,128)(2,1)S(1)}, u32[]{:S(2)}, u32[]{:S(2)}) async-start(bf16[8,128,128]{2,1,0:T(8,128)(2,1)} %last_solve.1), calls=%async_computation.2 | async-start | bytes 524288 | tf_op jit(solution)/shard_map/all_to_all | solution.py:318
  160.8 8.8 %all-to-all-done.2 = bf16[8,128,128]{2,1,0:T(8,128)(2,1)S(1)} async-done(((bf16[8,128,128]{2,1,0:T(8,128)(2,1)}), bf16[8,128,128]{2,1,0:T(8,128)(2,1)S(1)}, u32[]{:S(2)}, u32[]{:S(2)}) %all-to-all-start.2) | async-done | bytes 262176 | tf_op jit(solution)/shard_map/all_to_all | solution.py:318
  169.6 0.7 constant_dynamic-slice_fusion
  (29 shorter events, 0.8 us)
Async XLA Ops:
  0.0 50.4 %copy-start.1 = (bf16[16,1,128,128]{3,2,1,0:T(8,128)(2,1)S(1)}, bf16[16,1,128,128]{3,2,1,0:T(8,128)(2,1)}, u32[]{:S(2)}) copy-start(bf16[16,1,128,128]{3,2,1,0:T(8,128)(2,1)} %refs_0_.5) | copy-start | bytes 1572868
  0.0 51.4 %copy-start.3 = (s32[16,1,32,1]{2,3,1,0:T(1,128)S(1)}, s32[16,1,32,1]{2,3,1,0:T(1,128)}, u32[]{:S(2)}) copy-start(s32[16,1,32,1]{2,3,1,0:T(1,128)} %param.7) | copy-start | bytes 6148
  0.0 9.0 %all-to-all-start = ((bf16[4,128,128]{2,1,0:T(8,128)(2,1)}), bf16[4,128,128]{2,1,0:T(8,128)(2,1)S(1)}, u32[]{:S(2)}, u32[]{:S(2)}) async-start(bf16[4,128,128]{2,1,0:T(8,128)(2,1)} %bitcast.50), calls=%async_computation | async-start | bytes 262144 | tf_op jit(solution)/shard_map/all_to_all | solution.py:239
  5.4 3.7 %collective-permute-start = (bf16[2,128,128]{2,1,0:T(8,128)(2,1)S(1)}, bf16[2,128,128]{2,1,0:T(8,128)(2,1)S(1)}, u32[]{:S(2)}, u32[]{:S(2)}) collective-permute-start(bf16[2,128,128]{2,1,0:T(8,128)(2,1)S(1)} %dynamic-slice_bitcast_fusion), channel_id=1, source_target_pairs={{0,0},{1,8},{2,16},{3,24},{4,1},{5,9},{6,17},{7,25},{8,2},{9,10},{... | collective-permute-start | bytes 196616 | tf_op jit(solution)/shard_map/ppermute | solution.py:245
  10.0 27.7 %all-to-all-start.1 = ((bf16[8,2,128,128]{3,2,1,0:T(8,128)(2,1)}), bf16[8,2,128,128]{3,2,1,0:T(8,128)(2,1)S(1)}, u32[]{:S(2)}, u32[]{:S(2)}) async-start(bf16[8,2,128,128]{3,2,1,0:T(8,128)(2,1)} %solve_copies.1), calls=%async_computation.1 | async-start | bytes 1048576 | tf_op jit(solution)/shard_map/all_to_all | solution.py:248
  20.5 0.9 collective-permute-start.1
  37.8 0.7 copy-start.2
  50.6 10.1 %collective-permute-start.3 = (bf16[4,128,128]{2,1,0:T(8,128)(2,1)S(1)}, bf16[4,128,128]{2,1,0:T(8,128)(2,1)S(1)}, u32[]{:S(2)}, u32[]{:S(2)}) collective-permute-start(bf16[4,128,128]{2,1,0:T(8,128)(2,1)S(1)} %sum_and_solve.5.refs_0_), channel_id=1, source_target_pairs={{0,4},{1,12},{2,20},{3,28},{4,0},{5,8},{6,16},{7,24},{8,5},{9,13},... | collective-permute-start | bytes 393224 | tf_op jit(solution)/shard_map/ppermute | solution.py:213
  50.7 10.1 %collective-permute-start.2 = (bf16[4,128,128]{2,1,0:T(8,128)(2,1)S(1)}, bf16[4,128,128]{2,1,0:T(8,128)(2,1)S(1)}, u32[]{:S(2)}, u32[]{:S(2)}) collective-permute-start(bf16[4,128,128]{2,1,0:T(8,128)(2,1)S(1)} %sum_and_solve.5.refs_0_), channel_id=1, source_target_pairs={{0,0},{1,8},{2,16},{3,24},{4,4},{5,12},{6,20},{7,28},{8,1},{9,9},{... | collective-permute-start | bytes 393224 | tf_op jit(solution)/shard_map/ppermute | solution.py:213
  71.5 17.5 %copy-start = (bf16[16,1,128,128]{3,2,1,0:T(8,128)(2,1)S(1)}, bf16[16,1,128,128]{3,2,1,0:T(8,128)(2,1)}, u32[]{:S(2)}) copy-start(bf16[16,1,128,128]{3,2,1,0:T(8,128)(2,1)} %inverse_ref.1) | copy-start | bytes 1572868
  71.5 5.6 %collective-permute-start.5 = (bf16[2,128,128]{2,1,0:T(8,128)(2,1)S(1)}, bf16[2,128,128]{2,1,0:T(8,128)(2,1)S(1)}, u32[]{:S(2)}, u32[]{:S(2)}) collective-permute-start(bf16[2,128,128]{2,1,0:T(8,128)(2,1)S(1)} %sum_and_solve.6.refs_0_), channel_id=1, source_target_pairs={{0,4},{1,12},{2,20},{3,28},{4,0},{5,8},{6,16},{7,24},{8,5},{9,13},... | collective-permute-start | bytes 196616 | tf_op jit(solution)/shard_map/ppermute | solution.py:213
  71.6 5.6 %collective-permute-start.4 = (bf16[2,128,128]{2,1,0:T(8,128)(2,1)S(1)}, bf16[2,128,128]{2,1,0:T(8,128)(2,1)S(1)}, u32[]{:S(2)}, u32[]{:S(2)}) collective-permute-start(bf16[2,128,128]{2,1,0:T(8,128)(2,1)S(1)} %sum_and_solve.6.refs_0_), channel_id=1, source_target_pairs={{0,0},{1,8},{2,16},{3,24},{4,4},{5,12},{6,20},{7,28},{8,1},{9,9},{... | collective-permute-start | bytes 196616 | tf_op jit(solution)/shard_map/ppermute | solution.py:213
  89.3 5.7 %collective-permute-start.7 = (bf16[2,128,128]{2,1,0:T(8,128)(2,1)S(1)}, bf16[2,128,128]{2,1,0:T(8,128)(2,1)S(1)}, u32[]{:S(2)}, u32[]{:S(2)}) collective-permute-start(bf16[2,128,128]{2,1,0:T(8,128)(2,1)S(1)} %sum_and_solve.7), channel_id=1, source_target_pairs={{0,4},{1,12},{2,20},{3,28},{4,0},{5,8},{6,16},{7,24},{8,5},{9,13},... | collective-permute-start | bytes 196616 | tf_op jit(solution)/shard_map/ppermute | solution.py:213
  89.6 5.4 %collective-permute-start.6 = (bf16[2,128,128]{2,1,0:T(8,128)(2,1)S(1)}, bf16[2,128,128]{2,1,0:T(8,128)(2,1)S(1)}, u32[]{:S(2)}, u32[]{:S(2)}) collective-permute-start(bf16[2,128,128]{2,1,0:T(8,128)(2,1)S(1)} %sum_and_solve.7), channel_id=1, source_target_pairs={{0,0},{1,8},{2,16},{3,24},{4,4},{5,12},{6,20},{7,28},{8,1},{9,9},{... | collective-permute-start | bytes 196616 | tf_op jit(solution)/shard_map/ppermute | solution.py:213
  108.1 5.5 %collective-permute-start.9 = (bf16[2,128,128]{2,1,0:T(8,128)(2,1)S(1)}, bf16[2,128,128]{2,1,0:T(8,128)(2,1)S(1)}, u32[]{:S(2)}, u32[]{:S(2)}) collective-permute-start(bf16[2,128,128]{2,1,0:T(8,128)(2,1)S(1)} %sum_and_solve.8), channel_id=1, source_target_pairs={{0,4},{1,12},{2,20},{3,28},{4,0},{5,8},{6,16},{7,24},{8,5},{9,13},... | collective-permute-start | bytes 196616 | tf_op jit(solution)/shard_map/ppermute | solution.py:213
  108.1 5.4 %collective-permute-start.8 = (bf16[2,128,128]{2,1,0:T(8,128)(2,1)S(1)}, bf16[2,128,128]{2,1,0:T(8,128)(2,1)S(1)}, u32[]{:S(2)}, u32[]{:S(2)}) collective-permute-start(bf16[2,128,128]{2,1,0:T(8,128)(2,1)S(1)} %sum_and_solve.8), channel_id=1, source_target_pairs={{0,0},{1,8},{2,16},{3,24},{4,4},{5,12},{6,20},{7,28},{8,1},{9,9},{... | collective-permute-start | bytes 196616 | tf_op jit(solution)/shard_map/ppermute | solution.py:213
  128.5 10.0 %collective-permute-start.11 = (bf16[4,128,128]{2,1,0:T(8,128)(2,1)S(1)}, bf16[4,128,128]{2,1,0:T(8,128)(2,1)S(1)}, u32[]{:S(2)}, u32[]{:S(2)}) collective-permute-start(bf16[4,128,128]{2,1,0:T(8,128)(2,1)S(1)} %sum_and_solve.9), channel_id=1, source_target_pairs={{0,4},{1,12},{2,20},{3,28},{4,0},{5,8},{6,16},{7,24},{8,5},{9,13},... | collective-permute-start | bytes 393224 | tf_op jit(solution)/shard_map/ppermute | solution.py:213
  129.7 8.7 %collective-permute-start.10 = (bf16[4,128,128]{2,1,0:T(8,128)(2,1)S(1)}, bf16[4,128,128]{2,1,0:T(8,128)(2,1)S(1)}, u32[]{:S(2)}, u32[]{:S(2)}) collective-permute-start(bf16[4,128,128]{2,1,0:T(8,128)(2,1)S(1)} %sum_and_solve.9), channel_id=1, source_target_pairs={{0,0},{1,8},{2,16},{3,24},{4,4},{5,12},{6,20},{7,28},{8,1},{9,9},{... | collective-permute-start | bytes 393224 | tf_op jit(solution)/shard_map/ppermute | solution.py:213
  141.8 5.5 %collective-permute-start.12 = (bf16[4,128,128]{2,1,0:T(8,128)(2,1)S(1)}, bf16[4,128,128]{2,1,0:T(8,128)(2,1)S(1)}, u32[]{:S(2)}, u32[]{:S(2)}) collective-permute-start(bf16[4,128,128]{2,1,0:T(8,128)(2,1)S(1)} %block_sums.21), channel_id=1, source_target_pairs={{0,8},{8,0},{1,9},{9,1},{2,10},{10,2},{3,11},{11,3},{4,12},{12,4},... | collective-permute-start | bytes 393224 | tf_op jit(solution)/shard_map/ppermute | solution.py:314
  147.3 6.6 %collective-permute-start.13 = (bf16[4,128,128]{2,1,0:T(8,128)(2,1)S(1)}, bf16[4,128,128]{2,1,0:T(8,128)(2,1)S(1)}, u32[]{:S(2)}, u32[]{:S(2)}) collective-permute-start(bf16[4,128,128]{2,1,0:T(8,128)(2,1)S(1)} %get-tuple-element.5), channel_id=1, source_target_pairs={{0,16},{16,0},{1,17},{17,1},{2,18},{18,2},{3,19},{19,3},{4,20},{20... | collective-permute-start | bytes 393224 | tf_op jit(solution)/shard_map/ppermute | solution.py:315
  155.4 14.2 %all-to-all-start.2 = ((bf16[8,128,128]{2,1,0:T(8,128)(2,1)}), bf16[8,128,128]{2,1,0:T(8,128)(2,1)S(1)}, u32[]{:S(2)}, u32[]{:S(2)}) async-start(bf16[8,128,128]{2,1,0:T(8,128)(2,1)} %last_solve.1), calls=%async_computation.2 | async-start | bytes 524288 | tf_op jit(solution)/shard_map/all_to_all | solution.py:318

commit v2 on v1

v2 whole, which is shorter than its diff:
```python
import math

import jax
import jax.numpy as jnp
from jax import lax
from jax.experimental import pallas as pl
from jax.experimental.pallas import tpu as pltpu
from jax.sharding import Mesh
from jax.sharding import PartitionSpec as P

ROW_AXES = ("hi", "lo")
COL_AXES = ("q", "s")
ALL_AXES = ROW_AXES + COL_AXES
VMEM_LIMIT = 16 * 1024 * 1024


def params():
    return pltpu.CompilerParams(vmem_limit_bytes=VMEM_LIMIT)


def lay_out(scalars, pattern, factor, after, parts):
    size = factor.shape[-1]
    shapes = [(len(groups(None)), rows, 2, size, size) for rows, _, groups, _ in parts]
    copy_count = sum(len(starts(None)) * len(groups(None)) for _, starts, groups, _ in parts)
    steps = sorted({step for _, _, _, step in parts})
    operands = [factor.reshape(factor.shape[0], -1, step, size, size) for step in steps]

    def kernel(scal, pat, *refs):
        factor_refs = dict(zip(steps, refs))
        out_refs = refs[len(steps) + 1 : -1]
        sems = refs[-1]
        copies = []
        for (rows, starts, groups, step), out_ref in zip(parts, out_refs):
            run = rows // len(starts(scal))
            part_copies = []
            for g, column in enumerate(groups(scal)):
                for n, start in enumerate(starts(scal)):
                    place = sum(map(len, copies)) + len(part_copies)
                    part_copies.append(
                        pltpu.make_async_copy(
                            factor_refs[step].at[
                                pl.ds(start, run), pl.ds(column // step, 2), column % step
                            ],
                            out_ref.at[g, pl.ds(n * run, run)],
                            sems.at[place],
                        )
                    )
            for copy in part_copies:
                copy.start()
            copies.append(part_copies)
        for (rows, starts, groups, step), out_ref, part_copies in zip(parts, out_refs, copies):
            for copy in part_copies:
                copy.wait()
            first_rows = starts(scal)
            run = rows // len(first_rows)
            for n, start in enumerate(first_rows):

                def clear(i, carry, n=n, start=start):
                    for g, column in enumerate(groups(scal)):
                        for k in range(2):

                            @pl.when(pat[start + i, column + k * step] == 0)
                            def _():
                                out_ref[g, n * run + i, k] = jnp.zeros((size, size), jnp.bfloat16)

                    return carry

                lax.fori_loop(0, run, clear, 0)

    return pl.pallas_call(
        kernel,
        grid_spec=pltpu.PrefetchScalarGridSpec(
            num_scalar_prefetch=2,
            grid=(1,),
            in_specs=[pl.BlockSpec(memory_space=pl.ANY)] * (len(steps) + 1),
            out_specs=[pl.BlockSpec(memory_space=pltpu.VMEM)] * len(parts),
            scratch_shapes=[pltpu.SemaphoreType.DMA((copy_count,))],
        ),
        out_shape=[jax.ShapeDtypeStruct(shape, jnp.bfloat16) for shape in shapes],
        compiler_params=params(),
        cost_estimate=pl.CostEstimate(
            flops=0, bytes_accessed=sum(8 * math.prod(shape) for shape in shapes), transcendentals=0
        ),
        name="lay_out",
    )(scalars, pattern, *[pltpu.with_memory_space_constraint(operand, pltpu.HBM) for operand in operands], after)


def block_sums(parts, first_row, row_count, acc, base, negate):
    size, rhs = parts[0][1][0].shape[1:]
    rows = slice(first_row, first_row + row_count)

    def kernel(*refs):
        refs = list(refs)
        out_ref = refs.pop()
        total = jnp.zeros((row_count * size, rhs), jnp.float32)
        for blocks, values in parts:
            blocks_ref = refs.pop(0)
            place = 0
            for value in values:
                value_ref = refs.pop(0)
                for start in range(0, value.shape[0], 2):
                    right = value_ref[start : start + 2].reshape(2 * size, rhs)
                    left = jnp.concatenate([blocks_ref[place, rows, n] for n in range(2)], axis=2)
                    left = left.reshape(row_count * size, 2 * size)
                    total = total + jnp.dot(left, right, preferred_element_type=jnp.float32)
                    place += 1
        total = total.reshape(row_count, size, rhs)
        if acc is not None:
            total = total + refs.pop(0)[acc[1] : acc[1] + row_count]
        if base is not None:
            total = total - refs.pop(0)[base[1] : base[1] + row_count].astype(jnp.float32)
        out_ref[...] = (-total if negate else total).astype(out_ref.dtype)

    operands = []
    for blocks, values in parts:
        operands += [blocks, *values]
    operands += [extra[0] for extra in (acc, base) if extra is not None]
    blocks_used = 2 * row_count * sum(blocks.shape[0] for blocks, _ in parts)
    return pl.pallas_call(
        kernel,
        out_shape=jax.ShapeDtypeStruct((row_count, size, rhs), jnp.bfloat16 if negate else jnp.float32),
        compiler_params=params(),
        cost_estimate=pl.CostEstimate(
            flops=2 * blocks_used * size * size * rhs, bytes_accessed=2 * blocks_used * size * size, transcendentals=0
        ),
        name="block_sums",
    )(*operands)


def sum_and_solve(gathered, base, inverses, row_start):
    parts, rows, size, rhs = gathered.shape

    def kernel(gathered_ref, *refs):
        refs = list(refs)
        base_ref = refs.pop(0) if base is not None else None
        out_ref = refs.pop()
        for i in range(rows):
            value = gathered_ref[0, i].astype(jnp.float32)
            for part in range(1, parts):
                value = value + gathered_ref[part, i].astype(jnp.float32)
            if base is not None:
                value = value + base_ref[i].astype(jnp.float32)
            value = value.astype(jnp.bfloat16)
            for inverse_ref in refs:
                value = jnp.dot(inverse_ref[i, 0], value, preferred_element_type=jnp.float32).astype(jnp.bfloat16)
            out_ref[i] = value

    operands = [gathered]
    in_specs = [pl.BlockSpec(gathered.shape, lambda g: (0, 0, 0, 0))]
    if base is not None:
        operands.append(base)
        in_specs.append(pl.BlockSpec(base.shape, lambda g: (0, 0, 0)))
    for inverse in inverses:
        operands.append(inverse)
        in_specs.append(pl.BlockSpec((rows, 1, size, size), lambda g: (row_start // rows, 0, 0, 0)))
    return pl.pallas_call(
        kernel,
        grid=(1,),
        in_specs=in_specs,
        out_specs=pl.BlockSpec((rows, size, rhs), lambda g: (0, 0, 0)),
        out_shape=jax.ShapeDtypeStruct((rows, size, rhs), jnp.bfloat16),
        compiler_params=params(),
        cost_estimate=pl.CostEstimate(
            flops=2 * rows * size * size * rhs, bytes_accessed=2 * (parts + 2) * rows * size * rhs, transcendentals=0
        ),
        name="sum_and_solve",
    )(*operands)


def solve_blocks(inverse, values):
    count, size, rhs = values.shape

    def kernel(inverse_ref, value_ref, out_ref):
        for i in range(count):
            out_ref[i] = jnp.dot(inverse_ref[i], value_ref[i], preferred_element_type=jnp.float32).astype(jnp.bfloat16)

    return pl.pallas_call(
        kernel,
        out_shape=jax.ShapeDtypeStruct(values.shape, jnp.bfloat16),
        compiler_params=params(),
        name="solve_blocks",
    )(inverse, values)


def last_solve(scalars, start_index, own, other, inverse, solved, copies):
    count, size, rhs = own.shape

    def kernel(scal, own_ref, other_ref, inverse_ref, solved_ref, out_ref):
        for h in range(count):
            value = (own_ref[h] + other_ref[h].astype(jnp.float32)).astype(jnp.bfloat16)
            value = jnp.dot(inverse_ref[h, 0], value, preferred_element_type=jnp.float32).astype(jnp.bfloat16)
            value = jnp.where(scal[start_index] > 0, value, solved_ref[h])
            for copy in range(copies):
                out_ref[h * copies + copy] = value

    full = lambda g, scal: (0, 0, 0)
    return pl.pallas_call(
        kernel,
        grid_spec=pltpu.PrefetchScalarGridSpec(
            num_scalar_prefetch=1,
            grid=(1,),
            in_specs=[
                pl.BlockSpec(own.shape, full),
                pl.BlockSpec(other.shape, full),
                pl.BlockSpec((count, 1, size, size), lambda g, scal: (0, 0, 0, 0)),
                pl.BlockSpec((count, size, rhs), full),
            ],
            out_specs=pl.BlockSpec((count * copies, size, rhs), full),
        ),
        out_shape=jax.ShapeDtypeStruct((count * copies, size, rhs), jnp.bfloat16),
        compiler_params=params(),
        name="last_solve",
    )(scalars, own, other, inverse, solved)


def on_device(right_sides, factor, pattern, lower_inverse, upper_inverse):
    lo_n = lax.axis_size("lo")
    prow_n = lax.axis_size("hi") * lo_n
    q_n = lax.axis_size("q")
    pcol_n = q_n * lax.axis_size("s")
    row_id = lax.axis_index("hi") * lo_n + lax.axis_index("lo")
    q_id = lax.axis_index("q")
    s_id = lax.axis_index("s")
    col_id = q_id * prow_n + s_id
    row_blocks, _, col_blocks, _, size, _ = factor.shape
    rhs = right_sides.shape[1]
    per = right_sides.shape[0] // size
    spread_n = pcol_n // per
    half = row_blocks // 2
    bounds = (0, half, 3 * row_blocks // 4, 7 * row_blocks // 8, row_blocks)
    cols = tuple(q_n * b for b in bounds)
    device = lambda r, c: r * pcol_n + c
    everyone = [(r, c) for r in range(prow_n) for c in range(pcol_n)]

    is_low = row_id < prow_n // 2
    lo_id = lax.axis_index("lo")
    entries = [q_id, col_id, lo_id, is_low.astype(jnp.int32)]
    scalars = jnp.stack([jnp.asarray(v, jnp.int32) for v in entries])
    pattern = pattern.reshape(row_blocks, col_blocks)
    first_low = half // per

    def route(t, r, c):
        q, s = divmod(c, prow_n)
        up, low = divmod(r, lo_n)
        if t == 0:
            return s, q * prow_n + (1 - up) * lo_n + low
        up = (up + 1 + s // lo_n + q) % 2
        return s, (q + t) % q_n * prow_n + up * lo_n + lo_n - 1 - low

    def spread(values):
        return [
            lax.ppermute(values, ALL_AXES, [(device(r, c), device(*route(t, r, c))) for r, c in everyone])
            for t in range(q_n)
        ]

    def spread_groups(first, last):
        def groups(scal):
            ids = [lax.rem(scal[0] + (q_n - t), q_n) if scal is not None else 0 for t in range(q_n)]
            return [q_n * m + q for q in ids for m in range(first, last, 2)]

        return groups

    def gather(partial):
        return lax.all_gather(partial, ROW_AXES, axis=0)

    def count(level):
        return bounds[level + 1] - bounds[level]

    def part(level, groups, step):
        return (count(level), lambda scal: [bounds[level]], groups, step)

    def laid_out(after, *parts):
        return lay_out(scalars, pattern, factor, after, parts)

    low_starts = lambda scal: [per * lax.rem(scal[2] + t, lo_n) if scal is not None else 0 for t in range(lo_n)]
    low_rows = (half, low_starts)
    late_rows = (count(2) + count(3), lambda scal: [bounds[2]])

    if per == prow_n and pcol_n & (pcol_n - 1) == 0:
        there = [(device(r, c), device(c % prow_n, r * q_n + c // prow_n)) for r, c in everyone]
        back = [(target, source) for source, target in there]
        inverse_rows = lax.dynamic_index_in_dim(
            lower_inverse[:half].reshape(first_low, per, size, size), row_id, 1, keepdims=False
        )
        inverse_rows = lax.ppermute(inverse_rows, ALL_AXES, there)
        blocks = lax.all_to_all(right_sides.reshape(per, size, rhs), ROW_AXES, 0, 0, tiled=True)
        own_zero = solve_blocks(inverse_rows, blocks[:first_low])

        def zero_groups(scal):
            ids = [scal[1] ^ t if scal is not None else 0 for t in range(pcol_n)]
            return [c + pcol_n * r for c in ids for r in range(0, first_low, 2)]

        def exchange(values, t):
            return lax.ppermute(values, ALL_AXES, [(device(r, c), device(r, c ^ t)) for r, c in everyone])

        zero = []
        for t in range(0, pcol_n, 2):
            even = exchange(own_zero, t) if t else own_zero
            zero += [even, exchange(even, 1)]
        (one_zero,) = laid_out(own_zero, part(1, zero_groups, pcol_n))
        zero_step = pcol_n

        rest = lax.ppermute(blocks, ALL_AXES, back)
        owned = (jnp.arange(per) == row_id)[None, :, None, None]
        base = jnp.where(owned, rest[:, None], jnp.zeros((), jnp.bfloat16)).reshape(row_blocks, size, rhs)
    else:
        group_rows = lax.all_gather(right_sides.reshape(per, size, rhs), COL_AXES, axis=0, tiled=True)
        picked = lax.dynamic_index_in_dim(group_rows.reshape(per, pcol_n, size, rhs), col_id, 1, keepdims=False)
        mine = lax.all_gather(picked, ROW_AXES, axis=0, tiled=True)
        own_zero = sum_and_solve(mine[None, :half], None, [lower_inverse], 0)
        zero_groups = spread_groups(0, half)
        zero_step = q_n
        (one_zero,) = laid_out(own_zero, part(1, zero_groups, zero_step))
        zero = spread(own_zero)
        base = jnp.where(row_id == 0, mine, jnp.zeros((), jnp.bfloat16))

    level_groups = [zero_groups] + [spread_groups(bounds[level], bounds[level + 1]) for level in range(1, 4)]
    partial = block_sums([(one_zero, zero)], 0, count(1), None, (base, bounds[1]), True)
    one_rows = sum_and_solve(gather(partial), None, [lower_inverse], bounds[1])
    one = spread(one_rows)
    late_zero, two_one = laid_out(one_rows, (*late_rows, zero_groups, zero_step), part(2, level_groups[1], q_n))
    late = block_sums([(late_zero, zero)], 0, count(2) + count(3), None, (base, bounds[2]), False)
    partial = block_sums([(two_one, one)], 0, count(2), (late, 0), None, True)
    two_rows = sum_and_solve(gather(partial), None, [lower_inverse], bounds[2])
    two = spread(two_rows)
    three_one, three_two, two_three = laid_out(
        two_rows,
        part(3, level_groups[1], q_n),
        part(3, level_groups[2], q_n),
        part(2, level_groups[3], q_n),
    )
    late = block_sums([(three_one, one)], 0, count(3), (late, count(2)), None, False)
    partial = block_sums([(three_two, two)], 0, count(3), (late, 0), None, True)
    three_solved = sum_and_solve(gather(partial), None, [lower_inverse, upper_inverse], bounds[3])
    three = spread(three_solved)
    one_three, one_two, zero_three = laid_out(
        three_solved, part(1, level_groups[3], q_n), part(1, level_groups[2], q_n), (*low_rows, level_groups[3], q_n)
    )
    base_zero = sum_and_solve(base[None, :half], None, [lower_inverse], 0)
    base_zero = lax.dynamic_slice_in_dim(jnp.concatenate([base_zero, base_zero]), per * lo_id, half, 0)
    partial = block_sums([(two_three, three)], 0, count(2), None, None, True)
    two_solved = sum_and_solve(gather(partial), two_rows, [upper_inverse], bounds[2])
    two = spread(two_solved)
    zero_two, zero_one = laid_out(two_solved, (*low_rows, level_groups[2], q_n), (*low_rows, level_groups[1], q_n))
    late = block_sums([(one_three, three)], 0, count(1), None, None, False)
    partial = block_sums([(one_two, two)], 0, count(1), (late, 0), None, True)
    one_solved = sum_and_solve(gather(partial), one_rows, [upper_inverse], bounds[1])
    one = spread(one_solved)
    upper = block_sums([(zero_three, three), (zero_two, two)], 0, half, None, (base_zero, 0), False)
    chunks = [block_sums([(zero_one, one)], t * per, per, (upper, t * per), None, True) for t in range(1, lo_n)]
    own = block_sums([(zero_one, one)], 0, per, (upper, 0), None, True).astype(jnp.float32)
    for t in range(1, lo_n):
        pairs = [((lo, (lo + t) % lo_n)) for lo in range(lo_n)]
        own = own + lax.ppermute(chunks[t - 1], "lo", pairs).astype(jnp.float32)
    other = lax.ppermute(own.astype(jnp.bfloat16), "hi", [(0, 1), (1, 0)])
    solved = jnp.concatenate([one_solved, two_solved, three_solved], axis=0)
    solved = lax.dynamic_slice_in_dim(solved, per * lo_id, per, 0)
    last_inverse = lax.dynamic_slice_in_dim(upper_inverse, per * lo_id, per, 0)
    slots = last_solve(scalars, 3, own, other, last_inverse, solved, spread_n)
    received = lax.all_to_all(slots, COL_AXES, 0, 0, tiled=True)
    mine = lax.dynamic_slice_in_dim(received, lax.rem(col_id, spread_n) * per, per, 0)
    return mine.reshape(per * size, rhs)


def solution(mesh):
    prow_n, pcol_n = mesh.shape["prow"], mesh.shape["pcol"]
    fine = Mesh(mesh.devices.reshape(2, prow_n // 2, pcol_n // prow_n, prow_n), ALL_AXES)
    placed = (
        P(ALL_AXES, None),
        P(None, COL_AXES, None, ROW_AXES, None, None),
        P(None, COL_AXES, None, ROW_AXES),
        P(None, COL_AXES, None, None),
        P(None, COL_AXES, None, None),
    )
    return jax.shard_map(on_device, mesh=fine, in_specs=placed, out_specs=P(ALL_AXES, None), check_vma=False)
```

time: 171 us -> 137 us (0.80)
  waiting for transfers between devices: 49.1 us -> 27.5 us
  starting transfers between devices: 31.4 us -> 48.2 us
  Pallas kernels: 37.7 us -> 21.9 us
  blocking collectives: 49 us -> 35.4 us
    ppermute x11 -> x18, starting transfers between devices: 5.87 us -> 37.5 us  [the longest x10 20.5 us: spread(): lax.ppermute(values, ALL_AXES, [(device(r, c), device(*route(t, r, c))) f...]
    all_to_all x1 -> x0, waiting for transfers between devices: 16.3 us -> none  [on_device(): zero_vals = lax.all_to_all(copies, COL_AXES, 0, 0, tiled=True)]
    pallas_call x12 -> x17, Pallas kernels: 35.2 us -> 19.2 us  [the longest x5 14.4 us: lay_out(): pl.pallas_call(kernel, grid_spec=pltpu.PrefetchScalarGridSpec(num_scalar_...]
    all_gather x5, blocking collectives: 49 us -> 35.4 us  [gather(): return lax.all_gather(partial, ROW_AXES, axis=0)]
    all_to_all x1 -> x0, starting transfers between devices: 10.4 us -> none  [on_device(): zero_vals = lax.all_to_all(copies, COL_AXES, 0, 0, tiled=True)]
    ppermute x11 -> x18, waiting for transfers between devices: 16.9 us -> 9.5 us  [the longest x10 6.69 us: spread(): lax.ppermute(values, ALL_AXES, [(device(r, c), device(*route(t, r, c))) f...]
    ppermute x1, starting transfers between devices: 2.49 us -> 0.07 us  [on_device(): other = lax.ppermute(own.astype(jnp.bfloat16), 'hi', [(0, 1), (1, 0)])]
    all_to_all x1, starting transfers between devices: 5.45 us -> 3.41 us  [on_device(): received = lax.all_to_all(slots, COL_AXES, 0, 0, tiled=True)]
  transfers between devices with their start and end apart: 17 -> 23, of which waited for: 9 -> 10; matrix products, arithmetic and copies ran while one was open for 1% -> 1% of each run, Pallas kernels for 11% -> 13%
where the time goes in v2:
time: 137 us; the launch traced here: 136 us
  starting transfers between devices  48.2 us (35%)
  blocking collectives  35.4 us (26%)
  waiting for transfers between devices  27.5 us (20%)
  Pallas kernels  21.9 us (16%)
  local copies, waits for them, and re-layouts  2.48 us (2%)
    all_gather x5, blocking collectives, gather(): return lax.all_gather(partial, ROW_AXES, axis=0)  35.4 us
    ppermute x10, starting transfers between devices, spread(): lax.ppermute(values, ALL_AXES, [(device(r, c), device(*route(t, r, c))) f...  20.5 us
    ppermute x7, starting transfers between devices, exchange(): lax.ppermute(values, ALL_AXES, [(device(r, c), device(r, c ^ t)) for r, c...  16.3 us
    pallas_call x5, Pallas kernels, lay_out(): pl.pallas_call(kernel, grid_spec=pltpu.PrefetchScalarGridSpec(num_scalar_...  14.4 us
    all_to_all x1, waiting for transfers between devices, on_device(): received = lax.all_to_all(slots, COL_AXES, 0, 0, tiled=True)  8.83 us
    ppermute x10, waiting for transfers between devices, spread(): lax.ppermute(values, ALL_AXES, [(device(r, c), device(*route(t, r, c))) f...  6.69 us
    ppermute x1, waiting for transfers between devices, on_device(): other = lax.ppermute(own.astype(jnp.bfloat16), 'hi', [(0, 1), (1, 0)])  5.62 us
    pallas_call x11, Pallas kernels, block_sums(): pl.pallas_call(kernel, out_shape=jax.ShapeDtypeStruct((row_count, size, r...  4.64 us
  transfers between devices with their start and end apart: 23, of which 10 were waited for; matrix products, arithmetic and copies ran while one was open for 1% of the time, Pallas kernels for 13%

profile of v2, /device:TPU:0, one launch (start us, length us, event | category | flops | bytes accessed | tf_op | source)
XLA Modules:
  0.0 136.3 jit_solution(10072881886562257354)
XLA Ops:
  0.0 4.2 %all-to-all-start = ((bf16[4,128,128]{2,1,0:T(8,128)(2,1)}), bf16[4,128,128]{2,1,0:T(8,128)(2,1)S(1)}, u32[]{:S(2)}, u32[]{:S(2)}) async-start(bf16[4,128,128]{2,1,0:T(8,128)(2,1)} %bitcast.40), calls=%async_computation | async-start | bytes 262144 | tf_op jit(solution)/shard_map/all_to_all | solution.py:286
  4.2 1.0 slice.10
  5.2 0.7 collective-permute-start
  5.9 3.0 %all-to-all-done = bf16[4,128,128]{2,1,0:T(8,128)(2,1)S(1)} async-done(((bf16[4,128,128]{2,1,0:T(8,128)(2,1)}), bf16[4,128,128]{2,1,0:T(8,128)(2,1)S(1)}, u32[]{:S(2)}, u32[]{:S(2)}) %all-to-all-start) | async-done | bytes 131104 | tf_op jit(solution)/shard_map/all_to_all | solution.py:286
  9.0 4.1 %collective-permute-start.2 = (bf16[2,128,128]{2,1,0:T(8,128)(2,1)S(1)}, bf16[2,128,128]{2,1,0:T(8,128)(2,1)S(1)}, u32[]{:S(2)}, u32[]{:S(2)}) collective-permute-start(bf16[2,128,128]{2,1,0:T(8,128)(2,1)S(1)} %solve_blocks.1.refs_1_), channel_id=1, source_target_pairs={{0,2},{1,3},{2,0},{3,1},{4,6},{5,7},{6,4},{7,5},{8,10},{9,11},{10,... | collective-permute-start | bytes 196616 | tf_op jit(solution)/shard_map/ppermute | solution.py:294
  13.2 5.7 %collective-permute-start.4 = (bf16[2,128,128]{2,1,0:T(8,128)(2,1)S(1)}, bf16[2,128,128]{2,1,0:T(8,128)(2,1)S(1)}, u32[]{:S(2)}, u32[]{:S(2)}) collective-permute-start(bf16[2,128,128]{2,1,0:T(8,128)(2,1)S(1)} %solve_blocks.1.refs_1_), channel_id=1, source_target_pairs={{0,4},{1,5},{2,6},{3,7},{4,0},{5,1},{6,2},{7,3},{8,12},{9,13},{10,... | collective-permute-start | bytes 196616 | tf_op jit(solution)/shard_map/ppermute | solution.py:294
  18.8 0.7 collective-permute-start.8
  19.6 4.4 %collective-permute-start.1 = (bf16[2,128,128]{2,1,0:T(8,128)(2,1)S(1)}, bf16[2,128,128]{2,1,0:T(8,128)(2,1)S(1)}, u32[]{:S(2)}, u32[]{:S(2)}) collective-permute-start(bf16[2,128,128]{2,1,0:T(8,128)(2,1)S(1)} %solve_blocks.1.refs_1_), channel_id=1, source_target_pairs={{0,1},{1,0},{2,3},{3,2},{4,5},{5,4},{6,7},{7,6},{8,9},{9,8},{10,11... | collective-permute-start | bytes 196616 | tf_op jit(solution)/shard_map/ppermute | solution.py:294
  24.1 1.9 %collective-permute-start.5 = (bf16[2,128,128]{2,1,0:T(8,128)(2,1)S(1)}, bf16[2,128,128]{2,1,0:T(8,128)(2,1)S(1)}, u32[]{:S(2)}, u32[]{:S(2)}) collective-permute-start(bf16[2,128,128]{2,1,0:T(8,128)(2,1)S(1)} %collective-permute-done.4.refs_5_), channel_id=1, source_target_pairs={{0,1},{1,0},{2,3},{3,2},{4,5},{5,4},{6,7},{7,6},{8,9},{9,8},{10,11... | collective-permute-start | bytes 196616 | tf_op jit(solution)/shard_map/ppermute | solution.py:294
  26.2 0.7 copy-done.2
  26.9 2.9 %lay_out.5.refs_0_ = bf16[8,4,2,128,128]{4,3,2,1,0:T(8,128)(2,1)S(1)} custom-call(s32[4]{0:T(128)S(1)} %pad_add_fusion.scal, s32[16,32]{1,0:T(8,128)S(1)} %bitcast.28, bf16[16,4,8,128,128]{4,3,2,1,0:T(8,128)(2,1)} %bitcast.33, bf16[2,128,128]{2,1,0:T(8,128)(2,1)S(1)} %solve_blocks.1.refs_1_), custom_call_target="tpu_custom_call" | custom-call | bytes 8388608 | tf_op jit(solution)/shard_map/lay_out/pallas_call | solution.py:70
  30.1 2.1 %collective-permute-done.5.refs_6_ = bf16[2,128,128]{2,1,0:T(8,128)(2,1)S(1)} collective-permute-done((bf16[2,128,128]{2,1,0:T(8,128)(2,1)S(1)}, bf16[2,128,128]{2,1,0:T(8,128)(2,1)S(1)}, u32[]{:S(2)}, u32[]{:S(2)}) %collective-permute-start.5) | collective-permute-done | bytes 65568 | tf_op jit(solution)/shard_map/ppermute | solution.py:294
  32.2 0.7 collective-permute-done.7.refs_8_
  32.9 0.7 block_sums.11
  33.6 6.8 %all-gather = bf16[16,128,128]{2,1,0:T(8,128)(2,1)S(1)} all-gather(bf16[4,128,128]{2,1,0:T(8,128)(2,1)S(1)} %block_sums.11), channel_id=2, replica_groups=mesh['hi'=2,'lo'=2,'q'=2,'s'=4] {'hi','lo'}, dimensions={0}, use_global_device_ids=true | all-gather | bytes 655360 | tf_op jit(solution)/shard_map/all_gather | solution.py:264
  40.5 4.8 %collective-permute-start.10 = (bf16[4,128,128]{2,1,0:T(8,128)(2,1)S(1)}, bf16[4,128,128]{2,1,0:T(8,128)(2,1)S(1)}, u32[]{:S(2)}, u32[]{:S(2)}) collective-permute-start(bf16[4,128,128]{2,1,0:T(8,128)(2,1)S(1)} %sum_and_solve.6.refs_2_.refs_0_), channel_id=1, source_target_pairs={{0,7},{1,15},{2,21},{3,29},{4,1},{5,9},{6,19},{7,27},{8,6},{9,14},... | collective-permute-start | bytes 393224 | tf_op jit(solution)/shard_map/ppermute | solution.py:252
  45.3 0.5 collective-permute-start.9
  45.8 3.2 %lay_out.6 = (bf16[8,4,2,128,128]{4,3,2,1,0:T(8,128)(2,1)S(1)}, bf16[4,2,2,128,128]{4,3,2,1,0:T(8,128)(2,1)S(1)}) custom-call(s32[4]{0:T(128)S(1)} %pad_add_fusion.scal, s32[16,32]{1,0:T(8,128)S(1)} %bitcast.29, bf16[16,16,2,128,128]{4,3,2,1,0:T(8,128)(2,1)} %bitcast.34, bf16[16,4,8,128,128]{4,3,2,1,0:T(8,128)(2,1)} %bitcast.35, ...), custom_call_target="tpu_custom_call" | custom-call | bytes 10485760 | tf_op jit(solution)/shard_map/lay_out/pallas_call | solution.py:70
  49.0 0.7 block_sums.12.refs_3_
  49.8 2.3 %collective-permute-done.10.refs_2_ = bf16[4,128,128]{2,1,0:T(8,128)(2,1)S(1)} collective-permute-done((bf16[4,128,128]{2,1,0:T(8,128)(2,1)S(1)}, bf16[4,128,128]{2,1,0:T(8,128)(2,1)S(1)}, u32[]{:S(2)}, u32[]{:S(2)}) %collective-permute-start.10) | collective-permute-done | bytes 131104 | tf_op jit(solution)/shard_map/ppermute | solution.py:252
  52.4 6.3 %all-gather.1 = bf16[8,128,128]{2,1,0:T(8,128)(2,1)S(1)} all-gather(bf16[2,128,128]{2,1,0:T(8,128)(2,1)S(1)} %block_sums.13), channel_id=3, replica_groups=mesh['hi'=2,'lo'=2,'q'=2,'s'=4] {'hi','lo'}, dimensions={0}, use_global_device_ids=true | all-gather | bytes 327680 | tf_op jit(solution)/shard_map/all_gather | solution.py:264
  58.8 1.7 %collective-permute-start.11 = (bf16[2,128,128]{2,1,0:T(8,128)(2,1)S(1)}, bf16[2,128,128]{2,1,0:T(8,128)(2,1)S(1)}, u32[]{:S(2)}, u32[]{:S(2)}) collective-permute-start(bf16[2,128,128]{2,1,0:T(8,128)(2,1)S(1)} %sum_and_solve.7.refs_1_.refs_0_), channel_id=1, source_target_pairs={{0,2},{1,10},{2,18},{3,26},{4,6},{5,14},{6,22},{7,30},{8,3},{9,11}... | collective-permute-start | bytes 196616 | tf_op jit(solution)/shard_map/ppermute | solution.py:252
  60.5 2.9 %collective-permute-start.12 = (bf16[2,128,128]{2,1,0:T(8,128)(2,1)S(1)}, bf16[2,128,128]{2,1,0:T(8,128)(2,1)S(1)}, u32[]{:S(2)}, u32[]{:S(2)}) collective-permute-start(bf16[2,128,128]{2,1,0:T(8,128)(2,1)S(1)} %sum_and_solve.7.refs_1_.refs_0_), channel_id=1, source_target_pairs={{0,7},{1,15},{2,21},{3,29},{4,1},{5,9},{6,19},{7,27},{8,6},{9,14},... | collective-permute-start | bytes 196616 | tf_op jit(solution)/shard_map/ppermute | solution.py:252
  63.4 2.2 %lay_out.7 = (bf16[4,2,2,128,128]{4,3,2,1,0:T(8,128)(2,1)S(1)}, bf16[2,2,2,128,128]{4,3,2,1,0:T(8,128)(2,1)S(1)}, bf16[2,2,2,128,128]{4,3,2,1,0:T(8,128)(2,1)S(1)}) custom-call(s32[4]{0:T(128)S(1)} %pad_add_fusion.scal, s32[16,32]{1,0:T(8,128)S(1)} %bitcast.30, bf16[16,16,2,128,128]{4,3,2,1,0:T(8,128)(2,1)} %bitcast.36, ...), custom_call_target="tpu_custom_call" | custom-call | bytes 4194304 | tf_op jit(solution)/shard_map/lay_out/pallas_call | solution.py:70
  66.2 7.0 %all-gather.2 = bf16[8,128,128]{2,1,0:T(8,128)(2,1)S(1)} all-gather(bf16[2,128,128]{2,1,0:T(8,128)(2,1)S(1)} %block_sums.15), channel_id=4, replica_groups=mesh['hi'=2,'lo'=2,'q'=2,'s'=4] {'hi','lo'}, dimensions={0}, use_global_device_ids=true | all-gather | bytes 327680 | tf_op jit(solution)/shard_map/all_gather | solution.py:264
  73.5 0.8 collective-permute-start.13
  74.3 2.6 %collective-permute-start.14 = (bf16[2,128,128]{2,1,0:T(8,128)(2,1)S(1)}, bf16[2,128,128]{2,1,0:T(8,128)(2,1)S(1)}, u32[]{:S(2)}, u32[]{:S(2)}) collective-permute-start(bf16[2,128,128]{2,1,0:T(8,128)(2,1)S(1)} %sum_and_solve.8.refs_1_), channel_id=1, source_target_pairs={{0,7},{1,15},{2,21},{3,29},{4,1},{5,9},{6,19},{7,27},{8,6},{9,14},... | collective-permute-start | bytes 196616 | tf_op jit(solution)/shard_map/ppermute | solution.py:252
  76.9 1.0 collective-permute-done.13.refs_1_
  77.8 1.2 collective-permute-done.14.refs_2_
  79.2 7.8 %all-gather.3 = bf16[8,128,128]{2,1,0:T(8,128)(2,1)S(1)} all-gather(bf16[2,128,128]{2,1,0:T(8,128)(2,1)S(1)} %block_sums.16), channel_id=5, replica_groups=mesh['hi'=2,'lo'=2,'q'=2,'s'=4] {'hi','lo'}, dimensions={0}, use_global_device_ids=true | all-gather | bytes 327680 | tf_op jit(solution)/shard_map/all_gather | solution.py:264
  87.2 1.1 collective-permute-start.15
  88.3 3.0 %collective-permute-start.16 = (bf16[2,128,128]{2,1,0:T(8,128)(2,1)S(1)}, bf16[2,128,128]{2,1,0:T(8,128)(2,1)S(1)}, u32[]{:S(2)}, u32[]{:S(2)}) collective-permute-start(bf16[2,128,128]{2,1,0:T(8,128)(2,1)S(1)} %sum_and_solve.9.refs_1_), channel_id=1, source_target_pairs={{0,7},{1,15},{2,21},{3,29},{4,1},{5,9},{6,19},{7,27},{8,6},{9,14},... | collective-permute-start | bytes 196616 | tf_op jit(solution)/shard_map/ppermute | solution.py:252
  91.6 2.7 %lay_out.9 = (bf16[2,4,2,128,128]{4,3,2,1,0:T(8,128)(2,1)S(1)}, bf16[2,4,2,128,128]{4,3,2,1,0:T(8,128)(2,1)S(1)}, bf16[2,8,2,128,128]{4,3,2,1,0:T(8,128)(2,1)S(1)}) custom-call(s32[4]{0:T(128)S(1)} %pad_add_fusion.scal, s32[16,32]{1,0:T(8,128)S(1)} %bitcast.31, bf16[16,16,2,128,128]{4,3,2,1,0:T(8,128)(2,1)} %bitcast.37, ...), custom_call_target="tpu_custom_call" | custom-call | bytes 8388608 | tf_op jit(solution)/shard_map/lay_out/pallas_call | solution.py:70
  94.9 7.6 %all-gather.4 = bf16[16,128,128]{2,1,0:T(8,128)(2,1)S(1)} all-gather(bf16[4,128,128]{2,1,0:T(8,128)(2,1)S(1)} %block_sums.18), channel_id=6, replica_groups=mesh['hi'=2,'lo'=2,'q'=2,'s'=4] {'hi','lo'}, dimensions={0}, use_global_device_ids=true | all-gather | bytes 655360 | tf_op jit(solution)/shard_map/all_gather | solution.py:264
  102.7 1.3 collective-permute-start.17
  104.1 2.0 %collective-permute-start.18 = (bf16[4,128,128]{2,1,0:T(8,128)(2,1)S(1)}, bf16[4,128,128]{2,1,0:T(8,128)(2,1)S(1)}, u32[]{:S(2)}, u32[]{:S(2)}) collective-permute-start(bf16[4,128,128]{2,1,0:T(8,128)(2,1)S(1)} %sum_and_solve.10), channel_id=1, source_target_pairs={{0,7},{1,15},{2,21},{3,29},{4,1},{5,9},{6,19},{7,27},{8,6},{9,14},... | collective-permute-start | bytes 393224 | tf_op jit(solution)/shard_map/ppermute | solution.py:252
  106.1 3.3 %lay_out.8 = (bf16[2,8,2,128,128]{4,3,2,1,0:T(8,128)(2,1)S(1)}, bf16[4,8,2,128,128]{4,3,2,1,0:T(8,128)(2,1)S(1)}) custom-call(s32[4]{0:T(128)S(1)} %pad_add_fusion.scal, s32[16,32]{1,0:T(8,128)S(1)} %bitcast.32, bf16[16,16,2,128,128]{4,3,2,1,0:T(8,128)(2,1)} %bitcast.38, bf16[2,128,128]{2,1,0:T(8,128)(2,1)S(1)} %sum_and_solve.9.refs_1_), custom_call_target="tpu_custom_call" | custom-call | bytes 12582912 | tf_op jit(solution)/shard_map/lay_out/pallas_call | solution.py:70
  109.4 0.7 block_sums.19.refs_3_
  110.2 2.2 %collective-permute-done.18.refs_2_ = bf16[4,128,128]{2,1,0:T(8,128)(2,1)S(1)} collective-permute-done((bf16[4,128,128]{2,1,0:T(8,128)(2,1)S(1)}, bf16[4,128,128]{2,1,0:T(8,128)(2,1)S(1)}, u32[]{:S(2)}, u32[]{:S(2)}) %collective-permute-start.18) | collective-permute-done | bytes 131104 | tf_op jit(solution)/shard_map/ppermute | solution.py:252
  112.4 0.4 block_sums.21
  112.8 2.3 %collective-permute-start.19 = (bf16[4,128,128]{2,1,0:T(8,128)(2,1)S(1)}, bf16[4,128,128]{2,1,0:T(8,128)(2,1)S(1)}, u32[]{:S(2)}, u32[]{:S(2)}) collective-permute-start(bf16[4,128,128]{2,1,0:T(8,128)(2,1)S(1)} %block_sums.21), channel_id=1, source_target_pairs={{0,8},{8,0},{1,9},{9,1},{2,10},{10,2},{3,11},{11,3},{4,12},{12,4},... | collective-permute-start | bytes 393224 | tf_op jit(solution)/shard_map/ppermute | solution.py:354
  115.1 0.4 block_sums.20
  115.6 0.5 collective-permute-done.19
  116.3 5.6 %collective-permute-done.20.other_ref = bf16[4,128,128]{2,1,0:T(8,128)(2,1)S(1)} collective-permute-done((bf16[4,128,128]{2,1,0:T(8,128)(2,1)S(1)}, bf16[4,128,128]{2,1,0:T(8,128)(2,1)S(1)}, u32[]{:S(2)}, u32[]{:S(2)}) %collective-permute-start.20) | collective-permute-done | bytes 131104 | tf_op jit(solution)/shard_map/ppermute | solution.py:355
  122.0 1.4 %last_solve.1 = bf16[8,128,128]{2,1,0:T(8,128)(2,1)} custom-call(s32[4]{0:T(128)S(1)} %pad_add_fusion.scal, f32[4,128,128]{2,1,0:T(8,128)S(1)} %get-tuple-element.26.own_ref, bf16[4,128,128]{2,1,0:T(8,128)(2,1)S(1)} %collective-permute-done.20.other_ref, bf16[4,1,128,128]{3,2,1,0:T(8,128)(2,1)S(1)} %constant_dynamic-slice_fusion.1.inverse_ref, ...), custom_call_target="tpu_custom_call" | custom-call | tf_op jit(solution)/shard_map/last_solve/pallas_call | solution.py:197
  123.4 3.4 %all-to-all-start.1 = ((bf16[8,128,128]{2,1,0:T(8,128)(2,1)}), bf16[8,128,128]{2,1,0:T(8,128)(2,1)S(1)}, u32[]{:S(2)}, u32[]{:S(2)}) async-start(bf16[8,128,128]{2,1,0:T(8,128)(2,1)} %last_solve.1), calls=%async_computation.1 | async-start | bytes 524288 | tf_op jit(solution)/shard_map/all_to_all | solution.py:360
  126.8 8.8 %all-to-all-done.1 = bf16[8,128,128]{2,1,0:T(8,128)(2,1)S(1)} async-done(((bf16[8,128,128]{2,1,0:T(8,128)(2,1)}), bf16[8,128,128]{2,1,0:T(8,128)(2,1)S(1)}, u32[]{:S(2)}, u32[]{:S(2)}) %all-to-all-start.1) | async-done | bytes 262176 | tf_op jit(solution)/shard_map/all_to_all | solution.py:360
  135.6 0.7 constant_dynamic-slice_fusion
  (50 shorter events, 4.0 us)
Async XLA Ops:
  0.0 8.9 %all-to-all-start = ((bf16[4,128,128]{2,1,0:T(8,128)(2,1)}), bf16[4,128,128]{2,1,0:T(8,128)(2,1)S(1)}, u32[]{:S(2)}, u32[]{:S(2)}) async-start(bf16[4,128,128]{2,1,0:T(8,128)(2,1)} %bitcast.40), calls=%async_computation | async-start | bytes 262144 | tf_op jit(solution)/shard_map/all_to_all | solution.py:286
  5.2 3.7 %collective-permute-start = (bf16[2,128,128]{2,1,0:T(8,128)(2,1)S(1)}, bf16[2,128,128]{2,1,0:T(8,128)(2,1)S(1)}, u32[]{:S(2)}, u32[]{:S(2)}) collective-permute-start(bf16[2,128,128]{2,1,0:T(8,128)(2,1)S(1)} %dynamic-slice_bitcast_fusion), channel_id=1, source_target_pairs={{0,0},{1,8},{2,16},{3,24},{4,1},{5,9},{6,17},{7,25},{8,2},{9,10},{... | collective-permute-start | bytes 196616 | tf_op jit(solution)/shard_map/ppermute | solution.py:285
  9.0 15.0 %collective-permute-start.2 = (bf16[2,128,128]{2,1,0:T(8,128)(2,1)S(1)}, bf16[2,128,128]{2,1,0:T(8,128)(2,1)S(1)}, u32[]{:S(2)}, u32[]{:S(2)}) collective-permute-start(bf16[2,128,128]{2,1,0:T(8,128)(2,1)S(1)} %solve_blocks.1.refs_1_), channel_id=1, source_target_pairs={{0,2},{1,3},{2,0},{3,1},{4,6},{5,7},{6,4},{7,5},{8,10},{9,11},{10,... | collective-permute-start | bytes 196616 | tf_op jit(solution)/shard_map/ppermute | solution.py:294
  13.2 11.0 %collective-permute-start.4 = (bf16[2,128,128]{2,1,0:T(8,128)(2,1)S(1)}, bf16[2,128,128]{2,1,0:T(8,128)(2,1)S(1)}, u32[]{:S(2)}, u32[]{:S(2)}) collective-permute-start(bf16[2,128,128]{2,1,0:T(8,128)(2,1)S(1)} %solve_blocks.1.refs_1_), channel_id=1, source_target_pairs={{0,4},{1,5},{2,6},{3,7},{4,0},{5,1},{6,2},{7,3},{8,12},{9,13},{10,... | collective-permute-start | bytes 196616 | tf_op jit(solution)/shard_map/ppermute | solution.py:294
  18.8 7.2 %collective-permute-start.6 = (bf16[2,128,128]{2,1,0:T(8,128)(2,1)S(1)}, bf16[2,128,128]{2,1,0:T(8,128)(2,1)S(1)}, u32[]{:S(2)}, u32[]{:S(2)}) collective-permute-start(bf16[2,128,128]{2,1,0:T(8,128)(2,1)S(1)} %solve_blocks.1.refs_1_), channel_id=1, source_target_pairs={{0,6},{1,7},{2,4},{3,5},{4,2},{5,3},{6,0},{7,1},{8,14},{9,15},{10,... | collective-permute-start | bytes 196616 | tf_op jit(solution)/shard_map/ppermute | solution.py:294
  18.8 11.0 %collective-permute-start.8 = (bf16[4,128,128]{2,1,0:T(8,128)(2,1)S(1)}, bf16[4,128,128]{2,1,0:T(8,128)(2,1)S(1)}, u32[]{:S(2)}, u32[]{:S(2)}) collective-permute-start(bf16[4,128,128]{2,1,0:T(8,128)(2,1)S(1)} %all-to-all-done), channel_id=1, source_target_pairs={{0,0},{8,1},{16,2},{24,3},{1,4},{9,5},{17,6},{25,7},{2,8},{10,9},{... | collective-permute-start | bytes 393224 | tf_op jit(solution)/shard_map/ppermute | solution.py:303
  19.6 10.4 %collective-permute-start.1 = (bf16[2,128,128]{2,1,0:T(8,128)(2,1)S(1)}, bf16[2,128,128]{2,1,0:T(8,128)(2,1)S(1)}, u32[]{:S(2)}, u32[]{:S(2)}) collective-permute-start(bf16[2,128,128]{2,1,0:T(8,128)(2,1)S(1)} %solve_blocks.1.refs_1_), channel_id=1, source_target_pairs={{0,1},{1,0},{2,3},{3,2},{4,5},{5,4},{6,7},{7,6},{8,9},{9,8},{10,11... | collective-permute-start | bytes 196616 | tf_op jit(solution)/shard_map/ppermute | solution.py:294
  24.0 6.0 %collective-permute-start.3 = (bf16[2,128,128]{2,1,0:T(8,128)(2,1)S(1)}, bf16[2,128,128]{2,1,0:T(8,128)(2,1)S(1)}, u32[]{:S(2)}, u32[]{:S(2)}) collective-permute-start(bf16[2,128,128]{2,1,0:T(8,128)(2,1)S(1)} %collective-permute-done.2.refs_3_), channel_id=1, source_target_pairs={{0,1},{1,0},{2,3},{3,2},{4,5},{5,4},{6,7},{7,6},{8,9},{9,8},{10,11... | collective-permute-start | bytes 196616 | tf_op jit(solution)/shard_map/ppermute | solution.py:294
  24.1 8.1 %collective-permute-start.5 = (bf16[2,128,128]{2,1,0:T(8,128)(2,1)S(1)}, bf16[2,128,128]{2,1,0:T(8,128)(2,1)S(1)}, u32[]{:S(2)}, u32[]{:S(2)}) collective-permute-start(bf16[2,128,128]{2,1,0:T(8,128)(2,1)S(1)} %collective-permute-done.4.refs_5_), channel_id=1, source_target_pairs={{0,1},{1,0},{2,3},{3,2},{4,5},{5,4},{6,7},{7,6},{8,9},{9,8},{10,11... | collective-permute-start | bytes 196616 | tf_op jit(solution)/shard_map/ppermute | solution.py:294
  26.1 6.8 %collective-permute-start.7 = (bf16[2,128,128]{2,1,0:T(8,128)(2,1)S(1)}, bf16[2,128,128]{2,1,0:T(8,128)(2,1)S(1)}, u32[]{:S(2)}, u32[]{:S(2)}) collective-permute-start(bf16[2,128,128]{2,1,0:T(8,128)(2,1)S(1)} %collective-permute-done.6.refs_7_), channel_id=1, source_target_pairs={{0,1},{1,0},{2,3},{3,2},{4,5},{5,4},{6,7},{7,6},{8,9},{9,8},{10,11... | collective-permute-start | bytes 196616 | tf_op jit(solution)/shard_map/ppermute | solution.py:294
  26.2 0.7 copy-start.2
  30.0 10.3 %copy-start = (bf16[16,1,128,128]{3,2,1,0:T(8,128)(2,1)S(1)}, bf16[16,1,128,128]{3,2,1,0:T(8,128)(2,1)}, u32[]{:S(2)}) copy-start(bf16[16,1,128,128]{3,2,1,0:T(8,128)(2,1)} %refs_0_.7) | copy-start | bytes 1572868
  30.0 15.8 %copy-start.3 = (s32[16,1,32,1]{2,3,1,0:T(1,128)S(1)}, s32[16,1,32,1]{2,3,1,0:T(1,128)}, u32[]{:S(2)}) copy-start(s32[16,1,32,1]{2,3,1,0:T(1,128)} %param.7) | copy-start | bytes 6148
  40.5 11.5 %collective-permute-start.10 = (bf16[4,128,128]{2,1,0:T(8,128)(2,1)S(1)}, bf16[4,128,128]{2,1,0:T(8,128)(2,1)S(1)}, u32[]{:S(2)}, u32[]{:S(2)}) collective-permute-start(bf16[4,128,128]{2,1,0:T(8,128)(2,1)S(1)} %sum_and_solve.6.refs_2_.refs_0_), channel_id=1, source_target_pairs={{0,7},{1,15},{2,21},{3,29},{4,1},{5,9},{6,19},{7,27},{8,6},{9,14},... | collective-permute-start | bytes 393224 | tf_op jit(solution)/shard_map/ppermute | solution.py:252
  45.3 6.8 %collective-permute-start.9 = (bf16[4,128,128]{2,1,0:T(8,128)(2,1)S(1)}, bf16[4,128,128]{2,1,0:T(8,128)(2,1)S(1)}, u32[]{:S(2)}, u32[]{:S(2)}) collective-permute-start(bf16[4,128,128]{2,1,0:T(8,128)(2,1)S(1)} %sum_and_solve.6.refs_2_.refs_0_), channel_id=1, source_target_pairs={{0,2},{1,10},{2,18},{3,26},{4,6},{5,14},{6,22},{7,30},{8,3},{9,11}... | collective-permute-start | bytes 393224 | tf_op jit(solution)/shard_map/ppermute | solution.py:252
  58.8 7.1 %collective-permute-start.11 = (bf16[2,128,128]{2,1,0:T(8,128)(2,1)S(1)}, bf16[2,128,128]{2,1,0:T(8,128)(2,1)S(1)}, u32[]{:S(2)}, u32[]{:S(2)}) collective-permute-start(bf16[2,128,128]{2,1,0:T(8,128)(2,1)S(1)} %sum_and_solve.7.refs_1_.refs_0_), channel_id=1, source_target_pairs={{0,2},{1,10},{2,18},{3,26},{4,6},{5,14},{6,22},{7,30},{8,3},{9,11}... | collective-permute-start | bytes 196616 | tf_op jit(solution)/shard_map/ppermute | solution.py:252
  60.5 5.5 %collective-permute-start.12 = (bf16[2,128,128]{2,1,0:T(8,128)(2,1)S(1)}, bf16[2,128,128]{2,1,0:T(8,128)(2,1)S(1)}, u32[]{:S(2)}, u32[]{:S(2)}) collective-permute-start(bf16[2,128,128]{2,1,0:T(8,128)(2,1)S(1)} %sum_and_solve.7.refs_1_.refs_0_), channel_id=1, source_target_pairs={{0,7},{1,15},{2,21},{3,29},{4,1},{5,9},{6,19},{7,27},{8,6},{9,14},... | collective-permute-start | bytes 196616 | tf_op jit(solution)/shard_map/ppermute | solution.py:252
  65.6 7.6 %copy-start.1 = (bf16[16,1,128,128]{3,2,1,0:T(8,128)(2,1)S(1)}, bf16[16,1,128,128]{3,2,1,0:T(8,128)(2,1)}, u32[]{:S(2)}) copy-start(bf16[16,1,128,128]{3,2,1,0:T(8,128)(2,1)} %refs_1_.5) | copy-start | bytes 1572868
  73.5 4.3 %collective-permute-start.13 = (bf16[2,128,128]{2,1,0:T(8,128)(2,1)S(1)}, bf16[2,128,128]{2,1,0:T(8,128)(2,1)S(1)}, u32[]{:S(2)}, u32[]{:S(2)}) collective-permute-start(bf16[2,128,128]{2,1,0:T(8,128)(2,1)S(1)} %sum_and_solve.8.refs_1_), channel_id=1, source_target_pairs={{0,2},{1,10},{2,18},{3,26},{4,6},{5,14},{6,22},{7,30},{8,3},{9,11}... | collective-permute-start | bytes 196616 | tf_op jit(solution)/shard_map/ppermute | solution.py:252
  74.3 4.7 %collective-permute-start.14 = (bf16[2,128,128]{2,1,0:T(8,128)(2,1)S(1)}, bf16[2,128,128]{2,1,0:T(8,128)(2,1)S(1)}, u32[]{:S(2)}, u32[]{:S(2)}) collective-permute-start(bf16[2,128,128]{2,1,0:T(8,128)(2,1)S(1)} %sum_and_solve.8.refs_1_), channel_id=1, source_target_pairs={{0,7},{1,15},{2,21},{3,29},{4,1},{5,9},{6,19},{7,27},{8,6},{9,14},... | collective-permute-start | bytes 196616 | tf_op jit(solution)/shard_map/ppermute | solution.py:252
  87.2 7.4 %collective-permute-start.15 = (bf16[2,128,128]{2,1,0:T(8,128)(2,1)S(1)}, bf16[2,128,128]{2,1,0:T(8,128)(2,1)S(1)}, u32[]{:S(2)}, u32[]{:S(2)}) collective-permute-start(bf16[2,128,128]{2,1,0:T(8,128)(2,1)S(1)} %sum_and_solve.9.refs_1_), channel_id=1, source_target_pairs={{0,2},{1,10},{2,18},{3,26},{4,6},{5,14},{6,22},{7,30},{8,3},{9,11}... | collective-permute-start | bytes 196616 | tf_op jit(solution)/shard_map/ppermute | solution.py:252
  88.3 6.3 %collective-permute-start.16 = (bf16[2,128,128]{2,1,0:T(8,128)(2,1)S(1)}, bf16[2,128,128]{2,1,0:T(8,128)(2,1)S(1)}, u32[]{:S(2)}, u32[]{:S(2)}) collective-permute-start(bf16[2,128,128]{2,1,0:T(8,128)(2,1)S(1)} %sum_and_solve.9.refs_1_), channel_id=1, source_target_pairs={{0,7},{1,15},{2,21},{3,29},{4,1},{5,9},{6,19},{7,27},{8,6},{9,14},... | collective-permute-start | bytes 196616 | tf_op jit(solution)/shard_map/ppermute | solution.py:252
  102.7 7.4 %collective-permute-start.17 = (bf16[4,128,128]{2,1,0:T(8,128)(2,1)S(1)}, bf16[4,128,128]{2,1,0:T(8,128)(2,1)S(1)}, u32[]{:S(2)}, u32[]{:S(2)}) collective-permute-start(bf16[4,128,128]{2,1,0:T(8,128)(2,1)S(1)} %sum_and_solve.10), channel_id=1, source_target_pairs={{0,2},{1,10},{2,18},{3,26},{4,6},{5,14},{6,22},{7,30},{8,3},{9,11}... | collective-permute-start | bytes 393224 | tf_op jit(solution)/shard_map/ppermute | solution.py:252
  104.1 8.3 %collective-permute-start.18 = (bf16[4,128,128]{2,1,0:T(8,128)(2,1)S(1)}, bf16[4,128,128]{2,1,0:T(8,128)(2,1)S(1)}, u32[]{:S(2)}, u32[]{:S(2)}) collective-permute-start(bf16[4,128,128]{2,1,0:T(8,128)(2,1)S(1)} %sum_and_solve.10), channel_id=1, source_target_pairs={{0,7},{1,15},{2,21},{3,29},{4,1},{5,9},{6,19},{7,27},{8,6},{9,14},... | collective-permute-start | bytes 393224 | tf_op jit(solution)/shard_map/ppermute | solution.py:252
  112.8 3.3 %collective-permute-start.19 = (bf16[4,128,128]{2,1,0:T(8,128)(2,1)S(1)}, bf16[4,128,128]{2,1,0:T(8,128)(2,1)S(1)}, u32[]{:S(2)}, u32[]{:S(2)}) collective-permute-start(bf16[4,128,128]{2,1,0:T(8,128)(2,1)S(1)} %block_sums.21), channel_id=1, source_target_pairs={{0,8},{8,0},{1,9},{9,1},{2,10},{10,2},{3,11},{11,3},{4,12},{12,4},... | collective-permute-start | bytes 393224 | tf_op jit(solution)/shard_map/ppermute | solution.py:354
  116.1 5.8 %collective-permute-start.20 = (bf16[4,128,128]{2,1,0:T(8,128)(2,1)S(1)}, bf16[4,128,128]{2,1,0:T(8,128)(2,1)S(1)}, u32[]{:S(2)}, u32[]{:S(2)}) collective-permute-start(bf16[4,128,128]{2,1,0:T(8,128)(2,1)S(1)} %get-tuple-element.25), channel_id=1, source_target_pairs={{0,16},{16,0},{1,17},{17,1},{2,18},{18,2},{3,19},{19,3},{4,20},{20... | collective-permute-start | bytes 393224 | tf_op jit(solution)/shard_map/ppermute | solution.py:355
  123.4 12.3 %all-to-all-start.1 = ((bf16[8,128,128]{2,1,0:T(8,128)(2,1)}), bf16[8,128,128]{2,1,0:T(8,128)(2,1)S(1)}, u32[]{:S(2)}, u32[]{:S(2)}) async-start(bf16[8,128,128]{2,1,0:T(8,128)(2,1)} %last_solve.1), calls=%async_computation.1 | async-start | bytes 524288 | tf_op jit(solution)/shard_map/all_to_all | solution.py:360

commit v3 on v2

--- a/solution.py
+++ b/solution.py
@@ -27,7 +27,7 @@
 
     def kernel(scal, pat, *refs):
         factor_refs = dict(zip(steps, refs))
-        out_refs = refs[len(steps) + 1 : -1]
+        out_refs = refs[len(steps) + len(after) : -1]
         sems = refs[-1]
         copies = []
         for (rows, starts, groups, step), out_ref in zip(parts, out_refs):
@@ -49,30 +49,24 @@
                 copy.start()
             copies.append(part_copies)
         for (rows, starts, groups, step), out_ref, part_copies in zip(parts, out_refs, copies):
-            for copy in part_copies:
-                copy.wait()
             first_rows = starts(scal)
             run = rows // len(first_rows)
-            for n, start in enumerate(first_rows):
-
-                def clear(i, carry, n=n, start=start):
-                    for g, column in enumerate(groups(scal)):
+            for g, column in enumerate(groups(scal)):
+                for n, start in enumerate(first_rows):
+                    part_copies[g * len(first_rows) + n].wait()
+                    for i in range(run):
                         for k in range(2):
 
                             @pl.when(pat[start + i, column + k * step] == 0)
-                            def _():
+                            def _(g=g, n=n, i=i, k=k, run=run, out_ref=out_ref):
                                 out_ref[g, n * run + i, k] = jnp.zeros((size, size), jnp.bfloat16)
-
-                    return carry
-
-                lax.fori_loop(0, run, clear, 0)
 
     return pl.pallas_call(
         kernel,
         grid_spec=pltpu.PrefetchScalarGridSpec(
             num_scalar_prefetch=2,
             grid=(1,),
-            in_specs=[pl.BlockSpec(memory_space=pl.ANY)] * (len(steps) + 1),
+            in_specs=[pl.BlockSpec(memory_space=pl.ANY)] * (len(steps) + len(after)),
             out_specs=[pl.BlockSpec(memory_space=pltpu.VMEM)] * len(parts),
             scratch_shapes=[pltpu.SemaphoreType.DMA((copy_count,))],
         ),
@@ -82,7 +76,7 @@
             flops=0, bytes_accessed=sum(8 * math.prod(shape) for shape in shapes), transcendentals=0
         ),
         name="lay_out",
-    )(scalars, pattern, *[pltpu.with_memory_space_constraint(operand, pltpu.HBM) for operand in operands], after)
+    )(scalars, pattern, *[pltpu.with_memory_space_constraint(operand, pltpu.HBM) for operand in operands], *after)
 
 
 def block_sums(parts, first_row, row_count, acc, base, negate):
@@ -127,59 +121,82 @@
     )(*operands)
 
 
-def sum_and_solve(gathered, base, inverses, row_start):
-    parts, rows, size, rhs = gathered.shape
-
-    def kernel(gathered_ref, *refs):
-        refs = list(refs)
-        base_ref = refs.pop(0) if base is not None else None
-        out_ref = refs.pop()
+def sum_and_solve(terms, inverses, row_start):
+    rows, size, rhs = terms[0].shape
+    term_count = len(terms)
+
+    def kernel(*refs):
+        term_refs = refs[:term_count]
+        inverse_refs = refs[term_count:-1]
         for i in range(rows):
-            value = gathered_ref[0, i].astype(jnp.float32)
-            for part in range(1, parts):
-                value = value + gathered_ref[part, i].astype(jnp.float32)
-            if base is not None:
-                value = value + base_ref[i].astype(jnp.float32)
+            value = term_refs[0][i].astype(jnp.float32)
+            for ref in term_refs[1:]:
+                value = value + ref[i].astype(jnp.float32)
             value = value.astype(jnp.bfloat16)
-            for inverse_ref in refs:
+            for inverse_ref in inverse_refs:
                 value = jnp.dot(inverse_ref[i, 0], value, preferred_element_type=jnp.float32).astype(jnp.bfloat16)
-            out_ref[i] = value
-
-    operands = [gathered]
-    in_specs = [pl.BlockSpec(gathered.shape, lambda g: (0, 0, 0, 0))]
-    if base is not None:
-        operands.append(base)
-        in_specs.append(pl.BlockSpec(base.shape, lambda g: (0, 0, 0)))
-    for inverse in inverses:
-        operands.append(inverse)
-        in_specs.append(pl.BlockSpec((rows, 1, size, size), lambda g: (row_start // rows, 0, 0, 0)))
+            refs[-1][i] = value
+
+    whole = pl.BlockSpec((rows, size, rhs), lambda g: (0, 0, 0))
+    inverse = pl.BlockSpec((rows, 1, size, size), lambda g: (row_start // rows, 0, 0, 0))
     return pl.pallas_call(
         kernel,
         grid=(1,),
-        in_specs=in_specs,
-        out_specs=pl.BlockSpec((rows, size, rhs), lambda g: (0, 0, 0)),
+        in_specs=[whole] * term_count + [inverse] * len(inverses),
+        out_specs=whole,
         out_shape=jax.ShapeDtypeStruct((rows, size, rhs), jnp.bfloat16),
         compiler_params=params(),
         cost_estimate=pl.CostEstimate(
-            flops=2 * rows * size * size * rhs, bytes_accessed=2 * (parts + 2) * rows * size * rhs, transcendentals=0
+            flops=2 * rows * size * size * rhs, bytes_accessed=2 * (term_count + 2) * rows * size * rhs, transcendentals=0
         ),
         name="sum_and_solve",
-    )(*operands)
-
-
-def solve_blocks(inverse, values):
+    )(*terms, *inverses)
+
+
+def solve_blocks(inverse, values, after):
     count, size, rhs = values.shape
 
-    def kernel(inverse_ref, value_ref, out_ref):
+    def kernel(inverse_ref, value_ref, *refs):
+        out_ref = refs[-1]
         for i in range(count):
             out_ref[i] = jnp.dot(inverse_ref[i], value_ref[i], preferred_element_type=jnp.float32).astype(jnp.bfloat16)
 
     return pl.pallas_call(
         kernel,
+        in_specs=[pl.BlockSpec(memory_space=pltpu.VMEM)] * 2 + [pl.BlockSpec(memory_space=pl.ANY)] * len(after),
         out_shape=jax.ShapeDtypeStruct(values.shape, jnp.bfloat16),
         compiler_params=params(),
         name="solve_blocks",
-    )(inverse, values)
+    )(inverse, values, *after)
+
+
+def low_base(scalars, zero, keep, per, q_n, lo_n):
+    chunks, size, rhs = zero[0].shape
+    scalars = jnp.concatenate([scalars, keep[None].astype(jnp.int32)])
+
+    def kernel(scal, *refs):
+        out_ref = refs[-1]
+        for h in range(per):
+            source = scal[1] ^ (h * q_n + scal[0])
+            for r in range(chunks):
+                value = jnp.zeros((size, rhs), jnp.bfloat16)
+                for t, ref in enumerate(refs[:-1]):
+                    value = jnp.where((source == t) & (scal[4] > 0), ref[r], value)
+                place = lax.rem(r + lo_n - scal[2], lo_n)
+                out_ref[place * per + h] = value
+
+    return pl.pallas_call(
+        kernel,
+        grid_spec=pltpu.PrefetchScalarGridSpec(
+            num_scalar_prefetch=1,
+            grid=(1,),
+            in_specs=[pl.BlockSpec(memory_space=pltpu.VMEM)] * len(zero),
+            out_specs=pl.BlockSpec(memory_space=pltpu.VMEM),
+        ),
+        out_shape=jax.ShapeDtypeStruct((chunks * per, size, rhs), jnp.bfloat16),
+        compiler_params=params(),
+        name="low_base",
+    )(scalars, *zero)
 
 
 def last_solve(scalars, start_index, own, other, inverse, solved, copies):
@@ -250,8 +267,8 @@
     def spread(values):
         return [
             lax.ppermute(values, ALL_AXES, [(device(r, c), device(*route(t, r, c))) for r, c in everyone])
-            for t in range(q_n)
-        ]
+            for t in reversed(range(q_n))
+        ][::-1]
 
     def spread_groups(first, last):
         def groups(scal):
@@ -260,8 +277,15 @@
 
         return groups
 
-    def gather(partial):
-        return lax.all_gather(partial, ROW_AXES, axis=0)
+    def summands(partial):
+        step = 1
+        while True:
+            pairs = [(device(r, c), device(r ^ step, c)) for r, c in everyone]
+            other = lax.ppermute(partial, ALL_AXES, pairs)
+            step *= 2
+            if step == prow_n:
+                return [partial, other]
+            partial = partial + other
 
     def count(level):
         return bounds[level + 1] - bounds[level]
@@ -277,14 +301,17 @@
     late_rows = (count(2) + count(3), lambda scal: [bounds[2]])
 
     if per == prow_n and pcol_n & (pcol_n - 1) == 0:
-        there = [(device(r, c), device(c % prow_n, r * q_n + c // prow_n)) for r, c in everyone]
+
+        def chunk(r, c):
+            q, s = c // prow_n, c % prow_n
+            return (r // lo_n + s // lo_n + 1 + q) % 2 * lo_n + r % lo_n
+
+        there = [(device(r, c), device(c % prow_n, chunk(r, c) * q_n + c // prow_n)) for r, c in everyone]
         back = [(target, source) for source, target in there]
+        chunk_id = chunk(row_id, col_id)
         inverse_rows = lax.dynamic_index_in_dim(
-            lower_inverse[:half].reshape(first_low, per, size, size), row_id, 1, keepdims=False
+            lower_inverse[:half].reshape(first_low, per, size, size), chunk_id, 1, keepdims=False
         )
-        inverse_rows = lax.ppermute(inverse_rows, ALL_AXES, there)
-        blocks = lax.all_to_all(right_sides.reshape(per, size, rhs), ROW_AXES, 0, 0, tiled=True)
-        own_zero = solve_blocks(inverse_rows, blocks[:first_low])
 
         def zero_groups(scal):
             ids = [scal[1] ^ t if scal is not None else 0 for t in range(pcol_n)]
@@ -293,58 +320,63 @@
         def exchange(values, t):
             return lax.ppermute(values, ALL_AXES, [(device(r, c), device(r, c ^ t)) for r, c in everyone])
 
+        inverse_rows, blocks = lax.optimization_barrier((inverse_rows, right_sides.reshape(per, size, rhs)))
+        (one_zero,) = laid_out([inverse_rows], part(1, zero_groups, pcol_n))
+        inverse_rows = lax.ppermute(inverse_rows, ALL_AXES, there)
+        blocks = lax.all_to_all(blocks, ROW_AXES, 0, 0, tiled=True)
+        rest = lax.ppermute(blocks[first_low:], ALL_AXES, back)
+        own_zero = solve_blocks(inverse_rows, blocks[:first_low], [one_zero])
+        even = {t: exchange(own_zero, t) for t in range(pcol_n - 2, 0, -2)}
+        even[0] = own_zero
         zero = []
         for t in range(0, pcol_n, 2):
-            even = exchange(own_zero, t) if t else own_zero
-            zero += [even, exchange(even, 1)]
-        (one_zero,) = laid_out(own_zero, part(1, zero_groups, pcol_n))
+            zero += [even[t], exchange(even[t], 1)]
         zero_step = pcol_n
 
-        rest = lax.ppermute(blocks, ALL_AXES, back)
-        owned = (jnp.arange(per) == row_id)[None, :, None, None]
-        base = jnp.where(owned, rest[:, None], jnp.zeros((), jnp.bfloat16)).reshape(row_blocks, size, rhs)
+        owned = (jnp.arange(per) == chunk_id)[None, :, None, None]
+        base = jnp.where(owned, rest[:, None], jnp.zeros((), jnp.bfloat16)).reshape(row_blocks - half, size, rhs)
+        base_zero = low_base(scalars, zero, row_id == s_id, per, q_n, lo_n)
     else:
         group_rows = lax.all_gather(right_sides.reshape(per, size, rhs), COL_AXES, axis=0, tiled=True)
         picked = lax.dynamic_index_in_dim(group_rows.reshape(per, pcol_n, size, rhs), col_id, 1, keepdims=False)
         mine = lax.all_gather(picked, ROW_AXES, axis=0, tiled=True)
-        own_zero = sum_and_solve(mine[None, :half], None, [lower_inverse], 0)
+        own_zero = sum_and_solve([mine[:half]], [lower_inverse], 0)
         zero_groups = spread_groups(0, half)
         zero_step = q_n
-        (one_zero,) = laid_out(own_zero, part(1, zero_groups, zero_step))
+        (one_zero,) = laid_out([own_zero], part(1, zero_groups, zero_step))
         zero = spread(own_zero)
-        base = jnp.where(row_id == 0, mine, jnp.zeros((), jnp.bfloat16))
+        base = jnp.where(row_id == 0, mine[half:], jnp.zeros((), jnp.bfloat16))
+        base_zero = jnp.where(row_id == 0, own_zero, jnp.zeros((), jnp.bfloat16))
+        base_zero = lax.dynamic_slice_in_dim(jnp.concatenate([base_zero, base_zero]), per * lo_id, half, 0)
 
     level_groups = [zero_groups] + [spread_groups(bounds[level], bounds[level + 1]) for level in range(1, 4)]
-    partial = block_sums([(one_zero, zero)], 0, count(1), None, (base, bounds[1]), True)
-    one_rows = sum_and_solve(gather(partial), None, [lower_inverse], bounds[1])
+    partial = block_sums([(one_zero, zero)], 0, count(1), None, (base, 0), True)
+    one_rows = sum_and_solve(summands(partial), [lower_inverse], bounds[1])
     one = spread(one_rows)
-    late_zero, two_one = laid_out(one_rows, (*late_rows, zero_groups, zero_step), part(2, level_groups[1], q_n))
-    late = block_sums([(late_zero, zero)], 0, count(2) + count(3), None, (base, bounds[2]), False)
+    late_zero, two_one = laid_out([one_rows, base_zero], (*late_rows, zero_groups, zero_step), part(2, level_groups[1], q_n))
+    late = block_sums([(late_zero, zero)], 0, count(2) + count(3), None, (base, bounds[2] - half), False)
     partial = block_sums([(two_one, one)], 0, count(2), (late, 0), None, True)
-    two_rows = sum_and_solve(gather(partial), None, [lower_inverse], bounds[2])
+    two_rows = sum_and_solve(summands(partial), [lower_inverse], bounds[2])
     two = spread(two_rows)
-    three_one, three_two, two_three = laid_out(
-        two_rows,
-        part(3, level_groups[1], q_n),
-        part(3, level_groups[2], q_n),
-        part(2, level_groups[3], q_n),
-    )
+    three_one, three_two = laid_out([two_rows], part(3, level_groups[1], q_n), part(3, level_groups[2], q_n))
     late = block_sums([(three_one, one)], 0, count(3), (late, count(2)), None, False)
     partial = block_sums([(three_two, two)], 0, count(3), (late, 0), None, True)
-    three_solved = sum_and_solve(gather(partial), None, [lower_inverse, upper_inverse], bounds[3])
+    three_solved = sum_and_solve(summands(partial), [lower_inverse, upper_inverse], bounds[3])
     three = spread(three_solved)
-    one_three, one_two, zero_three = laid_out(
-        three_solved, part(1, level_groups[3], q_n), part(1, level_groups[2], q_n), (*low_rows, level_groups[3], q_n)
+    two_three, one_three, one_two, zero_three = laid_out(
+        [three_solved],
+        part(2, level_groups[3], q_n),
+        part(1, level_groups[3], q_n),
+        part(1, level_groups[2], q_n),
+        (*low_rows, level_groups[3], q_n),
     )
-    base_zero = sum_and_solve(base[None, :half], None, [lower_inverse], 0)
-    base_zero = lax.dynamic_slice_in_dim(jnp.concatenate([base_zero, base_zero]), per * lo_id, half, 0)
     partial = block_sums([(two_three, three)], 0, count(2), None, None, True)
-    two_solved = sum_and_solve(gather(partial), two_rows, [upper_inverse], bounds[2])
+    two_solved = sum_and_solve(summands(partial) + [two_rows], [upper_inverse], bounds[2])
     two = spread(two_solved)
-    zero_two, zero_one = laid_out(two_solved, (*low_rows, level_groups[2], q_n), (*low_rows, level_groups[1], q_n))
+    zero_two, zero_one = laid_out([two_solved], (*low_rows, level_groups[2], q_n), (*low_rows, level_groups[1], q_n))
     late = block_sums([(one_three, three)], 0, count(1), None, None, False)
     partial = block_sums([(one_two, two)], 0, count(1), (late, 0), None, True)
-    one_solved = sum_and_solve(gather(partial), one_rows, [upper_inverse], bounds[1])
+    one_solved = sum_and_solve(summands(partial) + [one_rows], [upper_inverse], bounds[1])
     one = spread(one_solved)
     upper = block_sums([(zero_three, three), (zero_two, two)], 0, half, None, (base_zero, 0), False)
     chunks = [block_sums([(zero_one, one)], t * per, per, (upper, t * per), None, True) for t in range(1, lo_n)]

time: 137 us -> 130 us (0.949)
  blocking collectives: 35.4 us -> 0 us
  waiting for transfers between devices: 27.5 us -> 47.2 us
  starting transfers between devices: 48.2 us -> 56.9 us
  other arithmetic: 0.51 us -> 2.24 us
    all_gather x5 -> x0, blocking collectives: 35.4 us -> none  [gather(): return lax.all_gather(partial, ROW_AXES, axis=0)]
    ppermute x1 -> x11, waiting for transfers between devices: 0.01 us -> 24.1 us  [the longest x10 22.2 us: summands(): other = lax.ppermute(partial, ALL_AXES, pairs)]
    ppermute x1 -> x11, starting transfers between devices: 0.66 us -> 15.8 us  [the longest x10 12.9 us: summands(): other = lax.ppermute(partial, ALL_AXES, pairs)]
    ppermute x7, starting transfers between devices: 16.3 us -> 9.28 us  [exchange(): lax.ppermute(values, ALL_AXES, [(device(r, c), device(r, c ^ t)) for r, c...]
    ppermute x10, starting transfers between devices: 20.5 us -> 16.7 us  [spread(): lax.ppermute(values, ALL_AXES, [(device(r, c), device(*route(t, r, c))) f...]
    all_to_all x1, waiting for transfers between devices: 2.97 us -> 0.01 us  [on_device(): blocks = lax.all_to_all(blocks, ROW_AXES, 0, 0, tiled=True)]
    ppermute x1, starting transfers between devices: 0.66 us -> 3.19 us  [on_device(): inverse_rows = lax.ppermute(inverse_rows, ALL_AXES, there)]
    pallas_call x5, Pallas kernels: 14.4 us -> 12 us  [lay_out(): pl.pallas_call(kernel, grid_spec=pltpu.PrefetchScalarGridSpec(num_scalar_...]
  transfers between devices with their start and end apart: 23 -> 33, of which waited for: 10 -> 22; matrix products, arithmetic and copies ran while one was open for 1% -> 1% of each run, Pallas kernels for 13% -> 12%
where the time goes in v3:
time: 130 us
  starting transfers between devices  56.9 us (44%)
  waiting for transfers between devices  47.2 us (36%)
  Pallas kernels  20.6 us (16%)
  local copies, waits for them, and re-layouts  2.56 us (2%)
  other arithmetic  2.24 us (2%)
    ppermute x10, waiting for transfers between devices, summands(): other = lax.ppermute(partial, ALL_AXES, pairs)  22.2 us
    ppermute x10, starting transfers between devices, spread(): lax.ppermute(values, ALL_AXES, [(device(r, c), device(*route(t, r, c))) f...  16.7 us
    ppermute x10, starting transfers between devices, summands(): other = lax.ppermute(partial, ALL_AXES, pairs)  12.9 us
    pallas_call x5, Pallas kernels, lay_out(): pl.pallas_call(kernel, grid_spec=pltpu.PrefetchScalarGridSpec(num_scalar_...  12 us
    ppermute x7, starting transfers between devices, exchange(): lax.ppermute(values, ALL_AXES, [(device(r, c), device(r, c ^ t)) for r, c...  9.28 us
    all_to_all x1, waiting for transfers between devices, on_device(): received = lax.all_to_all(slots, COL_AXES, 0, 0, tiled=True)  8.84 us
    ppermute x10, waiting for transfers between devices, spread(): lax.ppermute(values, ALL_AXES, [(device(r, c), device(*route(t, r, c))) f...  7.59 us
    pallas_call x11, Pallas kernels, block_sums(): pl.pallas_call(kernel, out_shape=jax.ShapeDtypeStruct((row_count, size, r...  5.26 us
  transfers between devices with their start and end apart: 33, of which 22 were waited for; matrix products, arithmetic and copies ran while one was open for 1% of the time, Pallas kernels for 12%

profile of v3, /device:TPU:0, one launch (start us, length us, event | category | flops | bytes accessed | tf_op | source)
XLA Modules:
  0.0 129.8 jit_solution(11877387155099210243)
XLA Ops:
  0.0 1.0 slice.9
  1.0 4.2 %all-to-all-start = ((bf16[4,128,128]{2,1,0:T(8,128)(2,1)}), bf16[4,128,128]{2,1,0:T(8,128)(2,1)S(1)}, u32[]{:S(2)}, u32[]{:S(2)}) async-start(bf16[4,128,128]{2,1,0:T(8,128)(2,1)} %bitcast.29), calls=%async_computation | async-start | bytes 262144 | tf_op jit(solution)/shard_map/all_to_all | solution.py:326
  5.2 3.2 %collective-permute-start = (bf16[2,128,128]{2,1,0:T(8,128)(2,1)S(1)}, bf16[2,128,128]{2,1,0:T(8,128)(2,1)S(1)}, u32[]{:S(2)}, u32[]{:S(2)}) collective-permute-start(bf16[2,128,128]{2,1,0:T(8,128)(2,1)S(1)} %dynamic-slice_bitcast_fusion.refs_1_), channel_id=1, source_target_pairs={{0,4},{1,12},{2,16},{3,24},{4,1},{5,9},{6,21},{7,29},{8,6},{9,14},... | collective-permute-start | bytes 196616 | tf_op jit(solution)/shard_map/ppermute | solution.py:325
  9.2 2.3 %lay_out.5.refs_0_ = bf16[8,4,2,128,128]{4,3,2,1,0:T(8,128)(2,1)S(1)} custom-call(s32[4]{0:T(128)S(1)} %pad_add_fusion.scal, s32[16,32]{1,0:T(8,128)S(1)} %bitcast.17, bf16[16,4,8,128,128]{4,3,2,1,0:T(8,128)(2,1)} %bitcast.22, bf16[2,128,128]{2,1,0:T(8,128)(2,1)S(1)} %dynamic-slice_bitcast_fusion.refs_1_), custom_call_target="tpu_custom_call" | custom-call | bytes 8388608 | tf_op jit(solution)/shard_map/lay_out/pallas_call | solution.py:64
  11.7 1.9 %collective-permute-start.2 = (bf16[2,128,128]{2,1,0:T(8,128)(2,1)S(1)}, bf16[2,128,128]{2,1,0:T(8,128)(2,1)S(1)}, u32[]{:S(2)}, u32[]{:S(2)}) collective-permute-start(bf16[2,128,128]{2,1,0:T(8,128)(2,1)S(1)} %solve_blocks.1.refs_1_.refs_0_), channel_id=1, source_target_pairs={{0,2},{1,3},{2,0},{3,1},{4,6},{5,7},{6,4},{7,5},{8,10},{9,11},{10,... | collective-permute-start | bytes 196616 | tf_op jit(solution)/shard_map/ppermute | solution.py:321
  13.6 2.5 %collective-permute-start.4 = (bf16[2,128,128]{2,1,0:T(8,128)(2,1)S(1)}, bf16[2,128,128]{2,1,0:T(8,128)(2,1)S(1)}, u32[]{:S(2)}, u32[]{:S(2)}) collective-permute-start(bf16[2,128,128]{2,1,0:T(8,128)(2,1)S(1)} %solve_blocks.1.refs_1_.refs_0_), channel_id=1, source_target_pairs={{0,4},{1,5},{2,6},{3,7},{4,0},{5,1},{6,2},{7,3},{8,12},{9,13},{10,... | collective-permute-start | bytes 196616 | tf_op jit(solution)/shard_map/ppermute | solution.py:321
  16.2 2.1 %collective-permute-start.1 = (bf16[2,128,128]{2,1,0:T(8,128)(2,1)S(1)}, bf16[2,128,128]{2,1,0:T(8,128)(2,1)S(1)}, u32[]{:S(2)}, u32[]{:S(2)}) collective-permute-start(bf16[2,128,128]{2,1,0:T(8,128)(2,1)S(1)} %solve_blocks.1.refs_1_.refs_0_), channel_id=1, source_target_pairs={{0,1},{1,0},{2,3},{3,2},{4,5},{5,4},{6,7},{7,6},{8,9},{9,8},{10,11... | collective-permute-start | bytes 196616 | tf_op jit(solution)/shard_map/ppermute | solution.py:321
  18.3 2.8 %collective-permute-start.8 = (bf16[2,128,128]{2,1,0:T(8,128)(2,1)S(1)}, bf16[2,128,128]{2,1,0:T(8,128)(2,1)S(1)}, u32[]{:S(2)}, u32[]{:S(2)}) collective-permute-start(bf16[2,128,128]{2,1,0:T(8,128)(2,1)S(1)} %get-tuple-element.31), channel_id=1, source_target_pairs={{4,0},{12,1},{16,2},{24,3},{1,4},{9,5},{21,6},{29,7},{6,8},{14,9},... | collective-permute-start | bytes 196616 | tf_op jit(solution)/shard_map/ppermute | solution.py:327
  21.1 2.0 %collective-permute-start.5 = (bf16[2,128,128]{2,1,0:T(8,128)(2,1)S(1)}, bf16[2,128,128]{2,1,0:T(8,128)(2,1)S(1)}, u32[]{:S(2)}, u32[]{:S(2)}) collective-permute-start(bf16[2,128,128]{2,1,0:T(8,128)(2,1)S(1)} %collective-permute-done.4.refs_5_.refs_4_), channel_id=1, source_target_pairs={{0,1},{1,0},{2,3},{3,2},{4,5},{5,4},{6,7},{7,6},{8,9},{9,8},{10,11... | collective-permute-start | bytes 196616 | tf_op jit(solution)/shard_map/ppermute | solution.py:321
  24.0 1.8 %collective-permute-done.8 = bf16[2,128,128]{2,1,0:T(8,128)(2,1)S(1)} collective-permute-done((bf16[2,128,128]{2,1,0:T(8,128)(2,1)S(1)}, bf16[2,128,128]{2,1,0:T(8,128)(2,1)S(1)}, u32[]{:S(2)}, u32[]{:S(2)}) %collective-permute-start.8) | collective-permute-done | bytes 65568 | tf_op jit(solution)/shard_map/ppermute | solution.py:327
  28.7 1.0 collective-permute-done.9
  29.8 1.8 %collective-permute-start.10 = (bf16[4,128,128]{2,1,0:T(8,128)(2,1)S(1)}, bf16[4,128,128]{2,1,0:T(8,128)(2,1)S(1)}, u32[]{:S(2)}, u32[]{:S(2)}) collective-permute-start(bf16[4,128,128]{2,1,0:T(8,128)(2,1)S(1)} %add.72.refs_0_), channel_id=1, source_target_pairs={{0,16},{1,17},{2,18},{3,19},{4,20},{5,21},{6,22},{7,23},{8,24},{9,... | collective-permute-start | bytes 393224 | tf_op jit(solution)/shard_map/ppermute | solution.py:284
  31.6 4.0 %collective-permute-done.10.refs_1_ = bf16[4,128,128]{2,1,0:T(8,128)(2,1)S(1)} collective-permute-done((bf16[4,128,128]{2,1,0:T(8,128)(2,1)S(1)}, bf16[4,128,128]{2,1,0:T(8,128)(2,1)S(1)}, u32[]{:S(2)}, u32[]{:S(2)}) %collective-permute-start.10) | collective-permute-done | bytes 131104 | tf_op jit(solution)/shard_map/ppermute | solution.py:284
  35.8 1.9 %collective-permute-start.11 = (bf16[4,128,128]{2,1,0:T(8,128)(2,1)S(1)}, bf16[4,128,128]{2,1,0:T(8,128)(2,1)S(1)}, u32[]{:S(2)}, u32[]{:S(2)}) collective-permute-start(bf16[4,128,128]{2,1,0:T(8,128)(2,1)S(1)} %sum_and_solve.5.refs_2_), channel_id=1, source_target_pairs={{0,2},{1,10},{2,18},{3,26},{4,6},{5,14},{6,22},{7,30},{8,3},{9,11}... | collective-permute-start | bytes 393224 | tf_op jit(solution)/shard_map/ppermute | solution.py:269
  37.6 2.0 %collective-permute-start.12 = (bf16[4,128,128]{2,1,0:T(8,128)(2,1)S(1)}, bf16[4,128,128]{2,1,0:T(8,128)(2,1)S(1)}, u32[]{:S(2)}, u32[]{:S(2)}) collective-permute-start(bf16[4,128,128]{2,1,0:T(8,128)(2,1)S(1)} %sum_and_solve.5.refs_2_), channel_id=1, source_target_pairs={{0,7},{1,15},{2,21},{3,29},{4,1},{5,9},{6,19},{7,27},{8,6},{9,14},... | collective-permute-start | bytes 393224 | tf_op jit(solution)/shard_map/ppermute | solution.py:269
  40.5 2.5 %lay_out.6 = (bf16[8,4,2,128,128]{4,3,2,1,0:T(8,128)(2,1)S(1)}, bf16[4,2,2,128,128]{4,3,2,1,0:T(8,128)(2,1)S(1)}) custom-call(s32[4]{0:T(128)S(1)} %pad_add_fusion.scal, s32[16,32]{1,0:T(8,128)S(1)} %bitcast.18, bf16[16,16,2,128,128]{4,3,2,1,0:T(8,128)(2,1)} %bitcast.23, bf16[16,4,8,128,128]{4,3,2,1,0:T(8,128)(2,1)} %bitcast.24, ...), custom_call_target="tpu_custom_call" | custom-call | bytes 10485760 | tf_op jit(solution)/shard_map/lay_out/pallas_call | solution.py:64
  43.8 2.9 %collective-permute-done.12.refs_2_ = bf16[4,128,128]{2,1,0:T(8,128)(2,1)S(1)} collective-permute-done((bf16[4,128,128]{2,1,0:T(8,128)(2,1)S(1)}, bf16[4,128,128]{2,1,0:T(8,128)(2,1)S(1)}, u32[]{:S(2)}, u32[]{:S(2)}) %collective-permute-start.12) | collective-permute-done | bytes 131104 | tf_op jit(solution)/shard_map/ppermute | solution.py:269
  47.2 1.2 collective-permute-done.13
  49.1 3.6 %collective-permute-done.14.refs_1_ = bf16[2,128,128]{2,1,0:T(8,128)(2,1)S(1)} collective-permute-done((bf16[2,128,128]{2,1,0:T(8,128)(2,1)S(1)}, bf16[2,128,128]{2,1,0:T(8,128)(2,1)S(1)}, u32[]{:S(2)}, u32[]{:S(2)}) %collective-permute-start.14) | collective-permute-done | bytes 65568 | tf_op jit(solution)/shard_map/ppermute | solution.py:284
  52.8 1.2 collective-permute-start.15
  54.0 1.6 %collective-permute-start.16 = (bf16[2,128,128]{2,1,0:T(8,128)(2,1)S(1)}, bf16[2,128,128]{2,1,0:T(8,128)(2,1)S(1)}, u32[]{:S(2)}, u32[]{:S(2)}) collective-permute-start(bf16[2,128,128]{2,1,0:T(8,128)(2,1)S(1)} %sum_and_solve.6.refs_1_.refs_2_), channel_id=1, source_target_pairs={{0,7},{1,15},{2,21},{3,29},{4,1},{5,9},{6,19},{7,27},{8,6},{9,14},... | collective-permute-start | bytes 196616 | tf_op jit(solution)/shard_map/ppermute | solution.py:269
  55.6 2.0 %lay_out.7 = (bf16[4,2,2,128,128]{4,3,2,1,0:T(8,128)(2,1)S(1)}, bf16[2,2,2,128,128]{4,3,2,1,0:T(8,128)(2,1)S(1)}) custom-call(s32[4]{0:T(128)S(1)} %pad_add_fusion.scal, s32[16,32]{1,0:T(8,128)S(1)} %bitcast.19, bf16[16,16,2,128,128]{4,3,2,1,0:T(8,128)(2,1)} %bitcast.25, bf16[2,128,128]{2,1,0:T(8,128)(2,1)S(1)} %sum_and_solve.6.refs_1_.refs_2_), custom_call_target="tpu_custom_call" | custom-call | bytes 3145728 | tf_op jit(solution)/shard_map/lay_out/pallas_call | solution.py:64
  57.9 2.3 %collective-permute-done.16.refs_2_ = bf16[2,128,128]{2,1,0:T(8,128)(2,1)S(1)} collective-permute-done((bf16[2,128,128]{2,1,0:T(8,128)(2,1)S(1)}, bf16[2,128,128]{2,1,0:T(8,128)(2,1)S(1)}, u32[]{:S(2)}, u32[]{:S(2)}) %collective-permute-start.16) | collective-permute-done | bytes 65568 | tf_op jit(solution)/shard_map/ppermute | solution.py:269
  61.2 0.9 collective-permute-done.17
  62.2 1.3 %collective-permute-start.18 = (bf16[2,128,128]{2,1,0:T(8,128)(2,1)S(1)}, bf16[2,128,128]{2,1,0:T(8,128)(2,1)S(1)}, u32[]{:S(2)}, u32[]{:S(2)}) collective-permute-start(bf16[2,128,128]{2,1,0:T(8,128)(2,1)S(1)} %add.74.refs_0_), channel_id=1, source_target_pairs={{0,16},{1,17},{2,18},{3,19},{4,20},{5,21},{6,22},{7,23},{8,24},{9,... | collective-permute-start | bytes 196616 | tf_op jit(solution)/shard_map/ppermute | solution.py:284
  63.5 3.1 %collective-permute-done.18.refs_1_ = bf16[2,128,128]{2,1,0:T(8,128)(2,1)S(1)} collective-permute-done((bf16[2,128,128]{2,1,0:T(8,128)(2,1)S(1)}, bf16[2,128,128]{2,1,0:T(8,128)(2,1)S(1)}, u32[]{:S(2)}, u32[]{:S(2)}) %collective-permute-start.18) | collective-permute-done | bytes 65568 | tf_op jit(solution)/shard_map/ppermute | solution.py:284
  67.1 2.6 %collective-permute-start.20 = (bf16[2,128,128]{2,1,0:T(8,128)(2,1)S(1)}, bf16[2,128,128]{2,1,0:T(8,128)(2,1)S(1)}, u32[]{:S(2)}, u32[]{:S(2)}) collective-permute-start(bf16[2,128,128]{2,1,0:T(8,128)(2,1)S(1)} %sum_and_solve.7.refs_1_), channel_id=1, source_target_pairs={{0,7},{1,15},{2,21},{3,29},{4,1},{5,9},{6,19},{7,27},{8,6},{9,14},... | collective-permute-start | bytes 196616 | tf_op jit(solution)/shard_map/ppermute | solution.py:269
  69.7 2.5 %lay_out.8 = (bf16[2,2,2,128,128]{4,3,2,1,0:T(8,128)(2,1)S(1)}, bf16[2,4,2,128,128]{4,3,2,1,0:T(8,128)(2,1)S(1)}, bf16[2,4,2,128,128]{4,3,2,1,0:T(8,128)(2,1)S(1)}, bf16[2,8,2,128,128]{4,3,2,1,0:T(8,128)(2,1)S(1)}) custom-call(s32[4]{0:T(128)S(1)} %pad_add_fusion.scal, s32[16,32]{1,0:T(8,128)S(1)} %bitcast.20, bf16[16,16,2,128,128]{4,3,2,1,0:T(8,128)(2,1)} %bitcast.26, ...), custom_call_target="tpu_custom_call" | custom-call | bytes 9437184 | tf_op jit(solution)/shard_map/lay_out/pallas_call | solution.py:64
  72.5 1.4 %collective-permute-start.21 = (bf16[2,128,128]{2,1,0:T(8,128)(2,1)S(1)}, bf16[2,128,128]{2,1,0:T(8,128)(2,1)S(1)}, u32[]{:S(2)}, u32[]{:S(2)}) collective-permute-start(bf16[2,128,128]{2,1,0:T(8,128)(2,1)S(1)} %block_sums.16), channel_id=1, source_target_pairs={{0,8},{1,9},{2,10},{3,11},{4,12},{5,13},{6,14},{7,15},{8,0},{9,1},... | collective-permute-start | bytes 196616 | tf_op jit(solution)/shard_map/ppermute | solution.py:284
  73.9 0.9 collective-permute-done.21
  74.8 2.3 %collective-permute-start.22 = (bf16[2,128,128]{2,1,0:T(8,128)(2,1)S(1)}, bf16[2,128,128]{2,1,0:T(8,128)(2,1)S(1)}, u32[]{:S(2)}, u32[]{:S(2)}) collective-permute-start(bf16[2,128,128]{2,1,0:T(8,128)(2,1)S(1)} %add.75.refs_0_), channel_id=1, source_target_pairs={{0,16},{1,17},{2,18},{3,19},{4,20},{5,21},{6,22},{7,23},{8,24},{9,... | collective-permute-start | bytes 196616 | tf_op jit(solution)/shard_map/ppermute | solution.py:284
  77.1 2.6 %collective-permute-done.22.refs_1_ = bf16[2,128,128]{2,1,0:T(8,128)(2,1)S(1)} collective-permute-done((bf16[2,128,128]{2,1,0:T(8,128)(2,1)S(1)}, bf16[2,128,128]{2,1,0:T(8,128)(2,1)S(1)}, u32[]{:S(2)}, u32[]{:S(2)}) %collective-permute-start.22) | collective-permute-done | bytes 65568 | tf_op jit(solution)/shard_map/ppermute | solution.py:284
  80.8 2.9 %collective-permute-start.24 = (bf16[2,128,128]{2,1,0:T(8,128)(2,1)S(1)}, bf16[2,128,128]{2,1,0:T(8,128)(2,1)S(1)}, u32[]{:S(2)}, u32[]{:S(2)}) collective-permute-start(bf16[2,128,128]{2,1,0:T(8,128)(2,1)S(1)} %sum_and_solve.8.refs_1_), channel_id=1, source_target_pairs={{0,7},{1,15},{2,21},{3,29},{4,1},{5,9},{6,19},{7,27},{8,6},{9,14},... | collective-permute-start | bytes 196616 | tf_op jit(solution)/shard_map/ppermute | solution.py:269
  84.0 0.9 collective-permute-done.23.refs_1_.refs_4_
  86.1 1.4 %collective-permute-start.25 = (bf16[4,128,128]{2,1,0:T(8,128)(2,1)S(1)}, bf16[4,128,128]{2,1,0:T(8,128)(2,1)S(1)}, u32[]{:S(2)}, u32[]{:S(2)}) collective-permute-start(bf16[4,128,128]{2,1,0:T(8,128)(2,1)S(1)} %block_sums.18), channel_id=1, source_target_pairs={{0,8},{1,9},{2,10},{3,11},{4,12},{5,13},{6,14},{7,15},{8,0},{9,1},... | collective-permute-start | bytes 393224 | tf_op jit(solution)/shard_map/ppermute | solution.py:284
  87.5 1.0 collective-permute-done.25
  88.5 2.5 %collective-permute-start.26 = (bf16[4,128,128]{2,1,0:T(8,128)(2,1)S(1)}, bf16[4,128,128]{2,1,0:T(8,128)(2,1)S(1)}, u32[]{:S(2)}, u32[]{:S(2)}) collective-permute-start(bf16[4,128,128]{2,1,0:T(8,128)(2,1)S(1)} %add.76.refs_0_), channel_id=1, source_target_pairs={{0,16},{1,17},{2,18},{3,19},{4,20},{5,21},{6,22},{7,23},{8,24},{9,... | collective-permute-start | bytes 393224 | tf_op jit(solution)/shard_map/ppermute | solution.py:284
  90.9 4.0 %collective-permute-done.26.refs_1_ = bf16[4,128,128]{2,1,0:T(8,128)(2,1)S(1)} collective-permute-done((bf16[4,128,128]{2,1,0:T(8,128)(2,1)S(1)}, bf16[4,128,128]{2,1,0:T(8,128)(2,1)S(1)}, u32[]{:S(2)}, u32[]{:S(2)}) %collective-permute-start.26) | collective-permute-done | bytes 131104 | tf_op jit(solution)/shard_map/ppermute | solution.py:284
  96.0 2.5 %collective-permute-start.28 = (bf16[4,128,128]{2,1,0:T(8,128)(2,1)S(1)}, bf16[4,128,128]{2,1,0:T(8,128)(2,1)S(1)}, u32[]{:S(2)}, u32[]{:S(2)}) collective-permute-start(bf16[4,128,128]{2,1,0:T(8,128)(2,1)S(1)} %sum_and_solve.9), channel_id=1, source_target_pairs={{0,7},{1,15},{2,21},{3,29},{4,1},{5,9},{6,19},{7,27},{8,6},{9,14},... | collective-permute-start | bytes 393224 | tf_op jit(solution)/shard_map/ppermute | solution.py:269
  98.5 2.7 %lay_out.9 = (bf16[2,8,2,128,128]{4,3,2,1,0:T(8,128)(2,1)S(1)}, bf16[4,8,2,128,128]{4,3,2,1,0:T(8,128)(2,1)S(1)}) custom-call(s32[4]{0:T(128)S(1)} %pad_add_fusion.scal, s32[16,32]{1,0:T(8,128)S(1)} %bitcast.21, bf16[16,16,2,128,128]{4,3,2,1,0:T(8,128)(2,1)} %bitcast.27, bf16[2,128,128]{2,1,0:T(8,128)(2,1)S(1)} %sum_and_solve.8.refs_1_), custom_call_target="tpu_custom_call" | custom-call | bytes 12582912 | tf_op jit(solution)/shard_map/lay_out/pallas_call | solution.py:64
  102.6 1.1 block_sums.21
  103.7 3.7 %collective-permute-start.29 = (bf16[4,128,128]{2,1,0:T(8,128)(2,1)}, bf16[4,128,128]{2,1,0:T(8,128)(2,1)}, u32[]{:S(2)}, u32[]{:S(2)}) collective-permute-start(bf16[4,128,128]{2,1,0:T(8,128)(2,1)} %block_sums.21), channel_id=1, source_target_pairs={{0,8},{8,0},{1,9},{9,1},{2,10},{10,2},{3,11},{11,3},{4,12},{12,4},... | collective-permute-start | bytes 393224 | tf_op jit(solution)/shard_map/ppermute | solution.py:386
  108.7 0.9 fusion.2
  110.3 1.0 fusion.1.solved_ref
  111.3 4.2 %collective-permute-done.30.other_ref = bf16[4,128,128]{2,1,0:T(8,128)(2,1)S(1)} collective-permute-done((bf16[4,128,128]{2,1,0:T(8,128)(2,1)S(1)}, bf16[4,128,128]{2,1,0:T(8,128)(2,1)S(1)}, u32[]{:S(2)}, u32[]{:S(2)}) %collective-permute-start.30) | collective-permute-done | bytes 131104 | tf_op jit(solution)/shard_map/ppermute | solution.py:387
  115.5 1.4 %last_solve.1 = bf16[8,128,128]{2,1,0:T(8,128)(2,1)} custom-call(s32[4]{0:T(128)S(1)} %pad_add_fusion.scal, f32[4,128,128]{2,1,0:T(8,128)S(1)} %get-tuple-element.30.own_ref, bf16[4,128,128]{2,1,0:T(8,128)(2,1)S(1)} %collective-permute-done.30.other_ref, bf16[4,1,128,128]{3,2,1,0:T(8,128)(2,1)S(1)} %constant_dynamic-slice_fusion.1.inverse_ref, ...), custom_call_target="tpu_custom_call" | custom-call | tf_op jit(solution)/shard_map/last_solve/pallas_call | solution.py:214
  116.9 3.4 %all-to-all-start.1 = ((bf16[8,128,128]{2,1,0:T(8,128)(2,1)}), bf16[8,128,128]{2,1,0:T(8,128)(2,1)S(1)}, u32[]{:S(2)}, u32[]{:S(2)}) async-start(bf16[8,128,128]{2,1,0:T(8,128)(2,1)} %last_solve.1), calls=%async_computation.1 | async-start | bytes 524288 | tf_op jit(solution)/shard_map/all_to_all | solution.py:392
  120.3 8.8 %all-to-all-done.1 = bf16[8,128,128]{2,1,0:T(8,128)(2,1)S(1)} async-done(((bf16[8,128,128]{2,1,0:T(8,128)(2,1)}), bf16[8,128,128]{2,1,0:T(8,128)(2,1)S(1)}, u32[]{:S(2)}, u32[]{:S(2)}) %all-to-all-start.1) | async-done | bytes 262176 | tf_op jit(solution)/shard_map/all_to_all | solution.py:392
  (70 shorter events, 17.6 us)
Async XLA Ops:
  1.0 10.5 %all-to-all-start = ((bf16[4,128,128]{2,1,0:T(8,128)(2,1)}), bf16[4,128,128]{2,1,0:T(8,128)(2,1)S(1)}, u32[]{:S(2)}, u32[]{:S(2)}) async-start(bf16[4,128,128]{2,1,0:T(8,128)(2,1)} %bitcast.29), calls=%async_computation | async-start | bytes 262144 | tf_op jit(solution)/shard_map/all_to_all | solution.py:326
  5.2 6.3 %collective-permute-start = (bf16[2,128,128]{2,1,0:T(8,128)(2,1)S(1)}, bf16[2,128,128]{2,1,0:T(8,128)(2,1)S(1)}, u32[]{:S(2)}, u32[]{:S(2)}) collective-permute-start(bf16[2,128,128]{2,1,0:T(8,128)(2,1)S(1)} %dynamic-slice_bitcast_fusion.refs_1_), channel_id=1, source_target_pairs={{0,4},{1,12},{2,16},{3,24},{4,1},{5,9},{6,21},{7,29},{8,6},{9,14},... | collective-permute-start | bytes 196616 | tf_op jit(solution)/shard_map/ppermute | solution.py:325
  8.5 0.7 copy-start.3
  11.7 23.9 %copy-start = (bf16[16,1,128,128]{3,2,1,0:T(8,128)(2,1)S(1)}, bf16[16,1,128,128]{3,2,1,0:T(8,128)(2,1)}, u32[]{:S(2)}) copy-start(bf16[16,1,128,128]{3,2,1,0:T(8,128)(2,1)} %refs_2_.5) | copy-start | bytes 1572868
  11.7 9.3 %collective-permute-start.2 = (bf16[2,128,128]{2,1,0:T(8,128)(2,1)S(1)}, bf16[2,128,128]{2,1,0:T(8,128)(2,1)S(1)}, u32[]{:S(2)}, u32[]{:S(2)}) collective-permute-start(bf16[2,128,128]{2,1,0:T(8,128)(2,1)S(1)} %solve_blocks.1.refs_1_.refs_0_), channel_id=1, source_target_pairs={{0,2},{1,3},{2,0},{3,1},{4,6},{5,7},{6,4},{7,5},{8,10},{9,11},{10,... | collective-permute-start | bytes 196616 | tf_op jit(solution)/shard_map/ppermute | solution.py:321
  13.6 7.5 %collective-permute-start.4 = (bf16[2,128,128]{2,1,0:T(8,128)(2,1)S(1)}, bf16[2,128,128]{2,1,0:T(8,128)(2,1)S(1)}, u32[]{:S(2)}, u32[]{:S(2)}) collective-permute-start(bf16[2,128,128]{2,1,0:T(8,128)(2,1)S(1)} %solve_blocks.1.refs_1_.refs_0_), channel_id=1, source_target_pairs={{0,4},{1,5},{2,6},{3,7},{4,0},{5,1},{6,2},{7,3},{8,12},{9,13},{10,... | collective-permute-start | bytes 196616 | tf_op jit(solution)/shard_map/ppermute | solution.py:321
  16.1 7.0 %collective-permute-start.6 = (bf16[2,128,128]{2,1,0:T(8,128)(2,1)S(1)}, bf16[2,128,128]{2,1,0:T(8,128)(2,1)S(1)}, u32[]{:S(2)}, u32[]{:S(2)}) collective-permute-start(bf16[2,128,128]{2,1,0:T(8,128)(2,1)S(1)} %solve_blocks.1.refs_1_.refs_0_), channel_id=1, source_target_pairs={{0,6},{1,7},{2,4},{3,5},{4,2},{5,3},{6,0},{7,1},{8,14},{9,15},{10,... | collective-permute-start | bytes 196616 | tf_op jit(solution)/shard_map/ppermute | solution.py:321
  16.2 9.7 %collective-permute-start.1 = (bf16[2,128,128]{2,1,0:T(8,128)(2,1)S(1)}, bf16[2,128,128]{2,1,0:T(8,128)(2,1)S(1)}, u32[]{:S(2)}, u32[]{:S(2)}) collective-permute-start(bf16[2,128,128]{2,1,0:T(8,128)(2,1)S(1)} %solve_blocks.1.refs_1_.refs_0_), channel_id=1, source_target_pairs={{0,1},{1,0},{2,3},{3,2},{4,5},{5,4},{6,7},{7,6},{8,9},{9,8},{10,11... | collective-permute-start | bytes 196616 | tf_op jit(solution)/shard_map/ppermute | solution.py:321
  18.3 7.5 %collective-permute-start.8 = (bf16[2,128,128]{2,1,0:T(8,128)(2,1)S(1)}, bf16[2,128,128]{2,1,0:T(8,128)(2,1)S(1)}, u32[]{:S(2)}, u32[]{:S(2)}) collective-permute-start(bf16[2,128,128]{2,1,0:T(8,128)(2,1)S(1)} %get-tuple-element.31), channel_id=1, source_target_pairs={{4,0},{12,1},{16,2},{24,3},{1,4},{9,5},{21,6},{29,7},{6,8},{14,9},... | collective-permute-start | bytes 196616 | tf_op jit(solution)/shard_map/ppermute | solution.py:327
  21.1 4.9 %collective-permute-start.3 = (bf16[2,128,128]{2,1,0:T(8,128)(2,1)S(1)}, bf16[2,128,128]{2,1,0:T(8,128)(2,1)S(1)}, u32[]{:S(2)}, u32[]{:S(2)}) collective-permute-start(bf16[2,128,128]{2,1,0:T(8,128)(2,1)S(1)} %collective-permute-done.2.refs_3_.refs_2_), channel_id=1, source_target_pairs={{0,1},{1,0},{2,3},{3,2},{4,5},{5,4},{6,7},{7,6},{8,9},{9,8},{10,11... | collective-permute-start | bytes 196616 | tf_op jit(solution)/shard_map/ppermute | solution.py:321
  21.1 5.7 %collective-permute-start.5 = (bf16[2,128,128]{2,1,0:T(8,128)(2,1)S(1)}, bf16[2,128,128]{2,1,0:T(8,128)(2,1)S(1)}, u32[]{:S(2)}, u32[]{:S(2)}) collective-permute-start(bf16[2,128,128]{2,1,0:T(8,128)(2,1)S(1)} %collective-permute-done.4.refs_5_.refs_4_), channel_id=1, source_target_pairs={{0,1},{1,0},{2,3},{3,2},{4,5},{5,4},{6,7},{7,6},{8,9},{9,8},{10,11... | collective-permute-start | bytes 196616 | tf_op jit(solution)/shard_map/ppermute | solution.py:321
  23.1 4.4 %collective-permute-start.7 = (bf16[2,128,128]{2,1,0:T(8,128)(2,1)S(1)}, bf16[2,128,128]{2,1,0:T(8,128)(2,1)S(1)}, u32[]{:S(2)}, u32[]{:S(2)}) collective-permute-start(bf16[2,128,128]{2,1,0:T(8,128)(2,1)S(1)} %collective-permute-done.6.refs_7_.refs_6_), channel_id=1, source_target_pairs={{0,1},{1,0},{2,3},{3,2},{4,5},{5,4},{6,7},{7,6},{8,9},{9,8},{10,11... | collective-permute-start | bytes 196616 | tf_op jit(solution)/shard_map/ppermute | solution.py:321
  25.9 14.6 %copy-start.4 = (s32[16,1,32,1]{2,3,1,0:T(1,128)S(1)}, s32[16,1,32,1]{2,3,1,0:T(1,128)}, u32[]{:S(2)}) copy-start(s32[16,1,32,1]{2,3,1,0:T(1,128)} %param.7) | copy-start | bytes 6148
  28.2 1.5 %collective-permute-start.9 = (bf16[4,128,128]{2,1,0:T(8,128)(2,1)S(1)}, bf16[4,128,128]{2,1,0:T(8,128)(2,1)S(1)}, u32[]{:S(2)}, u32[]{:S(2)}) collective-permute-start(bf16[4,128,128]{2,1,0:T(8,128)(2,1)S(1)} %block_sums.11), channel_id=1, source_target_pairs={{0,8},{1,9},{2,10},{3,11},{4,12},{5,13},{6,14},{7,15},{8,0},{9,1},... | collective-permute-start | bytes 393224 | tf_op jit(solution)/shard_map/ppermute | solution.py:284
  29.8 5.8 %collective-permute-start.10 = (bf16[4,128,128]{2,1,0:T(8,128)(2,1)S(1)}, bf16[4,128,128]{2,1,0:T(8,128)(2,1)S(1)}, u32[]{:S(2)}, u32[]{:S(2)}) collective-permute-start(bf16[4,128,128]{2,1,0:T(8,128)(2,1)S(1)} %add.72.refs_0_), channel_id=1, source_target_pairs={{0,16},{1,17},{2,18},{3,19},{4,20},{5,21},{6,22},{7,23},{8,24},{9,... | collective-permute-start | bytes 393224 | tf_op jit(solution)/shard_map/ppermute | solution.py:284
  35.8 8.0 %collective-permute-start.11 = (bf16[4,128,128]{2,1,0:T(8,128)(2,1)S(1)}, bf16[4,128,128]{2,1,0:T(8,128)(2,1)S(1)}, u32[]{:S(2)}, u32[]{:S(2)}) collective-permute-start(bf16[4,128,128]{2,1,0:T(8,128)(2,1)S(1)} %sum_and_solve.5.refs_2_), channel_id=1, source_target_pairs={{0,2},{1,10},{2,18},{3,26},{4,6},{5,14},{6,22},{7,30},{8,3},{9,11}... | collective-permute-start | bytes 393224 | tf_op jit(solution)/shard_map/ppermute | solution.py:269
  37.6 9.1 %collective-permute-start.12 = (bf16[4,128,128]{2,1,0:T(8,128)(2,1)S(1)}, bf16[4,128,128]{2,1,0:T(8,128)(2,1)S(1)}, u32[]{:S(2)}, u32[]{:S(2)}) collective-permute-start(bf16[4,128,128]{2,1,0:T(8,128)(2,1)S(1)} %sum_and_solve.5.refs_2_), channel_id=1, source_target_pairs={{0,7},{1,15},{2,21},{3,29},{4,1},{5,9},{6,19},{7,27},{8,6},{9,14},... | collective-permute-start | bytes 393224 | tf_op jit(solution)/shard_map/ppermute | solution.py:269
  47.0 1.3 %collective-permute-start.13 = (bf16[2,128,128]{2,1,0:T(8,128)(2,1)S(1)}, bf16[2,128,128]{2,1,0:T(8,128)(2,1)S(1)}, u32[]{:S(2)}, u32[]{:S(2)}) collective-permute-start(bf16[2,128,128]{2,1,0:T(8,128)(2,1)S(1)} %block_sums.13), channel_id=1, source_target_pairs={{0,8},{1,9},{2,10},{3,11},{4,12},{5,13},{6,14},{7,15},{8,0},{9,1},... | collective-permute-start | bytes 196616 | tf_op jit(solution)/shard_map/ppermute | solution.py:284
  48.4 4.3 %collective-permute-start.14 = (bf16[2,128,128]{2,1,0:T(8,128)(2,1)S(1)}, bf16[2,128,128]{2,1,0:T(8,128)(2,1)S(1)}, u32[]{:S(2)}, u32[]{:S(2)}) collective-permute-start(bf16[2,128,128]{2,1,0:T(8,128)(2,1)S(1)} %add.73.refs_0_), channel_id=1, source_target_pairs={{0,16},{1,17},{2,18},{3,19},{4,20},{5,21},{6,22},{7,23},{8,24},{9,... | collective-permute-start | bytes 196616 | tf_op jit(solution)/shard_map/ppermute | solution.py:284
  52.8 5.0 %collective-permute-start.15 = (bf16[2,128,128]{2,1,0:T(8,128)(2,1)S(1)}, bf16[2,128,128]{2,1,0:T(8,128)(2,1)S(1)}, u32[]{:S(2)}, u32[]{:S(2)}) collective-permute-start(bf16[2,128,128]{2,1,0:T(8,128)(2,1)S(1)} %sum_and_solve.6.refs_1_.refs_2_), channel_id=1, source_target_pairs={{0,2},{1,10},{2,18},{3,26},{4,6},{5,14},{6,22},{7,30},{8,3},{9,11}... | collective-permute-start | bytes 196616 | tf_op jit(solution)/shard_map/ppermute | solution.py:269
  54.0 6.2 %collective-permute-start.16 = (bf16[2,128,128]{2,1,0:T(8,128)(2,1)S(1)}, bf16[2,128,128]{2,1,0:T(8,128)(2,1)S(1)}, u32[]{:S(2)}, u32[]{:S(2)}) collective-permute-start(bf16[2,128,128]{2,1,0:T(8,128)(2,1)S(1)} %sum_and_solve.6.refs_1_.refs_2_), channel_id=1, source_target_pairs={{0,7},{1,15},{2,21},{3,29},{4,1},{5,9},{6,19},{7,27},{8,6},{9,14},... | collective-permute-start | bytes 196616 | tf_op jit(solution)/shard_map/ppermute | solution.py:269
  57.6 9.0 %copy-start.1 = (bf16[16,1,128,128]{3,2,1,0:T(8,128)(2,1)S(1)}, bf16[16,1,128,128]{3,2,1,0:T(8,128)(2,1)}, u32[]{:S(2)}) copy-start(bf16[16,1,128,128]{3,2,1,0:T(8,128)(2,1)} %refs_3_.5) | copy-start | bytes 1572868
  60.4 1.7 %collective-permute-start.17 = (bf16[2,128,128]{2,1,0:T(8,128)(2,1)S(1)}, bf16[2,128,128]{2,1,0:T(8,128)(2,1)S(1)}, u32[]{:S(2)}, u32[]{:S(2)}) collective-permute-start(bf16[2,128,128]{2,1,0:T(8,128)(2,1)S(1)} %block_sums.15), channel_id=1, source_target_pairs={{0,8},{1,9},{2,10},{3,11},{4,12},{5,13},{6,14},{7,15},{8,0},{9,1},... | collective-permute-start | bytes 196616 | tf_op jit(solution)/shard_map/ppermute | solution.py:284
  62.2 4.4 %collective-permute-start.18 = (bf16[2,128,128]{2,1,0:T(8,128)(2,1)S(1)}, bf16[2,128,128]{2,1,0:T(8,128)(2,1)S(1)}, u32[]{:S(2)}, u32[]{:S(2)}) collective-permute-start(bf16[2,128,128]{2,1,0:T(8,128)(2,1)S(1)} %add.74.refs_0_), channel_id=1, source_target_pairs={{0,16},{1,17},{2,18},{3,19},{4,20},{5,21},{6,22},{7,23},{8,24},{9,... | collective-permute-start | bytes 196616 | tf_op jit(solution)/shard_map/ppermute | solution.py:284
  66.9 5.3 %collective-permute-start.19 = (bf16[2,128,128]{2,1,0:T(8,128)(2,1)S(1)}, bf16[2,128,128]{2,1,0:T(8,128)(2,1)S(1)}, u32[]{:S(2)}, u32[]{:S(2)}) collective-permute-start(bf16[2,128,128]{2,1,0:T(8,128)(2,1)S(1)} %sum_and_solve.7.refs_1_), channel_id=1, source_target_pairs={{0,2},{1,10},{2,18},{3,26},{4,6},{5,14},{6,22},{7,30},{8,3},{9,11}... | collective-permute-start | bytes 196616 | tf_op jit(solution)/shard_map/ppermute | solution.py:269
  67.1 5.1 %collective-permute-start.20 = (bf16[2,128,128]{2,1,0:T(8,128)(2,1)S(1)}, bf16[2,128,128]{2,1,0:T(8,128)(2,1)S(1)}, u32[]{:S(2)}, u32[]{:S(2)}) collective-permute-start(bf16[2,128,128]{2,1,0:T(8,128)(2,1)S(1)} %sum_and_solve.7.refs_1_), channel_id=1, source_target_pairs={{0,7},{1,15},{2,21},{3,29},{4,1},{5,9},{6,19},{7,27},{8,6},{9,14},... | collective-permute-start | bytes 196616 | tf_op jit(solution)/shard_map/ppermute | solution.py:269
  72.5 2.3 %collective-permute-start.21 = (bf16[2,128,128]{2,1,0:T(8,128)(2,1)S(1)}, bf16[2,128,128]{2,1,0:T(8,128)(2,1)S(1)}, u32[]{:S(2)}, u32[]{:S(2)}) collective-permute-start(bf16[2,128,128]{2,1,0:T(8,128)(2,1)S(1)} %block_sums.16), channel_id=1, source_target_pairs={{0,8},{1,9},{2,10},{3,11},{4,12},{5,13},{6,14},{7,15},{8,0},{9,1},... | collective-permute-start | bytes 196616 | tf_op jit(solution)/shard_map/ppermute | solution.py:284
  74.8 4.9 %collective-permute-start.22 = (bf16[2,128,128]{2,1,0:T(8,128)(2,1)S(1)}, bf16[2,128,128]{2,1,0:T(8,128)(2,1)S(1)}, u32[]{:S(2)}, u32[]{:S(2)}) collective-permute-start(bf16[2,128,128]{2,1,0:T(8,128)(2,1)S(1)} %add.75.refs_0_), channel_id=1, source_target_pairs={{0,16},{1,17},{2,18},{3,19},{4,20},{5,21},{6,22},{7,23},{8,24},{9,... | collective-permute-start | bytes 196616 | tf_op jit(solution)/shard_map/ppermute | solution.py:284
  79.9 5.0 %collective-permute-start.23 = (bf16[2,128,128]{2,1,0:T(8,128)(2,1)S(1)}, bf16[2,128,128]{2,1,0:T(8,128)(2,1)S(1)}, u32[]{:S(2)}, u32[]{:S(2)}) collective-permute-start(bf16[2,128,128]{2,1,0:T(8,128)(2,1)S(1)} %sum_and_solve.8.refs_1_), channel_id=1, source_target_pairs={{0,2},{1,10},{2,18},{3,26},{4,6},{5,14},{6,22},{7,30},{8,3},{9,11}... | collective-permute-start | bytes 196616 | tf_op jit(solution)/shard_map/ppermute | solution.py:269
  80.8 5.0 %collective-permute-start.24 = (bf16[2,128,128]{2,1,0:T(8,128)(2,1)S(1)}, bf16[2,128,128]{2,1,0:T(8,128)(2,1)S(1)}, u32[]{:S(2)}, u32[]{:S(2)}) collective-permute-start(bf16[2,128,128]{2,1,0:T(8,128)(2,1)S(1)} %sum_and_solve.8.refs_1_), channel_id=1, source_target_pairs={{0,7},{1,15},{2,21},{3,29},{4,1},{5,9},{6,19},{7,27},{8,6},{9,14},... | collective-permute-start | bytes 196616 | tf_op jit(solution)/shard_map/ppermute | solution.py:269
  86.1 2.4 %collective-permute-start.25 = (bf16[4,128,128]{2,1,0:T(8,128)(2,1)S(1)}, bf16[4,128,128]{2,1,0:T(8,128)(2,1)S(1)}, u32[]{:S(2)}, u32[]{:S(2)}) collective-permute-start(bf16[4,128,128]{2,1,0:T(8,128)(2,1)S(1)} %block_sums.18), channel_id=1, source_target_pairs={{0,8},{1,9},{2,10},{3,11},{4,12},{5,13},{6,14},{7,15},{8,0},{9,1},... | collective-permute-start | bytes 393224 | tf_op jit(solution)/shard_map/ppermute | solution.py:284
  88.5 6.5 %collective-permute-start.26 = (bf16[4,128,128]{2,1,0:T(8,128)(2,1)S(1)}, bf16[4,128,128]{2,1,0:T(8,128)(2,1)S(1)}, u32[]{:S(2)}, u32[]{:S(2)}) collective-permute-start(bf16[4,128,128]{2,1,0:T(8,128)(2,1)S(1)} %add.76.refs_0_), channel_id=1, source_target_pairs={{0,16},{1,17},{2,18},{3,19},{4,20},{5,21},{6,22},{7,23},{8,24},{9,... | collective-permute-start | bytes 393224 | tf_op jit(solution)/shard_map/ppermute | solution.py:284
  95.2 6.1 %copy-start.2 = (bf16[4,128,128]{2,1,0:T(8,128)(2,1)}, bf16[4,128,128]{2,1,0:T(8,128)(2,1)S(1)}, u32[]{:S(2)}) copy-start(bf16[4,128,128]{2,1,0:T(8,128)(2,1)S(1)} %sum_and_solve.9) | copy-start | bytes 393220
  95.2 6.8 %collective-permute-start.27 = (bf16[4,128,128]{2,1,0:T(8,128)(2,1)S(1)}, bf16[4,128,128]{2,1,0:T(8,128)(2,1)S(1)}, u32[]{:S(2)}, u32[]{:S(2)}) collective-permute-start(bf16[4,128,128]{2,1,0:T(8,128)(2,1)S(1)} %sum_and_solve.9), channel_id=1, source_target_pairs={{0,2},{1,10},{2,18},{3,26},{4,6},{5,14},{6,22},{7,30},{8,3},{9,11}... | collective-permute-start | bytes 393224 | tf_op jit(solution)/shard_map/ppermute | solution.py:269
  96.0 6.6 %collective-permute-start.28 = (bf16[4,128,128]{2,1,0:T(8,128)(2,1)S(1)}, bf16[4,128,128]{2,1,0:T(8,128)(2,1)S(1)}, u32[]{:S(2)}, u32[]{:S(2)}) collective-permute-start(bf16[4,128,128]{2,1,0:T(8,128)(2,1)S(1)} %sum_and_solve.9), channel_id=1, source_target_pairs={{0,7},{1,15},{2,21},{3,29},{4,1},{5,9},{6,19},{7,27},{8,6},{9,14},... | collective-permute-start | bytes 393224 | tf_op jit(solution)/shard_map/ppermute | solution.py:269
  103.7 5.0 %collective-permute-start.29 = (bf16[4,128,128]{2,1,0:T(8,128)(2,1)}, bf16[4,128,128]{2,1,0:T(8,128)(2,1)}, u32[]{:S(2)}, u32[]{:S(2)}) collective-permute-start(bf16[4,128,128]{2,1,0:T(8,128)(2,1)} %block_sums.21), channel_id=1, source_target_pairs={{0,8},{8,0},{1,9},{9,1},{2,10},{10,2},{3,11},{11,3},{4,12},{12,4},... | collective-permute-start | bytes 393224 | tf_op jit(solution)/shard_map/ppermute | solution.py:386
  109.6 5.8 %collective-permute-start.30 = (bf16[4,128,128]{2,1,0:T(8,128)(2,1)S(1)}, bf16[4,128,128]{2,1,0:T(8,128)(2,1)S(1)}, u32[]{:S(2)}, u32[]{:S(2)}) collective-permute-start(bf16[4,128,128]{2,1,0:T(8,128)(2,1)S(1)} %get-tuple-element.29), channel_id=1, source_target_pairs={{0,16},{16,0},{1,17},{17,1},{2,18},{18,2},{3,19},{19,3},{4,20},{20... | collective-permute-start | bytes 393224 | tf_op jit(solution)/shard_map/ppermute | solution.py:387
  116.9 12.3 %all-to-all-start.1 = ((bf16[8,128,128]{2,1,0:T(8,128)(2,1)}), bf16[8,128,128]{2,1,0:T(8,128)(2,1)S(1)}, u32[]{:S(2)}, u32[]{:S(2)}) async-start(bf16[8,128,128]{2,1,0:T(8,128)(2,1)} %last_solve.1), calls=%async_computation.1 | async-start | bytes 524288 | tf_op jit(solution)/shard_map/all_to_all | solution.py:392

commit v4 on v3

--- a/solution.py
+++ b/solution.py
@@ -121,6 +121,33 @@
     )(*operands)
 
 
+def low_sums(blocks, values, acc, chunks):
+    rows, size, rhs = acc.shape
+
+    def kernel(blocks_ref, *refs):
+        value_refs, acc_ref, out_refs = refs[: len(values)], refs[len(values)], refs[len(values) + 1 :]
+        total = acc_ref[...].reshape(rows * size, rhs)
+        place = 0
+        for value, ref in zip(values, value_refs):
+            for start in range(0, value.shape[0], 2):
+                left = jnp.concatenate([blocks_ref[place, :, n] for n in range(2)], axis=2)
+                right = ref[start : start + 2].reshape(2 * size, rhs)
+                total = total + jnp.dot(
+                    left.reshape(rows * size, 2 * size), right, preferred_element_type=jnp.float32
+                )
+                place += 1
+        total = (-total).astype(jnp.bfloat16).reshape(chunks, rows // chunks, size, rhs)
+        for n, ref in enumerate(out_refs):
+            ref[...] = total[n]
+
+    return pl.pallas_call(
+        kernel,
+        out_shape=[jax.ShapeDtypeStruct((rows // chunks, size, rhs), jnp.bfloat16)] * chunks,
+        compiler_params=params(),
+        name="low_sums",
+    )(blocks, *values, acc)
+
+
 def sum_and_solve(terms, inverses, row_start):
     rows, size, rhs = terms[0].shape
     term_count = len(terms)
@@ -278,12 +305,12 @@
         return groups
 
     def summands(partial):
-        step = 1
+        step = prow_n // 2
         while True:
             pairs = [(device(r, c), device(r ^ step, c)) for r, c in everyone]
             other = lax.ppermute(partial, ALL_AXES, pairs)
-            step *= 2
-            if step == prow_n:
+            step //= 2
+            if step == 0:
                 return [partial, other]
             partial = partial + other
 
@@ -379,8 +406,8 @@
     one_solved = sum_and_solve(summands(partial) + [one_rows], [upper_inverse], bounds[1])
     one = spread(one_solved)
     upper = block_sums([(zero_three, three), (zero_two, two)], 0, half, None, (base_zero, 0), False)
-    chunks = [block_sums([(zero_one, one)], t * per, per, (upper, t * per), None, True) for t in range(1, lo_n)]
-    own = block_sums([(zero_one, one)], 0, per, (upper, 0), None, True).astype(jnp.float32)
+    own, *chunks = low_sums(zero_one, one, upper, lo_n)
+    own = own.astype(jnp.float32)
     for t in range(1, lo_n):
         pairs = [((lo, (lo + t) % lo_n)) for lo in range(lo_n)]
         own = own + lax.ppermute(chunks[t - 1], "lo", pairs).astype(jnp.float32)

time: 130 us -> 129 us (level)
  other arithmetic: 2.24 us -> 0.44 us
    ppermute x10, starting transfers between devices: 16.7 us -> 20.5 us  [spread(): lax.ppermute(values, ALL_AXES, [(device(r, c), device(*route(t, r, c))) f...]
    ppermute x1, starting transfers between devices: 3.7 us -> 2.13 us  [on_device(): own = own + lax.ppermute(chunks[t - 1], 'lo', pairs).astype(jnp.float32)]
    pallas_call x11 -> x9, Pallas kernels: 5.26 us -> 3.72 us  [block_sums(): pl.pallas_call(kernel, out_shape=jax.ShapeDtypeStruct((row_count, size, r...]
    ppermute x1, waiting for transfers between devices: 4.15 us -> 5.62 us  [on_device(): other = lax.ppermute(own.astype(jnp.bfloat16), 'hi', [(0, 1), (1, 0)])]
    ppermute x10, waiting for transfers between devices: 7.59 us -> 6.22 us  [spread(): lax.ppermute(values, ALL_AXES, [(device(r, c), device(*route(t, r, c))) f...]
  transfers between devices with their start and end apart: 33 -> 33, of which waited for: 22 -> 20; matrix products, arithmetic and copies ran while one was open for 1% -> 0% of each run, Pallas kernels for 12% -> 12%
where the time goes in v4:
time: 129 us; the launch traced here: 128 us
  starting transfers between devices  57.9 us (45%)
  waiting for transfers between devices  47.1 us (37%)
  Pallas kernels  19.8 us (15%)
  local copies, waits for them, and re-layouts  2.57 us (2%)
    ppermute x10, waiting for transfers between devices, summands(): other = lax.ppermute(partial, ALL_AXES, pairs)  22 us
    ppermute x10, starting transfers between devices, spread(): lax.ppermute(values, ALL_AXES, [(device(r, c), device(*route(t, r, c))) f...  20.5 us
    ppermute x10, starting transfers between devices, summands(): other = lax.ppermute(partial, ALL_AXES, pairs)  12.2 us
    pallas_call x5, Pallas kernels, lay_out(): pl.pallas_call(kernel, grid_spec=pltpu.PrefetchScalarGridSpec(num_scalar_...  12.1 us
    ppermute x7, starting transfers between devices, exchange(): lax.ppermute(values, ALL_AXES, [(device(r, c), device(r, c ^ t)) for r, c...  9.29 us
    all_to_all x1, waiting for transfers between devices, on_device(): received = lax.all_to_all(slots, COL_AXES, 0, 0, tiled=True)  8.83 us
    ppermute x10, waiting for transfers between devices, spread(): lax.ppermute(values, ALL_AXES, [(device(r, c), device(*route(t, r, c))) f...  6.22 us
    ppermute x1, waiting for transfers between devices, on_device(): other = lax.ppermute(own.astype(jnp.bfloat16), 'hi', [(0, 1), (1, 0)])  5.62 us
  transfers between devices with their start and end apart: 33, of which 20 were waited for; matrix products, arithmetic and copies ran while one was open for 0% of the time, Pallas kernels for 12%

profile of v4, /device:TPU:0, one launch (start us, length us, event | category | flops | bytes accessed | tf_op | source)
XLA Modules:
  0.0 128.2 jit_solution(3071176741917810664)
XLA Ops:
  0.0 1.0 slice.9
  1.0 4.2 %all-to-all-start = ((bf16[4,128,128]{2,1,0:T(8,128)(2,1)}), bf16[4,128,128]{2,1,0:T(8,128)(2,1)S(1)}, u32[]{:S(2)}, u32[]{:S(2)}) async-start(bf16[4,128,128]{2,1,0:T(8,128)(2,1)} %bitcast.29), calls=%async_computation | async-start | bytes 262144 | tf_op jit(solution)/shard_map/all_to_all | solution.py:353
  5.2 3.2 %collective-permute-start = (bf16[2,128,128]{2,1,0:T(8,128)(2,1)S(1)}, bf16[2,128,128]{2,1,0:T(8,128)(2,1)S(1)}, u32[]{:S(2)}, u32[]{:S(2)}) collective-permute-start(bf16[2,128,128]{2,1,0:T(8,128)(2,1)S(1)} %dynamic-slice_bitcast_fusion.refs_1_), channel_id=1, source_target_pairs={{0,4},{1,12},{2,16},{3,24},{4,1},{5,9},{6,21},{7,29},{8,6},{9,14},... | collective-permute-start | bytes 196616 | tf_op jit(solution)/shard_map/ppermute | solution.py:352
  9.2 2.3 %lay_out.5.refs_0_ = bf16[8,4,2,128,128]{4,3,2,1,0:T(8,128)(2,1)S(1)} custom-call(s32[4]{0:T(128)S(1)} %pad_add_fusion.scal, s32[16,32]{1,0:T(8,128)S(1)} %bitcast.17, bf16[16,4,8,128,128]{4,3,2,1,0:T(8,128)(2,1)} %bitcast.22, bf16[2,128,128]{2,1,0:T(8,128)(2,1)S(1)} %dynamic-slice_bitcast_fusion.refs_1_), custom_call_target="tpu_custom_call" | custom-call | bytes 8388608 | tf_op jit(solution)/shard_map/lay_out/pallas_call | solution.py:64
  11.7 1.9 %collective-permute-start.2 = (bf16[2,128,128]{2,1,0:T(8,128)(2,1)S(1)}, bf16[2,128,128]{2,1,0:T(8,128)(2,1)S(1)}, u32[]{:S(2)}, u32[]{:S(2)}) collective-permute-start(bf16[2,128,128]{2,1,0:T(8,128)(2,1)S(1)} %solve_blocks.1.refs_1_.refs_0_), channel_id=1, source_target_pairs={{0,2},{1,3},{2,0},{3,1},{4,6},{5,7},{6,4},{7,5},{8,10},{9,11},{10,... | collective-permute-start | bytes 196616 | tf_op jit(solution)/shard_map/ppermute | solution.py:348
  13.6 2.5 %collective-permute-start.4 = (bf16[2,128,128]{2,1,0:T(8,128)(2,1)S(1)}, bf16[2,128,128]{2,1,0:T(8,128)(2,1)S(1)}, u32[]{:S(2)}, u32[]{:S(2)}) collective-permute-start(bf16[2,128,128]{2,1,0:T(8,128)(2,1)S(1)} %solve_blocks.1.refs_1_.refs_0_), channel_id=1, source_target_pairs={{0,4},{1,5},{2,6},{3,7},{4,0},{5,1},{6,2},{7,3},{8,12},{9,13},{10,... | collective-permute-start | bytes 196616 | tf_op jit(solution)/shard_map/ppermute | solution.py:348
  16.2 2.1 %collective-permute-start.1 = (bf16[2,128,128]{2,1,0:T(8,128)(2,1)S(1)}, bf16[2,128,128]{2,1,0:T(8,128)(2,1)S(1)}, u32[]{:S(2)}, u32[]{:S(2)}) collective-permute-start(bf16[2,128,128]{2,1,0:T(8,128)(2,1)S(1)} %solve_blocks.1.refs_1_.refs_0_), channel_id=1, source_target_pairs={{0,1},{1,0},{2,3},{3,2},{4,5},{5,4},{6,7},{7,6},{8,9},{9,8},{10,11... | collective-permute-start | bytes 196616 | tf_op jit(solution)/shard_map/ppermute | solution.py:348
  18.3 2.8 %collective-permute-start.8 = (bf16[2,128,128]{2,1,0:T(8,128)(2,1)S(1)}, bf16[2,128,128]{2,1,0:T(8,128)(2,1)S(1)}, u32[]{:S(2)}, u32[]{:S(2)}) collective-permute-start(bf16[2,128,128]{2,1,0:T(8,128)(2,1)S(1)} %get-tuple-element.35), channel_id=1, source_target_pairs={{4,0},{12,1},{16,2},{24,3},{1,4},{9,5},{21,6},{29,7},{6,8},{14,9},... | collective-permute-start | bytes 196616 | tf_op jit(solution)/shard_map/ppermute | solution.py:354
  21.1 2.0 %collective-permute-start.5 = (bf16[2,128,128]{2,1,0:T(8,128)(2,1)S(1)}, bf16[2,128,128]{2,1,0:T(8,128)(2,1)S(1)}, u32[]{:S(2)}, u32[]{:S(2)}) collective-permute-start(bf16[2,128,128]{2,1,0:T(8,128)(2,1)S(1)} %collective-permute-done.4.refs_5_.refs_4_), channel_id=1, source_target_pairs={{0,1},{1,0},{2,3},{3,2},{4,5},{5,4},{6,7},{7,6},{8,9},{9,8},{10,11... | collective-permute-start | bytes 196616 | tf_op jit(solution)/shard_map/ppermute | solution.py:348
  24.0 1.8 %collective-permute-done.8 = bf16[2,128,128]{2,1,0:T(8,128)(2,1)S(1)} collective-permute-done((bf16[2,128,128]{2,1,0:T(8,128)(2,1)S(1)}, bf16[2,128,128]{2,1,0:T(8,128)(2,1)S(1)}, u32[]{:S(2)}, u32[]{:S(2)}) %collective-permute-start.8) | collective-permute-done | bytes 65568 | tf_op jit(solution)/shard_map/ppermute | solution.py:354
  26.8 0.8 collective-permute-done.7.refs_8_.refs_7_
  28.2 1.9 %collective-permute-start.9 = (bf16[4,128,128]{2,1,0:T(8,128)(2,1)S(1)}, bf16[4,128,128]{2,1,0:T(8,128)(2,1)S(1)}, u32[]{:S(2)}, u32[]{:S(2)}) collective-permute-start(bf16[4,128,128]{2,1,0:T(8,128)(2,1)S(1)} %block_sums.9), channel_id=1, source_target_pairs={{0,16},{1,17},{2,18},{3,19},{4,20},{5,21},{6,22},{7,23},{8,24},{9,... | collective-permute-start | bytes 393224 | tf_op jit(solution)/shard_map/ppermute | solution.py:311
  30.1 4.0 %collective-permute-done.9 = bf16[4,128,128]{2,1,0:T(8,128)(2,1)S(1)} collective-permute-done((bf16[4,128,128]{2,1,0:T(8,128)(2,1)S(1)}, bf16[4,128,128]{2,1,0:T(8,128)(2,1)S(1)}, u32[]{:S(2)}, u32[]{:S(2)}) %collective-permute-start.9) | collective-permute-done | bytes 131104 | tf_op jit(solution)/shard_map/ppermute | solution.py:311
  34.3 1.3 %collective-permute-done.10.refs_1_ = bf16[4,128,128]{2,1,0:T(8,128)(2,1)S(1)} collective-permute-done((bf16[4,128,128]{2,1,0:T(8,128)(2,1)S(1)}, bf16[4,128,128]{2,1,0:T(8,128)(2,1)S(1)}, u32[]{:S(2)}, u32[]{:S(2)}) %collective-permute-start.10) | collective-permute-done | bytes 131104 | tf_op jit(solution)/shard_map/ppermute | solution.py:311
  35.8 1.3 collective-permute-start.11
  37.0 2.8 %collective-permute-start.12 = (bf16[4,128,128]{2,1,0:T(8,128)(2,1)S(1)}, bf16[4,128,128]{2,1,0:T(8,128)(2,1)S(1)}, u32[]{:S(2)}, u32[]{:S(2)}) collective-permute-start(bf16[4,128,128]{2,1,0:T(8,128)(2,1)S(1)} %sum_and_solve.5.refs_2_), channel_id=1, source_target_pairs={{0,7},{1,15},{2,21},{3,29},{4,1},{5,9},{6,19},{7,27},{8,6},{9,14},... | collective-permute-start | bytes 393224 | tf_op jit(solution)/shard_map/ppermute | solution.py:296
  40.7 2.5 %lay_out.6 = (bf16[8,4,2,128,128]{4,3,2,1,0:T(8,128)(2,1)S(1)}, bf16[4,2,2,128,128]{4,3,2,1,0:T(8,128)(2,1)S(1)}) custom-call(s32[4]{0:T(128)S(1)} %pad_add_fusion.scal, s32[16,32]{1,0:T(8,128)S(1)} %bitcast.18, bf16[16,16,2,128,128]{4,3,2,1,0:T(8,128)(2,1)} %bitcast.23, bf16[16,4,8,128,128]{4,3,2,1,0:T(8,128)(2,1)} %bitcast.24, ...), custom_call_target="tpu_custom_call" | custom-call | bytes 10485760 | tf_op jit(solution)/shard_map/lay_out/pallas_call | solution.py:64
  44.0 1.8 %collective-permute-done.12.refs_2_ = bf16[4,128,128]{2,1,0:T(8,128)(2,1)S(1)} collective-permute-done((bf16[4,128,128]{2,1,0:T(8,128)(2,1)S(1)}, bf16[4,128,128]{2,1,0:T(8,128)(2,1)S(1)}, u32[]{:S(2)}, u32[]{:S(2)}) %collective-permute-start.12) | collective-permute-done | bytes 131104 | tf_op jit(solution)/shard_map/ppermute | solution.py:296
  46.5 3.9 %collective-permute-done.13 = bf16[2,128,128]{2,1,0:T(8,128)(2,1)S(1)} collective-permute-done((bf16[2,128,128]{2,1,0:T(8,128)(2,1)S(1)}, bf16[2,128,128]{2,1,0:T(8,128)(2,1)S(1)}, u32[]{:S(2)}, u32[]{:S(2)}) %collective-permute-start.13) | collective-permute-done | bytes 65568 | tf_op jit(solution)/shard_map/ppermute | solution.py:311
  50.5 1.2 collective-permute-done.14.refs_1_
  52.4 2.7 %collective-permute-start.16 = (bf16[2,128,128]{2,1,0:T(8,128)(2,1)S(1)}, bf16[2,128,128]{2,1,0:T(8,128)(2,1)S(1)}, u32[]{:S(2)}, u32[]{:S(2)}) collective-permute-start(bf16[2,128,128]{2,1,0:T(8,128)(2,1)S(1)} %sum_and_solve.6.refs_1_.refs_2_), channel_id=1, source_target_pairs={{0,7},{1,15},{2,21},{3,29},{4,1},{5,9},{6,19},{7,27},{8,6},{9,14},... | collective-permute-start | bytes 196616 | tf_op jit(solution)/shard_map/ppermute | solution.py:296
  55.1 2.0 %lay_out.7 = (bf16[4,2,2,128,128]{4,3,2,1,0:T(8,128)(2,1)S(1)}, bf16[2,2,2,128,128]{4,3,2,1,0:T(8,128)(2,1)S(1)}) custom-call(s32[4]{0:T(128)S(1)} %pad_add_fusion.scal, s32[16,32]{1,0:T(8,128)S(1)} %bitcast.19, bf16[16,16,2,128,128]{4,3,2,1,0:T(8,128)(2,1)} %bitcast.25, bf16[2,128,128]{2,1,0:T(8,128)(2,1)S(1)} %sum_and_solve.6.refs_1_.refs_2_), custom_call_target="tpu_custom_call" | custom-call | bytes 3145728 | tf_op jit(solution)/shard_map/lay_out/pallas_call | solution.py:64
  57.6 3.8 %collective-permute-start.17 = (bf16[2,128,128]{2,1,0:T(8,128)(2,1)S(1)}, bf16[2,128,128]{2,1,0:T(8,128)(2,1)S(1)}, u32[]{:S(2)}, u32[]{:S(2)}) collective-permute-start(bf16[2,128,128]{2,1,0:T(8,128)(2,1)S(1)} %block_sums.13), channel_id=1, source_target_pairs={{0,16},{1,17},{2,18},{3,19},{4,20},{5,21},{6,22},{7,23},{8,24},{9,... | collective-permute-start | bytes 196616 | tf_op jit(solution)/shard_map/ppermute | solution.py:311
  61.4 2.2 %collective-permute-done.17 = bf16[2,128,128]{2,1,0:T(8,128)(2,1)S(1)} collective-permute-done((bf16[2,128,128]{2,1,0:T(8,128)(2,1)S(1)}, bf16[2,128,128]{2,1,0:T(8,128)(2,1)S(1)}, u32[]{:S(2)}, u32[]{:S(2)}) %collective-permute-start.17) | collective-permute-done | bytes 65568 | tf_op jit(solution)/shard_map/ppermute | solution.py:311
  63.6 1.0 collective-permute-start.18
  64.6 0.9 collective-permute-done.18.refs_1_
  66.1 3.4 %collective-permute-start.20 = (bf16[2,128,128]{2,1,0:T(8,128)(2,1)S(1)}, bf16[2,128,128]{2,1,0:T(8,128)(2,1)S(1)}, u32[]{:S(2)}, u32[]{:S(2)}) collective-permute-start(bf16[2,128,128]{2,1,0:T(8,128)(2,1)S(1)} %sum_and_solve.7.refs_1_), channel_id=1, source_target_pairs={{0,7},{1,15},{2,21},{3,29},{4,1},{5,9},{6,19},{7,27},{8,6},{9,14},... | collective-permute-start | bytes 196616 | tf_op jit(solution)/shard_map/ppermute | solution.py:296
  69.6 2.5 %lay_out.8 = (bf16[2,2,2,128,128]{4,3,2,1,0:T(8,128)(2,1)S(1)}, bf16[2,4,2,128,128]{4,3,2,1,0:T(8,128)(2,1)S(1)}, bf16[2,4,2,128,128]{4,3,2,1,0:T(8,128)(2,1)S(1)}, bf16[2,8,2,128,128]{4,3,2,1,0:T(8,128)(2,1)S(1)}) custom-call(s32[4]{0:T(128)S(1)} %pad_add_fusion.scal, s32[16,32]{1,0:T(8,128)S(1)} %bitcast.20, bf16[16,16,2,128,128]{4,3,2,1,0:T(8,128)(2,1)} %bitcast.26, ...), custom_call_target="tpu_custom_call" | custom-call | bytes 9437184 | tf_op jit(solution)/shard_map/lay_out/pallas_call | solution.py:64
  72.3 2.0 %collective-permute-start.21 = (bf16[2,128,128]{2,1,0:T(8,128)(2,1)S(1)}, bf16[2,128,128]{2,1,0:T(8,128)(2,1)S(1)}, u32[]{:S(2)}, u32[]{:S(2)}) collective-permute-start(bf16[2,128,128]{2,1,0:T(8,128)(2,1)S(1)} %block_sums.14), channel_id=1, source_target_pairs={{0,16},{1,17},{2,18},{3,19},{4,20},{5,21},{6,22},{7,23},{8,24},{9,... | collective-permute-start | bytes 196616 | tf_op jit(solution)/shard_map/ppermute | solution.py:311
  74.3 2.7 %collective-permute-done.21 = bf16[2,128,128]{2,1,0:T(8,128)(2,1)S(1)} collective-permute-done((bf16[2,128,128]{2,1,0:T(8,128)(2,1)S(1)}, bf16[2,128,128]{2,1,0:T(8,128)(2,1)S(1)}, u32[]{:S(2)}, u32[]{:S(2)}) %collective-permute-start.21) | collective-permute-done | bytes 65568 | tf_op jit(solution)/shard_map/ppermute | solution.py:311
  77.2 1.1 collective-permute-done.22.refs_1_
  78.5 1.7 %collective-permute-start.23 = (bf16[2,128,128]{2,1,0:T(8,128)(2,1)S(1)}, bf16[2,128,128]{2,1,0:T(8,128)(2,1)S(1)}, u32[]{:S(2)}, u32[]{:S(2)}) collective-permute-start(bf16[2,128,128]{2,1,0:T(8,128)(2,1)S(1)} %sum_and_solve.8.refs_1_), channel_id=1, source_target_pairs={{0,2},{1,10},{2,18},{3,26},{4,6},{5,14},{6,22},{7,30},{8,3},{9,11}... | collective-permute-start | bytes 196616 | tf_op jit(solution)/shard_map/ppermute | solution.py:296
  80.2 3.5 %collective-permute-start.24 = (bf16[2,128,128]{2,1,0:T(8,128)(2,1)S(1)}, bf16[2,128,128]{2,1,0:T(8,128)(2,1)S(1)}, u32[]{:S(2)}, u32[]{:S(2)}) collective-permute-start(bf16[2,128,128]{2,1,0:T(8,128)(2,1)S(1)} %sum_and_solve.8.refs_1_), channel_id=1, source_target_pairs={{0,7},{1,15},{2,21},{3,29},{4,1},{5,9},{6,19},{7,27},{8,6},{9,14},... | collective-permute-start | bytes 196616 | tf_op jit(solution)/shard_map/ppermute | solution.py:296
  84.0 1.6 %collective-permute-done.24.refs_2_.refs_5_ = bf16[2,128,128]{2,1,0:T(8,128)(2,1)S(1)} collective-permute-done((bf16[2,128,128]{2,1,0:T(8,128)(2,1)S(1)}, bf16[2,128,128]{2,1,0:T(8,128)(2,1)S(1)}, u32[]{:S(2)}, u32[]{:S(2)}) %collective-permute-start.24) | collective-permute-done | bytes 65568 | tf_op jit(solution)/shard_map/ppermute | solution.py:296
  85.9 1.4 %collective-permute-start.25 = (bf16[4,128,128]{2,1,0:T(8,128)(2,1)S(1)}, bf16[4,128,128]{2,1,0:T(8,128)(2,1)S(1)}, u32[]{:S(2)}, u32[]{:S(2)}) collective-permute-start(bf16[4,128,128]{2,1,0:T(8,128)(2,1)S(1)} %block_sums.16), channel_id=1, source_target_pairs={{0,16},{1,17},{2,18},{3,19},{4,20},{5,21},{6,22},{7,23},{8,24},{9,... | collective-permute-start | bytes 393224 | tf_op jit(solution)/shard_map/ppermute | solution.py:311
  87.3 3.6 %collective-permute-done.25 = bf16[4,128,128]{2,1,0:T(8,128)(2,1)S(1)} collective-permute-done((bf16[4,128,128]{2,1,0:T(8,128)(2,1)S(1)}, bf16[4,128,128]{2,1,0:T(8,128)(2,1)S(1)}, u32[]{:S(2)}, u32[]{:S(2)}) %collective-permute-start.25) | collective-permute-done | bytes 131104 | tf_op jit(solution)/shard_map/ppermute | solution.py:311
  91.0 1.3 %collective-permute-start.26 = (bf16[4,128,128]{2,1,0:T(8,128)(2,1)S(1)}, bf16[4,128,128]{2,1,0:T(8,128)(2,1)S(1)}, u32[]{:S(2)}, u32[]{:S(2)}) collective-permute-start(bf16[4,128,128]{2,1,0:T(8,128)(2,1)S(1)} %add.76.refs_0_), channel_id=1, source_target_pairs={{0,8},{1,9},{2,10},{3,11},{4,12},{5,13},{6,14},{7,15},{8,0},{9,1},... | collective-permute-start | bytes 393224 | tf_op jit(solution)/shard_map/ppermute | solution.py:311
  92.3 1.0 collective-permute-done.26.refs_1_
  93.5 1.7 %collective-permute-start.27 = (bf16[4,128,128]{2,1,0:T(8,128)(2,1)S(1)}, bf16[4,128,128]{2,1,0:T(8,128)(2,1)S(1)}, u32[]{:S(2)}, u32[]{:S(2)}) collective-permute-start(bf16[4,128,128]{2,1,0:T(8,128)(2,1)S(1)} %sum_and_solve.9), channel_id=1, source_target_pairs={{0,2},{1,10},{2,18},{3,26},{4,6},{5,14},{6,22},{7,30},{8,3},{9,11}... | collective-permute-start | bytes 393224 | tf_op jit(solution)/shard_map/ppermute | solution.py:296
  95.2 2.6 %collective-permute-start.28 = (bf16[4,128,128]{2,1,0:T(8,128)(2,1)S(1)}, bf16[4,128,128]{2,1,0:T(8,128)(2,1)S(1)}, u32[]{:S(2)}, u32[]{:S(2)}) collective-permute-start(bf16[4,128,128]{2,1,0:T(8,128)(2,1)S(1)} %sum_and_solve.9), channel_id=1, source_target_pairs={{0,7},{1,15},{2,21},{3,29},{4,1},{5,9},{6,19},{7,27},{8,6},{9,14},... | collective-permute-start | bytes 393224 | tf_op jit(solution)/shard_map/ppermute | solution.py:296
  97.8 2.8 %lay_out.9 = (bf16[2,8,2,128,128]{4,3,2,1,0:T(8,128)(2,1)S(1)}, bf16[4,8,2,128,128]{4,3,2,1,0:T(8,128)(2,1)S(1)}) custom-call(s32[4]{0:T(128)S(1)} %pad_add_fusion.scal, s32[16,32]{1,0:T(8,128)S(1)} %bitcast.21, bf16[16,16,2,128,128]{4,3,2,1,0:T(8,128)(2,1)} %bitcast.27, bf16[2,128,128]{2,1,0:T(8,128)(2,1)S(1)} %sum_and_solve.8.refs_1_), custom_call_target="tpu_custom_call" | custom-call | bytes 12582912 | tf_op jit(solution)/shard_map/lay_out/pallas_call | solution.py:64
  101.3 2.8 %collective-permute-done.28.refs_1_ = bf16[4,128,128]{2,1,0:T(8,128)(2,1)S(1)} collective-permute-done((bf16[4,128,128]{2,1,0:T(8,128)(2,1)S(1)}, bf16[4,128,128]{2,1,0:T(8,128)(2,1)S(1)}, u32[]{:S(2)}, u32[]{:S(2)}) %collective-permute-start.28) | collective-permute-done | bytes 131104 | tf_op jit(solution)/shard_map/ppermute | solution.py:296
  104.8 2.1 %collective-permute-start.29 = (bf16[4,128,128]{2,1,0:T(8,128)(2,1)S(1)}, bf16[4,128,128]{2,1,0:T(8,128)(2,1)S(1)}, u32[]{:S(2)}, u32[]{:S(2)}) collective-permute-start(bf16[4,128,128]{2,1,0:T(8,128)(2,1)S(1)} %get-tuple-element.32), channel_id=1, source_target_pairs={{0,8},{8,0},{1,9},{9,1},{2,10},{10,2},{3,11},{11,3},{4,12},{12,4},... | collective-permute-start | bytes 393224 | tf_op jit(solution)/shard_map/ppermute | solution.py:413
  107.0 1.0 collective-permute-done.29
  108.2 5.6 %collective-permute-done.30.other_ref = bf16[4,128,128]{2,1,0:T(8,128)(2,1)S(1)} collective-permute-done((bf16[4,128,128]{2,1,0:T(8,128)(2,1)S(1)}, bf16[4,128,128]{2,1,0:T(8,128)(2,1)S(1)}, u32[]{:S(2)}, u32[]{:S(2)}) %collective-permute-start.30) | collective-permute-done | bytes 131104 | tf_op jit(solution)/shard_map/ppermute | solution.py:414
  113.8 1.4 %last_solve.1 = bf16[8,128,128]{2,1,0:T(8,128)(2,1)} custom-call(s32[4]{0:T(128)S(1)} %pad_add_fusion.scal, f32[4,128,128]{2,1,0:T(8,128)S(1)} %get-tuple-element.34.own_ref, bf16[4,128,128]{2,1,0:T(8,128)(2,1)S(1)} %collective-permute-done.30.other_ref, bf16[4,1,128,128]{3,2,1,0:T(8,128)(2,1)S(1)} %constant_dynamic-slice_fusion.1.inverse_ref, ...), custom_call_target="tpu_custom_call" | custom-call | tf_op jit(solution)/shard_map/last_solve/pallas_call | solution.py:241
  115.2 3.4 %all-to-all-start.1 = ((bf16[8,128,128]{2,1,0:T(8,128)(2,1)}), bf16[8,128,128]{2,1,0:T(8,128)(2,1)S(1)}, u32[]{:S(2)}, u32[]{:S(2)}) async-start(bf16[8,128,128]{2,1,0:T(8,128)(2,1)} %last_solve.1), calls=%async_computation.1 | async-start | bytes 524288 | tf_op jit(solution)/shard_map/all_to_all | solution.py:419
  118.7 8.8 %all-to-all-done.1 = bf16[8,128,128]{2,1,0:T(8,128)(2,1)S(1)} async-done(((bf16[8,128,128]{2,1,0:T(8,128)(2,1)}), bf16[8,128,128]{2,1,0:T(8,128)(2,1)S(1)}, u32[]{:S(2)}, u32[]{:S(2)}) %all-to-all-start.1) | async-done | bytes 262176 | tf_op jit(solution)/shard_map/all_to_all | solution.py:419
  (67 shorter events, 11.8 us)
Async XLA Ops:
  1.0 10.5 %all-to-all-start = ((bf16[4,128,128]{2,1,0:T(8,128)(2,1)}), bf16[4,128,128]{2,1,0:T(8,128)(2,1)S(1)}, u32[]{:S(2)}, u32[]{:S(2)}) async-start(bf16[4,128,128]{2,1,0:T(8,128)(2,1)} %bitcast.29), calls=%async_computation | async-start | bytes 262144 | tf_op jit(solution)/shard_map/all_to_all | solution.py:353
  5.2 6.3 %collective-permute-start = (bf16[2,128,128]{2,1,0:T(8,128)(2,1)S(1)}, bf16[2,128,128]{2,1,0:T(8,128)(2,1)S(1)}, u32[]{:S(2)}, u32[]{:S(2)}) collective-permute-start(bf16[2,128,128]{2,1,0:T(8,128)(2,1)S(1)} %dynamic-slice_bitcast_fusion.refs_1_), channel_id=1, source_target_pairs={{0,4},{1,12},{2,16},{3,24},{4,1},{5,9},{6,21},{7,29},{8,6},{9,14},... | collective-permute-start | bytes 196616 | tf_op jit(solution)/shard_map/ppermute | solution.py:352
  8.5 0.7 copy-start.2
  11.7 23.9 %copy-start = (bf16[16,1,128,128]{3,2,1,0:T(8,128)(2,1)S(1)}, bf16[16,1,128,128]{3,2,1,0:T(8,128)(2,1)}, u32[]{:S(2)}) copy-start(bf16[16,1,128,128]{3,2,1,0:T(8,128)(2,1)} %refs_2_.5) | copy-start | bytes 1572868
  11.7 9.4 %collective-permute-start.2 = (bf16[2,128,128]{2,1,0:T(8,128)(2,1)S(1)}, bf16[2,128,128]{2,1,0:T(8,128)(2,1)S(1)}, u32[]{:S(2)}, u32[]{:S(2)}) collective-permute-start(bf16[2,128,128]{2,1,0:T(8,128)(2,1)S(1)} %solve_blocks.1.refs_1_.refs_0_), channel_id=1, source_target_pairs={{0,2},{1,3},{2,0},{3,1},{4,6},{5,7},{6,4},{7,5},{8,10},{9,11},{10,... | collective-permute-start | bytes 196616 | tf_op jit(solution)/shard_map/ppermute | solution.py:348
  13.6 7.5 %collective-permute-start.4 = (bf16[2,128,128]{2,1,0:T(8,128)(2,1)S(1)}, bf16[2,128,128]{2,1,0:T(8,128)(2,1)S(1)}, u32[]{:S(2)}, u32[]{:S(2)}) collective-permute-start(bf16[2,128,128]{2,1,0:T(8,128)(2,1)S(1)} %solve_blocks.1.refs_1_.refs_0_), channel_id=1, source_target_pairs={{0,4},{1,5},{2,6},{3,7},{4,0},{5,1},{6,2},{7,3},{8,12},{9,13},{10,... | collective-permute-start | bytes 196616 | tf_op jit(solution)/shard_map/ppermute | solution.py:348
  16.1 7.0 %collective-permute-start.6 = (bf16[2,128,128]{2,1,0:T(8,128)(2,1)S(1)}, bf16[2,128,128]{2,1,0:T(8,128)(2,1)S(1)}, u32[]{:S(2)}, u32[]{:S(2)}) collective-permute-start(bf16[2,128,128]{2,1,0:T(8,128)(2,1)S(1)} %solve_blocks.1.refs_1_.refs_0_), channel_id=1, source_target_pairs={{0,6},{1,7},{2,4},{3,5},{4,2},{5,3},{6,0},{7,1},{8,14},{9,15},{10,... | collective-permute-start | bytes 196616 | tf_op jit(solution)/shard_map/ppermute | solution.py:348
  16.2 9.7 %collective-permute-start.1 = (bf16[2,128,128]{2,1,0:T(8,128)(2,1)S(1)}, bf16[2,128,128]{2,1,0:T(8,128)(2,1)S(1)}, u32[]{:S(2)}, u32[]{:S(2)}) collective-permute-start(bf16[2,128,128]{2,1,0:T(8,128)(2,1)S(1)} %solve_blocks.1.refs_1_.refs_0_), channel_id=1, source_target_pairs={{0,1},{1,0},{2,3},{3,2},{4,5},{5,4},{6,7},{7,6},{8,9},{9,8},{10,11... | collective-permute-start | bytes 196616 | tf_op jit(solution)/shard_map/ppermute | solution.py:348
  18.3 7.5 %collective-permute-start.8 = (bf16[2,128,128]{2,1,0:T(8,128)(2,1)S(1)}, bf16[2,128,128]{2,1,0:T(8,128)(2,1)S(1)}, u32[]{:S(2)}, u32[]{:S(2)}) collective-permute-start(bf16[2,128,128]{2,1,0:T(8,128)(2,1)S(1)} %get-tuple-element.35), channel_id=1, source_target_pairs={{4,0},{12,1},{16,2},{24,3},{1,4},{9,5},{21,6},{29,7},{6,8},{14,9},... | collective-permute-start | bytes 196616 | tf_op jit(solution)/shard_map/ppermute | solution.py:354
  21.1 4.9 %collective-permute-start.3 = (bf16[2,128,128]{2,1,0:T(8,128)(2,1)S(1)}, bf16[2,128,128]{2,1,0:T(8,128)(2,1)S(1)}, u32[]{:S(2)}, u32[]{:S(2)}) collective-permute-start(bf16[2,128,128]{2,1,0:T(8,128)(2,1)S(1)} %collective-permute-done.2.refs_3_.refs_2_), channel_id=1, source_target_pairs={{0,1},{1,0},{2,3},{3,2},{4,5},{5,4},{6,7},{7,6},{8,9},{9,8},{10,11... | collective-permute-start | bytes 196616 | tf_op jit(solution)/shard_map/ppermute | solution.py:348
  21.1 5.7 %collective-permute-start.5 = (bf16[2,128,128]{2,1,0:T(8,128)(2,1)S(1)}, bf16[2,128,128]{2,1,0:T(8,128)(2,1)S(1)}, u32[]{:S(2)}, u32[]{:S(2)}) collective-permute-start(bf16[2,128,128]{2,1,0:T(8,128)(2,1)S(1)} %collective-permute-done.4.refs_5_.refs_4_), channel_id=1, source_target_pairs={{0,1},{1,0},{2,3},{3,2},{4,5},{5,4},{6,7},{7,6},{8,9},{9,8},{10,11... | collective-permute-start | bytes 196616 | tf_op jit(solution)/shard_map/ppermute | solution.py:348
  23.1 4.4 %collective-permute-start.7 = (bf16[2,128,128]{2,1,0:T(8,128)(2,1)S(1)}, bf16[2,128,128]{2,1,0:T(8,128)(2,1)S(1)}, u32[]{:S(2)}, u32[]{:S(2)}) collective-permute-start(bf16[2,128,128]{2,1,0:T(8,128)(2,1)S(1)} %collective-permute-done.6.refs_7_.refs_6_), channel_id=1, source_target_pairs={{0,1},{1,0},{2,3},{3,2},{4,5},{5,4},{6,7},{7,6},{8,9},{9,8},{10,11... | collective-permute-start | bytes 196616 | tf_op jit(solution)/shard_map/ppermute | solution.py:348
  25.9 14.8 %copy-start.3 = (s32[16,1,32,1]{2,3,1,0:T(1,128)S(1)}, s32[16,1,32,1]{2,3,1,0:T(1,128)}, u32[]{:S(2)}) copy-start(s32[16,1,32,1]{2,3,1,0:T(1,128)} %param.7) | copy-start | bytes 6148
  28.2 5.9 %collective-permute-start.9 = (bf16[4,128,128]{2,1,0:T(8,128)(2,1)S(1)}, bf16[4,128,128]{2,1,0:T(8,128)(2,1)S(1)}, u32[]{:S(2)}, u32[]{:S(2)}) collective-permute-start(bf16[4,128,128]{2,1,0:T(8,128)(2,1)S(1)} %block_sums.9), channel_id=1, source_target_pairs={{0,16},{1,17},{2,18},{3,19},{4,20},{5,21},{6,22},{7,23},{8,24},{9,... | collective-permute-start | bytes 393224 | tf_op jit(solution)/shard_map/ppermute | solution.py:311
  34.2 1.4 %collective-permute-start.10 = (bf16[4,128,128]{2,1,0:T(8,128)(2,1)S(1)}, bf16[4,128,128]{2,1,0:T(8,128)(2,1)S(1)}, u32[]{:S(2)}, u32[]{:S(2)}) collective-permute-start(bf16[4,128,128]{2,1,0:T(8,128)(2,1)S(1)} %add.72.refs_0_), channel_id=1, source_target_pairs={{0,8},{1,9},{2,10},{3,11},{4,12},{5,13},{6,14},{7,15},{8,0},{9,1},... | collective-permute-start | bytes 393224 | tf_op jit(solution)/shard_map/ppermute | solution.py:311
  35.8 8.2 %collective-permute-start.11 = (bf16[4,128,128]{2,1,0:T(8,128)(2,1)S(1)}, bf16[4,128,128]{2,1,0:T(8,128)(2,1)S(1)}, u32[]{:S(2)}, u32[]{:S(2)}) collective-permute-start(bf16[4,128,128]{2,1,0:T(8,128)(2,1)S(1)} %sum_and_solve.5.refs_2_), channel_id=1, source_target_pairs={{0,2},{1,10},{2,18},{3,26},{4,6},{5,14},{6,22},{7,30},{8,3},{9,11}... | collective-permute-start | bytes 393224 | tf_op jit(solution)/shard_map/ppermute | solution.py:296
  37.0 8.7 %collective-permute-start.12 = (bf16[4,128,128]{2,1,0:T(8,128)(2,1)S(1)}, bf16[4,128,128]{2,1,0:T(8,128)(2,1)S(1)}, u32[]{:S(2)}, u32[]{:S(2)}) collective-permute-start(bf16[4,128,128]{2,1,0:T(8,128)(2,1)S(1)} %sum_and_solve.5.refs_2_), channel_id=1, source_target_pairs={{0,7},{1,15},{2,21},{3,29},{4,1},{5,9},{6,19},{7,27},{8,6},{9,14},... | collective-permute-start | bytes 393224 | tf_op jit(solution)/shard_map/ppermute | solution.py:296
  46.1 4.3 %collective-permute-start.13 = (bf16[2,128,128]{2,1,0:T(8,128)(2,1)S(1)}, bf16[2,128,128]{2,1,0:T(8,128)(2,1)S(1)}, u32[]{:S(2)}, u32[]{:S(2)}) collective-permute-start(bf16[2,128,128]{2,1,0:T(8,128)(2,1)S(1)} %block_sums.11), channel_id=1, source_target_pairs={{0,16},{1,17},{2,18},{3,19},{4,20},{5,21},{6,22},{7,23},{8,24},{9,... | collective-permute-start | bytes 196616 | tf_op jit(solution)/shard_map/ppermute | solution.py:311
  50.4 1.3 %collective-permute-start.14 = (bf16[2,128,128]{2,1,0:T(8,128)(2,1)S(1)}, bf16[2,128,128]{2,1,0:T(8,128)(2,1)S(1)}, u32[]{:S(2)}, u32[]{:S(2)}) collective-permute-start(bf16[2,128,128]{2,1,0:T(8,128)(2,1)S(1)} %add.73.refs_0_), channel_id=1, source_target_pairs={{0,8},{1,9},{2,10},{3,11},{4,12},{5,13},{6,14},{7,15},{8,0},{9,1},... | collective-permute-start | bytes 196616 | tf_op jit(solution)/shard_map/ppermute | solution.py:311
  51.9 5.4 %collective-permute-start.15 = (bf16[2,128,128]{2,1,0:T(8,128)(2,1)S(1)}, bf16[2,128,128]{2,1,0:T(8,128)(2,1)S(1)}, u32[]{:S(2)}, u32[]{:S(2)}) collective-permute-start(bf16[2,128,128]{2,1,0:T(8,128)(2,1)S(1)} %sum_and_solve.6.refs_1_.refs_2_), channel_id=1, source_target_pairs={{0,2},{1,10},{2,18},{3,26},{4,6},{5,14},{6,22},{7,30},{8,3},{9,11}... | collective-permute-start | bytes 196616 | tf_op jit(solution)/shard_map/ppermute | solution.py:296
  52.4 5.0 %collective-permute-start.16 = (bf16[2,128,128]{2,1,0:T(8,128)(2,1)S(1)}, bf16[2,128,128]{2,1,0:T(8,128)(2,1)S(1)}, u32[]{:S(2)}, u32[]{:S(2)}) collective-permute-start(bf16[2,128,128]{2,1,0:T(8,128)(2,1)S(1)} %sum_and_solve.6.refs_1_.refs_2_), channel_id=1, source_target_pairs={{0,7},{1,15},{2,21},{3,29},{4,1},{5,9},{6,19},{7,27},{8,6},{9,14},... | collective-permute-start | bytes 196616 | tf_op jit(solution)/shard_map/ppermute | solution.py:296
  57.0 8.5 %copy-start.1 = (bf16[16,1,128,128]{3,2,1,0:T(8,128)(2,1)S(1)}, bf16[16,1,128,128]{3,2,1,0:T(8,128)(2,1)}, u32[]{:S(2)}) copy-start(bf16[16,1,128,128]{3,2,1,0:T(8,128)(2,1)} %refs_3_.5) | copy-start | bytes 1572868
  57.6 6.1 %collective-permute-start.17 = (bf16[2,128,128]{2,1,0:T(8,128)(2,1)S(1)}, bf16[2,128,128]{2,1,0:T(8,128)(2,1)S(1)}, u32[]{:S(2)}, u32[]{:S(2)}) collective-permute-start(bf16[2,128,128]{2,1,0:T(8,128)(2,1)S(1)} %block_sums.13), channel_id=1, source_target_pairs={{0,16},{1,17},{2,18},{3,19},{4,20},{5,21},{6,22},{7,23},{8,24},{9,... | collective-permute-start | bytes 196616 | tf_op jit(solution)/shard_map/ppermute | solution.py:311
  63.6 1.9 %collective-permute-start.18 = (bf16[2,128,128]{2,1,0:T(8,128)(2,1)S(1)}, bf16[2,128,128]{2,1,0:T(8,128)(2,1)S(1)}, u32[]{:S(2)}, u32[]{:S(2)}) collective-permute-start(bf16[2,128,128]{2,1,0:T(8,128)(2,1)S(1)} %add.74.refs_0_), channel_id=1, source_target_pairs={{0,8},{1,9},{2,10},{3,11},{4,12},{5,13},{6,14},{7,15},{8,0},{9,1},... | collective-permute-start | bytes 196616 | tf_op jit(solution)/shard_map/ppermute | solution.py:311
  65.8 6.3 %collective-permute-start.19 = (bf16[2,128,128]{2,1,0:T(8,128)(2,1)S(1)}, bf16[2,128,128]{2,1,0:T(8,128)(2,1)S(1)}, u32[]{:S(2)}, u32[]{:S(2)}) collective-permute-start(bf16[2,128,128]{2,1,0:T(8,128)(2,1)S(1)} %sum_and_solve.7.refs_1_), channel_id=1, source_target_pairs={{0,2},{1,10},{2,18},{3,26},{4,6},{5,14},{6,22},{7,30},{8,3},{9,11}... | collective-permute-start | bytes 196616 | tf_op jit(solution)/shard_map/ppermute | solution.py:296
  66.1 5.9 %collective-permute-start.20 = (bf16[2,128,128]{2,1,0:T(8,128)(2,1)S(1)}, bf16[2,128,128]{2,1,0:T(8,128)(2,1)S(1)}, u32[]{:S(2)}, u32[]{:S(2)}) collective-permute-start(bf16[2,128,128]{2,1,0:T(8,128)(2,1)S(1)} %sum_and_solve.7.refs_1_), channel_id=1, source_target_pairs={{0,7},{1,15},{2,21},{3,29},{4,1},{5,9},{6,19},{7,27},{8,6},{9,14},... | collective-permute-start | bytes 196616 | tf_op jit(solution)/shard_map/ppermute | solution.py:296
  72.3 4.7 %collective-permute-start.21 = (bf16[2,128,128]{2,1,0:T(8,128)(2,1)S(1)}, bf16[2,128,128]{2,1,0:T(8,128)(2,1)S(1)}, u32[]{:S(2)}, u32[]{:S(2)}) collective-permute-start(bf16[2,128,128]{2,1,0:T(8,128)(2,1)S(1)} %block_sums.14), channel_id=1, source_target_pairs={{0,16},{1,17},{2,18},{3,19},{4,20},{5,21},{6,22},{7,23},{8,24},{9,... | collective-permute-start | bytes 196616 | tf_op jit(solution)/shard_map/ppermute | solution.py:311
  77.0 1.3 %collective-permute-start.22 = (bf16[2,128,128]{2,1,0:T(8,128)(2,1)S(1)}, bf16[2,128,128]{2,1,0:T(8,128)(2,1)S(1)}, u32[]{:S(2)}, u32[]{:S(2)}) collective-permute-start(bf16[2,128,128]{2,1,0:T(8,128)(2,1)S(1)} %add.75.refs_0_), channel_id=1, source_target_pairs={{0,8},{1,9},{2,10},{3,11},{4,12},{5,13},{6,14},{7,15},{8,0},{9,1},... | collective-permute-start | bytes 196616 | tf_op jit(solution)/shard_map/ppermute | solution.py:311
  78.5 5.5 %collective-permute-start.23 = (bf16[2,128,128]{2,1,0:T(8,128)(2,1)S(1)}, bf16[2,128,128]{2,1,0:T(8,128)(2,1)S(1)}, u32[]{:S(2)}, u32[]{:S(2)}) collective-permute-start(bf16[2,128,128]{2,1,0:T(8,128)(2,1)S(1)} %sum_and_solve.8.refs_1_), channel_id=1, source_target_pairs={{0,2},{1,10},{2,18},{3,26},{4,6},{5,14},{6,22},{7,30},{8,3},{9,11}... | collective-permute-start | bytes 196616 | tf_op jit(solution)/shard_map/ppermute | solution.py:296
  80.2 5.4 %collective-permute-start.24 = (bf16[2,128,128]{2,1,0:T(8,128)(2,1)S(1)}, bf16[2,128,128]{2,1,0:T(8,128)(2,1)S(1)}, u32[]{:S(2)}, u32[]{:S(2)}) collective-permute-start(bf16[2,128,128]{2,1,0:T(8,128)(2,1)S(1)} %sum_and_solve.8.refs_1_), channel_id=1, source_target_pairs={{0,7},{1,15},{2,21},{3,29},{4,1},{5,9},{6,19},{7,27},{8,6},{9,14},... | collective-permute-start | bytes 196616 | tf_op jit(solution)/shard_map/ppermute | solution.py:296
  85.9 5.0 %collective-permute-start.25 = (bf16[4,128,128]{2,1,0:T(8,128)(2,1)S(1)}, bf16[4,128,128]{2,1,0:T(8,128)(2,1)S(1)}, u32[]{:S(2)}, u32[]{:S(2)}) collective-permute-start(bf16[4,128,128]{2,1,0:T(8,128)(2,1)S(1)} %block_sums.16), channel_id=1, source_target_pairs={{0,16},{1,17},{2,18},{3,19},{4,20},{5,21},{6,22},{7,23},{8,24},{9,... | collective-permute-start | bytes 393224 | tf_op jit(solution)/shard_map/ppermute | solution.py:311
  91.0 2.3 %collective-permute-start.26 = (bf16[4,128,128]{2,1,0:T(8,128)(2,1)S(1)}, bf16[4,128,128]{2,1,0:T(8,128)(2,1)S(1)}, u32[]{:S(2)}, u32[]{:S(2)}) collective-permute-start(bf16[4,128,128]{2,1,0:T(8,128)(2,1)S(1)} %add.76.refs_0_), channel_id=1, source_target_pairs={{0,8},{1,9},{2,10},{3,11},{4,12},{5,13},{6,14},{7,15},{8,0},{9,1},... | collective-permute-start | bytes 393224 | tf_op jit(solution)/shard_map/ppermute | solution.py:311
  93.5 7.8 %collective-permute-start.27 = (bf16[4,128,128]{2,1,0:T(8,128)(2,1)S(1)}, bf16[4,128,128]{2,1,0:T(8,128)(2,1)S(1)}, u32[]{:S(2)}, u32[]{:S(2)}) collective-permute-start(bf16[4,128,128]{2,1,0:T(8,128)(2,1)S(1)} %sum_and_solve.9), channel_id=1, source_target_pairs={{0,2},{1,10},{2,18},{3,26},{4,6},{5,14},{6,22},{7,30},{8,3},{9,11}... | collective-permute-start | bytes 393224 | tf_op jit(solution)/shard_map/ppermute | solution.py:296
  95.2 8.9 %collective-permute-start.28 = (bf16[4,128,128]{2,1,0:T(8,128)(2,1)S(1)}, bf16[4,128,128]{2,1,0:T(8,128)(2,1)S(1)}, u32[]{:S(2)}, u32[]{:S(2)}) collective-permute-start(bf16[4,128,128]{2,1,0:T(8,128)(2,1)S(1)} %sum_and_solve.9), channel_id=1, source_target_pairs={{0,7},{1,15},{2,21},{3,29},{4,1},{5,9},{6,19},{7,27},{8,6},{9,14},... | collective-permute-start | bytes 393224 | tf_op jit(solution)/shard_map/ppermute | solution.py:296
  104.8 3.1 %collective-permute-start.29 = (bf16[4,128,128]{2,1,0:T(8,128)(2,1)S(1)}, bf16[4,128,128]{2,1,0:T(8,128)(2,1)S(1)}, u32[]{:S(2)}, u32[]{:S(2)}) collective-permute-start(bf16[4,128,128]{2,1,0:T(8,128)(2,1)S(1)} %get-tuple-element.32), channel_id=1, source_target_pairs={{0,8},{8,0},{1,9},{9,1},{2,10},{10,2},{3,11},{11,3},{4,12},{12,4},... | collective-permute-start | bytes 393224 | tf_op jit(solution)/shard_map/ppermute | solution.py:413
  108.0 5.8 %collective-permute-start.30 = (bf16[4,128,128]{2,1,0:T(8,128)(2,1)S(1)}, bf16[4,128,128]{2,1,0:T(8,128)(2,1)S(1)}, u32[]{:S(2)}, u32[]{:S(2)}) collective-permute-start(bf16[4,128,128]{2,1,0:T(8,128)(2,1)S(1)} %get-tuple-element.33), channel_id=1, source_target_pairs={{0,16},{16,0},{1,17},{17,1},{2,18},{18,2},{3,19},{19,3},{4,20},{20... | collective-permute-start | bytes 393224 | tf_op jit(solution)/shard_map/ppermute | solution.py:414
  115.2 12.3 %all-to-all-start.1 = ((bf16[8,128,128]{2,1,0:T(8,128)(2,1)}), bf16[8,128,128]{2,1,0:T(8,128)(2,1)S(1)}, u32[]{:S(2)}, u32[]{:S(2)}) async-start(bf16[8,128,128]{2,1,0:T(8,128)(2,1)} %last_solve.1), calls=%async_computation.1 | async-start | bytes 524288 | tf_op jit(solution)/shard_map/all_to_all | solution.py:419

commit v5 on v4

--- a/solution.py
+++ b/solution.py
@@ -208,7 +208,7 @@
             for r in range(chunks):
                 value = jnp.zeros((size, rhs), jnp.bfloat16)
                 for t, ref in enumerate(refs[:-1]):
-                    value = jnp.where((source == t) & (scal[4] > 0), ref[r], value)
+                    value = jnp.where((source == t) & (scal[3] > 0), ref[r], value)
                 place = lax.rem(r + lo_n - scal[2], lo_n)
                 out_ref[place * per + h] = value
 
@@ -226,35 +226,23 @@
     )(scalars, *zero)
 
 
-def last_solve(scalars, start_index, own, other, inverse, solved, copies):
+def last_solve(own, other, inverse, solved, copies):
     count, size, rhs = own.shape
 
-    def kernel(scal, own_ref, other_ref, inverse_ref, solved_ref, out_ref):
+    def kernel(own_ref, other_ref, inverse_ref, solved_ref, out_ref):
         for h in range(count):
             value = (own_ref[h] + other_ref[h].astype(jnp.float32)).astype(jnp.bfloat16)
-            value = jnp.dot(inverse_ref[h, 0], value, preferred_element_type=jnp.float32).astype(jnp.bfloat16)
-            value = jnp.where(scal[start_index] > 0, value, solved_ref[h])
+            value = jnp.dot(inverse_ref[h, 0], value, preferred_element_type=jnp.float32)
+            value = (value + solved_ref[h].astype(jnp.float32)).astype(jnp.bfloat16)
             for copy in range(copies):
                 out_ref[h * copies + copy] = value
 
-    full = lambda g, scal: (0, 0, 0)
-    return pl.pallas_call(
-        kernel,
-        grid_spec=pltpu.PrefetchScalarGridSpec(
-            num_scalar_prefetch=1,
-            grid=(1,),
-            in_specs=[
-                pl.BlockSpec(own.shape, full),
-                pl.BlockSpec(other.shape, full),
-                pl.BlockSpec((count, 1, size, size), lambda g, scal: (0, 0, 0, 0)),
-                pl.BlockSpec((count, size, rhs), full),
-            ],
-            out_specs=pl.BlockSpec((count * copies, size, rhs), full),
-        ),
+    return pl.pallas_call(
+        kernel,
         out_shape=jax.ShapeDtypeStruct((count * copies, size, rhs), jnp.bfloat16),
         compiler_params=params(),
         name="last_solve",
-    )(scalars, own, other, inverse, solved)
+    )(own, other, inverse, solved)
 
 
 def on_device(right_sides, factor, pattern, lower_inverse, upper_inverse):
@@ -277,8 +265,9 @@
     everyone = [(r, c) for r in range(prow_n) for c in range(pcol_n)]
 
     is_low = row_id < prow_n // 2
+    hi_id = lax.axis_index("hi")
     lo_id = lax.axis_index("lo")
-    entries = [q_id, col_id, lo_id, is_low.astype(jnp.int32)]
+    entries = [q_id, col_id, lo_id]
     scalars = jnp.stack([jnp.asarray(v, jnp.int32) for v in entries])
     pattern = pattern.reshape(row_blocks, col_blocks)
     first_low = half // per
@@ -327,7 +316,7 @@
     low_rows = (half, low_starts)
     late_rows = (count(2) + count(3), lambda scal: [bounds[2]])
 
-    if per == prow_n and pcol_n & (pcol_n - 1) == 0:
+    if per == prow_n and lo_n == 2 and pcol_n & (pcol_n - 1) == 0:
 
         def chunk(r, c):
             q, s = c // prow_n, c % prow_n
@@ -347,10 +336,15 @@
         def exchange(values, t):
             return lax.ppermute(values, ALL_AXES, [(device(r, c), device(r, c ^ t)) for r, c in everyone])
 
-        inverse_rows, blocks = lax.optimization_barrier((inverse_rows, right_sides.reshape(per, size, rhs)))
         (one_zero,) = laid_out([inverse_rows], part(1, zero_groups, pcol_n))
         inverse_rows = lax.ppermute(inverse_rows, ALL_AXES, there)
-        blocks = lax.all_to_all(blocks, ROW_AXES, 0, 0, tiled=True)
+        blocks = right_sides.reshape(2, 2, size, rhs)
+        for axis, name, index in ((0, "hi", hi_id), (1, "lo", lo_id)):
+            other = lax.dynamic_index_in_dim(blocks, 1 - index, axis, keepdims=False)
+            other = lax.ppermute(other, name, [(0, 1), (1, 0)])
+            own = lax.dynamic_index_in_dim(blocks, index, axis, keepdims=False)
+            blocks = jnp.where(index == 0, jnp.stack([own, other], axis), jnp.stack([other, own], axis))
+        blocks = blocks.reshape(per, size, rhs)
         rest = lax.ppermute(blocks[first_low:], ALL_AXES, back)
         own_zero = solve_blocks(inverse_rows, blocks[:first_low], [one_zero])
         even = {t: exchange(own_zero, t) for t in range(pcol_n - 2, 0, -2)}
@@ -415,7 +409,9 @@
     solved = jnp.concatenate([one_solved, two_solved, three_solved], axis=0)
     solved = lax.dynamic_slice_in_dim(solved, per * lo_id, per, 0)
     last_inverse = lax.dynamic_slice_in_dim(upper_inverse, per * lo_id, per, 0)
-    slots = last_solve(scalars, 3, own, other, last_inverse, solved, spread_n)
+    last_inverse = jnp.where(is_low, last_inverse, jnp.zeros((), jnp.bfloat16))
+    solved = jnp.where(is_low, jnp.zeros((), jnp.bfloat16), solved)
+    slots = last_solve(own, other, last_inverse, solved, spread_n)
     received = lax.all_to_all(slots, COL_AXES, 0, 0, tiled=True)
     mine = lax.dynamic_slice_in_dim(received, lax.rem(col_id, spread_n) * per, per, 0)
     return mine.reshape(per * size, rhs)

time: 129 us -> 127 us (0.984)
    all_to_all x1 -> x0, starting transfers between devices: 4.25 us -> none  [on_device(): blocks = lax.all_to_all(blocks, ROW_AXES, 0, 0, tiled=True)]
    ppermute x0 -> x2, starting transfers between devices: none -> 4.23 us  [on_device(): other = lax.ppermute(other, name, [(0, 1), (1, 0)])]
    ppermute x10, waiting for transfers between devices: 22 us -> 20.1 us  [summands(): other = lax.ppermute(partial, ALL_AXES, pairs)]
    ppermute x1, starting transfers between devices: 2.83 us -> 1.41 us  [on_device(): rest = lax.ppermute(blocks[first_low:], ALL_AXES, back)]
    ppermute x10, starting transfers between devices: 12.2 us -> 13.6 us  [summands(): other = lax.ppermute(partial, ALL_AXES, pairs)]
    ppermute x7, starting transfers between devices: 9.29 us -> 8 us  [exchange(): lax.ppermute(values, ALL_AXES, [(device(r, c), device(r, c ^ t)) for r, c...]
  transfers between devices with their start and end apart: 33 -> 34, of which waited for: 20 -> 21; matrix products, arithmetic and copies ran while one was open for 0% -> 1% of each run, Pallas kernels for 12% -> 12%
where the time goes in v5:
time: 127 us
  starting transfers between devices  56.9 us (45%)
  waiting for transfers between devices  46 us (36%)
  Pallas kernels  19.3 us (15%)
  local copies, waits for them, and re-layouts  3.37 us (3%)
    ppermute x10, starting transfers between devices, spread(): lax.ppermute(values, ALL_AXES, [(device(r, c), device(*route(t, r, c))) f...  21.5 us
    ppermute x10, waiting for transfers between devices, summands(): other = lax.ppermute(partial, ALL_AXES, pairs)  20.1 us
    ppermute x10, starting transfers between devices, summands(): other = lax.ppermute(partial, ALL_AXES, pairs)  13.6 us
    pallas_call x5, Pallas kernels, lay_out(): pl.pallas_call(kernel, grid_spec=pltpu.PrefetchScalarGridSpec(num_scalar_...  12 us
    all_to_all x1, waiting for transfers between devices, on_device(): received = lax.all_to_all(slots, COL_AXES, 0, 0, tiled=True)  8.84 us
    ppermute x7, starting transfers between devices, exchange(): lax.ppermute(values, ALL_AXES, [(device(r, c), device(r, c ^ t)) for r, c...  8 us
    ppermute x10, waiting for transfers between devices, spread(): lax.ppermute(values, ALL_AXES, [(device(r, c), device(*route(t, r, c))) f...  6.02 us
    ppermute x1, waiting for transfers between devices, on_device(): other = lax.ppermute(own.astype(jnp.bfloat16), 'hi', [(0, 1), (1, 0)])  5.61 us
  transfers between devices with their start and end apart: 34, of which 21 were waited for; matrix products, arithmetic and copies ran while one was open for 1% of the time, Pallas kernels for 12%

profile of v5, /device:TPU:0, one launch (start us, length us, event | category | flops | bytes accessed | tf_op | source)
XLA Modules:
  0.0 126.5 jit_solution(6413163080326345036)
XLA Ops:
  0.9 3.0 %collective-permute-start.1 = (bf16[2,128,128]{2,1,0:T(8,128)(2,1)S(1)}, bf16[2,128,128]{2,1,0:T(8,128)(2,1)S(1)}, u32[]{:S(2)}, u32[]{:S(2)}) collective-permute-start(bf16[2,128,128]{2,1,0:T(8,128)(2,1)S(1)} %get-tuple-element.36), channel_id=1, source_target_pairs={{0,16},{16,0},{1,17},{17,1},{2,18},{18,2},{3,19},{19,3},{4,20},{20... | collective-permute-start | bytes 196616 | tf_op jit(solution)/shard_map/ppermute | solution.py:344
  3.9 1.0 slice.15
  4.9 2.6 %collective-permute-start = (bf16[2,128,128]{2,1,0:T(8,128)(2,1)S(1)}, bf16[2,128,128]{2,1,0:T(8,128)(2,1)S(1)}, u32[]{:S(2)}, u32[]{:S(2)}) collective-permute-start(bf16[2,128,128]{2,1,0:T(8,128)(2,1)S(1)} %dynamic-slice_bitcast_fusion.2.refs_1_), channel_id=1, source_target_pairs={{0,4},{1,12},{2,16},{3,24},{4,1},{5,9},{6,21},{7,29},{8,6},{9,14},... | collective-permute-start | bytes 196616 | tf_op jit(solution)/shard_map/ppermute | solution.py:340
  7.6 1.2 collective-permute-start.2
  9.6 2.3 %lay_out.5.refs_0_ = bf16[8,4,2,128,128]{4,3,2,1,0:T(8,128)(2,1)S(1)} custom-call(s32[3]{0:T(128)S(1)} %pad_add_fusion.scal, s32[16,32]{1,0:T(8,128)S(1)} %bitcast.26, bf16[16,4,8,128,128]{4,3,2,1,0:T(8,128)(2,1)} %bitcast.31, bf16[2,128,128]{2,1,0:T(8,128)(2,1)S(1)} %dynamic-slice_bitcast_fusion.2.refs_1_), custom_call_target="tpu_custom_call" | custom-call | bytes 8388608 | tf_op jit(solution)/shard_map/lay_out/pallas_call | solution.py:64
  12.2 2.9 %collective-permute-start.6 = (bf16[2,128,128]{2,1,0:T(8,128)(2,1)S(1)}, bf16[2,128,128]{2,1,0:T(8,128)(2,1)S(1)}, u32[]{:S(2)}, u32[]{:S(2)}) collective-permute-start(bf16[2,128,128]{2,1,0:T(8,128)(2,1)S(1)} %solve_blocks.1.refs_1_.refs_0_), channel_id=1, source_target_pairs={{0,4},{1,5},{2,6},{3,7},{4,0},{5,1},{6,2},{7,3},{8,12},{9,13},{10,... | collective-permute-start | bytes 196616 | tf_op jit(solution)/shard_map/ppermute | solution.py:337
  15.1 1.5 %collective-permute-start.8 = (bf16[2,128,128]{2,1,0:T(8,128)(2,1)S(1)}, bf16[2,128,128]{2,1,0:T(8,128)(2,1)S(1)}, u32[]{:S(2)}, u32[]{:S(2)}) collective-permute-start(bf16[2,128,128]{2,1,0:T(8,128)(2,1)S(1)} %solve_blocks.1.refs_1_.refs_0_), channel_id=1, source_target_pairs={{0,6},{1,7},{2,4},{3,5},{4,2},{5,3},{6,0},{7,1},{8,14},{9,15},{10,... | collective-permute-start | bytes 196616 | tf_op jit(solution)/shard_map/ppermute | solution.py:337
  17.4 1.4 %collective-permute-start.10 = (bf16[2,128,128]{2,1,0:T(8,128)(2,1)S(1)}, bf16[2,128,128]{2,1,0:T(8,128)(2,1)S(1)}, u32[]{:S(2)}, u32[]{:S(2)}) collective-permute-start(bf16[2,128,128]{2,1,0:T(8,128)(2,1)S(1)} %get-tuple-element.31), channel_id=1, source_target_pairs={{4,0},{12,1},{16,2},{24,3},{1,4},{9,5},{21,6},{29,7},{6,8},{14,9},... | collective-permute-start | bytes 196616 | tf_op jit(solution)/shard_map/ppermute | solution.py:348
  20.2 0.9 collective-permute-start.7
  21.3 1.2 collective-permute-start.9
  22.6 1.8 %collective-permute-done.10 = bf16[2,128,128]{2,1,0:T(8,128)(2,1)S(1)} collective-permute-done((bf16[2,128,128]{2,1,0:T(8,128)(2,1)S(1)}, bf16[2,128,128]{2,1,0:T(8,128)(2,1)S(1)}, u32[]{:S(2)}, u32[]{:S(2)}) %collective-permute-start.10) | collective-permute-done | bytes 65568 | tf_op jit(solution)/shard_map/ppermute | solution.py:348
  24.8 1.4 %collective-permute-done.9.refs_8_.refs_7_ = bf16[2,128,128]{2,1,0:T(8,128)(2,1)S(1)} collective-permute-done((bf16[2,128,128]{2,1,0:T(8,128)(2,1)S(1)}, bf16[2,128,128]{2,1,0:T(8,128)(2,1)S(1)}, u32[]{:S(2)}, u32[]{:S(2)}) %collective-permute-start.9) | collective-permute-done | bytes 65568 | tf_op jit(solution)/shard_map/ppermute | solution.py:337
  26.9 2.1 %collective-permute-start.11 = (bf16[4,128,128]{2,1,0:T(8,128)(2,1)S(1)}, bf16[4,128,128]{2,1,0:T(8,128)(2,1)S(1)}, u32[]{:S(2)}, u32[]{:S(2)}) collective-permute-start(bf16[4,128,128]{2,1,0:T(8,128)(2,1)S(1)} %block_sums.9), channel_id=1, source_target_pairs={{0,16},{1,17},{2,18},{3,19},{4,20},{5,21},{6,22},{7,23},{8,24},{9,... | collective-permute-start | bytes 393224 | tf_op jit(solution)/shard_map/ppermute | solution.py:300
  29.0 3.5 %collective-permute-done.11 = bf16[4,128,128]{2,1,0:T(8,128)(2,1)S(1)} collective-permute-done((bf16[4,128,128]{2,1,0:T(8,128)(2,1)S(1)}, bf16[4,128,128]{2,1,0:T(8,128)(2,1)S(1)}, u32[]{:S(2)}, u32[]{:S(2)}) %collective-permute-start.11) | collective-permute-done | bytes 131104 | tf_op jit(solution)/shard_map/ppermute | solution.py:300
  32.5 1.3 %collective-permute-done.12.refs_1_ = bf16[4,128,128]{2,1,0:T(8,128)(2,1)S(1)} collective-permute-done((bf16[4,128,128]{2,1,0:T(8,128)(2,1)S(1)}, bf16[4,128,128]{2,1,0:T(8,128)(2,1)S(1)}, u32[]{:S(2)}, u32[]{:S(2)}) %collective-permute-start.12) | collective-permute-done | bytes 131104 | tf_op jit(solution)/shard_map/ppermute | solution.py:300
  34.1 1.5 %collective-permute-start.13 = (bf16[4,128,128]{2,1,0:T(8,128)(2,1)S(1)}, bf16[4,128,128]{2,1,0:T(8,128)(2,1)S(1)}, u32[]{:S(2)}, u32[]{:S(2)}) collective-permute-start(bf16[4,128,128]{2,1,0:T(8,128)(2,1)S(1)} %sum_and_solve.5.refs_2_), channel_id=1, source_target_pairs={{0,2},{1,10},{2,18},{3,26},{4,6},{5,14},{6,22},{7,30},{8,3},{9,11}... | collective-permute-start | bytes 393224 | tf_op jit(solution)/shard_map/ppermute | solution.py:285
  35.5 3.6 %collective-permute-start.14 = (bf16[4,128,128]{2,1,0:T(8,128)(2,1)S(1)}, bf16[4,128,128]{2,1,0:T(8,128)(2,1)S(1)}, u32[]{:S(2)}, u32[]{:S(2)}) collective-permute-start(bf16[4,128,128]{2,1,0:T(8,128)(2,1)S(1)} %sum_and_solve.5.refs_2_), channel_id=1, source_target_pairs={{0,7},{1,15},{2,21},{3,29},{4,1},{5,9},{6,19},{7,27},{8,6},{9,14},... | collective-permute-start | bytes 393224 | tf_op jit(solution)/shard_map/ppermute | solution.py:285
  40.0 2.5 %lay_out.6 = (bf16[8,4,2,128,128]{4,3,2,1,0:T(8,128)(2,1)S(1)}, bf16[4,2,2,128,128]{4,3,2,1,0:T(8,128)(2,1)S(1)}) custom-call(s32[3]{0:T(128)S(1)} %pad_add_fusion.scal, s32[16,32]{1,0:T(8,128)S(1)} %bitcast.27, bf16[16,16,2,128,128]{4,3,2,1,0:T(8,128)(2,1)} %bitcast.32, bf16[16,4,8,128,128]{4,3,2,1,0:T(8,128)(2,1)} %bitcast.33, ...), custom_call_target="tpu_custom_call" | custom-call | bytes 10485760 | tf_op jit(solution)/shard_map/lay_out/pallas_call | solution.py:64
  44.2 2.2 %collective-permute-start.15 = (bf16[2,128,128]{2,1,0:T(8,128)(2,1)S(1)}, bf16[2,128,128]{2,1,0:T(8,128)(2,1)S(1)}, u32[]{:S(2)}, u32[]{:S(2)}) collective-permute-start(bf16[2,128,128]{2,1,0:T(8,128)(2,1)S(1)} %block_sums.11), channel_id=1, source_target_pairs={{0,16},{1,17},{2,18},{3,19},{4,20},{5,21},{6,22},{7,23},{8,24},{9,... | collective-permute-start | bytes 196616 | tf_op jit(solution)/shard_map/ppermute | solution.py:300
  46.4 2.8 %collective-permute-done.15 = bf16[2,128,128]{2,1,0:T(8,128)(2,1)S(1)} collective-permute-done((bf16[2,128,128]{2,1,0:T(8,128)(2,1)S(1)}, bf16[2,128,128]{2,1,0:T(8,128)(2,1)S(1)}, u32[]{:S(2)}, u32[]{:S(2)}) %collective-permute-start.15) | collective-permute-done | bytes 65568 | tf_op jit(solution)/shard_map/ppermute | solution.py:300
  49.4 1.1 collective-permute-done.16.refs_1_
  50.7 1.2 collective-permute-start.17
  51.9 2.9 %collective-permute-start.18 = (bf16[2,128,128]{2,1,0:T(8,128)(2,1)S(1)}, bf16[2,128,128]{2,1,0:T(8,128)(2,1)S(1)}, u32[]{:S(2)}, u32[]{:S(2)}) collective-permute-start(bf16[2,128,128]{2,1,0:T(8,128)(2,1)S(1)} %sum_and_solve.6.refs_1_.refs_2_), channel_id=1, source_target_pairs={{0,7},{1,15},{2,21},{3,29},{4,1},{5,9},{6,19},{7,27},{8,6},{9,14},... | collective-permute-start | bytes 196616 | tf_op jit(solution)/shard_map/ppermute | solution.py:285
  54.8 2.0 %lay_out.7 = (bf16[4,2,2,128,128]{4,3,2,1,0:T(8,128)(2,1)S(1)}, bf16[2,2,2,128,128]{4,3,2,1,0:T(8,128)(2,1)S(1)}) custom-call(s32[3]{0:T(128)S(1)} %pad_add_fusion.scal, s32[16,32]{1,0:T(8,128)S(1)} %bitcast.28, bf16[16,16,2,128,128]{4,3,2,1,0:T(8,128)(2,1)} %bitcast.34, bf16[2,128,128]{2,1,0:T(8,128)(2,1)S(1)} %sum_and_solve.6.refs_1_.refs_2_), custom_call_target="tpu_custom_call" | custom-call | bytes 3145728 | tf_op jit(solution)/shard_map/lay_out/pallas_call | solution.py:64
  57.3 3.1 %collective-permute-start.19 = (bf16[2,128,128]{2,1,0:T(8,128)(2,1)S(1)}, bf16[2,128,128]{2,1,0:T(8,128)(2,1)S(1)}, u32[]{:S(2)}, u32[]{:S(2)}) collective-permute-start(bf16[2,128,128]{2,1,0:T(8,128)(2,1)S(1)} %block_sums.13), channel_id=1, source_target_pairs={{0,16},{1,17},{2,18},{3,19},{4,20},{5,21},{6,22},{7,23},{8,24},{9,... | collective-permute-start | bytes 196616 | tf_op jit(solution)/shard_map/ppermute | solution.py:300
  60.4 2.2 %collective-permute-done.19 = bf16[2,128,128]{2,1,0:T(8,128)(2,1)S(1)} collective-permute-done((bf16[2,128,128]{2,1,0:T(8,128)(2,1)S(1)}, bf16[2,128,128]{2,1,0:T(8,128)(2,1)S(1)}, u32[]{:S(2)}, u32[]{:S(2)}) %collective-permute-start.19) | collective-permute-done | bytes 65568 | tf_op jit(solution)/shard_map/ppermute | solution.py:300
  63.3 0.9 collective-permute-done.20.refs_1_
  64.9 3.6 %collective-permute-start.22 = (bf16[2,128,128]{2,1,0:T(8,128)(2,1)S(1)}, bf16[2,128,128]{2,1,0:T(8,128)(2,1)S(1)}, u32[]{:S(2)}, u32[]{:S(2)}) collective-permute-start(bf16[2,128,128]{2,1,0:T(8,128)(2,1)S(1)} %sum_and_solve.7.refs_1_), channel_id=1, source_target_pairs={{0,7},{1,15},{2,21},{3,29},{4,1},{5,9},{6,19},{7,27},{8,6},{9,14},... | collective-permute-start | bytes 196616 | tf_op jit(solution)/shard_map/ppermute | solution.py:285
  68.5 2.5 %lay_out.8 = (bf16[2,2,2,128,128]{4,3,2,1,0:T(8,128)(2,1)S(1)}, bf16[2,4,2,128,128]{4,3,2,1,0:T(8,128)(2,1)S(1)}, bf16[2,4,2,128,128]{4,3,2,1,0:T(8,128)(2,1)S(1)}, bf16[2,8,2,128,128]{4,3,2,1,0:T(8,128)(2,1)S(1)}) custom-call(s32[3]{0:T(128)S(1)} %pad_add_fusion.scal, s32[16,32]{1,0:T(8,128)S(1)} %bitcast.29, bf16[16,16,2,128,128]{4,3,2,1,0:T(8,128)(2,1)} %bitcast.35, ...), custom_call_target="tpu_custom_call" | custom-call | bytes 9437184 | tf_op jit(solution)/shard_map/lay_out/pallas_call | solution.py:64
  71.3 1.7 %collective-permute-start.23 = (bf16[2,128,128]{2,1,0:T(8,128)(2,1)S(1)}, bf16[2,128,128]{2,1,0:T(8,128)(2,1)S(1)}, u32[]{:S(2)}, u32[]{:S(2)}) collective-permute-start(bf16[2,128,128]{2,1,0:T(8,128)(2,1)S(1)} %block_sums.14), channel_id=1, source_target_pairs={{0,16},{1,17},{2,18},{3,19},{4,20},{5,21},{6,22},{7,23},{8,24},{9,... | collective-permute-start | bytes 196616 | tf_op jit(solution)/shard_map/ppermute | solution.py:300
  73.0 2.6 %collective-permute-done.23 = bf16[2,128,128]{2,1,0:T(8,128)(2,1)S(1)} collective-permute-done((bf16[2,128,128]{2,1,0:T(8,128)(2,1)S(1)}, bf16[2,128,128]{2,1,0:T(8,128)(2,1)S(1)}, u32[]{:S(2)}, u32[]{:S(2)}) %collective-permute-start.23) | collective-permute-done | bytes 65568 | tf_op jit(solution)/shard_map/ppermute | solution.py:300
  76.2 0.9 collective-permute-done.24.refs_1_
  77.3 2.1 %collective-permute-start.25 = (bf16[2,128,128]{2,1,0:T(8,128)(2,1)S(1)}, bf16[2,128,128]{2,1,0:T(8,128)(2,1)S(1)}, u32[]{:S(2)}, u32[]{:S(2)}) collective-permute-start(bf16[2,128,128]{2,1,0:T(8,128)(2,1)S(1)} %sum_and_solve.8.refs_1_), channel_id=1, source_target_pairs={{0,2},{1,10},{2,18},{3,26},{4,6},{5,14},{6,22},{7,30},{8,3},{9,11}... | collective-permute-start | bytes 196616 | tf_op jit(solution)/shard_map/ppermute | solution.py:285
  79.4 2.9 %collective-permute-start.26 = (bf16[2,128,128]{2,1,0:T(8,128)(2,1)S(1)}, bf16[2,128,128]{2,1,0:T(8,128)(2,1)S(1)}, u32[]{:S(2)}, u32[]{:S(2)}) collective-permute-start(bf16[2,128,128]{2,1,0:T(8,128)(2,1)S(1)} %sum_and_solve.8.refs_1_), channel_id=1, source_target_pairs={{0,7},{1,15},{2,21},{3,29},{4,1},{5,9},{6,19},{7,27},{8,6},{9,14},... | collective-permute-start | bytes 196616 | tf_op jit(solution)/shard_map/ppermute | solution.py:285
  82.6 2.1 %collective-permute-done.26.refs_2_.refs_5_ = bf16[2,128,128]{2,1,0:T(8,128)(2,1)S(1)} collective-permute-done((bf16[2,128,128]{2,1,0:T(8,128)(2,1)S(1)}, bf16[2,128,128]{2,1,0:T(8,128)(2,1)S(1)}, u32[]{:S(2)}, u32[]{:S(2)}) %collective-permute-start.26) | collective-permute-done | bytes 65568 | tf_op jit(solution)/shard_map/ppermute | solution.py:285
  85.0 1.4 %collective-permute-start.27 = (bf16[4,128,128]{2,1,0:T(8,128)(2,1)S(1)}, bf16[4,128,128]{2,1,0:T(8,128)(2,1)S(1)}, u32[]{:S(2)}, u32[]{:S(2)}) collective-permute-start(bf16[4,128,128]{2,1,0:T(8,128)(2,1)S(1)} %block_sums.16), channel_id=1, source_target_pairs={{0,16},{1,17},{2,18},{3,19},{4,20},{5,21},{6,22},{7,23},{8,24},{9,... | collective-permute-start | bytes 393224 | tf_op jit(solution)/shard_map/ppermute | solution.py:300
  86.3 3.7 %collective-permute-done.27 = bf16[4,128,128]{2,1,0:T(8,128)(2,1)S(1)} collective-permute-done((bf16[4,128,128]{2,1,0:T(8,128)(2,1)S(1)}, bf16[4,128,128]{2,1,0:T(8,128)(2,1)S(1)}, u32[]{:S(2)}, u32[]{:S(2)}) %collective-permute-start.27) | collective-permute-done | bytes 131104 | tf_op jit(solution)/shard_map/ppermute | solution.py:300
  90.1 1.7 %collective-permute-start.28 = (bf16[4,128,128]{2,1,0:T(8,128)(2,1)S(1)}, bf16[4,128,128]{2,1,0:T(8,128)(2,1)S(1)}, u32[]{:S(2)}, u32[]{:S(2)}) collective-permute-start(bf16[4,128,128]{2,1,0:T(8,128)(2,1)S(1)} %add.96.refs_0_), channel_id=1, source_target_pairs={{0,8},{1,9},{2,10},{3,11},{4,12},{5,13},{6,14},{7,15},{8,0},{9,1},... | collective-permute-start | bytes 393224 | tf_op jit(solution)/shard_map/ppermute | solution.py:300
  91.8 1.0 collective-permute-done.28.refs_1_
  93.0 1.2 collective-permute-start.29
  94.2 2.1 %collective-permute-start.30 = (bf16[4,128,128]{2,1,0:T(8,128)(2,1)S(1)}, bf16[4,128,128]{2,1,0:T(8,128)(2,1)S(1)}, u32[]{:S(2)}, u32[]{:S(2)}) collective-permute-start(bf16[4,128,128]{2,1,0:T(8,128)(2,1)S(1)} %sum_and_solve.9), channel_id=1, source_target_pairs={{0,7},{1,15},{2,21},{3,29},{4,1},{5,9},{6,19},{7,27},{8,6},{9,14},... | collective-permute-start | bytes 393224 | tf_op jit(solution)/shard_map/ppermute | solution.py:285
  96.3 2.7 %lay_out.9 = (bf16[2,8,2,128,128]{4,3,2,1,0:T(8,128)(2,1)S(1)}, bf16[4,8,2,128,128]{4,3,2,1,0:T(8,128)(2,1)S(1)}) custom-call(s32[3]{0:T(128)S(1)} %pad_add_fusion.scal, s32[16,32]{1,0:T(8,128)S(1)} %bitcast.30, bf16[16,16,2,128,128]{4,3,2,1,0:T(8,128)(2,1)} %bitcast.36, bf16[2,128,128]{2,1,0:T(8,128)(2,1)S(1)} %sum_and_solve.8.refs_1_), custom_call_target="tpu_custom_call" | custom-call | bytes 12582912 | tf_op jit(solution)/shard_map/lay_out/pallas_call | solution.py:64
  99.8 3.2 %collective-permute-done.30.refs_1_ = bf16[4,128,128]{2,1,0:T(8,128)(2,1)S(1)} collective-permute-done((bf16[4,128,128]{2,1,0:T(8,128)(2,1)S(1)}, bf16[4,128,128]{2,1,0:T(8,128)(2,1)S(1)}, u32[]{:S(2)}, u32[]{:S(2)}) %collective-permute-start.30) | collective-permute-done | bytes 131104 | tf_op jit(solution)/shard_map/ppermute | solution.py:285
  103.7 2.1 %collective-permute-start.31 = (bf16[4,128,128]{2,1,0:T(8,128)(2,1)S(1)}, bf16[4,128,128]{2,1,0:T(8,128)(2,1)S(1)}, u32[]{:S(2)}, u32[]{:S(2)}) collective-permute-start(bf16[4,128,128]{2,1,0:T(8,128)(2,1)S(1)} %get-tuple-element.28), channel_id=1, source_target_pairs={{0,8},{8,0},{1,9},{9,1},{2,10},{10,2},{3,11},{11,3},{4,12},{12,4},... | collective-permute-start | bytes 393224 | tf_op jit(solution)/shard_map/ppermute | solution.py:407
  105.8 1.0 collective-permute-done.31
  107.1 5.6 %collective-permute-done.32.other_ref = bf16[4,128,128]{2,1,0:T(8,128)(2,1)S(1)} collective-permute-done((bf16[4,128,128]{2,1,0:T(8,128)(2,1)S(1)}, bf16[4,128,128]{2,1,0:T(8,128)(2,1)S(1)}, u32[]{:S(2)}, u32[]{:S(2)}) %collective-permute-start.32) | collective-permute-done | bytes 131104 | tf_op jit(solution)/shard_map/ppermute | solution.py:408
  113.6 3.4 %all-to-all-start = ((bf16[8,128,128]{2,1,0:T(8,128)(2,1)}), bf16[8,128,128]{2,1,0:T(8,128)(2,1)S(1)}, u32[]{:S(2)}, u32[]{:S(2)}) async-start(bf16[8,128,128]{2,1,0:T(8,128)(2,1)} %last_solve.1), calls=%async_computation | async-start | bytes 524288 | tf_op jit(solution)/shard_map/all_to_all | solution.py:415
  117.0 8.8 %all-to-all-done = bf16[8,128,128]{2,1,0:T(8,128)(2,1)S(1)} async-done(((bf16[8,128,128]{2,1,0:T(8,128)(2,1)}), bf16[8,128,128]{2,1,0:T(8,128)(2,1)S(1)}, u32[]{:S(2)}, u32[]{:S(2)}) %all-to-all-start) | async-done | bytes 262176 | tf_op jit(solution)/shard_map/all_to_all | solution.py:415
  (73 shorter events, 15.5 us)
Async XLA Ops:
  0.9 6.7 %collective-permute-start.1 = (bf16[2,128,128]{2,1,0:T(8,128)(2,1)S(1)}, bf16[2,128,128]{2,1,0:T(8,128)(2,1)S(1)}, u32[]{:S(2)}, u32[]{:S(2)}) collective-permute-start(bf16[2,128,128]{2,1,0:T(8,128)(2,1)S(1)} %get-tuple-element.36), channel_id=1, source_target_pairs={{0,16},{16,0},{1,17},{17,1},{2,18},{18,2},{3,19},{19,3},{4,20},{20... | collective-permute-start | bytes 196616 | tf_op jit(solution)/shard_map/ppermute | solution.py:344
  4.9 7.0 %collective-permute-start = (bf16[2,128,128]{2,1,0:T(8,128)(2,1)S(1)}, bf16[2,128,128]{2,1,0:T(8,128)(2,1)S(1)}, u32[]{:S(2)}, u32[]{:S(2)}) collective-permute-start(bf16[2,128,128]{2,1,0:T(8,128)(2,1)S(1)} %dynamic-slice_bitcast_fusion.2.refs_1_), channel_id=1, source_target_pairs={{0,4},{1,12},{2,16},{3,24},{4,1},{5,9},{6,21},{7,29},{8,6},{9,14},... | collective-permute-start | bytes 196616 | tf_op jit(solution)/shard_map/ppermute | solution.py:340
  7.6 4.3 %collective-permute-start.2 = (bf16[2,128,128]{2,1,0:T(8,128)(2,1)S(1)}, bf16[2,128,128]{2,1,0:T(8,128)(2,1)S(1)}, u32[]{:S(2)}, u32[]{:S(2)}) collective-permute-start(bf16[2,128,128]{2,1,0:T(8,128)(2,1)S(1)} %get-tuple-element.34), channel_id=1, source_target_pairs={{0,8},{8,0},{1,9},{9,1},{2,10},{10,2},{3,11},{11,3},{4,12},{12,4},... | collective-permute-start | bytes 196616 | tf_op jit(solution)/shard_map/ppermute | solution.py:344
  8.9 0.7 copy-start.2
  12.1 21.8 %copy-start = (bf16[16,1,128,128]{3,2,1,0:T(8,128)(2,1)S(1)}, bf16[16,1,128,128]{3,2,1,0:T(8,128)(2,1)}, u32[]{:S(2)}) copy-start(bf16[16,1,128,128]{3,2,1,0:T(8,128)(2,1)} %refs_2_.5) | copy-start | bytes 1572868
  12.1 6.7 %collective-permute-start.4 = (bf16[2,128,128]{2,1,0:T(8,128)(2,1)S(1)}, bf16[2,128,128]{2,1,0:T(8,128)(2,1)S(1)}, u32[]{:S(2)}, u32[]{:S(2)}) collective-permute-start(bf16[2,128,128]{2,1,0:T(8,128)(2,1)S(1)} %solve_blocks.1.refs_1_.refs_0_), channel_id=1, source_target_pairs={{0,2},{1,3},{2,0},{3,1},{4,6},{5,7},{6,4},{7,5},{8,10},{9,11},{10,... | collective-permute-start | bytes 196616 | tf_op jit(solution)/shard_map/ppermute | solution.py:337
  12.2 7.9 %collective-permute-start.6 = (bf16[2,128,128]{2,1,0:T(8,128)(2,1)S(1)}, bf16[2,128,128]{2,1,0:T(8,128)(2,1)S(1)}, u32[]{:S(2)}, u32[]{:S(2)}) collective-permute-start(bf16[2,128,128]{2,1,0:T(8,128)(2,1)S(1)} %solve_blocks.1.refs_1_.refs_0_), channel_id=1, source_target_pairs={{0,4},{1,5},{2,6},{3,7},{4,0},{5,1},{6,2},{7,3},{8,12},{9,13},{10,... | collective-permute-start | bytes 196616 | tf_op jit(solution)/shard_map/ppermute | solution.py:337
  15.1 6.2 %collective-permute-start.8 = (bf16[2,128,128]{2,1,0:T(8,128)(2,1)S(1)}, bf16[2,128,128]{2,1,0:T(8,128)(2,1)S(1)}, u32[]{:S(2)}, u32[]{:S(2)}) collective-permute-start(bf16[2,128,128]{2,1,0:T(8,128)(2,1)S(1)} %solve_blocks.1.refs_1_.refs_0_), channel_id=1, source_target_pairs={{0,6},{1,7},{2,4},{3,5},{4,2},{5,3},{6,0},{7,1},{8,14},{9,15},{10,... | collective-permute-start | bytes 196616 | tf_op jit(solution)/shard_map/ppermute | solution.py:337
  16.6 8.0 %collective-permute-start.3 = (bf16[2,128,128]{2,1,0:T(8,128)(2,1)S(1)}, bf16[2,128,128]{2,1,0:T(8,128)(2,1)S(1)}, u32[]{:S(2)}, u32[]{:S(2)}) collective-permute-start(bf16[2,128,128]{2,1,0:T(8,128)(2,1)S(1)} %solve_blocks.1.refs_1_.refs_0_), channel_id=1, source_target_pairs={{0,1},{1,0},{2,3},{3,2},{4,5},{5,4},{6,7},{7,6},{8,9},{9,8},{10,11... | collective-permute-start | bytes 196616 | tf_op jit(solution)/shard_map/ppermute | solution.py:337
  17.4 7.1 %collective-permute-start.10 = (bf16[2,128,128]{2,1,0:T(8,128)(2,1)S(1)}, bf16[2,128,128]{2,1,0:T(8,128)(2,1)S(1)}, u32[]{:S(2)}, u32[]{:S(2)}) collective-permute-start(bf16[2,128,128]{2,1,0:T(8,128)(2,1)S(1)} %get-tuple-element.31), channel_id=1, source_target_pairs={{4,0},{12,1},{16,2},{24,3},{1,4},{9,5},{21,6},{29,7},{6,8},{14,9},... | collective-permute-start | bytes 196616 | tf_op jit(solution)/shard_map/ppermute | solution.py:348
  18.8 5.8 %collective-permute-start.5 = (bf16[2,128,128]{2,1,0:T(8,128)(2,1)S(1)}, bf16[2,128,128]{2,1,0:T(8,128)(2,1)S(1)}, u32[]{:S(2)}, u32[]{:S(2)}) collective-permute-start(bf16[2,128,128]{2,1,0:T(8,128)(2,1)S(1)} %collective-permute-done.4.refs_3_.refs_2_), channel_id=1, source_target_pairs={{0,1},{1,0},{2,3},{3,2},{4,5},{5,4},{6,7},{7,6},{8,9},{9,8},{10,11... | collective-permute-start | bytes 196616 | tf_op jit(solution)/shard_map/ppermute | solution.py:337
  20.2 4.7 %collective-permute-start.7 = (bf16[2,128,128]{2,1,0:T(8,128)(2,1)S(1)}, bf16[2,128,128]{2,1,0:T(8,128)(2,1)S(1)}, u32[]{:S(2)}, u32[]{:S(2)}) collective-permute-start(bf16[2,128,128]{2,1,0:T(8,128)(2,1)S(1)} %collective-permute-done.6.refs_5_.refs_4_), channel_id=1, source_target_pairs={{0,1},{1,0},{2,3},{3,2},{4,5},{5,4},{6,7},{7,6},{8,9},{9,8},{10,11... | collective-permute-start | bytes 196616 | tf_op jit(solution)/shard_map/ppermute | solution.py:337
  21.3 4.9 %collective-permute-start.9 = (bf16[2,128,128]{2,1,0:T(8,128)(2,1)S(1)}, bf16[2,128,128]{2,1,0:T(8,128)(2,1)S(1)}, u32[]{:S(2)}, u32[]{:S(2)}) collective-permute-start(bf16[2,128,128]{2,1,0:T(8,128)(2,1)S(1)} %collective-permute-done.8.refs_7_.refs_6_), channel_id=1, source_target_pairs={{0,1},{1,0},{2,3},{3,2},{4,5},{5,4},{6,7},{7,6},{8,9},{9,8},{10,11... | collective-permute-start | bytes 196616 | tf_op jit(solution)/shard_map/ppermute | solution.py:337
  24.6 15.4 %copy-start.3 = (s32[16,1,32,1]{2,3,1,0:T(1,128)S(1)}, s32[16,1,32,1]{2,3,1,0:T(1,128)}, u32[]{:S(2)}) copy-start(s32[16,1,32,1]{2,3,1,0:T(1,128)} %param.7) | copy-start | bytes 6148
  26.9 5.5 %collective-permute-start.11 = (bf16[4,128,128]{2,1,0:T(8,128)(2,1)S(1)}, bf16[4,128,128]{2,1,0:T(8,128)(2,1)S(1)}, u32[]{:S(2)}, u32[]{:S(2)}) collective-permute-start(bf16[4,128,128]{2,1,0:T(8,128)(2,1)S(1)} %block_sums.9), channel_id=1, source_target_pairs={{0,16},{1,17},{2,18},{3,19},{4,20},{5,21},{6,22},{7,23},{8,24},{9,... | collective-permute-start | bytes 393224 | tf_op jit(solution)/shard_map/ppermute | solution.py:300
  32.5 1.4 %collective-permute-start.12 = (bf16[4,128,128]{2,1,0:T(8,128)(2,1)S(1)}, bf16[4,128,128]{2,1,0:T(8,128)(2,1)S(1)}, u32[]{:S(2)}, u32[]{:S(2)}) collective-permute-start(bf16[4,128,128]{2,1,0:T(8,128)(2,1)S(1)} %add.92.refs_0_), channel_id=1, source_target_pairs={{0,8},{1,9},{2,10},{3,11},{4,12},{5,13},{6,14},{7,15},{8,0},{9,1},... | collective-permute-start | bytes 393224 | tf_op jit(solution)/shard_map/ppermute | solution.py:300
  34.1 9.2 %collective-permute-start.13 = (bf16[4,128,128]{2,1,0:T(8,128)(2,1)S(1)}, bf16[4,128,128]{2,1,0:T(8,128)(2,1)S(1)}, u32[]{:S(2)}, u32[]{:S(2)}) collective-permute-start(bf16[4,128,128]{2,1,0:T(8,128)(2,1)S(1)} %sum_and_solve.5.refs_2_), channel_id=1, source_target_pairs={{0,2},{1,10},{2,18},{3,26},{4,6},{5,14},{6,22},{7,30},{8,3},{9,11}... | collective-permute-start | bytes 393224 | tf_op jit(solution)/shard_map/ppermute | solution.py:285
  35.5 8.4 %collective-permute-start.14 = (bf16[4,128,128]{2,1,0:T(8,128)(2,1)S(1)}, bf16[4,128,128]{2,1,0:T(8,128)(2,1)S(1)}, u32[]{:S(2)}, u32[]{:S(2)}) collective-permute-start(bf16[4,128,128]{2,1,0:T(8,128)(2,1)S(1)} %sum_and_solve.5.refs_2_), channel_id=1, source_target_pairs={{0,7},{1,15},{2,21},{3,29},{4,1},{5,9},{6,19},{7,27},{8,6},{9,14},... | collective-permute-start | bytes 393224 | tf_op jit(solution)/shard_map/ppermute | solution.py:285
  44.2 5.0 %collective-permute-start.15 = (bf16[2,128,128]{2,1,0:T(8,128)(2,1)S(1)}, bf16[2,128,128]{2,1,0:T(8,128)(2,1)S(1)}, u32[]{:S(2)}, u32[]{:S(2)}) collective-permute-start(bf16[2,128,128]{2,1,0:T(8,128)(2,1)S(1)} %block_sums.11), channel_id=1, source_target_pairs={{0,16},{1,17},{2,18},{3,19},{4,20},{5,21},{6,22},{7,23},{8,24},{9,... | collective-permute-start | bytes 196616 | tf_op jit(solution)/shard_map/ppermute | solution.py:300
  49.3 1.3 %collective-permute-start.16 = (bf16[2,128,128]{2,1,0:T(8,128)(2,1)S(1)}, bf16[2,128,128]{2,1,0:T(8,128)(2,1)S(1)}, u32[]{:S(2)}, u32[]{:S(2)}) collective-permute-start(bf16[2,128,128]{2,1,0:T(8,128)(2,1)S(1)} %add.93.refs_0_), channel_id=1, source_target_pairs={{0,8},{1,9},{2,10},{3,11},{4,12},{5,13},{6,14},{7,15},{8,0},{9,1},... | collective-permute-start | bytes 196616 | tf_op jit(solution)/shard_map/ppermute | solution.py:300
  50.7 6.3 %collective-permute-start.17 = (bf16[2,128,128]{2,1,0:T(8,128)(2,1)S(1)}, bf16[2,128,128]{2,1,0:T(8,128)(2,1)S(1)}, u32[]{:S(2)}, u32[]{:S(2)}) collective-permute-start(bf16[2,128,128]{2,1,0:T(8,128)(2,1)S(1)} %sum_and_solve.6.refs_1_.refs_2_), channel_id=1, source_target_pairs={{0,2},{1,10},{2,18},{3,26},{4,6},{5,14},{6,22},{7,30},{8,3},{9,11}... | collective-permute-start | bytes 196616 | tf_op jit(solution)/shard_map/ppermute | solution.py:285
  51.9 5.2 %collective-permute-start.18 = (bf16[2,128,128]{2,1,0:T(8,128)(2,1)S(1)}, bf16[2,128,128]{2,1,0:T(8,128)(2,1)S(1)}, u32[]{:S(2)}, u32[]{:S(2)}) collective-permute-start(bf16[2,128,128]{2,1,0:T(8,128)(2,1)S(1)} %sum_and_solve.6.refs_1_.refs_2_), channel_id=1, source_target_pairs={{0,7},{1,15},{2,21},{3,29},{4,1},{5,9},{6,19},{7,27},{8,6},{9,14},... | collective-permute-start | bytes 196616 | tf_op jit(solution)/shard_map/ppermute | solution.py:285
  56.8 7.5 %copy-start.1 = (bf16[16,1,128,128]{3,2,1,0:T(8,128)(2,1)S(1)}, bf16[16,1,128,128]{3,2,1,0:T(8,128)(2,1)}, u32[]{:S(2)}) copy-start(bf16[16,1,128,128]{3,2,1,0:T(8,128)(2,1)} %refs_3_.5) | copy-start | bytes 1572868
  57.3 5.3 %collective-permute-start.19 = (bf16[2,128,128]{2,1,0:T(8,128)(2,1)S(1)}, bf16[2,128,128]{2,1,0:T(8,128)(2,1)S(1)}, u32[]{:S(2)}, u32[]{:S(2)}) collective-permute-start(bf16[2,128,128]{2,1,0:T(8,128)(2,1)S(1)} %block_sums.13), channel_id=1, source_target_pairs={{0,16},{1,17},{2,18},{3,19},{4,20},{5,21},{6,22},{7,23},{8,24},{9,... | collective-permute-start | bytes 196616 | tf_op jit(solution)/shard_map/ppermute | solution.py:300
  62.7 1.5 %collective-permute-start.20 = (bf16[2,128,128]{2,1,0:T(8,128)(2,1)S(1)}, bf16[2,128,128]{2,1,0:T(8,128)(2,1)S(1)}, u32[]{:S(2)}, u32[]{:S(2)}) collective-permute-start(bf16[2,128,128]{2,1,0:T(8,128)(2,1)S(1)} %add.94.refs_0_), channel_id=1, source_target_pairs={{0,8},{1,9},{2,10},{3,11},{4,12},{5,13},{6,14},{7,15},{8,0},{9,1},... | collective-permute-start | bytes 196616 | tf_op jit(solution)/shard_map/ppermute | solution.py:300
  64.5 6.5 %collective-permute-start.21 = (bf16[2,128,128]{2,1,0:T(8,128)(2,1)S(1)}, bf16[2,128,128]{2,1,0:T(8,128)(2,1)S(1)}, u32[]{:S(2)}, u32[]{:S(2)}) collective-permute-start(bf16[2,128,128]{2,1,0:T(8,128)(2,1)S(1)} %sum_and_solve.7.refs_1_), channel_id=1, source_target_pairs={{0,2},{1,10},{2,18},{3,26},{4,6},{5,14},{6,22},{7,30},{8,3},{9,11}... | collective-permute-start | bytes 196616 | tf_op jit(solution)/shard_map/ppermute | solution.py:285
  64.9 6.1 %collective-permute-start.22 = (bf16[2,128,128]{2,1,0:T(8,128)(2,1)S(1)}, bf16[2,128,128]{2,1,0:T(8,128)(2,1)S(1)}, u32[]{:S(2)}, u32[]{:S(2)}) collective-permute-start(bf16[2,128,128]{2,1,0:T(8,128)(2,1)S(1)} %sum_and_solve.7.refs_1_), channel_id=1, source_target_pairs={{0,7},{1,15},{2,21},{3,29},{4,1},{5,9},{6,19},{7,27},{8,6},{9,14},... | collective-permute-start | bytes 196616 | tf_op jit(solution)/shard_map/ppermute | solution.py:285
  71.3 4.3 %collective-permute-start.23 = (bf16[2,128,128]{2,1,0:T(8,128)(2,1)S(1)}, bf16[2,128,128]{2,1,0:T(8,128)(2,1)S(1)}, u32[]{:S(2)}, u32[]{:S(2)}) collective-permute-start(bf16[2,128,128]{2,1,0:T(8,128)(2,1)S(1)} %block_sums.14), channel_id=1, source_target_pairs={{0,16},{1,17},{2,18},{3,19},{4,20},{5,21},{6,22},{7,23},{8,24},{9,... | collective-permute-start | bytes 196616 | tf_op jit(solution)/shard_map/ppermute | solution.py:300
  75.6 1.5 %collective-permute-start.24 = (bf16[2,128,128]{2,1,0:T(8,128)(2,1)S(1)}, bf16[2,128,128]{2,1,0:T(8,128)(2,1)S(1)}, u32[]{:S(2)}, u32[]{:S(2)}) collective-permute-start(bf16[2,128,128]{2,1,0:T(8,128)(2,1)S(1)} %add.95.refs_0_), channel_id=1, source_target_pairs={{0,8},{1,9},{2,10},{3,11},{4,12},{5,13},{6,14},{7,15},{8,0},{9,1},... | collective-permute-start | bytes 196616 | tf_op jit(solution)/shard_map/ppermute | solution.py:300
  77.3 5.3 %collective-permute-start.25 = (bf16[2,128,128]{2,1,0:T(8,128)(2,1)S(1)}, bf16[2,128,128]{2,1,0:T(8,128)(2,1)S(1)}, u32[]{:S(2)}, u32[]{:S(2)}) collective-permute-start(bf16[2,128,128]{2,1,0:T(8,128)(2,1)S(1)} %sum_and_solve.8.refs_1_), channel_id=1, source_target_pairs={{0,2},{1,10},{2,18},{3,26},{4,6},{5,14},{6,22},{7,30},{8,3},{9,11}... | collective-permute-start | bytes 196616 | tf_op jit(solution)/shard_map/ppermute | solution.py:285
  79.4 5.3 %collective-permute-start.26 = (bf16[2,128,128]{2,1,0:T(8,128)(2,1)S(1)}, bf16[2,128,128]{2,1,0:T(8,128)(2,1)S(1)}, u32[]{:S(2)}, u32[]{:S(2)}) collective-permute-start(bf16[2,128,128]{2,1,0:T(8,128)(2,1)S(1)} %sum_and_solve.8.refs_1_), channel_id=1, source_target_pairs={{0,7},{1,15},{2,21},{3,29},{4,1},{5,9},{6,19},{7,27},{8,6},{9,14},... | collective-permute-start | bytes 196616 | tf_op jit(solution)/shard_map/ppermute | solution.py:285
  85.0 5.0 %collective-permute-start.27 = (bf16[4,128,128]{2,1,0:T(8,128)(2,1)S(1)}, bf16[4,128,128]{2,1,0:T(8,128)(2,1)S(1)}, u32[]{:S(2)}, u32[]{:S(2)}) collective-permute-start(bf16[4,128,128]{2,1,0:T(8,128)(2,1)S(1)} %block_sums.16), channel_id=1, source_target_pairs={{0,16},{1,17},{2,18},{3,19},{4,20},{5,21},{6,22},{7,23},{8,24},{9,... | collective-permute-start | bytes 393224 | tf_op jit(solution)/shard_map/ppermute | solution.py:300
  90.1 2.7 %collective-permute-start.28 = (bf16[4,128,128]{2,1,0:T(8,128)(2,1)S(1)}, bf16[4,128,128]{2,1,0:T(8,128)(2,1)S(1)}, u32[]{:S(2)}, u32[]{:S(2)}) collective-permute-start(bf16[4,128,128]{2,1,0:T(8,128)(2,1)S(1)} %add.96.refs_0_), channel_id=1, source_target_pairs={{0,8},{1,9},{2,10},{3,11},{4,12},{5,13},{6,14},{7,15},{8,0},{9,1},... | collective-permute-start | bytes 393224 | tf_op jit(solution)/shard_map/ppermute | solution.py:300
  93.0 6.8 %collective-permute-start.29 = (bf16[4,128,128]{2,1,0:T(8,128)(2,1)S(1)}, bf16[4,128,128]{2,1,0:T(8,128)(2,1)S(1)}, u32[]{:S(2)}, u32[]{:S(2)}) collective-permute-start(bf16[4,128,128]{2,1,0:T(8,128)(2,1)S(1)} %sum_and_solve.9), channel_id=1, source_target_pairs={{0,2},{1,10},{2,18},{3,26},{4,6},{5,14},{6,22},{7,30},{8,3},{9,11}... | collective-permute-start | bytes 393224 | tf_op jit(solution)/shard_map/ppermute | solution.py:285
  94.2 8.8 %collective-permute-start.30 = (bf16[4,128,128]{2,1,0:T(8,128)(2,1)S(1)}, bf16[4,128,128]{2,1,0:T(8,128)(2,1)S(1)}, u32[]{:S(2)}, u32[]{:S(2)}) collective-permute-start(bf16[4,128,128]{2,1,0:T(8,128)(2,1)S(1)} %sum_and_solve.9), channel_id=1, source_target_pairs={{0,7},{1,15},{2,21},{3,29},{4,1},{5,9},{6,19},{7,27},{8,6},{9,14},... | collective-permute-start | bytes 393224 | tf_op jit(solution)/shard_map/ppermute | solution.py:285
  103.7 3.1 %collective-permute-start.31 = (bf16[4,128,128]{2,1,0:T(8,128)(2,1)S(1)}, bf16[4,128,128]{2,1,0:T(8,128)(2,1)S(1)}, u32[]{:S(2)}, u32[]{:S(2)}) collective-permute-start(bf16[4,128,128]{2,1,0:T(8,128)(2,1)S(1)} %get-tuple-element.28), channel_id=1, source_target_pairs={{0,8},{8,0},{1,9},{9,1},{2,10},{10,2},{3,11},{11,3},{4,12},{12,4},... | collective-permute-start | bytes 393224 | tf_op jit(solution)/shard_map/ppermute | solution.py:407
  106.9 5.8 %collective-permute-start.32 = (bf16[4,128,128]{2,1,0:T(8,128)(2,1)S(1)}, bf16[4,128,128]{2,1,0:T(8,128)(2,1)S(1)}, u32[]{:S(2)}, u32[]{:S(2)}) collective-permute-start(bf16[4,128,128]{2,1,0:T(8,128)(2,1)S(1)} %get-tuple-element.29), channel_id=1, source_target_pairs={{0,16},{16,0},{1,17},{17,1},{2,18},{18,2},{3,19},{19,3},{4,20},{20... | collective-permute-start | bytes 393224 | tf_op jit(solution)/shard_map/ppermute | solution.py:408
  113.6 12.3 %all-to-all-start = ((bf16[8,128,128]{2,1,0:T(8,128)(2,1)}), bf16[8,128,128]{2,1,0:T(8,128)(2,1)S(1)}, u32[]{:S(2)}, u32[]{:S(2)}) async-start(bf16[8,128,128]{2,1,0:T(8,128)(2,1)} %last_solve.1), calls=%async_computation | async-start | bytes 524288 | tf_op jit(solution)/shard_map/all_to_all | solution.py:415

commit v6 on v5

--- a/solution.py
+++ b/solution.py
@@ -411,9 +411,28 @@
     last_inverse = lax.dynamic_slice_in_dim(upper_inverse, per * lo_id, per, 0)
     last_inverse = jnp.where(is_low, last_inverse, jnp.zeros((), jnp.bfloat16))
     solved = jnp.where(is_low, jnp.zeros((), jnp.bfloat16), solved)
-    slots = last_solve(own, other, last_inverse, solved, spread_n)
-    received = lax.all_to_all(slots, COL_AXES, 0, 0, tiled=True)
-    mine = lax.dynamic_slice_in_dim(received, lax.rem(col_id, spread_n) * per, per, 0)
+    if spread_n == 2 and per & (per - 1) == 0:
+        upper_id, last_id = col_id // 2, col_id % 2
+        rows = last_solve(own, other, last_inverse, solved, 1)
+
+        def pick(blocks, index):
+            return lax.dynamic_index_in_dim(blocks, index, 0, keepdims=False)
+
+        def crossed(values, t):
+            return lax.ppermute(values, ALL_AXES, [(device(r, c), device(r, c ^ t)) for r, c in everyone])
+
+        received = [crossed(pick(rows, upper_id ^ t), 2 * t) for t in range(per - 1, 0, -1)]
+        received = jnp.stack([pick(rows, upper_id)] + received[::-1])
+        kept, sent = [
+            jnp.stack([pick(received, upper_id ^ (per // 2 * p + i)) for i in range(per // 2)])
+            for p in (last_id, 1 - last_id)
+        ]
+        sent = crossed(sent, 1)
+        mine = jnp.where(last_id == 0, jnp.stack([kept, sent], 1), jnp.stack([sent, kept], 1))
+    else:
+        slots = last_solve(own, other, last_inverse, solved, spread_n)
+        received = lax.all_to_all(slots, COL_AXES, 0, 0, tiled=True)
+        mine = lax.dynamic_slice_in_dim(received, lax.rem(col_id, spread_n) * per, per, 0)
     return mine.reshape(per * size, rhs)
 
 

time: 127 us -> 126 us (level)
  waiting for transfers between devices: 46 us -> 44 us
  starting transfers between devices: 56.9 us -> 58.3 us
    all_to_all x1 -> x0, waiting for transfers between devices: 8.84 us -> none  [on_device(): received = lax.all_to_all(slots, COL_AXES, 0, 0, tiled=True)]
    ppermute x0 -> x4, waiting for transfers between devices: none -> 6.71 us  [crossed(): lax.ppermute(values, ALL_AXES, [(device(r, c), device(r, c ^ t)) for r, c...]
    ppermute x0 -> x4, starting transfers between devices: none -> 4.91 us  [crossed(): lax.ppermute(values, ALL_AXES, [(device(r, c), device(r, c ^ t)) for r, c...]
    all_to_all x1 -> x0, starting transfers between devices: 3.41 us -> none  [on_device(): received = lax.all_to_all(slots, COL_AXES, 0, 0, tiled=True)]
  transfers between devices with their start and end apart: 34 -> 37, of which waited for: 21 -> 23; matrix products, arithmetic and copies ran while one was open for 1% -> 1% of each run, Pallas kernels for 12% -> 12%
where the time goes in v6:
time: 126 us; the launch traced here: 125 us
  starting transfers between devices  58.3 us (46%)
  waiting for transfers between devices  44 us (35%)
  Pallas kernels  18.5 us (15%)
  local copies, waits for them, and re-layouts  3.41 us (3%)
    ppermute x10, starting transfers between devices, spread(): lax.ppermute(values, ALL_AXES, [(device(r, c), device(*route(t, r, c))) f...  21.5 us
    ppermute x10, waiting for transfers between devices, summands(): other = lax.ppermute(partial, ALL_AXES, pairs)  20.2 us
    ppermute x10, starting transfers between devices, summands(): other = lax.ppermute(partial, ALL_AXES, pairs)  13.5 us
    pallas_call x5, Pallas kernels, lay_out(): pl.pallas_call(kernel, grid_spec=pltpu.PrefetchScalarGridSpec(num_scalar_...  12 us
    ppermute x7, starting transfers between devices, exchange(): lax.ppermute(values, ALL_AXES, [(device(r, c), device(r, c ^ t)) for r, c...  7.97 us
    ppermute x4, waiting for transfers between devices, crossed(): lax.ppermute(values, ALL_AXES, [(device(r, c), device(r, c ^ t)) for r, c...  6.71 us
    ppermute x10, waiting for transfers between devices, spread(): lax.ppermute(values, ALL_AXES, [(device(r, c), device(*route(t, r, c))) f...  6.06 us
    ppermute x1, waiting for transfers between devices, on_device(): other = lax.ppermute(own.astype(jnp.bfloat16), 'hi', [(0, 1), (1, 0)])  5.58 us
  transfers between devices with their start and end apart: 37, of which 23 were waited for; matrix products, arithmetic and copies ran while one was open for 1% of the time, Pallas kernels for 12%

profile of v6, /device:TPU:0, one launch (start us, length us, event | category | flops | bytes accessed | tf_op | source)
XLA Modules:
  0.0 125.3 jit_solution(8875284135788426368)
XLA Ops:
  0.9 3.0 %collective-permute-start.1 = (bf16[2,128,128]{2,1,0:T(8,128)(2,1)S(1)}, bf16[2,128,128]{2,1,0:T(8,128)(2,1)S(1)}, u32[]{:S(2)}, u32[]{:S(2)}) collective-permute-start(bf16[2,128,128]{2,1,0:T(8,128)(2,1)S(1)} %get-tuple-element.44), channel_id=1, source_target_pairs={{0,16},{16,0},{1,17},{17,1},{2,18},{18,2},{3,19},{19,3},{4,20},{20... | collective-permute-start | bytes 196616 | tf_op jit(solution)/shard_map/ppermute | solution.py:344
  3.9 1.0 slice.15
  4.9 2.6 %collective-permute-start = (bf16[2,128,128]{2,1,0:T(8,128)(2,1)S(1)}, bf16[2,128,128]{2,1,0:T(8,128)(2,1)S(1)}, u32[]{:S(2)}, u32[]{:S(2)}) collective-permute-start(bf16[2,128,128]{2,1,0:T(8,128)(2,1)S(1)} %dynamic-slice_bitcast_fusion.2.refs_1_), channel_id=1, source_target_pairs={{0,4},{1,12},{2,16},{3,24},{4,1},{5,9},{6,21},{7,29},{8,6},{9,14},... | collective-permute-start | bytes 196616 | tf_op jit(solution)/shard_map/ppermute | solution.py:340
  7.6 1.2 collective-permute-start.2
  9.6 2.3 %lay_out.5.refs_0_ = bf16[8,4,2,128,128]{4,3,2,1,0:T(8,128)(2,1)S(1)} custom-call(s32[3]{0:T(128)S(1)} %pad_add_fusion.scal, s32[16,32]{1,0:T(8,128)S(1)} %bitcast.38, bf16[16,4,8,128,128]{4,3,2,1,0:T(8,128)(2,1)} %bitcast.43, bf16[2,128,128]{2,1,0:T(8,128)(2,1)S(1)} %dynamic-slice_bitcast_fusion.2.refs_1_), custom_call_target="tpu_custom_call" | custom-call | bytes 8388608 | tf_op jit(solution)/shard_map/lay_out/pallas_call | solution.py:64
  12.2 2.9 %collective-permute-start.6 = (bf16[2,128,128]{2,1,0:T(8,128)(2,1)S(1)}, bf16[2,128,128]{2,1,0:T(8,128)(2,1)S(1)}, u32[]{:S(2)}, u32[]{:S(2)}) collective-permute-start(bf16[2,128,128]{2,1,0:T(8,128)(2,1)S(1)} %solve_blocks.1.refs_1_.refs_0_), channel_id=1, source_target_pairs={{0,4},{1,5},{2,6},{3,7},{4,0},{5,1},{6,2},{7,3},{8,12},{9,13},{10,... | collective-permute-start | bytes 196616 | tf_op jit(solution)/shard_map/ppermute | solution.py:337
  15.1 1.5 %collective-permute-start.8 = (bf16[2,128,128]{2,1,0:T(8,128)(2,1)S(1)}, bf16[2,128,128]{2,1,0:T(8,128)(2,1)S(1)}, u32[]{:S(2)}, u32[]{:S(2)}) collective-permute-start(bf16[2,128,128]{2,1,0:T(8,128)(2,1)S(1)} %solve_blocks.1.refs_1_.refs_0_), channel_id=1, source_target_pairs={{0,6},{1,7},{2,4},{3,5},{4,2},{5,3},{6,0},{7,1},{8,14},{9,15},{10,... | collective-permute-start | bytes 196616 | tf_op jit(solution)/shard_map/ppermute | solution.py:337
  17.4 1.4 %collective-permute-start.10 = (bf16[2,128,128]{2,1,0:T(8,128)(2,1)S(1)}, bf16[2,128,128]{2,1,0:T(8,128)(2,1)S(1)}, u32[]{:S(2)}, u32[]{:S(2)}) collective-permute-start(bf16[2,128,128]{2,1,0:T(8,128)(2,1)S(1)} %get-tuple-element.39), channel_id=1, source_target_pairs={{4,0},{12,1},{16,2},{24,3},{1,4},{9,5},{21,6},{29,7},{6,8},{14,9},... | collective-permute-start | bytes 196616 | tf_op jit(solution)/shard_map/ppermute | solution.py:348
  21.3 1.2 collective-permute-start.9
  22.6 1.8 %collective-permute-done.10 = bf16[2,128,128]{2,1,0:T(8,128)(2,1)S(1)} collective-permute-done((bf16[2,128,128]{2,1,0:T(8,128)(2,1)S(1)}, bf16[2,128,128]{2,1,0:T(8,128)(2,1)S(1)}, u32[]{:S(2)}, u32[]{:S(2)}) %collective-permute-start.10) | collective-permute-done | bytes 65568 | tf_op jit(solution)/shard_map/ppermute | solution.py:348
  24.8 1.3 %collective-permute-done.9.refs_8_.refs_7_ = bf16[2,128,128]{2,1,0:T(8,128)(2,1)S(1)} collective-permute-done((bf16[2,128,128]{2,1,0:T(8,128)(2,1)S(1)}, bf16[2,128,128]{2,1,0:T(8,128)(2,1)S(1)}, u32[]{:S(2)}, u32[]{:S(2)}) %collective-permute-start.9) | collective-permute-done | bytes 65568 | tf_op jit(solution)/shard_map/ppermute | solution.py:337
  26.9 2.1 %collective-permute-start.11 = (bf16[4,128,128]{2,1,0:T(8,128)(2,1)S(1)}, bf16[4,128,128]{2,1,0:T(8,128)(2,1)S(1)}, u32[]{:S(2)}, u32[]{:S(2)}) collective-permute-start(bf16[4,128,128]{2,1,0:T(8,128)(2,1)S(1)} %block_sums.9), channel_id=1, source_target_pairs={{0,16},{1,17},{2,18},{3,19},{4,20},{5,21},{6,22},{7,23},{8,24},{9,... | collective-permute-start | bytes 393224 | tf_op jit(solution)/shard_map/ppermute | solution.py:300
  29.0 3.4 %collective-permute-done.11 = bf16[4,128,128]{2,1,0:T(8,128)(2,1)S(1)} collective-permute-done((bf16[4,128,128]{2,1,0:T(8,128)(2,1)S(1)}, bf16[4,128,128]{2,1,0:T(8,128)(2,1)S(1)}, u32[]{:S(2)}, u32[]{:S(2)}) %collective-permute-start.11) | collective-permute-done | bytes 131104 | tf_op jit(solution)/shard_map/ppermute | solution.py:300
  32.5 1.3 %collective-permute-done.12.refs_1_ = bf16[4,128,128]{2,1,0:T(8,128)(2,1)S(1)} collective-permute-done((bf16[4,128,128]{2,1,0:T(8,128)(2,1)S(1)}, bf16[4,128,128]{2,1,0:T(8,128)(2,1)S(1)}, u32[]{:S(2)}, u32[]{:S(2)}) %collective-permute-start.12) | collective-permute-done | bytes 131104 | tf_op jit(solution)/shard_map/ppermute | solution.py:300
  34.0 1.5 %collective-permute-start.13 = (bf16[4,128,128]{2,1,0:T(8,128)(2,1)S(1)}, bf16[4,128,128]{2,1,0:T(8,128)(2,1)S(1)}, u32[]{:S(2)}, u32[]{:S(2)}) collective-permute-start(bf16[4,128,128]{2,1,0:T(8,128)(2,1)S(1)} %sum_and_solve.5.refs_2_), channel_id=1, source_target_pairs={{0,2},{1,10},{2,18},{3,26},{4,6},{5,14},{6,22},{7,30},{8,3},{9,11}... | collective-permute-start | bytes 393224 | tf_op jit(solution)/shard_map/ppermute | solution.py:285
  35.5 3.6 %collective-permute-start.14 = (bf16[4,128,128]{2,1,0:T(8,128)(2,1)S(1)}, bf16[4,128,128]{2,1,0:T(8,128)(2,1)S(1)}, u32[]{:S(2)}, u32[]{:S(2)}) collective-permute-start(bf16[4,128,128]{2,1,0:T(8,128)(2,1)S(1)} %sum_and_solve.5.refs_2_), channel_id=1, source_target_pairs={{0,7},{1,15},{2,21},{3,29},{4,1},{5,9},{6,19},{7,27},{8,6},{9,14},... | collective-permute-start | bytes 393224 | tf_op jit(solution)/shard_map/ppermute | solution.py:285
  40.0 2.5 %lay_out.6 = (bf16[8,4,2,128,128]{4,3,2,1,0:T(8,128)(2,1)S(1)}, bf16[4,2,2,128,128]{4,3,2,1,0:T(8,128)(2,1)S(1)}) custom-call(s32[3]{0:T(128)S(1)} %pad_add_fusion.scal, s32[16,32]{1,0:T(8,128)S(1)} %bitcast.39, bf16[16,16,2,128,128]{4,3,2,1,0:T(8,128)(2,1)} %bitcast.44, bf16[16,4,8,128,128]{4,3,2,1,0:T(8,128)(2,1)} %bitcast.45, ...), custom_call_target="tpu_custom_call" | custom-call | bytes 10485760 | tf_op jit(solution)/shard_map/lay_out/pallas_call | solution.py:64
  44.2 2.2 %collective-permute-start.15 = (bf16[2,128,128]{2,1,0:T(8,128)(2,1)S(1)}, bf16[2,128,128]{2,1,0:T(8,128)(2,1)S(1)}, u32[]{:S(2)}, u32[]{:S(2)}) collective-permute-start(bf16[2,128,128]{2,1,0:T(8,128)(2,1)S(1)} %block_sums.11), channel_id=1, source_target_pairs={{0,16},{1,17},{2,18},{3,19},{4,20},{5,21},{6,22},{7,23},{8,24},{9,... | collective-permute-start | bytes 196616 | tf_op jit(solution)/shard_map/ppermute | solution.py:300
  46.4 2.8 %collective-permute-done.15 = bf16[2,128,128]{2,1,0:T(8,128)(2,1)S(1)} collective-permute-done((bf16[2,128,128]{2,1,0:T(8,128)(2,1)S(1)}, bf16[2,128,128]{2,1,0:T(8,128)(2,1)S(1)}, u32[]{:S(2)}, u32[]{:S(2)}) %collective-permute-start.15) | collective-permute-done | bytes 65568 | tf_op jit(solution)/shard_map/ppermute | solution.py:300
  49.4 1.1 collective-permute-done.16.refs_1_
  50.7 1.2 collective-permute-start.17
  51.9 2.9 %collective-permute-start.18 = (bf16[2,128,128]{2,1,0:T(8,128)(2,1)S(1)}, bf16[2,128,128]{2,1,0:T(8,128)(2,1)S(1)}, u32[]{:S(2)}, u32[]{:S(2)}) collective-permute-start(bf16[2,128,128]{2,1,0:T(8,128)(2,1)S(1)} %sum_and_solve.6.refs_1_.refs_2_), channel_id=1, source_target_pairs={{0,7},{1,15},{2,21},{3,29},{4,1},{5,9},{6,19},{7,27},{8,6},{9,14},... | collective-permute-start | bytes 196616 | tf_op jit(solution)/shard_map/ppermute | solution.py:285
  54.8 2.0 %lay_out.7 = (bf16[4,2,2,128,128]{4,3,2,1,0:T(8,128)(2,1)S(1)}, bf16[2,2,2,128,128]{4,3,2,1,0:T(8,128)(2,1)S(1)}) custom-call(s32[3]{0:T(128)S(1)} %pad_add_fusion.scal, s32[16,32]{1,0:T(8,128)S(1)} %bitcast.40, bf16[16,16,2,128,128]{4,3,2,1,0:T(8,128)(2,1)} %bitcast.46, bf16[2,128,128]{2,1,0:T(8,128)(2,1)S(1)} %sum_and_solve.6.refs_1_.refs_2_), custom_call_target="tpu_custom_call" | custom-call | bytes 3145728 | tf_op jit(solution)/shard_map/lay_out/pallas_call | solution.py:64
  57.3 3.1 %collective-permute-start.19 = (bf16[2,128,128]{2,1,0:T(8,128)(2,1)S(1)}, bf16[2,128,128]{2,1,0:T(8,128)(2,1)S(1)}, u32[]{:S(2)}, u32[]{:S(2)}) collective-permute-start(bf16[2,128,128]{2,1,0:T(8,128)(2,1)S(1)} %block_sums.13), channel_id=1, source_target_pairs={{0,16},{1,17},{2,18},{3,19},{4,20},{5,21},{6,22},{7,23},{8,24},{9,... | collective-permute-start | bytes 196616 | tf_op jit(solution)/shard_map/ppermute | solution.py:300
  60.4 2.3 %collective-permute-done.19 = bf16[2,128,128]{2,1,0:T(8,128)(2,1)S(1)} collective-permute-done((bf16[2,128,128]{2,1,0:T(8,128)(2,1)S(1)}, bf16[2,128,128]{2,1,0:T(8,128)(2,1)S(1)}, u32[]{:S(2)}, u32[]{:S(2)}) %collective-permute-start.19) | collective-permute-done | bytes 65568 | tf_op jit(solution)/shard_map/ppermute | solution.py:300
  63.3 0.9 collective-permute-done.20.refs_1_
  64.9 3.6 %collective-permute-start.22 = (bf16[2,128,128]{2,1,0:T(8,128)(2,1)S(1)}, bf16[2,128,128]{2,1,0:T(8,128)(2,1)S(1)}, u32[]{:S(2)}, u32[]{:S(2)}) collective-permute-start(bf16[2,128,128]{2,1,0:T(8,128)(2,1)S(1)} %sum_and_solve.7.refs_1_), channel_id=1, source_target_pairs={{0,7},{1,15},{2,21},{3,29},{4,1},{5,9},{6,19},{7,27},{8,6},{9,14},... | collective-permute-start | bytes 196616 | tf_op jit(solution)/shard_map/ppermute | solution.py:285
  68.5 2.5 %lay_out.8 = (bf16[2,2,2,128,128]{4,3,2,1,0:T(8,128)(2,1)S(1)}, bf16[2,4,2,128,128]{4,3,2,1,0:T(8,128)(2,1)S(1)}, bf16[2,4,2,128,128]{4,3,2,1,0:T(8,128)(2,1)S(1)}, bf16[2,8,2,128,128]{4,3,2,1,0:T(8,128)(2,1)S(1)}) custom-call(s32[3]{0:T(128)S(1)} %pad_add_fusion.scal, s32[16,32]{1,0:T(8,128)S(1)} %bitcast.41, bf16[16,16,2,128,128]{4,3,2,1,0:T(8,128)(2,1)} %bitcast.47, ...), custom_call_target="tpu_custom_call" | custom-call | bytes 9437184 | tf_op jit(solution)/shard_map/lay_out/pallas_call | solution.py:64
  71.3 1.7 %collective-permute-start.23 = (bf16[2,128,128]{2,1,0:T(8,128)(2,1)S(1)}, bf16[2,128,128]{2,1,0:T(8,128)(2,1)S(1)}, u32[]{:S(2)}, u32[]{:S(2)}) collective-permute-start(bf16[2,128,128]{2,1,0:T(8,128)(2,1)S(1)} %block_sums.14), channel_id=1, source_target_pairs={{0,16},{1,17},{2,18},{3,19},{4,20},{5,21},{6,22},{7,23},{8,24},{9,... | collective-permute-start | bytes 196616 | tf_op jit(solution)/shard_map/ppermute | solution.py:300
  73.0 2.7 %collective-permute-done.23 = bf16[2,128,128]{2,1,0:T(8,128)(2,1)S(1)} collective-permute-done((bf16[2,128,128]{2,1,0:T(8,128)(2,1)S(1)}, bf16[2,128,128]{2,1,0:T(8,128)(2,1)S(1)}, u32[]{:S(2)}, u32[]{:S(2)}) %collective-permute-start.23) | collective-permute-done | bytes 65568 | tf_op jit(solution)/shard_map/ppermute | solution.py:300
  77.3 2.1 %collective-permute-start.25 = (bf16[2,128,128]{2,1,0:T(8,128)(2,1)S(1)}, bf16[2,128,128]{2,1,0:T(8,128)(2,1)S(1)}, u32[]{:S(2)}, u32[]{:S(2)}) collective-permute-start(bf16[2,128,128]{2,1,0:T(8,128)(2,1)S(1)} %sum_and_solve.8.refs_1_), channel_id=1, source_target_pairs={{0,2},{1,10},{2,18},{3,26},{4,6},{5,14},{6,22},{7,30},{8,3},{9,11}... | collective-permute-start | bytes 196616 | tf_op jit(solution)/shard_map/ppermute | solution.py:285
  79.4 2.9 %collective-permute-start.26 = (bf16[2,128,128]{2,1,0:T(8,128)(2,1)S(1)}, bf16[2,128,128]{2,1,0:T(8,128)(2,1)S(1)}, u32[]{:S(2)}, u32[]{:S(2)}) collective-permute-start(bf16[2,128,128]{2,1,0:T(8,128)(2,1)S(1)} %sum_and_solve.8.refs_1_), channel_id=1, source_target_pairs={{0,7},{1,15},{2,21},{3,29},{4,1},{5,9},{6,19},{7,27},{8,6},{9,14},... | collective-permute-start | bytes 196616 | tf_op jit(solution)/shard_map/ppermute | solution.py:285
  82.6 2.1 %collective-permute-done.26.refs_2_.refs_5_ = bf16[2,128,128]{2,1,0:T(8,128)(2,1)S(1)} collective-permute-done((bf16[2,128,128]{2,1,0:T(8,128)(2,1)S(1)}, bf16[2,128,128]{2,1,0:T(8,128)(2,1)S(1)}, u32[]{:S(2)}, u32[]{:S(2)}) %collective-permute-start.26) | collective-permute-done | bytes 65568 | tf_op jit(solution)/shard_map/ppermute | solution.py:285
  85.0 1.3 %collective-permute-start.27 = (bf16[4,128,128]{2,1,0:T(8,128)(2,1)S(1)}, bf16[4,128,128]{2,1,0:T(8,128)(2,1)S(1)}, u32[]{:S(2)}, u32[]{:S(2)}) collective-permute-start(bf16[4,128,128]{2,1,0:T(8,128)(2,1)S(1)} %block_sums.16), channel_id=1, source_target_pairs={{0,16},{1,17},{2,18},{3,19},{4,20},{5,21},{6,22},{7,23},{8,24},{9,... | collective-permute-start | bytes 393224 | tf_op jit(solution)/shard_map/ppermute | solution.py:300
  86.3 3.7 %collective-permute-done.27 = bf16[4,128,128]{2,1,0:T(8,128)(2,1)S(1)} collective-permute-done((bf16[4,128,128]{2,1,0:T(8,128)(2,1)S(1)}, bf16[4,128,128]{2,1,0:T(8,128)(2,1)S(1)}, u32[]{:S(2)}, u32[]{:S(2)}) %collective-permute-start.27) | collective-permute-done | bytes 131104 | tf_op jit(solution)/shard_map/ppermute | solution.py:300
  90.1 1.7 %collective-permute-start.28 = (bf16[4,128,128]{2,1,0:T(8,128)(2,1)S(1)}, bf16[4,128,128]{2,1,0:T(8,128)(2,1)S(1)}, u32[]{:S(2)}, u32[]{:S(2)}) collective-permute-start(bf16[4,128,128]{2,1,0:T(8,128)(2,1)S(1)} %add.129.refs_0_), channel_id=1, source_target_pairs={{0,8},{1,9},{2,10},{3,11},{4,12},{5,13},{6,14},{7,15},{8,0},{9,1},... | collective-permute-start | bytes 393224 | tf_op jit(solution)/shard_map/ppermute | solution.py:300
  91.8 1.0 collective-permute-done.28.refs_1_
  93.0 1.2 collective-permute-start.29
  94.2 2.1 %collective-permute-start.30 = (bf16[4,128,128]{2,1,0:T(8,128)(2,1)S(1)}, bf16[4,128,128]{2,1,0:T(8,128)(2,1)S(1)}, u32[]{:S(2)}, u32[]{:S(2)}) collective-permute-start(bf16[4,128,128]{2,1,0:T(8,128)(2,1)S(1)} %sum_and_solve.9), channel_id=1, source_target_pairs={{0,7},{1,15},{2,21},{3,29},{4,1},{5,9},{6,19},{7,27},{8,6},{9,14},... | collective-permute-start | bytes 393224 | tf_op jit(solution)/shard_map/ppermute | solution.py:285
  96.3 2.7 %lay_out.9 = (bf16[2,8,2,128,128]{4,3,2,1,0:T(8,128)(2,1)S(1)}, bf16[4,8,2,128,128]{4,3,2,1,0:T(8,128)(2,1)S(1)}) custom-call(s32[3]{0:T(128)S(1)} %pad_add_fusion.scal, s32[16,32]{1,0:T(8,128)S(1)} %bitcast.42, bf16[16,16,2,128,128]{4,3,2,1,0:T(8,128)(2,1)} %bitcast.48, bf16[2,128,128]{2,1,0:T(8,128)(2,1)S(1)} %sum_and_solve.8.refs_1_), custom_call_target="tpu_custom_call" | custom-call | bytes 12582912 | tf_op jit(solution)/shard_map/lay_out/pallas_call | solution.py:64
  99.8 3.2 %collective-permute-done.30.refs_1_ = bf16[4,128,128]{2,1,0:T(8,128)(2,1)S(1)} collective-permute-done((bf16[4,128,128]{2,1,0:T(8,128)(2,1)S(1)}, bf16[4,128,128]{2,1,0:T(8,128)(2,1)S(1)}, u32[]{:S(2)}, u32[]{:S(2)}) %collective-permute-start.30) | collective-permute-done | bytes 131104 | tf_op jit(solution)/shard_map/ppermute | solution.py:285
  103.7 2.1 %collective-permute-start.31 = (bf16[4,128,128]{2,1,0:T(8,128)(2,1)S(1)}, bf16[4,128,128]{2,1,0:T(8,128)(2,1)S(1)}, u32[]{:S(2)}, u32[]{:S(2)}) collective-permute-start(bf16[4,128,128]{2,1,0:T(8,128)(2,1)S(1)} %get-tuple-element.28), channel_id=1, source_target_pairs={{0,8},{8,0},{1,9},{9,1},{2,10},{10,2},{3,11},{11,3},{4,12},{12,4},... | collective-permute-start | bytes 393224 | tf_op jit(solution)/shard_map/ppermute | solution.py:407
  105.8 1.0 collective-permute-done.31
  107.1 5.6 %collective-permute-done.32.other_ref = bf16[4,128,128]{2,1,0:T(8,128)(2,1)S(1)} collective-permute-done((bf16[4,128,128]{2,1,0:T(8,128)(2,1)S(1)}, bf16[4,128,128]{2,1,0:T(8,128)(2,1)S(1)}, u32[]{:S(2)}, u32[]{:S(2)}) %collective-permute-start.32) | collective-permute-done | bytes 131104 | tf_op jit(solution)/shard_map/ppermute | solution.py:408
  114.5 2.9 %collective-permute-start.35 = (bf16[128,128]{1,0:T(8,128)(2,1)S(1)}, bf16[128,128]{1,0:T(8,128)(2,1)S(1)}, u32[]{:S(2)}, u32[]{:S(2)}) collective-permute-start(bf16[128,128]{1,0:T(8,128)(2,1)S(1)} %get-tuple-element.36), channel_id=1, source_target_pairs={{0,6},{1,7},{2,4},{3,5},{4,2},{5,3},{6,0},{7,1},{8,14},{9,15},{10,... | collective-permute-start | bytes 98312 | tf_op jit(solution)/shard_map/ppermute | solution.py:422
  117.3 1.2 collective-permute-done.34
  118.6 1.6 %collective-permute-done.35 = bf16[128,128]{1,0:T(8,128)(2,1)S(1)} collective-permute-done((bf16[128,128]{1,0:T(8,128)(2,1)S(1)}, bf16[128,128]{1,0:T(8,128)(2,1)S(1)}, u32[]{:S(2)}, u32[]{:S(2)}) %collective-permute-start.35) | collective-permute-done | bytes 32800 | tf_op jit(solution)/shard_map/ppermute | solution.py:422
  120.7 3.9 %collective-permute-done.36 = bf16[2,128,128]{2,1,0:T(8,128)(2,1)S(1)} collective-permute-done((bf16[2,128,128]{2,1,0:T(8,128)(2,1)S(1)}, bf16[2,128,128]{2,1,0:T(8,128)(2,1)S(1)}, u32[]{:S(2)}, u32[]{:S(2)}) %collective-permute-start.36) | collective-permute-done | bytes 65568 | tf_op jit(solution)/shard_map/ppermute | solution.py:422
  (85 shorter events, 18.6 us)
Async XLA Ops:
  0.9 6.7 %collective-permute-start.1 = (bf16[2,128,128]{2,1,0:T(8,128)(2,1)S(1)}, bf16[2,128,128]{2,1,0:T(8,128)(2,1)S(1)}, u32[]{:S(2)}, u32[]{:S(2)}) collective-permute-start(bf16[2,128,128]{2,1,0:T(8,128)(2,1)S(1)} %get-tuple-element.44), channel_id=1, source_target_pairs={{0,16},{16,0},{1,17},{17,1},{2,18},{18,2},{3,19},{19,3},{4,20},{20... | collective-permute-start | bytes 196616 | tf_op jit(solution)/shard_map/ppermute | solution.py:344
  4.9 7.1 %collective-permute-start = (bf16[2,128,128]{2,1,0:T(8,128)(2,1)S(1)}, bf16[2,128,128]{2,1,0:T(8,128)(2,1)S(1)}, u32[]{:S(2)}, u32[]{:S(2)}) collective-permute-start(bf16[2,128,128]{2,1,0:T(8,128)(2,1)S(1)} %dynamic-slice_bitcast_fusion.2.refs_1_), channel_id=1, source_target_pairs={{0,4},{1,12},{2,16},{3,24},{4,1},{5,9},{6,21},{7,29},{8,6},{9,14},... | collective-permute-start | bytes 196616 | tf_op jit(solution)/shard_map/ppermute | solution.py:340
  7.6 4.3 %collective-permute-start.2 = (bf16[2,128,128]{2,1,0:T(8,128)(2,1)S(1)}, bf16[2,128,128]{2,1,0:T(8,128)(2,1)S(1)}, u32[]{:S(2)}, u32[]{:S(2)}) collective-permute-start(bf16[2,128,128]{2,1,0:T(8,128)(2,1)S(1)} %get-tuple-element.42), channel_id=1, source_target_pairs={{0,8},{8,0},{1,9},{9,1},{2,10},{10,2},{3,11},{11,3},{4,12},{12,4},... | collective-permute-start | bytes 196616 | tf_op jit(solution)/shard_map/ppermute | solution.py:344
  8.9 0.7 copy-start.2
  12.1 21.7 %copy-start = (bf16[16,1,128,128]{3,2,1,0:T(8,128)(2,1)S(1)}, bf16[16,1,128,128]{3,2,1,0:T(8,128)(2,1)}, u32[]{:S(2)}) copy-start(bf16[16,1,128,128]{3,2,1,0:T(8,128)(2,1)} %refs_2_.5) | copy-start | bytes 1572868
  12.1 6.7 %collective-permute-start.4 = (bf16[2,128,128]{2,1,0:T(8,128)(2,1)S(1)}, bf16[2,128,128]{2,1,0:T(8,128)(2,1)S(1)}, u32[]{:S(2)}, u32[]{:S(2)}) collective-permute-start(bf16[2,128,128]{2,1,0:T(8,128)(2,1)S(1)} %solve_blocks.1.refs_1_.refs_0_), channel_id=1, source_target_pairs={{0,2},{1,3},{2,0},{3,1},{4,6},{5,7},{6,4},{7,5},{8,10},{9,11},{10,... | collective-permute-start | bytes 196616 | tf_op jit(solution)/shard_map/ppermute | solution.py:337
  12.2 8.0 %collective-permute-start.6 = (bf16[2,128,128]{2,1,0:T(8,128)(2,1)S(1)}, bf16[2,128,128]{2,1,0:T(8,128)(2,1)S(1)}, u32[]{:S(2)}, u32[]{:S(2)}) collective-permute-start(bf16[2,128,128]{2,1,0:T(8,128)(2,1)S(1)} %solve_blocks.1.refs_1_.refs_0_), channel_id=1, source_target_pairs={{0,4},{1,5},{2,6},{3,7},{4,0},{5,1},{6,2},{7,3},{8,12},{9,13},{10,... | collective-permute-start | bytes 196616 | tf_op jit(solution)/shard_map/ppermute | solution.py:337
  15.1 6.2 %collective-permute-start.8 = (bf16[2,128,128]{2,1,0:T(8,128)(2,1)S(1)}, bf16[2,128,128]{2,1,0:T(8,128)(2,1)S(1)}, u32[]{:S(2)}, u32[]{:S(2)}) collective-permute-start(bf16[2,128,128]{2,1,0:T(8,128)(2,1)S(1)} %solve_blocks.1.refs_1_.refs_0_), channel_id=1, source_target_pairs={{0,6},{1,7},{2,4},{3,5},{4,2},{5,3},{6,0},{7,1},{8,14},{9,15},{10,... | collective-permute-start | bytes 196616 | tf_op jit(solution)/shard_map/ppermute | solution.py:337
  16.6 8.0 %collective-permute-start.3 = (bf16[2,128,128]{2,1,0:T(8,128)(2,1)S(1)}, bf16[2,128,128]{2,1,0:T(8,128)(2,1)S(1)}, u32[]{:S(2)}, u32[]{:S(2)}) collective-permute-start(bf16[2,128,128]{2,1,0:T(8,128)(2,1)S(1)} %solve_blocks.1.refs_1_.refs_0_), channel_id=1, source_target_pairs={{0,1},{1,0},{2,3},{3,2},{4,5},{5,4},{6,7},{7,6},{8,9},{9,8},{10,11... | collective-permute-start | bytes 196616 | tf_op jit(solution)/shard_map/ppermute | solution.py:337
  17.4 7.1 %collective-permute-start.10 = (bf16[2,128,128]{2,1,0:T(8,128)(2,1)S(1)}, bf16[2,128,128]{2,1,0:T(8,128)(2,1)S(1)}, u32[]{:S(2)}, u32[]{:S(2)}) collective-permute-start(bf16[2,128,128]{2,1,0:T(8,128)(2,1)S(1)} %get-tuple-element.39), channel_id=1, source_target_pairs={{4,0},{12,1},{16,2},{24,3},{1,4},{9,5},{21,6},{29,7},{6,8},{14,9},... | collective-permute-start | bytes 196616 | tf_op jit(solution)/shard_map/ppermute | solution.py:348
  18.8 5.8 %collective-permute-start.5 = (bf16[2,128,128]{2,1,0:T(8,128)(2,1)S(1)}, bf16[2,128,128]{2,1,0:T(8,128)(2,1)S(1)}, u32[]{:S(2)}, u32[]{:S(2)}) collective-permute-start(bf16[2,128,128]{2,1,0:T(8,128)(2,1)S(1)} %collective-permute-done.4.refs_3_.refs_2_), channel_id=1, source_target_pairs={{0,1},{1,0},{2,3},{3,2},{4,5},{5,4},{6,7},{7,6},{8,9},{9,8},{10,11... | collective-permute-start | bytes 196616 | tf_op jit(solution)/shard_map/ppermute | solution.py:337
  20.2 4.7 %collective-permute-start.7 = (bf16[2,128,128]{2,1,0:T(8,128)(2,1)S(1)}, bf16[2,128,128]{2,1,0:T(8,128)(2,1)S(1)}, u32[]{:S(2)}, u32[]{:S(2)}) collective-permute-start(bf16[2,128,128]{2,1,0:T(8,128)(2,1)S(1)} %collective-permute-done.6.refs_5_.refs_4_), channel_id=1, source_target_pairs={{0,1},{1,0},{2,3},{3,2},{4,5},{5,4},{6,7},{7,6},{8,9},{9,8},{10,11... | collective-permute-start | bytes 196616 | tf_op jit(solution)/shard_map/ppermute | solution.py:337
  21.3 4.9 %collective-permute-start.9 = (bf16[2,128,128]{2,1,0:T(8,128)(2,1)S(1)}, bf16[2,128,128]{2,1,0:T(8,128)(2,1)S(1)}, u32[]{:S(2)}, u32[]{:S(2)}) collective-permute-start(bf16[2,128,128]{2,1,0:T(8,128)(2,1)S(1)} %collective-permute-done.8.refs_7_.refs_6_), channel_id=1, source_target_pairs={{0,1},{1,0},{2,3},{3,2},{4,5},{5,4},{6,7},{7,6},{8,9},{9,8},{10,11... | collective-permute-start | bytes 196616 | tf_op jit(solution)/shard_map/ppermute | solution.py:337
  24.6 15.4 %copy-start.3 = (s32[16,1,32,1]{2,3,1,0:T(1,128)S(1)}, s32[16,1,32,1]{2,3,1,0:T(1,128)}, u32[]{:S(2)}) copy-start(s32[16,1,32,1]{2,3,1,0:T(1,128)} %param.7) | copy-start | bytes 6148
  26.9 5.5 %collective-permute-start.11 = (bf16[4,128,128]{2,1,0:T(8,128)(2,1)S(1)}, bf16[4,128,128]{2,1,0:T(8,128)(2,1)S(1)}, u32[]{:S(2)}, u32[]{:S(2)}) collective-permute-start(bf16[4,128,128]{2,1,0:T(8,128)(2,1)S(1)} %block_sums.9), channel_id=1, source_target_pairs={{0,16},{1,17},{2,18},{3,19},{4,20},{5,21},{6,22},{7,23},{8,24},{9,... | collective-permute-start | bytes 393224 | tf_op jit(solution)/shard_map/ppermute | solution.py:300
  32.4 1.4 %collective-permute-start.12 = (bf16[4,128,128]{2,1,0:T(8,128)(2,1)S(1)}, bf16[4,128,128]{2,1,0:T(8,128)(2,1)S(1)}, u32[]{:S(2)}, u32[]{:S(2)}) collective-permute-start(bf16[4,128,128]{2,1,0:T(8,128)(2,1)S(1)} %add.125.refs_0_), channel_id=1, source_target_pairs={{0,8},{1,9},{2,10},{3,11},{4,12},{5,13},{6,14},{7,15},{8,0},{9,1},... | collective-permute-start | bytes 393224 | tf_op jit(solution)/shard_map/ppermute | solution.py:300
  34.0 9.2 %collective-permute-start.13 = (bf16[4,128,128]{2,1,0:T(8,128)(2,1)S(1)}, bf16[4,128,128]{2,1,0:T(8,128)(2,1)S(1)}, u32[]{:S(2)}, u32[]{:S(2)}) collective-permute-start(bf16[4,128,128]{2,1,0:T(8,128)(2,1)S(1)} %sum_and_solve.5.refs_2_), channel_id=1, source_target_pairs={{0,2},{1,10},{2,18},{3,26},{4,6},{5,14},{6,22},{7,30},{8,3},{9,11}... | collective-permute-start | bytes 393224 | tf_op jit(solution)/shard_map/ppermute | solution.py:285
  35.5 8.4 %collective-permute-start.14 = (bf16[4,128,128]{2,1,0:T(8,128)(2,1)S(1)}, bf16[4,128,128]{2,1,0:T(8,128)(2,1)S(1)}, u32[]{:S(2)}, u32[]{:S(2)}) collective-permute-start(bf16[4,128,128]{2,1,0:T(8,128)(2,1)S(1)} %sum_and_solve.5.refs_2_), channel_id=1, source_target_pairs={{0,7},{1,15},{2,21},{3,29},{4,1},{5,9},{6,19},{7,27},{8,6},{9,14},... | collective-permute-start | bytes 393224 | tf_op jit(solution)/shard_map/ppermute | solution.py:285
  44.2 5.0 %collective-permute-start.15 = (bf16[2,128,128]{2,1,0:T(8,128)(2,1)S(1)}, bf16[2,128,128]{2,1,0:T(8,128)(2,1)S(1)}, u32[]{:S(2)}, u32[]{:S(2)}) collective-permute-start(bf16[2,128,128]{2,1,0:T(8,128)(2,1)S(1)} %block_sums.11), channel_id=1, source_target_pairs={{0,16},{1,17},{2,18},{3,19},{4,20},{5,21},{6,22},{7,23},{8,24},{9,... | collective-permute-start | bytes 196616 | tf_op jit(solution)/shard_map/ppermute | solution.py:300
  49.2 1.3 %collective-permute-start.16 = (bf16[2,128,128]{2,1,0:T(8,128)(2,1)S(1)}, bf16[2,128,128]{2,1,0:T(8,128)(2,1)S(1)}, u32[]{:S(2)}, u32[]{:S(2)}) collective-permute-start(bf16[2,128,128]{2,1,0:T(8,128)(2,1)S(1)} %add.126.refs_0_), channel_id=1, source_target_pairs={{0,8},{1,9},{2,10},{3,11},{4,12},{5,13},{6,14},{7,15},{8,0},{9,1},... | collective-permute-start | bytes 196616 | tf_op jit(solution)/shard_map/ppermute | solution.py:300
  50.7 6.4 %collective-permute-start.17 = (bf16[2,128,128]{2,1,0:T(8,128)(2,1)S(1)}, bf16[2,128,128]{2,1,0:T(8,128)(2,1)S(1)}, u32[]{:S(2)}, u32[]{:S(2)}) collective-permute-start(bf16[2,128,128]{2,1,0:T(8,128)(2,1)S(1)} %sum_and_solve.6.refs_1_.refs_2_), channel_id=1, source_target_pairs={{0,2},{1,10},{2,18},{3,26},{4,6},{5,14},{6,22},{7,30},{8,3},{9,11}... | collective-permute-start | bytes 196616 | tf_op jit(solution)/shard_map/ppermute | solution.py:285
  51.9 5.2 %collective-permute-start.18 = (bf16[2,128,128]{2,1,0:T(8,128)(2,1)S(1)}, bf16[2,128,128]{2,1,0:T(8,128)(2,1)S(1)}, u32[]{:S(2)}, u32[]{:S(2)}) collective-permute-start(bf16[2,128,128]{2,1,0:T(8,128)(2,1)S(1)} %sum_and_solve.6.refs_1_.refs_2_), channel_id=1, source_target_pairs={{0,7},{1,15},{2,21},{3,29},{4,1},{5,9},{6,19},{7,27},{8,6},{9,14},... | collective-permute-start | bytes 196616 | tf_op jit(solution)/shard_map/ppermute | solution.py:285
  56.8 7.4 %copy-start.1 = (bf16[16,1,128,128]{3,2,1,0:T(8,128)(2,1)S(1)}, bf16[16,1,128,128]{3,2,1,0:T(8,128)(2,1)}, u32[]{:S(2)}) copy-start(bf16[16,1,128,128]{3,2,1,0:T(8,128)(2,1)} %refs_3_.5) | copy-start | bytes 1572868
  57.3 5.4 %collective-permute-start.19 = (bf16[2,128,128]{2,1,0:T(8,128)(2,1)S(1)}, bf16[2,128,128]{2,1,0:T(8,128)(2,1)S(1)}, u32[]{:S(2)}, u32[]{:S(2)}) collective-permute-start(bf16[2,128,128]{2,1,0:T(8,128)(2,1)S(1)} %block_sums.13), channel_id=1, source_target_pairs={{0,16},{1,17},{2,18},{3,19},{4,20},{5,21},{6,22},{7,23},{8,24},{9,... | collective-permute-start | bytes 196616 | tf_op jit(solution)/shard_map/ppermute | solution.py:300
  62.8 1.4 %collective-permute-start.20 = (bf16[2,128,128]{2,1,0:T(8,128)(2,1)S(1)}, bf16[2,128,128]{2,1,0:T(8,128)(2,1)S(1)}, u32[]{:S(2)}, u32[]{:S(2)}) collective-permute-start(bf16[2,128,128]{2,1,0:T(8,128)(2,1)S(1)} %add.127.refs_0_), channel_id=1, source_target_pairs={{0,8},{1,9},{2,10},{3,11},{4,12},{5,13},{6,14},{7,15},{8,0},{9,1},... | collective-permute-start | bytes 196616 | tf_op jit(solution)/shard_map/ppermute | solution.py:300
  64.5 6.5 %collective-permute-start.21 = (bf16[2,128,128]{2,1,0:T(8,128)(2,1)S(1)}, bf16[2,128,128]{2,1,0:T(8,128)(2,1)S(1)}, u32[]{:S(2)}, u32[]{:S(2)}) collective-permute-start(bf16[2,128,128]{2,1,0:T(8,128)(2,1)S(1)} %sum_and_solve.7.refs_1_), channel_id=1, source_target_pairs={{0,2},{1,10},{2,18},{3,26},{4,6},{5,14},{6,22},{7,30},{8,3},{9,11}... | collective-permute-start | bytes 196616 | tf_op jit(solution)/shard_map/ppermute | solution.py:285
  64.9 6.1 %collective-permute-start.22 = (bf16[2,128,128]{2,1,0:T(8,128)(2,1)S(1)}, bf16[2,128,128]{2,1,0:T(8,128)(2,1)S(1)}, u32[]{:S(2)}, u32[]{:S(2)}) collective-permute-start(bf16[2,128,128]{2,1,0:T(8,128)(2,1)S(1)} %sum_and_solve.7.refs_1_), channel_id=1, source_target_pairs={{0,7},{1,15},{2,21},{3,29},{4,1},{5,9},{6,19},{7,27},{8,6},{9,14},... | collective-permute-start | bytes 196616 | tf_op jit(solution)/shard_map/ppermute | solution.py:285
  71.3 4.4 %collective-permute-start.23 = (bf16[2,128,128]{2,1,0:T(8,128)(2,1)S(1)}, bf16[2,128,128]{2,1,0:T(8,128)(2,1)S(1)}, u32[]{:S(2)}, u32[]{:S(2)}) collective-permute-start(bf16[2,128,128]{2,1,0:T(8,128)(2,1)S(1)} %block_sums.14), channel_id=1, source_target_pairs={{0,16},{1,17},{2,18},{3,19},{4,20},{5,21},{6,22},{7,23},{8,24},{9,... | collective-permute-start | bytes 196616 | tf_op jit(solution)/shard_map/ppermute | solution.py:300
  75.7 1.4 %collective-permute-start.24 = (bf16[2,128,128]{2,1,0:T(8,128)(2,1)S(1)}, bf16[2,128,128]{2,1,0:T(8,128)(2,1)S(1)}, u32[]{:S(2)}, u32[]{:S(2)}) collective-permute-start(bf16[2,128,128]{2,1,0:T(8,128)(2,1)S(1)} %add.128.refs_0_), channel_id=1, source_target_pairs={{0,8},{1,9},{2,10},{3,11},{4,12},{5,13},{6,14},{7,15},{8,0},{9,1},... | collective-permute-start | bytes 196616 | tf_op jit(solution)/shard_map/ppermute | solution.py:300
  77.3 5.3 %collective-permute-start.25 = (bf16[2,128,128]{2,1,0:T(8,128)(2,1)S(1)}, bf16[2,128,128]{2,1,0:T(8,128)(2,1)S(1)}, u32[]{:S(2)}, u32[]{:S(2)}) collective-permute-start(bf16[2,128,128]{2,1,0:T(8,128)(2,1)S(1)} %sum_and_solve.8.refs_1_), channel_id=1, source_target_pairs={{0,2},{1,10},{2,18},{3,26},{4,6},{5,14},{6,22},{7,30},{8,3},{9,11}... | collective-permute-start | bytes 196616 | tf_op jit(solution)/shard_map/ppermute | solution.py:285
  79.4 5.3 %collective-permute-start.26 = (bf16[2,128,128]{2,1,0:T(8,128)(2,1)S(1)}, bf16[2,128,128]{2,1,0:T(8,128)(2,1)S(1)}, u32[]{:S(2)}, u32[]{:S(2)}) collective-permute-start(bf16[2,128,128]{2,1,0:T(8,128)(2,1)S(1)} %sum_and_solve.8.refs_1_), channel_id=1, source_target_pairs={{0,7},{1,15},{2,21},{3,29},{4,1},{5,9},{6,19},{7,27},{8,6},{9,14},... | collective-permute-start | bytes 196616 | tf_op jit(solution)/shard_map/ppermute | solution.py:285
  85.0 5.0 %collective-permute-start.27 = (bf16[4,128,128]{2,1,0:T(8,128)(2,1)S(1)}, bf16[4,128,128]{2,1,0:T(8,128)(2,1)S(1)}, u32[]{:S(2)}, u32[]{:S(2)}) collective-permute-start(bf16[4,128,128]{2,1,0:T(8,128)(2,1)S(1)} %block_sums.16), channel_id=1, source_target_pairs={{0,16},{1,17},{2,18},{3,19},{4,20},{5,21},{6,22},{7,23},{8,24},{9,... | collective-permute-start | bytes 393224 | tf_op jit(solution)/shard_map/ppermute | solution.py:300
  90.1 2.7 %collective-permute-start.28 = (bf16[4,128,128]{2,1,0:T(8,128)(2,1)S(1)}, bf16[4,128,128]{2,1,0:T(8,128)(2,1)S(1)}, u32[]{:S(2)}, u32[]{:S(2)}) collective-permute-start(bf16[4,128,128]{2,1,0:T(8,128)(2,1)S(1)} %add.129.refs_0_), channel_id=1, source_target_pairs={{0,8},{1,9},{2,10},{3,11},{4,12},{5,13},{6,14},{7,15},{8,0},{9,1},... | collective-permute-start | bytes 393224 | tf_op jit(solution)/shard_map/ppermute | solution.py:300
  93.0 6.8 %collective-permute-start.29 = (bf16[4,128,128]{2,1,0:T(8,128)(2,1)S(1)}, bf16[4,128,128]{2,1,0:T(8,128)(2,1)S(1)}, u32[]{:S(2)}, u32[]{:S(2)}) collective-permute-start(bf16[4,128,128]{2,1,0:T(8,128)(2,1)S(1)} %sum_and_solve.9), channel_id=1, source_target_pairs={{0,2},{1,10},{2,18},{3,26},{4,6},{5,14},{6,22},{7,30},{8,3},{9,11}... | collective-permute-start | bytes 393224 | tf_op jit(solution)/shard_map/ppermute | solution.py:285
  94.2 8.8 %collective-permute-start.30 = (bf16[4,128,128]{2,1,0:T(8,128)(2,1)S(1)}, bf16[4,128,128]{2,1,0:T(8,128)(2,1)S(1)}, u32[]{:S(2)}, u32[]{:S(2)}) collective-permute-start(bf16[4,128,128]{2,1,0:T(8,128)(2,1)S(1)} %sum_and_solve.9), channel_id=1, source_target_pairs={{0,7},{1,15},{2,21},{3,29},{4,1},{5,9},{6,19},{7,27},{8,6},{9,14},... | collective-permute-start | bytes 393224 | tf_op jit(solution)/shard_map/ppermute | solution.py:285
  103.7 3.1 %collective-permute-start.31 = (bf16[4,128,128]{2,1,0:T(8,128)(2,1)S(1)}, bf16[4,128,128]{2,1,0:T(8,128)(2,1)S(1)}, u32[]{:S(2)}, u32[]{:S(2)}) collective-permute-start(bf16[4,128,128]{2,1,0:T(8,128)(2,1)S(1)} %get-tuple-element.28), channel_id=1, source_target_pairs={{0,8},{8,0},{1,9},{9,1},{2,10},{10,2},{3,11},{11,3},{4,12},{12,4},... | collective-permute-start | bytes 393224 | tf_op jit(solution)/shard_map/ppermute | solution.py:407
  106.8 5.8 %collective-permute-start.32 = (bf16[4,128,128]{2,1,0:T(8,128)(2,1)S(1)}, bf16[4,128,128]{2,1,0:T(8,128)(2,1)S(1)}, u32[]{:S(2)}, u32[]{:S(2)}) collective-permute-start(bf16[4,128,128]{2,1,0:T(8,128)(2,1)S(1)} %get-tuple-element.29), channel_id=1, source_target_pairs={{0,16},{16,0},{1,17},{17,1},{2,18},{18,2},{3,19},{19,3},{4,20},{20... | collective-permute-start | bytes 393224 | tf_op jit(solution)/shard_map/ppermute | solution.py:408
  112.9 4.5 %collective-permute-start.33 = (bf16[128,128]{1,0:T(8,128)(2,1)S(1)}, bf16[128,128]{1,0:T(8,128)(2,1)S(1)}, u32[]{:S(2)}, u32[]{:S(2)}) collective-permute-start(bf16[128,128]{1,0:T(8,128)(2,1)S(1)} %get-tuple-element.38), channel_id=1, source_target_pairs={{0,2},{1,3},{2,0},{3,1},{4,6},{5,7},{6,4},{7,5},{8,10},{9,11},{10,... | collective-permute-start | bytes 98312 | tf_op jit(solution)/shard_map/ppermute | solution.py:422
  113.8 4.8 %collective-permute-start.34 = (bf16[128,128]{1,0:T(8,128)(2,1)S(1)}, bf16[128,128]{1,0:T(8,128)(2,1)S(1)}, u32[]{:S(2)}, u32[]{:S(2)}) collective-permute-start(bf16[128,128]{1,0:T(8,128)(2,1)S(1)} %get-tuple-element.37), channel_id=1, source_target_pairs={{0,4},{1,5},{2,6},{3,7},{4,0},{5,1},{6,2},{7,3},{8,12},{9,13},{10,... | collective-permute-start | bytes 98312 | tf_op jit(solution)/shard_map/ppermute | solution.py:422
  114.5 5.7 %collective-permute-start.35 = (bf16[128,128]{1,0:T(8,128)(2,1)S(1)}, bf16[128,128]{1,0:T(8,128)(2,1)S(1)}, u32[]{:S(2)}, u32[]{:S(2)}) collective-permute-start(bf16[128,128]{1,0:T(8,128)(2,1)S(1)} %get-tuple-element.36), channel_id=1, source_target_pairs={{0,6},{1,7},{2,4},{3,5},{4,2},{5,3},{6,0},{7,1},{8,14},{9,15},{10,... | collective-permute-start | bytes 98312 | tf_op jit(solution)/shard_map/ppermute | solution.py:422
  120.3 4.3 %collective-permute-start.36 = (bf16[2,128,128]{2,1,0:T(8,128)(2,1)S(1)}, bf16[2,128,128]{2,1,0:T(8,128)(2,1)S(1)}, u32[]{:S(2)}, u32[]{:S(2)}) collective-permute-start(bf16[2,128,128]{2,1,0:T(8,128)(2,1)S(1)} %pad_maximum_fusion.1), channel_id=1, source_target_pairs={{0,1},{1,0},{2,3},{3,2},{4,5},{5,4},{6,7},{7,6},{8,9},{9,8},{10,11... | collective-permute-start | bytes 196616 | tf_op jit(solution)/shard_map/ppermute | solution.py:422

commit v7 on v6

--- a/solution.py
+++ b/solution.py
@@ -76,7 +76,7 @@
             flops=0, bytes_accessed=sum(8 * math.prod(shape) for shape in shapes), transcendentals=0
         ),
         name="lay_out",
-    )(scalars, pattern, *[pltpu.with_memory_space_constraint(operand, pltpu.HBM) for operand in operands], *after)
+    )(scalars, pltpu.with_memory_space_constraint(pattern, pltpu.HBM), *[pltpu.with_memory_space_constraint(operand, pltpu.HBM) for operand in operands], *after)
 
 
 def block_sums(parts, first_row, row_count, acc, base, negate):
@@ -345,13 +345,13 @@
             own = lax.dynamic_index_in_dim(blocks, index, axis, keepdims=False)
             blocks = jnp.where(index == 0, jnp.stack([own, other], axis), jnp.stack([other, own], axis))
         blocks = blocks.reshape(per, size, rhs)
-        rest = lax.ppermute(blocks[first_low:], ALL_AXES, back)
         own_zero = solve_blocks(inverse_rows, blocks[:first_low], [one_zero])
         even = {t: exchange(own_zero, t) for t in range(pcol_n - 2, 0, -2)}
         even[0] = own_zero
         zero = []
         for t in range(0, pcol_n, 2):
             zero += [even[t], exchange(even[t], 1)]
+        rest = lax.ppermute(blocks[first_low:], ALL_AXES, back)
         zero_step = pcol_n
 
         owned = (jnp.arange(per) == chunk_id)[None, :, None, None]

time: 126 us -> 126 us (level)
  starting transfers between devices: 58.3 us -> 51.5 us
  waiting for transfers between devices: 44 us -> 50.6 us
    ppermute x10, waiting for transfers between devices: 20.2 us -> 25.4 us  [summands(): other = lax.ppermute(partial, ALL_AXES, pairs)]
    ppermute x10, starting transfers between devices: 13.5 us -> 8.29 us  [summands(): other = lax.ppermute(partial, ALL_AXES, pairs)]
    ppermute x10, starting transfers between devices: 21.5 us -> 19.7 us  [spread(): lax.ppermute(values, ALL_AXES, [(device(r, c), device(*route(t, r, c))) f...]
    ppermute x10, waiting for transfers between devices: 6.06 us -> 7.86 us  [spread(): lax.ppermute(values, ALL_AXES, [(device(r, c), device(*route(t, r, c))) f...]
  transfers between devices with their start and end apart: 37 -> 37, of which waited for: 23 -> 24; matrix products, arithmetic and copies ran while one was open for 1% -> 1% of each run, Pallas kernels for 12% -> 12%
where the time goes in v7:
time: 126 us; the launch traced here: 125 us
  starting transfers between devices  51.5 us (41%)
  waiting for transfers between devices  50.6 us (40%)
  Pallas kernels  19.3 us (15%)
  local copies, waits for them, and re-layouts  2.71 us (2%)
    ppermute x10, waiting for transfers between devices, summands(): other = lax.ppermute(partial, ALL_AXES, pairs)  25.4 us
    ppermute x10, starting transfers between devices, spread(): lax.ppermute(values, ALL_AXES, [(device(r, c), device(*route(t, r, c))) f...  19.7 us
    pallas_call x5, Pallas kernels, lay_out(): pl.pallas_call(kernel, grid_spec=pltpu.PrefetchScalarGridSpec(num_scalar_...  12.8 us
    ppermute x10, starting transfers between devices, summands(): other = lax.ppermute(partial, ALL_AXES, pairs)  8.29 us
    ppermute x7, starting transfers between devices, exchange(): lax.ppermute(values, ALL_AXES, [(device(r, c), device(r, c ^ t)) for r, c...  8.04 us
    ppermute x10, waiting for transfers between devices, spread(): lax.ppermute(values, ALL_AXES, [(device(r, c), device(*route(t, r, c))) f...  7.86 us
    ppermute x4, waiting for transfers between devices, crossed(): lax.ppermute(values, ALL_AXES, [(device(r, c), device(r, c ^ t)) for r, c...  5.99 us
    ppermute x1, waiting for transfers between devices, on_device(): other = lax.ppermute(own.astype(jnp.bfloat16), 'hi', [(0, 1), (1, 0)])  5.58 us
  transfers between devices with their start and end apart: 37, of which 24 were waited for; matrix products, arithmetic and copies ran while one was open for 1% of the time, Pallas kernels for 12%

profile of v7, /device:TPU:0, one launch (start us, length us, event | category | flops | bytes accessed | tf_op | source)
XLA Modules:
  0.0 125.1 jit_solution(10969707101842600513)
XLA Ops:
  0.0 0.9 constant_dynamic-slice_fusion.6
  0.9 3.0 %collective-permute-start.1 = (bf16[2,128,128]{2,1,0:T(8,128)(2,1)S(1)}, bf16[2,128,128]{2,1,0:T(8,128)(2,1)S(1)}, u32[]{:S(2)}, u32[]{:S(2)}) collective-permute-start(bf16[2,128,128]{2,1,0:T(8,128)(2,1)S(1)} %get-tuple-element.44), channel_id=1, source_target_pairs={{0,16},{16,0},{1,17},{17,1},{2,18},{18,2},{3,19},{19,3},{4,20},{20... | collective-permute-start | bytes 196616 | tf_op jit(solution)/shard_map/ppermute | solution.py:344
  3.9 1.0 slice.15
  4.9 2.6 %collective-permute-start = (bf16[2,128,128]{2,1,0:T(8,128)(2,1)S(1)}, bf16[2,128,128]{2,1,0:T(8,128)(2,1)S(1)}, u32[]{:S(2)}, u32[]{:S(2)}) collective-permute-start(bf16[2,128,128]{2,1,0:T(8,128)(2,1)S(1)} %dynamic-slice_bitcast_fusion.2.refs_1_), channel_id=1, source_target_pairs={{0,4},{1,12},{2,16},{3,24},{4,1},{5,9},{6,21},{7,29},{8,6},{9,14},... | collective-permute-start | bytes 196616 | tf_op jit(solution)/shard_map/ppermute | solution.py:340
  7.6 1.2 collective-permute-start.2
  8.9 2.5 %lay_out.5.refs_0_ = bf16[8,4,2,128,128]{4,3,2,1,0:T(8,128)(2,1)S(1)} custom-call(s32[3]{0:T(128)S(1)} %pad_add_fusion.scal, s32[16,32]{1,0:T(8,128)} %bitcast.45, bf16[16,4,8,128,128]{4,3,2,1,0:T(8,128)(2,1)} %bitcast.38, bf16[2,128,128]{2,1,0:T(8,128)(2,1)S(1)} %dynamic-slice_bitcast_fusion.2.refs_1_), custom_call_target="tpu_custom_call" | custom-call | bytes 8388608 | tf_op jit(solution)/shard_map/lay_out/pallas_call | solution.py:64
  12.0 3.1 %collective-permute-start.6 = (bf16[2,128,128]{2,1,0:T(8,128)(2,1)S(1)}, bf16[2,128,128]{2,1,0:T(8,128)(2,1)S(1)}, u32[]{:S(2)}, u32[]{:S(2)}) collective-permute-start(bf16[2,128,128]{2,1,0:T(8,128)(2,1)S(1)} %solve_blocks.1.refs_1_.refs_0_), channel_id=1, source_target_pairs={{0,4},{1,5},{2,6},{3,7},{4,0},{5,1},{6,2},{7,3},{8,12},{9,13},{10,... | collective-permute-start | bytes 196616 | tf_op jit(solution)/shard_map/ppermute | solution.py:337
  15.1 0.9 collective-permute-start.8
  16.0 1.4 %collective-permute-start.3 = (bf16[2,128,128]{2,1,0:T(8,128)(2,1)S(1)}, bf16[2,128,128]{2,1,0:T(8,128)(2,1)S(1)}, u32[]{:S(2)}, u32[]{:S(2)}) collective-permute-start(bf16[2,128,128]{2,1,0:T(8,128)(2,1)S(1)} %solve_blocks.1.refs_1_.refs_0_), channel_id=1, source_target_pairs={{0,1},{1,0},{2,3},{3,2},{4,5},{5,4},{6,7},{7,6},{8,9},{9,8},{10,11... | collective-permute-start | bytes 196616 | tf_op jit(solution)/shard_map/ppermute | solution.py:337
  17.4 1.4 %collective-permute-start.10 = (bf16[2,128,128]{2,1,0:T(8,128)(2,1)S(1)}, bf16[2,128,128]{2,1,0:T(8,128)(2,1)S(1)}, u32[]{:S(2)}, u32[]{:S(2)}) collective-permute-start(bf16[2,128,128]{2,1,0:T(8,128)(2,1)S(1)} %get-tuple-element.39), channel_id=1, source_target_pairs={{4,0},{12,1},{16,2},{24,3},{1,4},{9,5},{21,6},{29,7},{6,8},{14,9},... | collective-permute-start | bytes 196616 | tf_op jit(solution)/shard_map/ppermute | solution.py:354
  19.9 0.9 collective-permute-start.7
  20.8 0.9 collective-permute-done.8.refs_7_.refs_6_
  22.5 1.7 %collective-permute-done.10 = bf16[2,128,128]{2,1,0:T(8,128)(2,1)S(1)} collective-permute-done((bf16[2,128,128]{2,1,0:T(8,128)(2,1)S(1)}, bf16[2,128,128]{2,1,0:T(8,128)(2,1)S(1)}, u32[]{:S(2)}, u32[]{:S(2)}) %collective-permute-start.10) | collective-permute-done | bytes 65568 | tf_op jit(solution)/shard_map/ppermute | solution.py:354
  24.6 1.4 %collective-permute-done.9.refs_8_.refs_7_ = bf16[2,128,128]{2,1,0:T(8,128)(2,1)S(1)} collective-permute-done((bf16[2,128,128]{2,1,0:T(8,128)(2,1)S(1)}, bf16[2,128,128]{2,1,0:T(8,128)(2,1)S(1)}, u32[]{:S(2)}, u32[]{:S(2)}) %collective-permute-start.9) | collective-permute-done | bytes 65568 | tf_op jit(solution)/shard_map/ppermute | solution.py:337
  26.8 1.6 %collective-permute-start.11 = (bf16[4,128,128]{2,1,0:T(8,128)(2,1)S(1)}, bf16[4,128,128]{2,1,0:T(8,128)(2,1)S(1)}, u32[]{:S(2)}, u32[]{:S(2)}) collective-permute-start(bf16[4,128,128]{2,1,0:T(8,128)(2,1)S(1)} %block_sums.9), channel_id=1, source_target_pairs={{0,16},{1,17},{2,18},{3,19},{4,20},{5,21},{6,22},{7,23},{8,24},{9,... | collective-permute-start | bytes 393224 | tf_op jit(solution)/shard_map/ppermute | solution.py:300
  28.4 4.0 %collective-permute-done.11 = bf16[4,128,128]{2,1,0:T(8,128)(2,1)S(1)} collective-permute-done((bf16[4,128,128]{2,1,0:T(8,128)(2,1)S(1)}, bf16[4,128,128]{2,1,0:T(8,128)(2,1)S(1)}, u32[]{:S(2)}, u32[]{:S(2)}) %collective-permute-start.11) | collective-permute-done | bytes 131104 | tf_op jit(solution)/shard_map/ppermute | solution.py:300
  32.5 1.3 %collective-permute-done.12.refs_1_ = bf16[4,128,128]{2,1,0:T(8,128)(2,1)S(1)} collective-permute-done((bf16[4,128,128]{2,1,0:T(8,128)(2,1)S(1)}, bf16[4,128,128]{2,1,0:T(8,128)(2,1)S(1)}, u32[]{:S(2)}, u32[]{:S(2)}) %collective-permute-start.12) | collective-permute-done | bytes 131104 | tf_op jit(solution)/shard_map/ppermute | solution.py:300
  34.0 1.1 collective-permute-start.13
  35.1 3.5 %collective-permute-start.14 = (bf16[4,128,128]{2,1,0:T(8,128)(2,1)S(1)}, bf16[4,128,128]{2,1,0:T(8,128)(2,1)S(1)}, u32[]{:S(2)}, u32[]{:S(2)}) collective-permute-start(bf16[4,128,128]{2,1,0:T(8,128)(2,1)S(1)} %sum_and_solve.5.refs_2_), channel_id=1, source_target_pairs={{0,7},{1,15},{2,21},{3,29},{4,1},{5,9},{6,19},{7,27},{8,6},{9,14},... | collective-permute-start | bytes 393224 | tf_op jit(solution)/shard_map/ppermute | solution.py:285
  39.5 2.7 %lay_out.6 = (bf16[8,4,2,128,128]{4,3,2,1,0:T(8,128)(2,1)S(1)}, bf16[4,2,2,128,128]{4,3,2,1,0:T(8,128)(2,1)S(1)}) custom-call(s32[3]{0:T(128)S(1)} %pad_add_fusion.scal, s32[16,32]{1,0:T(8,128)} %bitcast.46, bf16[16,16,2,128,128]{4,3,2,1,0:T(8,128)(2,1)} %bitcast.39, bf16[16,4,8,128,128]{4,3,2,1,0:T(8,128)(2,1)} %bitcast.40, ...), custom_call_target="tpu_custom_call" | custom-call | bytes 10485760 | tf_op jit(solution)/shard_map/lay_out/pallas_call | solution.py:64
  42.9 0.8 collective-permute-done.14.refs_2_
  44.0 2.2 %collective-permute-start.15 = (bf16[2,128,128]{2,1,0:T(8,128)(2,1)S(1)}, bf16[2,128,128]{2,1,0:T(8,128)(2,1)S(1)}, u32[]{:S(2)}, u32[]{:S(2)}) collective-permute-start(bf16[2,128,128]{2,1,0:T(8,128)(2,1)S(1)} %block_sums.11), channel_id=1, source_target_pairs={{0,16},{1,17},{2,18},{3,19},{4,20},{5,21},{6,22},{7,23},{8,24},{9,... | collective-permute-start | bytes 196616 | tf_op jit(solution)/shard_map/ppermute | solution.py:300
  46.2 2.3 %collective-permute-done.15 = bf16[2,128,128]{2,1,0:T(8,128)(2,1)S(1)} collective-permute-done((bf16[2,128,128]{2,1,0:T(8,128)(2,1)S(1)}, bf16[2,128,128]{2,1,0:T(8,128)(2,1)S(1)}, u32[]{:S(2)}, u32[]{:S(2)}) %collective-permute-start.15) | collective-permute-done | bytes 65568 | tf_op jit(solution)/shard_map/ppermute | solution.py:300
  48.6 1.2 collective-permute-done.16.refs_1_
  50.0 1.9 %collective-permute-start.17 = (bf16[2,128,128]{2,1,0:T(8,128)(2,1)S(1)}, bf16[2,128,128]{2,1,0:T(8,128)(2,1)S(1)}, u32[]{:S(2)}, u32[]{:S(2)}) collective-permute-start(bf16[2,128,128]{2,1,0:T(8,128)(2,1)S(1)} %sum_and_solve.6.refs_1_.refs_2_), channel_id=1, source_target_pairs={{0,2},{1,10},{2,18},{3,26},{4,6},{5,14},{6,22},{7,30},{8,3},{9,11}... | collective-permute-start | bytes 196616 | tf_op jit(solution)/shard_map/ppermute | solution.py:285
  51.8 2.7 %collective-permute-start.18 = (bf16[2,128,128]{2,1,0:T(8,128)(2,1)S(1)}, bf16[2,128,128]{2,1,0:T(8,128)(2,1)S(1)}, u32[]{:S(2)}, u32[]{:S(2)}) collective-permute-start(bf16[2,128,128]{2,1,0:T(8,128)(2,1)S(1)} %sum_and_solve.6.refs_1_.refs_2_), channel_id=1, source_target_pairs={{0,7},{1,15},{2,21},{3,29},{4,1},{5,9},{6,19},{7,27},{8,6},{9,14},... | collective-permute-start | bytes 196616 | tf_op jit(solution)/shard_map/ppermute | solution.py:285
  54.5 2.1 %lay_out.7 = (bf16[4,2,2,128,128]{4,3,2,1,0:T(8,128)(2,1)S(1)}, bf16[2,2,2,128,128]{4,3,2,1,0:T(8,128)(2,1)S(1)}) custom-call(s32[3]{0:T(128)S(1)} %pad_add_fusion.scal, s32[16,32]{1,0:T(8,128)} %bitcast.47, bf16[16,16,2,128,128]{4,3,2,1,0:T(8,128)(2,1)} %bitcast.41, bf16[2,128,128]{2,1,0:T(8,128)(2,1)S(1)} %sum_and_solve.6.refs_1_.refs_2_), custom_call_target="tpu_custom_call" | custom-call | bytes 3145728 | tf_op jit(solution)/shard_map/lay_out/pallas_call | solution.py:64
  57.2 3.2 %collective-permute-start.19 = (bf16[2,128,128]{2,1,0:T(8,128)(2,1)S(1)}, bf16[2,128,128]{2,1,0:T(8,128)(2,1)S(1)}, u32[]{:S(2)}, u32[]{:S(2)}) collective-permute-start(bf16[2,128,128]{2,1,0:T(8,128)(2,1)S(1)} %block_sums.13), channel_id=1, source_target_pairs={{0,16},{1,17},{2,18},{3,19},{4,20},{5,21},{6,22},{7,23},{8,24},{9,... | collective-permute-start | bytes 196616 | tf_op jit(solution)/shard_map/ppermute | solution.py:300
  60.3 2.5 %collective-permute-done.19 = bf16[2,128,128]{2,1,0:T(8,128)(2,1)S(1)} collective-permute-done((bf16[2,128,128]{2,1,0:T(8,128)(2,1)S(1)}, bf16[2,128,128]{2,1,0:T(8,128)(2,1)S(1)}, u32[]{:S(2)}, u32[]{:S(2)}) %collective-permute-start.19) | collective-permute-done | bytes 65568 | tf_op jit(solution)/shard_map/ppermute | solution.py:300
  63.0 1.2 collective-permute-done.20.refs_1_
  65.0 4.3 %collective-permute-start.22 = (bf16[2,128,128]{2,1,0:T(8,128)(2,1)S(1)}, bf16[2,128,128]{2,1,0:T(8,128)(2,1)S(1)}, u32[]{:S(2)}, u32[]{:S(2)}) collective-permute-start(bf16[2,128,128]{2,1,0:T(8,128)(2,1)S(1)} %sum_and_solve.7.refs_1_), channel_id=1, source_target_pairs={{0,7},{1,15},{2,21},{3,29},{4,1},{5,9},{6,19},{7,27},{8,6},{9,14},... | collective-permute-start | bytes 196616 | tf_op jit(solution)/shard_map/ppermute | solution.py:285
  69.3 2.6 %lay_out.8 = (bf16[2,2,2,128,128]{4,3,2,1,0:T(8,128)(2,1)S(1)}, bf16[2,4,2,128,128]{4,3,2,1,0:T(8,128)(2,1)S(1)}, bf16[2,4,2,128,128]{4,3,2,1,0:T(8,128)(2,1)S(1)}, bf16[2,8,2,128,128]{4,3,2,1,0:T(8,128)(2,1)S(1)}) custom-call(s32[3]{0:T(128)S(1)} %pad_add_fusion.scal, s32[16,32]{1,0:T(8,128)} %bitcast.48, bf16[16,16,2,128,128]{4,3,2,1,0:T(8,128)(2,1)} %bitcast.42, ...), custom_call_target="tpu_custom_call" | custom-call | bytes 9437184 | tf_op jit(solution)/shard_map/lay_out/pallas_call | solution.py:64
  72.9 4.2 %collective-permute-done.23 = bf16[2,128,128]{2,1,0:T(8,128)(2,1)S(1)} collective-permute-done((bf16[2,128,128]{2,1,0:T(8,128)(2,1)S(1)}, bf16[2,128,128]{2,1,0:T(8,128)(2,1)S(1)}, u32[]{:S(2)}, u32[]{:S(2)}) %collective-permute-start.23) | collective-permute-done | bytes 65568 | tf_op jit(solution)/shard_map/ppermute | solution.py:300
  77.4 1.1 collective-permute-done.24.refs_1_
  79.2 3.3 %collective-permute-start.26 = (bf16[2,128,128]{2,1,0:T(8,128)(2,1)S(1)}, bf16[2,128,128]{2,1,0:T(8,128)(2,1)S(1)}, u32[]{:S(2)}, u32[]{:S(2)}) collective-permute-start(bf16[2,128,128]{2,1,0:T(8,128)(2,1)S(1)} %sum_and_solve.8.refs_1_), channel_id=1, source_target_pairs={{0,7},{1,15},{2,21},{3,29},{4,1},{5,9},{6,19},{7,27},{8,6},{9,14},... | collective-permute-start | bytes 196616 | tf_op jit(solution)/shard_map/ppermute | solution.py:285
  83.0 3.4 %collective-permute-done.26.refs_2_.refs_5_ = bf16[2,128,128]{2,1,0:T(8,128)(2,1)S(1)} collective-permute-done((bf16[2,128,128]{2,1,0:T(8,128)(2,1)S(1)}, bf16[2,128,128]{2,1,0:T(8,128)(2,1)S(1)}, u32[]{:S(2)}, u32[]{:S(2)}) %collective-permute-start.26) | collective-permute-done | bytes 65568 | tf_op jit(solution)/shard_map/ppermute | solution.py:285
  86.8 6.1 %collective-permute-done.27 = bf16[4,128,128]{2,1,0:T(8,128)(2,1)S(1)} collective-permute-done((bf16[4,128,128]{2,1,0:T(8,128)(2,1)S(1)}, bf16[4,128,128]{2,1,0:T(8,128)(2,1)S(1)}, u32[]{:S(2)}, u32[]{:S(2)}) %collective-permute-start.27) | collective-permute-done | bytes 131104 | tf_op jit(solution)/shard_map/ppermute | solution.py:300
  93.0 1.3 %collective-permute-done.28.refs_1_ = bf16[4,128,128]{2,1,0:T(8,128)(2,1)S(1)} collective-permute-done((bf16[4,128,128]{2,1,0:T(8,128)(2,1)S(1)}, bf16[4,128,128]{2,1,0:T(8,128)(2,1)S(1)}, u32[]{:S(2)}, u32[]{:S(2)}) %collective-permute-start.28) | collective-permute-done | bytes 131104 | tf_op jit(solution)/shard_map/ppermute | solution.py:300
  94.6 1.9 %collective-permute-start.30 = (bf16[4,128,128]{2,1,0:T(8,128)(2,1)S(1)}, bf16[4,128,128]{2,1,0:T(8,128)(2,1)S(1)}, u32[]{:S(2)}, u32[]{:S(2)}) collective-permute-start(bf16[4,128,128]{2,1,0:T(8,128)(2,1)S(1)} %sum_and_solve.9), channel_id=1, source_target_pairs={{0,7},{1,15},{2,21},{3,29},{4,1},{5,9},{6,19},{7,27},{8,6},{9,14},... | collective-permute-start | bytes 393224 | tf_op jit(solution)/shard_map/ppermute | solution.py:285
  96.5 2.9 %lay_out.9 = (bf16[2,8,2,128,128]{4,3,2,1,0:T(8,128)(2,1)S(1)}, bf16[4,8,2,128,128]{4,3,2,1,0:T(8,128)(2,1)S(1)}) custom-call(s32[3]{0:T(128)S(1)} %pad_add_fusion.scal, s32[16,32]{1,0:T(8,128)} %bitcast.49, bf16[16,16,2,128,128]{4,3,2,1,0:T(8,128)(2,1)} %bitcast.43, bf16[2,128,128]{2,1,0:T(8,128)(2,1)S(1)} %sum_and_solve.8.refs_1_), custom_call_target="tpu_custom_call" | custom-call | bytes 12582912 | tf_op jit(solution)/shard_map/lay_out/pallas_call | solution.py:64
  100.1 3.3 %collective-permute-done.30.refs_1_ = bf16[4,128,128]{2,1,0:T(8,128)(2,1)S(1)} collective-permute-done((bf16[4,128,128]{2,1,0:T(8,128)(2,1)S(1)}, bf16[4,128,128]{2,1,0:T(8,128)(2,1)S(1)}, u32[]{:S(2)}, u32[]{:S(2)}) %collective-permute-start.30) | collective-permute-done | bytes 131104 | tf_op jit(solution)/shard_map/ppermute | solution.py:285
  104.2 2.1 %collective-permute-start.31 = (bf16[4,128,128]{2,1,0:T(8,128)(2,1)S(1)}, bf16[4,128,128]{2,1,0:T(8,128)(2,1)S(1)}, u32[]{:S(2)}, u32[]{:S(2)}) collective-permute-start(bf16[4,128,128]{2,1,0:T(8,128)(2,1)S(1)} %get-tuple-element.28), channel_id=1, source_target_pairs={{0,8},{8,0},{1,9},{9,1},{2,10},{10,2},{3,11},{11,3},{4,12},{12,4},... | collective-permute-start | bytes 393224 | tf_op jit(solution)/shard_map/ppermute | solution.py:407
  106.3 1.0 collective-permute-done.31
  107.6 5.6 %collective-permute-done.32.other_ref = bf16[4,128,128]{2,1,0:T(8,128)(2,1)S(1)} collective-permute-done((bf16[4,128,128]{2,1,0:T(8,128)(2,1)S(1)}, bf16[4,128,128]{2,1,0:T(8,128)(2,1)S(1)}, u32[]{:S(2)}, u32[]{:S(2)}) %collective-permute-start.32) | collective-permute-done | bytes 131104 | tf_op jit(solution)/shard_map/ppermute | solution.py:408
  114.3 3.5 %collective-permute-start.35 = (bf16[128,128]{1,0:T(8,128)(2,1)S(1)}, bf16[128,128]{1,0:T(8,128)(2,1)S(1)}, u32[]{:S(2)}, u32[]{:S(2)}) collective-permute-start(bf16[128,128]{1,0:T(8,128)(2,1)S(1)} %get-tuple-element.36), channel_id=1, source_target_pairs={{0,6},{1,7},{2,4},{3,5},{4,2},{5,3},{6,0},{7,1},{8,14},{9,15},{10,... | collective-permute-start | bytes 98312 | tf_op jit(solution)/shard_map/ppermute | solution.py:422
  117.8 0.9 collective-permute-done.34
  118.7 1.4 %collective-permute-done.35 = bf16[128,128]{1,0:T(8,128)(2,1)S(1)} collective-permute-done((bf16[128,128]{1,0:T(8,128)(2,1)S(1)}, bf16[128,128]{1,0:T(8,128)(2,1)S(1)}, u32[]{:S(2)}, u32[]{:S(2)}) %collective-permute-start.35) | collective-permute-done | bytes 32800 | tf_op jit(solution)/shard_map/ppermute | solution.py:422
  120.7 3.8 %collective-permute-done.36 = bf16[2,128,128]{2,1,0:T(8,128)(2,1)S(1)} collective-permute-done((bf16[2,128,128]{2,1,0:T(8,128)(2,1)S(1)}, bf16[2,128,128]{2,1,0:T(8,128)(2,1)S(1)}, u32[]{:S(2)}, u32[]{:S(2)}) %collective-permute-start.36) | collective-permute-done | bytes 65568 | tf_op jit(solution)/shard_map/ppermute | solution.py:422
  (81 shorter events, 14.7 us)
Async XLA Ops:
  0.9 6.7 %collective-permute-start.1 = (bf16[2,128,128]{2,1,0:T(8,128)(2,1)S(1)}, bf16[2,128,128]{2,1,0:T(8,128)(2,1)S(1)}, u32[]{:S(2)}, u32[]{:S(2)}) collective-permute-start(bf16[2,128,128]{2,1,0:T(8,128)(2,1)S(1)} %get-tuple-element.44), channel_id=1, source_target_pairs={{0,16},{16,0},{1,17},{17,1},{2,18},{18,2},{3,19},{19,3},{4,20},{20... | collective-permute-start | bytes 196616 | tf_op jit(solution)/shard_map/ppermute | solution.py:344
  4.9 6.5 %collective-permute-start = (bf16[2,128,128]{2,1,0:T(8,128)(2,1)S(1)}, bf16[2,128,128]{2,1,0:T(8,128)(2,1)S(1)}, u32[]{:S(2)}, u32[]{:S(2)}) collective-permute-start(bf16[2,128,128]{2,1,0:T(8,128)(2,1)S(1)} %dynamic-slice_bitcast_fusion.2.refs_1_), channel_id=1, source_target_pairs={{0,4},{1,12},{2,16},{3,24},{4,1},{5,9},{6,21},{7,29},{8,6},{9,14},... | collective-permute-start | bytes 196616 | tf_op jit(solution)/shard_map/ppermute | solution.py:340
  7.6 3.7 %collective-permute-start.2 = (bf16[2,128,128]{2,1,0:T(8,128)(2,1)S(1)}, bf16[2,128,128]{2,1,0:T(8,128)(2,1)S(1)}, u32[]{:S(2)}, u32[]{:S(2)}) collective-permute-start(bf16[2,128,128]{2,1,0:T(8,128)(2,1)S(1)} %get-tuple-element.42), channel_id=1, source_target_pairs={{0,8},{8,0},{1,9},{9,1},{2,10},{10,2},{3,11},{11,3},{4,12},{12,4},... | collective-permute-start | bytes 196616 | tf_op jit(solution)/shard_map/ppermute | solution.py:344
  11.6 22.3 %copy-start = (bf16[16,1,128,128]{3,2,1,0:T(8,128)(2,1)S(1)}, bf16[16,1,128,128]{3,2,1,0:T(8,128)(2,1)}, u32[]{:S(2)}) copy-start(bf16[16,1,128,128]{3,2,1,0:T(8,128)(2,1)} %refs_2_.5) | copy-start | bytes 1572868
  11.6 7.2 %collective-permute-start.4 = (bf16[2,128,128]{2,1,0:T(8,128)(2,1)S(1)}, bf16[2,128,128]{2,1,0:T(8,128)(2,1)S(1)}, u32[]{:S(2)}, u32[]{:S(2)}) collective-permute-start(bf16[2,128,128]{2,1,0:T(8,128)(2,1)S(1)} %solve_blocks.1.refs_1_.refs_0_), channel_id=1, source_target_pairs={{0,2},{1,3},{2,0},{3,1},{4,6},{5,7},{6,4},{7,5},{8,10},{9,11},{10,... | collective-permute-start | bytes 196616 | tf_op jit(solution)/shard_map/ppermute | solution.py:337
  12.0 7.9 %collective-permute-start.6 = (bf16[2,128,128]{2,1,0:T(8,128)(2,1)S(1)}, bf16[2,128,128]{2,1,0:T(8,128)(2,1)S(1)}, u32[]{:S(2)}, u32[]{:S(2)}) collective-permute-start(bf16[2,128,128]{2,1,0:T(8,128)(2,1)S(1)} %solve_blocks.1.refs_1_.refs_0_), channel_id=1, source_target_pairs={{0,4},{1,5},{2,6},{3,7},{4,0},{5,1},{6,2},{7,3},{8,12},{9,13},{10,... | collective-permute-start | bytes 196616 | tf_op jit(solution)/shard_map/ppermute | solution.py:337
  15.1 6.6 %collective-permute-start.8 = (bf16[2,128,128]{2,1,0:T(8,128)(2,1)S(1)}, bf16[2,128,128]{2,1,0:T(8,128)(2,1)S(1)}, u32[]{:S(2)}, u32[]{:S(2)}) collective-permute-start(bf16[2,128,128]{2,1,0:T(8,128)(2,1)S(1)} %solve_blocks.1.refs_1_.refs_0_), channel_id=1, source_target_pairs={{0,6},{1,7},{2,4},{3,5},{4,2},{5,3},{6,0},{7,1},{8,14},{9,15},{10,... | collective-permute-start | bytes 196616 | tf_op jit(solution)/shard_map/ppermute | solution.py:337
  16.0 8.3 %collective-permute-start.3 = (bf16[2,128,128]{2,1,0:T(8,128)(2,1)S(1)}, bf16[2,128,128]{2,1,0:T(8,128)(2,1)S(1)}, u32[]{:S(2)}, u32[]{:S(2)}) collective-permute-start(bf16[2,128,128]{2,1,0:T(8,128)(2,1)S(1)} %solve_blocks.1.refs_1_.refs_0_), channel_id=1, source_target_pairs={{0,1},{1,0},{2,3},{3,2},{4,5},{5,4},{6,7},{7,6},{8,9},{9,8},{10,11... | collective-permute-start | bytes 196616 | tf_op jit(solution)/shard_map/ppermute | solution.py:337
  17.4 6.8 %collective-permute-start.10 = (bf16[2,128,128]{2,1,0:T(8,128)(2,1)S(1)}, bf16[2,128,128]{2,1,0:T(8,128)(2,1)S(1)}, u32[]{:S(2)}, u32[]{:S(2)}) collective-permute-start(bf16[2,128,128]{2,1,0:T(8,128)(2,1)S(1)} %get-tuple-element.39), channel_id=1, source_target_pairs={{4,0},{12,1},{16,2},{24,3},{1,4},{9,5},{21,6},{29,7},{6,8},{14,9},... | collective-permute-start | bytes 196616 | tf_op jit(solution)/shard_map/ppermute | solution.py:354
  18.8 5.5 %collective-permute-start.5 = (bf16[2,128,128]{2,1,0:T(8,128)(2,1)S(1)}, bf16[2,128,128]{2,1,0:T(8,128)(2,1)S(1)}, u32[]{:S(2)}, u32[]{:S(2)}) collective-permute-start(bf16[2,128,128]{2,1,0:T(8,128)(2,1)S(1)} %collective-permute-done.4.refs_3_.refs_2_), channel_id=1, source_target_pairs={{0,1},{1,0},{2,3},{3,2},{4,5},{5,4},{6,7},{7,6},{8,9},{9,8},{10,11... | collective-permute-start | bytes 196616 | tf_op jit(solution)/shard_map/ppermute | solution.py:337
  19.9 4.7 %collective-permute-start.7 = (bf16[2,128,128]{2,1,0:T(8,128)(2,1)S(1)}, bf16[2,128,128]{2,1,0:T(8,128)(2,1)S(1)}, u32[]{:S(2)}, u32[]{:S(2)}) collective-permute-start(bf16[2,128,128]{2,1,0:T(8,128)(2,1)S(1)} %collective-permute-done.6.refs_5_.refs_4_), channel_id=1, source_target_pairs={{0,1},{1,0},{2,3},{3,2},{4,5},{5,4},{6,7},{7,6},{8,9},{9,8},{10,11... | collective-permute-start | bytes 196616 | tf_op jit(solution)/shard_map/ppermute | solution.py:337
  21.7 4.4 %collective-permute-start.9 = (bf16[2,128,128]{2,1,0:T(8,128)(2,1)S(1)}, bf16[2,128,128]{2,1,0:T(8,128)(2,1)S(1)}, u32[]{:S(2)}, u32[]{:S(2)}) collective-permute-start(bf16[2,128,128]{2,1,0:T(8,128)(2,1)S(1)} %collective-permute-done.8.refs_7_.refs_6_), channel_id=1, source_target_pairs={{0,1},{1,0},{2,3},{3,2},{4,5},{5,4},{6,7},{7,6},{8,9},{9,8},{10,11... | collective-permute-start | bytes 196616 | tf_op jit(solution)/shard_map/ppermute | solution.py:337
  26.8 5.6 %collective-permute-start.11 = (bf16[4,128,128]{2,1,0:T(8,128)(2,1)S(1)}, bf16[4,128,128]{2,1,0:T(8,128)(2,1)S(1)}, u32[]{:S(2)}, u32[]{:S(2)}) collective-permute-start(bf16[4,128,128]{2,1,0:T(8,128)(2,1)S(1)} %block_sums.9), channel_id=1, source_target_pairs={{0,16},{1,17},{2,18},{3,19},{4,20},{5,21},{6,22},{7,23},{8,24},{9,... | collective-permute-start | bytes 393224 | tf_op jit(solution)/shard_map/ppermute | solution.py:300
  32.4 1.4 %collective-permute-start.12 = (bf16[4,128,128]{2,1,0:T(8,128)(2,1)S(1)}, bf16[4,128,128]{2,1,0:T(8,128)(2,1)S(1)}, u32[]{:S(2)}, u32[]{:S(2)}) collective-permute-start(bf16[4,128,128]{2,1,0:T(8,128)(2,1)S(1)} %add.125.refs_0_), channel_id=1, source_target_pairs={{0,8},{1,9},{2,10},{3,11},{4,12},{5,13},{6,14},{7,15},{8,0},{9,1},... | collective-permute-start | bytes 393224 | tf_op jit(solution)/shard_map/ppermute | solution.py:300
  34.0 8.9 %collective-permute-start.13 = (bf16[4,128,128]{2,1,0:T(8,128)(2,1)S(1)}, bf16[4,128,128]{2,1,0:T(8,128)(2,1)S(1)}, u32[]{:S(2)}, u32[]{:S(2)}) collective-permute-start(bf16[4,128,128]{2,1,0:T(8,128)(2,1)S(1)} %sum_and_solve.5.refs_2_), channel_id=1, source_target_pairs={{0,2},{1,10},{2,18},{3,26},{4,6},{5,14},{6,22},{7,30},{8,3},{9,11}... | collective-permute-start | bytes 393224 | tf_op jit(solution)/shard_map/ppermute | solution.py:285
  35.1 8.6 %collective-permute-start.14 = (bf16[4,128,128]{2,1,0:T(8,128)(2,1)S(1)}, bf16[4,128,128]{2,1,0:T(8,128)(2,1)S(1)}, u32[]{:S(2)}, u32[]{:S(2)}) collective-permute-start(bf16[4,128,128]{2,1,0:T(8,128)(2,1)S(1)} %sum_and_solve.5.refs_2_), channel_id=1, source_target_pairs={{0,7},{1,15},{2,21},{3,29},{4,1},{5,9},{6,19},{7,27},{8,6},{9,14},... | collective-permute-start | bytes 393224 | tf_op jit(solution)/shard_map/ppermute | solution.py:285
  44.0 4.5 %collective-permute-start.15 = (bf16[2,128,128]{2,1,0:T(8,128)(2,1)S(1)}, bf16[2,128,128]{2,1,0:T(8,128)(2,1)S(1)}, u32[]{:S(2)}, u32[]{:S(2)}) collective-permute-start(bf16[2,128,128]{2,1,0:T(8,128)(2,1)S(1)} %block_sums.11), channel_id=1, source_target_pairs={{0,16},{1,17},{2,18},{3,19},{4,20},{5,21},{6,22},{7,23},{8,24},{9,... | collective-permute-start | bytes 196616 | tf_op jit(solution)/shard_map/ppermute | solution.py:300
  48.5 1.3 %collective-permute-start.16 = (bf16[2,128,128]{2,1,0:T(8,128)(2,1)S(1)}, bf16[2,128,128]{2,1,0:T(8,128)(2,1)S(1)}, u32[]{:S(2)}, u32[]{:S(2)}) collective-permute-start(bf16[2,128,128]{2,1,0:T(8,128)(2,1)S(1)} %add.126.refs_0_), channel_id=1, source_target_pairs={{0,8},{1,9},{2,10},{3,11},{4,12},{5,13},{6,14},{7,15},{8,0},{9,1},... | collective-permute-start | bytes 196616 | tf_op jit(solution)/shard_map/ppermute | solution.py:300
  50.0 7.0 %collective-permute-start.17 = (bf16[2,128,128]{2,1,0:T(8,128)(2,1)S(1)}, bf16[2,128,128]{2,1,0:T(8,128)(2,1)S(1)}, u32[]{:S(2)}, u32[]{:S(2)}) collective-permute-start(bf16[2,128,128]{2,1,0:T(8,128)(2,1)S(1)} %sum_and_solve.6.refs_1_.refs_2_), channel_id=1, source_target_pairs={{0,2},{1,10},{2,18},{3,26},{4,6},{5,14},{6,22},{7,30},{8,3},{9,11}... | collective-permute-start | bytes 196616 | tf_op jit(solution)/shard_map/ppermute | solution.py:285
  51.8 5.1 %collective-permute-start.18 = (bf16[2,128,128]{2,1,0:T(8,128)(2,1)S(1)}, bf16[2,128,128]{2,1,0:T(8,128)(2,1)S(1)}, u32[]{:S(2)}, u32[]{:S(2)}) collective-permute-start(bf16[2,128,128]{2,1,0:T(8,128)(2,1)S(1)} %sum_and_solve.6.refs_1_.refs_2_), channel_id=1, source_target_pairs={{0,7},{1,15},{2,21},{3,29},{4,1},{5,9},{6,19},{7,27},{8,6},{9,14},... | collective-permute-start | bytes 196616 | tf_op jit(solution)/shard_map/ppermute | solution.py:285
  56.6 7.6 %copy-start.1 = (bf16[16,1,128,128]{3,2,1,0:T(8,128)(2,1)S(1)}, bf16[16,1,128,128]{3,2,1,0:T(8,128)(2,1)}, u32[]{:S(2)}) copy-start(bf16[16,1,128,128]{3,2,1,0:T(8,128)(2,1)} %refs_3_.5) | copy-start | bytes 1572868
  57.2 5.7 %collective-permute-start.19 = (bf16[2,128,128]{2,1,0:T(8,128)(2,1)S(1)}, bf16[2,128,128]{2,1,0:T(8,128)(2,1)S(1)}, u32[]{:S(2)}, u32[]{:S(2)}) collective-permute-start(bf16[2,128,128]{2,1,0:T(8,128)(2,1)S(1)} %block_sums.13), channel_id=1, source_target_pairs={{0,16},{1,17},{2,18},{3,19},{4,20},{5,21},{6,22},{7,23},{8,24},{9,... | collective-permute-start | bytes 196616 | tf_op jit(solution)/shard_map/ppermute | solution.py:300
  62.9 1.3 %collective-permute-start.20 = (bf16[2,128,128]{2,1,0:T(8,128)(2,1)S(1)}, bf16[2,128,128]{2,1,0:T(8,128)(2,1)S(1)}, u32[]{:S(2)}, u32[]{:S(2)}) collective-permute-start(bf16[2,128,128]{2,1,0:T(8,128)(2,1)S(1)} %add.127.refs_0_), channel_id=1, source_target_pairs={{0,8},{1,9},{2,10},{3,11},{4,12},{5,13},{6,14},{7,15},{8,0},{9,1},... | collective-permute-start | bytes 196616 | tf_op jit(solution)/shard_map/ppermute | solution.py:300
  64.5 7.4 %collective-permute-start.21 = (bf16[2,128,128]{2,1,0:T(8,128)(2,1)S(1)}, bf16[2,128,128]{2,1,0:T(8,128)(2,1)S(1)}, u32[]{:S(2)}, u32[]{:S(2)}) collective-permute-start(bf16[2,128,128]{2,1,0:T(8,128)(2,1)S(1)} %sum_and_solve.7.refs_1_), channel_id=1, source_target_pairs={{0,2},{1,10},{2,18},{3,26},{4,6},{5,14},{6,22},{7,30},{8,3},{9,11}... | collective-permute-start | bytes 196616 | tf_op jit(solution)/shard_map/ppermute | solution.py:285
  65.0 7.0 %collective-permute-start.22 = (bf16[2,128,128]{2,1,0:T(8,128)(2,1)S(1)}, bf16[2,128,128]{2,1,0:T(8,128)(2,1)S(1)}, u32[]{:S(2)}, u32[]{:S(2)}) collective-permute-start(bf16[2,128,128]{2,1,0:T(8,128)(2,1)S(1)} %sum_and_solve.7.refs_1_), channel_id=1, source_target_pairs={{0,7},{1,15},{2,21},{3,29},{4,1},{5,9},{6,19},{7,27},{8,6},{9,14},... | collective-permute-start | bytes 196616 | tf_op jit(solution)/shard_map/ppermute | solution.py:285
  72.2 5.0 %collective-permute-start.23 = (bf16[2,128,128]{2,1,0:T(8,128)(2,1)S(1)}, bf16[2,128,128]{2,1,0:T(8,128)(2,1)S(1)}, u32[]{:S(2)}, u32[]{:S(2)}) collective-permute-start(bf16[2,128,128]{2,1,0:T(8,128)(2,1)S(1)} %block_sums.14), channel_id=1, source_target_pairs={{0,16},{1,17},{2,18},{3,19},{4,20},{5,21},{6,22},{7,23},{8,24},{9,... | collective-permute-start | bytes 196616 | tf_op jit(solution)/shard_map/ppermute | solution.py:300
  77.2 1.3 %collective-permute-start.24 = (bf16[2,128,128]{2,1,0:T(8,128)(2,1)S(1)}, bf16[2,128,128]{2,1,0:T(8,128)(2,1)S(1)}, u32[]{:S(2)}, u32[]{:S(2)}) collective-permute-start(bf16[2,128,128]{2,1,0:T(8,128)(2,1)S(1)} %add.128.refs_0_), channel_id=1, source_target_pairs={{0,8},{1,9},{2,10},{3,11},{4,12},{5,13},{6,14},{7,15},{8,0},{9,1},... | collective-permute-start | bytes 196616 | tf_op jit(solution)/shard_map/ppermute | solution.py:300
  78.7 4.3 %collective-permute-start.25 = (bf16[2,128,128]{2,1,0:T(8,128)(2,1)S(1)}, bf16[2,128,128]{2,1,0:T(8,128)(2,1)S(1)}, u32[]{:S(2)}, u32[]{:S(2)}) collective-permute-start(bf16[2,128,128]{2,1,0:T(8,128)(2,1)S(1)} %sum_and_solve.8.refs_1_), channel_id=1, source_target_pairs={{0,2},{1,10},{2,18},{3,26},{4,6},{5,14},{6,22},{7,30},{8,3},{9,11}... | collective-permute-start | bytes 196616 | tf_op jit(solution)/shard_map/ppermute | solution.py:285
  79.2 7.3 %collective-permute-start.26 = (bf16[2,128,128]{2,1,0:T(8,128)(2,1)S(1)}, bf16[2,128,128]{2,1,0:T(8,128)(2,1)S(1)}, u32[]{:S(2)}, u32[]{:S(2)}) collective-permute-start(bf16[2,128,128]{2,1,0:T(8,128)(2,1)S(1)} %sum_and_solve.8.refs_1_), channel_id=1, source_target_pairs={{0,7},{1,15},{2,21},{3,29},{4,1},{5,9},{6,19},{7,27},{8,6},{9,14},... | collective-permute-start | bytes 196616 | tf_op jit(solution)/shard_map/ppermute | solution.py:285
  86.7 6.2 %collective-permute-start.27 = (bf16[4,128,128]{2,1,0:T(8,128)(2,1)S(1)}, bf16[4,128,128]{2,1,0:T(8,128)(2,1)S(1)}, u32[]{:S(2)}, u32[]{:S(2)}) collective-permute-start(bf16[4,128,128]{2,1,0:T(8,128)(2,1)S(1)} %block_sums.16), channel_id=1, source_target_pairs={{0,16},{1,17},{2,18},{3,19},{4,20},{5,21},{6,22},{7,23},{8,24},{9,... | collective-permute-start | bytes 393224 | tf_op jit(solution)/shard_map/ppermute | solution.py:300
  93.0 1.4 %collective-permute-start.28 = (bf16[4,128,128]{2,1,0:T(8,128)(2,1)S(1)}, bf16[4,128,128]{2,1,0:T(8,128)(2,1)S(1)}, u32[]{:S(2)}, u32[]{:S(2)}) collective-permute-start(bf16[4,128,128]{2,1,0:T(8,128)(2,1)S(1)} %add.129.refs_0_), channel_id=1, source_target_pairs={{0,8},{1,9},{2,10},{3,11},{4,12},{5,13},{6,14},{7,15},{8,0},{9,1},... | collective-permute-start | bytes 393224 | tf_op jit(solution)/shard_map/ppermute | solution.py:300
  94.6 5.6 %collective-permute-start.29 = (bf16[4,128,128]{2,1,0:T(8,128)(2,1)S(1)}, bf16[4,128,128]{2,1,0:T(8,128)(2,1)S(1)}, u32[]{:S(2)}, u32[]{:S(2)}) collective-permute-start(bf16[4,128,128]{2,1,0:T(8,128)(2,1)S(1)} %sum_and_solve.9), channel_id=1, source_target_pairs={{0,2},{1,10},{2,18},{3,26},{4,6},{5,14},{6,22},{7,30},{8,3},{9,11}... | collective-permute-start | bytes 393224 | tf_op jit(solution)/shard_map/ppermute | solution.py:285
  94.6 8.8 %collective-permute-start.30 = (bf16[4,128,128]{2,1,0:T(8,128)(2,1)S(1)}, bf16[4,128,128]{2,1,0:T(8,128)(2,1)S(1)}, u32[]{:S(2)}, u32[]{:S(2)}) collective-permute-start(bf16[4,128,128]{2,1,0:T(8,128)(2,1)S(1)} %sum_and_solve.9), channel_id=1, source_target_pairs={{0,7},{1,15},{2,21},{3,29},{4,1},{5,9},{6,19},{7,27},{8,6},{9,14},... | collective-permute-start | bytes 393224 | tf_op jit(solution)/shard_map/ppermute | solution.py:285
  104.2 3.1 %collective-permute-start.31 = (bf16[4,128,128]{2,1,0:T(8,128)(2,1)S(1)}, bf16[4,128,128]{2,1,0:T(8,128)(2,1)S(1)}, u32[]{:S(2)}, u32[]{:S(2)}) collective-permute-start(bf16[4,128,128]{2,1,0:T(8,128)(2,1)S(1)} %get-tuple-element.28), channel_id=1, source_target_pairs={{0,8},{8,0},{1,9},{9,1},{2,10},{10,2},{3,11},{11,3},{4,12},{12,4},... | collective-permute-start | bytes 393224 | tf_op jit(solution)/shard_map/ppermute | solution.py:407
  107.3 5.8 %collective-permute-start.32 = (bf16[4,128,128]{2,1,0:T(8,128)(2,1)S(1)}, bf16[4,128,128]{2,1,0:T(8,128)(2,1)S(1)}, u32[]{:S(2)}, u32[]{:S(2)}) collective-permute-start(bf16[4,128,128]{2,1,0:T(8,128)(2,1)S(1)} %get-tuple-element.29), channel_id=1, source_target_pairs={{0,16},{16,0},{1,17},{17,1},{2,18},{18,2},{3,19},{19,3},{4,20},{20... | collective-permute-start | bytes 393224 | tf_op jit(solution)/shard_map/ppermute | solution.py:408
  113.4 4.5 %collective-permute-start.33 = (bf16[128,128]{1,0:T(8,128)(2,1)S(1)}, bf16[128,128]{1,0:T(8,128)(2,1)S(1)}, u32[]{:S(2)}, u32[]{:S(2)}) collective-permute-start(bf16[128,128]{1,0:T(8,128)(2,1)S(1)} %get-tuple-element.38), channel_id=1, source_target_pairs={{0,2},{1,3},{2,0},{3,1},{4,6},{5,7},{6,4},{7,5},{8,10},{9,11},{10,... | collective-permute-start | bytes 98312 | tf_op jit(solution)/shard_map/ppermute | solution.py:422
  113.8 4.9 %collective-permute-start.34 = (bf16[128,128]{1,0:T(8,128)(2,1)S(1)}, bf16[128,128]{1,0:T(8,128)(2,1)S(1)}, u32[]{:S(2)}, u32[]{:S(2)}) collective-permute-start(bf16[128,128]{1,0:T(8,128)(2,1)S(1)} %get-tuple-element.37), channel_id=1, source_target_pairs={{0,4},{1,5},{2,6},{3,7},{4,0},{5,1},{6,2},{7,3},{8,12},{9,13},{10,... | collective-permute-start | bytes 98312 | tf_op jit(solution)/shard_map/ppermute | solution.py:422
  114.3 5.8 %collective-permute-start.35 = (bf16[128,128]{1,0:T(8,128)(2,1)S(1)}, bf16[128,128]{1,0:T(8,128)(2,1)S(1)}, u32[]{:S(2)}, u32[]{:S(2)}) collective-permute-start(bf16[128,128]{1,0:T(8,128)(2,1)S(1)} %get-tuple-element.36), channel_id=1, source_target_pairs={{0,6},{1,7},{2,4},{3,5},{4,2},{5,3},{6,0},{7,1},{8,14},{9,15},{10,... | collective-permute-start | bytes 98312 | tf_op jit(solution)/shard_map/ppermute | solution.py:422
  120.1 4.3 %collective-permute-start.36 = (bf16[2,128,128]{2,1,0:T(8,128)(2,1)S(1)}, bf16[2,128,128]{2,1,0:T(8,128)(2,1)S(1)}, u32[]{:S(2)}, u32[]{:S(2)}) collective-permute-start(bf16[2,128,128]{2,1,0:T(8,128)(2,1)S(1)} %pad_maximum_fusion.1), channel_id=1, source_target_pairs={{0,1},{1,0},{2,3},{3,2},{4,5},{5,4},{6,7},{7,6},{8,9},{9,8},{10,11... | collective-permute-start | bytes 196616 | tf_op jit(solution)/shard_map/ppermute | solution.py:422

commit v8 on v7

--- a/solution.py
+++ b/solution.py
@@ -336,7 +336,7 @@
         def exchange(values, t):
             return lax.ppermute(values, ALL_AXES, [(device(r, c), device(r, c ^ t)) for r, c in everyone])
 
-        (one_zero,) = laid_out([inverse_rows], part(1, zero_groups, pcol_n))
+        (first_zero,) = laid_out([inverse_rows], part(1, lambda scal: zero_groups(scal)[:2], pcol_n))
         inverse_rows = lax.ppermute(inverse_rows, ALL_AXES, there)
         blocks = right_sides.reshape(2, 2, size, rhs)
         for axis, name, index in ((0, "hi", hi_id), (1, "lo", lo_id)):
@@ -345,13 +345,15 @@
             own = lax.dynamic_index_in_dim(blocks, index, axis, keepdims=False)
             blocks = jnp.where(index == 0, jnp.stack([own, other], axis), jnp.stack([other, own], axis))
         blocks = blocks.reshape(per, size, rhs)
-        own_zero = solve_blocks(inverse_rows, blocks[:first_low], [one_zero])
+        own_zero = solve_blocks(inverse_rows, blocks[:first_low], [first_zero])
+        (rest_zero,) = laid_out([own_zero], part(1, lambda scal: zero_groups(scal)[2:], pcol_n))
         even = {t: exchange(own_zero, t) for t in range(pcol_n - 2, 0, -2)}
         even[0] = own_zero
         zero = []
         for t in range(0, pcol_n, 2):
             zero += [even[t], exchange(even[t], 1)]
         rest = lax.ppermute(blocks[first_low:], ALL_AXES, back)
+        one_zero = [(first_zero, zero[:2]), (rest_zero, zero[2:])]
         zero_step = pcol_n
 
         owned = (jnp.arange(per) == chunk_id)[None, :, None, None]
@@ -366,12 +368,13 @@
         zero_step = q_n
         (one_zero,) = laid_out([own_zero], part(1, zero_groups, zero_step))
         zero = spread(own_zero)
+        one_zero = [(one_zero, zero)]
         base = jnp.where(row_id == 0, mine[half:], jnp.zeros((), jnp.bfloat16))
         base_zero = jnp.where(row_id == 0, own_zero, jnp.zeros((), jnp.bfloat16))
         base_zero = lax.dynamic_slice_in_dim(jnp.concatenate([base_zero, base_zero]), per * lo_id, half, 0)
 
     level_groups = [zero_groups] + [spread_groups(bounds[level], bounds[level + 1]) for level in range(1, 4)]
-    partial = block_sums([(one_zero, zero)], 0, count(1), None, (base, 0), True)
+    partial = block_sums(one_zero, 0, count(1), None, (base, 0), True)
     one_rows = sum_and_solve(summands(partial), [lower_inverse], bounds[1])
     one = spread(one_rows)
     late_zero, two_one = laid_out([one_rows, base_zero], (*late_rows, zero_groups, zero_step), part(2, level_groups[1], q_n))

time: 126 us -> 126 us (level)
  waiting for transfers between devices: 50.6 us -> 42.7 us
  starting transfers between devices: 51.5 us -> 57.8 us
  Pallas kernels: 19.3 us -> 21 us
    ppermute x10, waiting for transfers between devices: 25.4 us -> 21.9 us  [summands(): other = lax.ppermute(partial, ALL_AXES, pairs)]
    ppermute x10, starting transfers between devices: 19.7 us -> 22.9 us  [spread(): lax.ppermute(values, ALL_AXES, [(device(r, c), device(*route(t, r, c))) f...]
    ppermute x10, starting transfers between devices: 8.29 us -> 10.8 us  [summands(): other = lax.ppermute(partial, ALL_AXES, pairs)]
    ppermute x10, waiting for transfers between devices: 7.86 us -> 5.81 us  [spread(): lax.ppermute(values, ALL_AXES, [(device(r, c), device(*route(t, r, c))) f...]
    pallas_call x5 -> x6, Pallas kernels: 12.8 us -> 14.5 us  [lay_out(): pl.pallas_call(kernel, grid_spec=pltpu.PrefetchScalarGridSpec(num_scalar_...]
    ppermute x1, waiting for transfers between devices: 1.71 us -> 0.01 us  [on_device(): rest = lax.ppermute(blocks[first_low:], ALL_AXES, back)]
  transfers between devices with their start and end apart: 37 -> 37, of which waited for: 24 -> 21; matrix products, arithmetic and copies ran while one was open for 1% -> 1% of each run, Pallas kernels for 12% -> 14%
where the time goes in v8:
time: 126 us; the launch traced here: 125 us
  starting transfers between devices  57.8 us (46%)
  waiting for transfers between devices  42.7 us (34%)
  Pallas kernels  21 us (17%)
  local copies, waits for them, and re-layouts  2.71 us (2%)
    ppermute x10, starting transfers between devices, spread(): lax.ppermute(values, ALL_AXES, [(device(r, c), device(*route(t, r, c))) f...  22.9 us
    ppermute x10, waiting for transfers between devices, summands(): other = lax.ppermute(partial, ALL_AXES, pairs)  21.9 us
    pallas_call x6, Pallas kernels, lay_out(): pl.pallas_call(kernel, grid_spec=pltpu.PrefetchScalarGridSpec(num_scalar_...  14.5 us
    ppermute x10, starting transfers between devices, summands(): other = lax.ppermute(partial, ALL_AXES, pairs)  10.8 us
    ppermute x7, starting transfers between devices, exchange(): lax.ppermute(values, ALL_AXES, [(device(r, c), device(r, c ^ t)) for r, c...  8.73 us
    ppermute x4, waiting for transfers between devices, crossed(): lax.ppermute(values, ALL_AXES, [(device(r, c), device(r, c ^ t)) for r, c...  6.1 us
    ppermute x10, waiting for transfers between devices, spread(): lax.ppermute(values, ALL_AXES, [(device(r, c), device(*route(t, r, c))) f...  5.81 us
    ppermute x4, starting transfers between devices, crossed(): lax.ppermute(values, ALL_AXES, [(device(r, c), device(r, c ^ t)) for r, c...  5.72 us
  transfers between devices with their start and end apart: 37, of which 21 were waited for; matrix products, arithmetic and copies ran while one was open for 1% of the time, Pallas kernels for 14%

profile of v8, /device:TPU:0, one launch (start us, length us, event | category | flops | bytes accessed | tf_op | source)
XLA Modules:
  0.0 125.3 jit_solution(17678777599790978978)
XLA Ops:
  0.9 3.0 %collective-permute-start.1 = (bf16[2,128,128]{2,1,0:T(8,128)(2,1)S(1)}, bf16[2,128,128]{2,1,0:T(8,128)(2,1)S(1)}, u32[]{:S(2)}, u32[]{:S(2)}) collective-permute-start(bf16[2,128,128]{2,1,0:T(8,128)(2,1)S(1)} %get-tuple-element.44), channel_id=1, source_target_pairs={{0,16},{16,0},{1,17},{17,1},{2,18},{18,2},{3,19},{19,3},{4,20},{20... | collective-permute-start | bytes 196616 | tf_op jit(solution)/shard_map/ppermute | solution.py:344
  4.9 2.6 %collective-permute-start = (bf16[2,128,128]{2,1,0:T(8,128)(2,1)S(1)}, bf16[2,128,128]{2,1,0:T(8,128)(2,1)S(1)}, u32[]{:S(2)}, u32[]{:S(2)}) collective-permute-start(bf16[2,128,128]{2,1,0:T(8,128)(2,1)S(1)} %dynamic-slice_bitcast_fusion.2.refs_1_), channel_id=1, source_target_pairs={{0,4},{1,12},{2,16},{3,24},{4,1},{5,9},{6,21},{7,29},{8,6},{9,14},... | collective-permute-start | bytes 196616 | tf_op jit(solution)/shard_map/ppermute | solution.py:340
  7.6 1.2 collective-permute-start.2
  8.9 1.9 %lay_out.6.refs_0_ = bf16[2,4,2,128,128]{4,3,2,1,0:T(8,128)(2,1)S(1)} custom-call(s32[3]{0:T(128)S(1)} %pad_add_fusion.scal, s32[16,32]{1,0:T(8,128)} %bitcast.46, bf16[16,4,8,128,128]{4,3,2,1,0:T(8,128)(2,1)} %bitcast.38, bf16[2,128,128]{2,1,0:T(8,128)(2,1)S(1)} %dynamic-slice_bitcast_fusion.2.refs_1_), custom_call_target="tpu_custom_call" | custom-call | bytes 2097152 | tf_op jit(solution)/shard_map/lay_out/pallas_call | solution.py:64
  12.0 3.1 %collective-permute-start.6 = (bf16[2,128,128]{2,1,0:T(8,128)(2,1)S(1)}, bf16[2,128,128]{2,1,0:T(8,128)(2,1)S(1)}, u32[]{:S(2)}, u32[]{:S(2)}) collective-permute-start(bf16[2,128,128]{2,1,0:T(8,128)(2,1)S(1)} %solve_blocks.1.refs_1_.refs_0_), channel_id=1, source_target_pairs={{0,4},{1,5},{2,6},{3,7},{4,0},{5,1},{6,2},{7,3},{8,12},{9,13},{10,... | collective-permute-start | bytes 196616 | tf_op jit(solution)/shard_map/ppermute | solution.py:337
  15.5 1.9 %collective-permute-start.3 = (bf16[2,128,128]{2,1,0:T(8,128)(2,1)S(1)}, bf16[2,128,128]{2,1,0:T(8,128)(2,1)S(1)}, u32[]{:S(2)}, u32[]{:S(2)}) collective-permute-start(bf16[2,128,128]{2,1,0:T(8,128)(2,1)S(1)} %solve_blocks.1.refs_1_.refs_0_), channel_id=1, source_target_pairs={{0,1},{1,0},{2,3},{3,2},{4,5},{5,4},{6,7},{7,6},{8,9},{9,8},{10,11... | collective-permute-start | bytes 196616 | tf_op jit(solution)/shard_map/ppermute | solution.py:337
  17.4 1.4 %collective-permute-start.10 = (bf16[2,128,128]{2,1,0:T(8,128)(2,1)S(1)}, bf16[2,128,128]{2,1,0:T(8,128)(2,1)S(1)}, u32[]{:S(2)}, u32[]{:S(2)}) collective-permute-start(bf16[2,128,128]{2,1,0:T(8,128)(2,1)S(1)} %get-tuple-element.39), channel_id=1, source_target_pairs={{4,0},{12,1},{16,2},{24,3},{1,4},{9,5},{21,6},{29,7},{6,8},{14,9},... | collective-permute-start | bytes 196616 | tf_op jit(solution)/shard_map/ppermute | solution.py:355
  19.7 1.1 collective-permute-start.7
  22.5 2.3 %lay_out.7.refs_3_ = bf16[6,4,2,128,128]{4,3,2,1,0:T(8,128)(2,1)S(1)} custom-call(s32[3]{0:T(128)S(1)} %pad_add_fusion.scal, s32[16,32]{1,0:T(8,128)} %bitcast.47, bf16[16,4,8,128,128]{4,3,2,1,0:T(8,128)(2,1)} %bitcast.39, bf16[2,128,128]{2,1,0:T(8,128)(2,1)S(1)} %solve_blocks.1.refs_1_.refs_0_), custom_call_target="tpu_custom_call" | custom-call | bytes 6291456 | tf_op jit(solution)/shard_map/lay_out/pallas_call | solution.py:64
  24.9 1.1 collective-permute-done.9.refs_9_.refs_7_.refs_8_
  26.7 1.1 collective-permute-start.11
  27.8 4.3 %collective-permute-done.11 = bf16[4,128,128]{2,1,0:T(8,128)(2,1)S(1)} collective-permute-done((bf16[4,128,128]{2,1,0:T(8,128)(2,1)S(1)}, bf16[4,128,128]{2,1,0:T(8,128)(2,1)S(1)}, u32[]{:S(2)}, u32[]{:S(2)}) %collective-permute-start.11) | collective-permute-done | bytes 131104 | tf_op jit(solution)/shard_map/ppermute | solution.py:300
  32.2 1.3 %collective-permute-done.12.refs_1_ = bf16[4,128,128]{2,1,0:T(8,128)(2,1)S(1)} collective-permute-done((bf16[4,128,128]{2,1,0:T(8,128)(2,1)S(1)}, bf16[4,128,128]{2,1,0:T(8,128)(2,1)S(1)}, u32[]{:S(2)}, u32[]{:S(2)}) %collective-permute-start.12) | collective-permute-done | bytes 131104 | tf_op jit(solution)/shard_map/ppermute | solution.py:300
  33.7 1.2 collective-permute-start.13
  34.9 4.0 %collective-permute-start.14 = (bf16[4,128,128]{2,1,0:T(8,128)(2,1)S(1)}, bf16[4,128,128]{2,1,0:T(8,128)(2,1)S(1)}, u32[]{:S(2)}, u32[]{:S(2)}) collective-permute-start(bf16[4,128,128]{2,1,0:T(8,128)(2,1)S(1)} %sum_and_solve.5.refs_2_), channel_id=1, source_target_pairs={{0,7},{1,15},{2,21},{3,29},{4,1},{5,9},{6,19},{7,27},{8,6},{9,14},... | collective-permute-start | bytes 393224 | tf_op jit(solution)/shard_map/ppermute | solution.py:285
  39.8 2.7 %lay_out.8 = (bf16[8,4,2,128,128]{4,3,2,1,0:T(8,128)(2,1)S(1)}, bf16[4,2,2,128,128]{4,3,2,1,0:T(8,128)(2,1)S(1)}) custom-call(s32[3]{0:T(128)S(1)} %pad_add_fusion.scal, s32[16,32]{1,0:T(8,128)} %bitcast.48, bf16[16,16,2,128,128]{4,3,2,1,0:T(8,128)(2,1)} %bitcast.40, bf16[16,4,8,128,128]{4,3,2,1,0:T(8,128)(2,1)} %bitcast.41, ...), custom_call_target="tpu_custom_call" | custom-call | bytes 10485760 | tf_op jit(solution)/shard_map/lay_out/pallas_call | solution.py:64
  44.0 1.8 %collective-permute-start.15 = (bf16[2,128,128]{2,1,0:T(8,128)(2,1)S(1)}, bf16[2,128,128]{2,1,0:T(8,128)(2,1)S(1)}, u32[]{:S(2)}, u32[]{:S(2)}) collective-permute-start(bf16[2,128,128]{2,1,0:T(8,128)(2,1)S(1)} %block_sums.11), channel_id=1, source_target_pairs={{0,16},{1,17},{2,18},{3,19},{4,20},{5,21},{6,22},{7,23},{8,24},{9,... | collective-permute-start | bytes 196616 | tf_op jit(solution)/shard_map/ppermute | solution.py:300
  45.8 2.7 %collective-permute-done.15 = bf16[2,128,128]{2,1,0:T(8,128)(2,1)S(1)} collective-permute-done((bf16[2,128,128]{2,1,0:T(8,128)(2,1)S(1)}, bf16[2,128,128]{2,1,0:T(8,128)(2,1)S(1)}, u32[]{:S(2)}, u32[]{:S(2)}) %collective-permute-start.15) | collective-permute-done | bytes 65568 | tf_op jit(solution)/shard_map/ppermute | solution.py:300
  48.6 1.2 collective-permute-done.16.refs_1_
  50.0 1.5 %collective-permute-start.17 = (bf16[2,128,128]{2,1,0:T(8,128)(2,1)S(1)}, bf16[2,128,128]{2,1,0:T(8,128)(2,1)S(1)}, u32[]{:S(2)}, u32[]{:S(2)}) collective-permute-start(bf16[2,128,128]{2,1,0:T(8,128)(2,1)S(1)} %sum_and_solve.6.refs_1_.refs_2_), channel_id=1, source_target_pairs={{0,2},{1,10},{2,18},{3,26},{4,6},{5,14},{6,22},{7,30},{8,3},{9,11}... | collective-permute-start | bytes 196616 | tf_op jit(solution)/shard_map/ppermute | solution.py:285
  51.5 3.2 %collective-permute-start.18 = (bf16[2,128,128]{2,1,0:T(8,128)(2,1)S(1)}, bf16[2,128,128]{2,1,0:T(8,128)(2,1)S(1)}, u32[]{:S(2)}, u32[]{:S(2)}) collective-permute-start(bf16[2,128,128]{2,1,0:T(8,128)(2,1)S(1)} %sum_and_solve.6.refs_1_.refs_2_), channel_id=1, source_target_pairs={{0,7},{1,15},{2,21},{3,29},{4,1},{5,9},{6,19},{7,27},{8,6},{9,14},... | collective-permute-start | bytes 196616 | tf_op jit(solution)/shard_map/ppermute | solution.py:285
  54.7 2.1 %lay_out.9 = (bf16[4,2,2,128,128]{4,3,2,1,0:T(8,128)(2,1)S(1)}, bf16[2,2,2,128,128]{4,3,2,1,0:T(8,128)(2,1)S(1)}) custom-call(s32[3]{0:T(128)S(1)} %pad_add_fusion.scal, s32[16,32]{1,0:T(8,128)} %bitcast.49, bf16[16,16,2,128,128]{4,3,2,1,0:T(8,128)(2,1)} %bitcast.42, bf16[2,128,128]{2,1,0:T(8,128)(2,1)S(1)} %sum_and_solve.6.refs_1_.refs_2_), custom_call_target="tpu_custom_call" | custom-call | bytes 3145728 | tf_op jit(solution)/shard_map/lay_out/pallas_call | solution.py:64
  57.4 2.9 %collective-permute-start.19 = (bf16[2,128,128]{2,1,0:T(8,128)(2,1)S(1)}, bf16[2,128,128]{2,1,0:T(8,128)(2,1)S(1)}, u32[]{:S(2)}, u32[]{:S(2)}) collective-permute-start(bf16[2,128,128]{2,1,0:T(8,128)(2,1)S(1)} %block_sums.13), channel_id=1, source_target_pairs={{0,16},{1,17},{2,18},{3,19},{4,20},{5,21},{6,22},{7,23},{8,24},{9,... | collective-permute-start | bytes 196616 | tf_op jit(solution)/shard_map/ppermute | solution.py:300
  60.3 2.2 %collective-permute-done.19 = bf16[2,128,128]{2,1,0:T(8,128)(2,1)S(1)} collective-permute-done((bf16[2,128,128]{2,1,0:T(8,128)(2,1)S(1)}, bf16[2,128,128]{2,1,0:T(8,128)(2,1)S(1)}, u32[]{:S(2)}, u32[]{:S(2)}) %collective-permute-start.19) | collective-permute-done | bytes 65568 | tf_op jit(solution)/shard_map/ppermute | solution.py:300
  62.7 1.2 collective-permute-done.20.refs_1_
  64.9 3.5 %collective-permute-start.22 = (bf16[2,128,128]{2,1,0:T(8,128)(2,1)S(1)}, bf16[2,128,128]{2,1,0:T(8,128)(2,1)S(1)}, u32[]{:S(2)}, u32[]{:S(2)}) collective-permute-start(bf16[2,128,128]{2,1,0:T(8,128)(2,1)S(1)} %sum_and_solve.7.refs_1_), channel_id=1, source_target_pairs={{0,7},{1,15},{2,21},{3,29},{4,1},{5,9},{6,19},{7,27},{8,6},{9,14},... | collective-permute-start | bytes 196616 | tf_op jit(solution)/shard_map/ppermute | solution.py:285
  68.4 2.6 %lay_out.10 = (bf16[2,2,2,128,128]{4,3,2,1,0:T(8,128)(2,1)S(1)}, bf16[2,4,2,128,128]{4,3,2,1,0:T(8,128)(2,1)S(1)}, bf16[2,4,2,128,128]{4,3,2,1,0:T(8,128)(2,1)S(1)}, bf16[2,8,2,128,128]{4,3,2,1,0:T(8,128)(2,1)S(1)}) custom-call(s32[3]{0:T(128)S(1)} %pad_add_fusion.scal, s32[16,32]{1,0:T(8,128)} %bitcast.50, bf16[16,16,2,128,128]{4,3,2,1,0:T(8,128)(2,1)} %bitcast.43, ...), custom_call_target="tpu_custom_call" | custom-call | bytes 9437184 | tf_op jit(solution)/shard_map/lay_out/pallas_call | solution.py:64
  71.2 1.8 %collective-permute-start.23 = (bf16[2,128,128]{2,1,0:T(8,128)(2,1)S(1)}, bf16[2,128,128]{2,1,0:T(8,128)(2,1)S(1)}, u32[]{:S(2)}, u32[]{:S(2)}) collective-permute-start(bf16[2,128,128]{2,1,0:T(8,128)(2,1)S(1)} %block_sums.14), channel_id=1, source_target_pairs={{0,16},{1,17},{2,18},{3,19},{4,20},{5,21},{6,22},{7,23},{8,24},{9,... | collective-permute-start | bytes 196616 | tf_op jit(solution)/shard_map/ppermute | solution.py:300
  73.0 3.1 %collective-permute-done.23 = bf16[2,128,128]{2,1,0:T(8,128)(2,1)S(1)} collective-permute-done((bf16[2,128,128]{2,1,0:T(8,128)(2,1)S(1)}, bf16[2,128,128]{2,1,0:T(8,128)(2,1)S(1)}, u32[]{:S(2)}, u32[]{:S(2)}) %collective-permute-start.23) | collective-permute-done | bytes 65568 | tf_op jit(solution)/shard_map/ppermute | solution.py:300
  76.3 1.1 collective-permute-done.24.refs_1_
  77.6 1.2 collective-permute-start.25
  78.8 3.4 %collective-permute-start.26 = (bf16[2,128,128]{2,1,0:T(8,128)(2,1)S(1)}, bf16[2,128,128]{2,1,0:T(8,128)(2,1)S(1)}, u32[]{:S(2)}, u32[]{:S(2)}) collective-permute-start(bf16[2,128,128]{2,1,0:T(8,128)(2,1)S(1)} %sum_and_solve.8.refs_1_), channel_id=1, source_target_pairs={{0,7},{1,15},{2,21},{3,29},{4,1},{5,9},{6,19},{7,27},{8,6},{9,14},... | collective-permute-start | bytes 196616 | tf_op jit(solution)/shard_map/ppermute | solution.py:285
  82.5 1.6 %collective-permute-done.26.refs_2_.refs_5_ = bf16[2,128,128]{2,1,0:T(8,128)(2,1)S(1)} collective-permute-done((bf16[2,128,128]{2,1,0:T(8,128)(2,1)S(1)}, bf16[2,128,128]{2,1,0:T(8,128)(2,1)S(1)}, u32[]{:S(2)}, u32[]{:S(2)}) %collective-permute-start.26) | collective-permute-done | bytes 65568 | tf_op jit(solution)/shard_map/ppermute | solution.py:285
  84.4 1.4 %collective-permute-start.27 = (bf16[4,128,128]{2,1,0:T(8,128)(2,1)S(1)}, bf16[4,128,128]{2,1,0:T(8,128)(2,1)S(1)}, u32[]{:S(2)}, u32[]{:S(2)}) collective-permute-start(bf16[4,128,128]{2,1,0:T(8,128)(2,1)S(1)} %block_sums.16), channel_id=1, source_target_pairs={{0,16},{1,17},{2,18},{3,19},{4,20},{5,21},{6,22},{7,23},{8,24},{9,... | collective-permute-start | bytes 393224 | tf_op jit(solution)/shard_map/ppermute | solution.py:300
  85.8 3.6 %collective-permute-done.27 = bf16[4,128,128]{2,1,0:T(8,128)(2,1)S(1)} collective-permute-done((bf16[4,128,128]{2,1,0:T(8,128)(2,1)S(1)}, bf16[4,128,128]{2,1,0:T(8,128)(2,1)S(1)}, u32[]{:S(2)}, u32[]{:S(2)}) %collective-permute-start.27) | collective-permute-done | bytes 131104 | tf_op jit(solution)/shard_map/ppermute | solution.py:300
  89.5 1.4 %collective-permute-start.28 = (bf16[4,128,128]{2,1,0:T(8,128)(2,1)S(1)}, bf16[4,128,128]{2,1,0:T(8,128)(2,1)S(1)}, u32[]{:S(2)}, u32[]{:S(2)}) collective-permute-start(bf16[4,128,128]{2,1,0:T(8,128)(2,1)S(1)} %add.129.refs_0_), channel_id=1, source_target_pairs={{0,8},{1,9},{2,10},{3,11},{4,12},{5,13},{6,14},{7,15},{8,0},{9,1},... | collective-permute-start | bytes 393224 | tf_op jit(solution)/shard_map/ppermute | solution.py:300
  90.9 1.0 collective-permute-done.28.refs_1_
  92.1 2.8 %collective-permute-start.29 = (bf16[4,128,128]{2,1,0:T(8,128)(2,1)S(1)}, bf16[4,128,128]{2,1,0:T(8,128)(2,1)S(1)}, u32[]{:S(2)}, u32[]{:S(2)}) collective-permute-start(bf16[4,128,128]{2,1,0:T(8,128)(2,1)S(1)} %sum_and_solve.9), channel_id=1, source_target_pairs={{0,2},{1,10},{2,18},{3,26},{4,6},{5,14},{6,22},{7,30},{8,3},{9,11}... | collective-permute-start | bytes 393224 | tf_op jit(solution)/shard_map/ppermute | solution.py:285
  94.8 1.4 %collective-permute-start.30 = (bf16[4,128,128]{2,1,0:T(8,128)(2,1)S(1)}, bf16[4,128,128]{2,1,0:T(8,128)(2,1)S(1)}, u32[]{:S(2)}, u32[]{:S(2)}) collective-permute-start(bf16[4,128,128]{2,1,0:T(8,128)(2,1)S(1)} %sum_and_solve.9), channel_id=1, source_target_pairs={{0,7},{1,15},{2,21},{3,29},{4,1},{5,9},{6,19},{7,27},{8,6},{9,14},... | collective-permute-start | bytes 393224 | tf_op jit(solution)/shard_map/ppermute | solution.py:285
  96.3 2.9 %lay_out.11 = (bf16[2,8,2,128,128]{4,3,2,1,0:T(8,128)(2,1)S(1)}, bf16[4,8,2,128,128]{4,3,2,1,0:T(8,128)(2,1)S(1)}) custom-call(s32[3]{0:T(128)S(1)} %pad_add_fusion.scal, s32[16,32]{1,0:T(8,128)} %bitcast.51, bf16[16,16,2,128,128]{4,3,2,1,0:T(8,128)(2,1)} %bitcast.44, bf16[2,128,128]{2,1,0:T(8,128)(2,1)S(1)} %sum_and_solve.8.refs_1_), custom_call_target="tpu_custom_call" | custom-call | bytes 12582912 | tf_op jit(solution)/shard_map/lay_out/pallas_call | solution.py:64
  99.9 3.7 %collective-permute-done.30.refs_1_ = bf16[4,128,128]{2,1,0:T(8,128)(2,1)S(1)} collective-permute-done((bf16[4,128,128]{2,1,0:T(8,128)(2,1)S(1)}, bf16[4,128,128]{2,1,0:T(8,128)(2,1)S(1)}, u32[]{:S(2)}, u32[]{:S(2)}) %collective-permute-start.30) | collective-permute-done | bytes 131104 | tf_op jit(solution)/shard_map/ppermute | solution.py:285
  104.3 1.3 %collective-permute-start.31 = (bf16[4,128,128]{2,1,0:T(8,128)(2,1)S(1)}, bf16[4,128,128]{2,1,0:T(8,128)(2,1)S(1)}, u32[]{:S(2)}, u32[]{:S(2)}) collective-permute-start(bf16[4,128,128]{2,1,0:T(8,128)(2,1)S(1)} %get-tuple-element.28), channel_id=1, source_target_pairs={{0,8},{8,0},{1,9},{9,1},{2,10},{10,2},{3,11},{11,3},{4,12},{12,4},... | collective-permute-start | bytes 393224 | tf_op jit(solution)/shard_map/ppermute | solution.py:410
  106.9 5.6 %collective-permute-done.32.other_ref = bf16[4,128,128]{2,1,0:T(8,128)(2,1)S(1)} collective-permute-done((bf16[4,128,128]{2,1,0:T(8,128)(2,1)S(1)}, bf16[4,128,128]{2,1,0:T(8,128)(2,1)S(1)}, u32[]{:S(2)}, u32[]{:S(2)}) %collective-permute-start.32) | collective-permute-done | bytes 131104 | tf_op jit(solution)/shard_map/ppermute | solution.py:411
  114.5 2.7 %collective-permute-start.35 = (bf16[128,128]{1,0:T(8,128)(2,1)S(1)}, bf16[128,128]{1,0:T(8,128)(2,1)S(1)}, u32[]{:S(2)}, u32[]{:S(2)}) collective-permute-start(bf16[128,128]{1,0:T(8,128)(2,1)S(1)} %get-tuple-element.36), channel_id=1, source_target_pairs={{0,6},{1,7},{2,4},{3,5},{4,2},{5,3},{6,0},{7,1},{8,14},{9,15},{10,... | collective-permute-start | bytes 98312 | tf_op jit(solution)/shard_map/ppermute | solution.py:425
  117.1 1.2 collective-permute-done.34
  118.3 1.9 %collective-permute-done.35 = bf16[128,128]{1,0:T(8,128)(2,1)S(1)} collective-permute-done((bf16[128,128]{1,0:T(8,128)(2,1)S(1)}, bf16[128,128]{1,0:T(8,128)(2,1)S(1)}, u32[]{:S(2)}, u32[]{:S(2)}) %collective-permute-start.35) | collective-permute-done | bytes 32800 | tf_op jit(solution)/shard_map/ppermute | solution.py:425
  120.2 1.3 %collective-permute-start.36 = (bf16[2,128,128]{2,1,0:T(8,128)(2,1)S(1)}, bf16[2,128,128]{2,1,0:T(8,128)(2,1)S(1)}, u32[]{:S(2)}, u32[]{:S(2)}) collective-permute-start(bf16[2,128,128]{2,1,0:T(8,128)(2,1)S(1)} %pad_maximum_fusion.1), channel_id=1, source_target_pairs={{0,1},{1,0},{2,3},{3,2},{4,5},{5,4},{6,7},{7,6},{8,9},{9,8},{10,11... | collective-permute-start | bytes 196616 | tf_op jit(solution)/shard_map/ppermute | solution.py:425
  121.5 3.1 %collective-permute-done.36 = bf16[2,128,128]{2,1,0:T(8,128)(2,1)S(1)} collective-permute-done((bf16[2,128,128]{2,1,0:T(8,128)(2,1)S(1)}, bf16[2,128,128]{2,1,0:T(8,128)(2,1)S(1)}, u32[]{:S(2)}, u32[]{:S(2)}) %collective-permute-start.36) | collective-permute-done | bytes 65568 | tf_op jit(solution)/shard_map/ppermute | solution.py:425
  (82 shorter events, 18.2 us)
Async XLA Ops:
  0.9 6.7 %collective-permute-start.1 = (bf16[2,128,128]{2,1,0:T(8,128)(2,1)S(1)}, bf16[2,128,128]{2,1,0:T(8,128)(2,1)S(1)}, u32[]{:S(2)}, u32[]{:S(2)}) collective-permute-start(bf16[2,128,128]{2,1,0:T(8,128)(2,1)S(1)} %get-tuple-element.44), channel_id=1, source_target_pairs={{0,16},{16,0},{1,17},{17,1},{2,18},{18,2},{3,19},{19,3},{4,20},{20... | collective-permute-start | bytes 196616 | tf_op jit(solution)/shard_map/ppermute | solution.py:344
  4.9 6.0 %collective-permute-start = (bf16[2,128,128]{2,1,0:T(8,128)(2,1)S(1)}, bf16[2,128,128]{2,1,0:T(8,128)(2,1)S(1)}, u32[]{:S(2)}, u32[]{:S(2)}) collective-permute-start(bf16[2,128,128]{2,1,0:T(8,128)(2,1)S(1)} %dynamic-slice_bitcast_fusion.2.refs_1_), channel_id=1, source_target_pairs={{0,4},{1,12},{2,16},{3,24},{4,1},{5,9},{6,21},{7,29},{8,6},{9,14},... | collective-permute-start | bytes 196616 | tf_op jit(solution)/shard_map/ppermute | solution.py:340
  7.6 3.2 %collective-permute-start.2 = (bf16[2,128,128]{2,1,0:T(8,128)(2,1)S(1)}, bf16[2,128,128]{2,1,0:T(8,128)(2,1)S(1)}, u32[]{:S(2)}, u32[]{:S(2)}) collective-permute-start(bf16[2,128,128]{2,1,0:T(8,128)(2,1)S(1)} %get-tuple-element.42), channel_id=1, source_target_pairs={{0,8},{8,0},{1,9},{9,1},{2,10},{10,2},{3,11},{11,3},{4,12},{12,4},... | collective-permute-start | bytes 196616 | tf_op jit(solution)/shard_map/ppermute | solution.py:344
  11.0 7.8 %collective-permute-start.4 = (bf16[2,128,128]{2,1,0:T(8,128)(2,1)S(1)}, bf16[2,128,128]{2,1,0:T(8,128)(2,1)S(1)}, u32[]{:S(2)}, u32[]{:S(2)}) collective-permute-start(bf16[2,128,128]{2,1,0:T(8,128)(2,1)S(1)} %solve_blocks.1.refs_1_.refs_0_), channel_id=1, source_target_pairs={{0,2},{1,3},{2,0},{3,1},{4,6},{5,7},{6,4},{7,5},{8,10},{9,11},{10,... | collective-permute-start | bytes 196616 | tf_op jit(solution)/shard_map/ppermute | solution.py:337
  12.0 7.7 %collective-permute-start.6 = (bf16[2,128,128]{2,1,0:T(8,128)(2,1)S(1)}, bf16[2,128,128]{2,1,0:T(8,128)(2,1)S(1)}, u32[]{:S(2)}, u32[]{:S(2)}) collective-permute-start(bf16[2,128,128]{2,1,0:T(8,128)(2,1)S(1)} %solve_blocks.1.refs_1_.refs_0_), channel_id=1, source_target_pairs={{0,4},{1,5},{2,6},{3,7},{4,0},{5,1},{6,2},{7,3},{8,12},{9,13},{10,... | collective-permute-start | bytes 196616 | tf_op jit(solution)/shard_map/ppermute | solution.py:337
  15.1 6.6 %collective-permute-start.8 = (bf16[2,128,128]{2,1,0:T(8,128)(2,1)S(1)}, bf16[2,128,128]{2,1,0:T(8,128)(2,1)S(1)}, u32[]{:S(2)}, u32[]{:S(2)}) collective-permute-start(bf16[2,128,128]{2,1,0:T(8,128)(2,1)S(1)} %solve_blocks.1.refs_1_.refs_0_), channel_id=1, source_target_pairs={{0,6},{1,7},{2,4},{3,5},{4,2},{5,3},{6,0},{7,1},{8,14},{9,15},{10,... | collective-permute-start | bytes 196616 | tf_op jit(solution)/shard_map/ppermute | solution.py:337
  15.5 9.4 %collective-permute-start.3 = (bf16[2,128,128]{2,1,0:T(8,128)(2,1)S(1)}, bf16[2,128,128]{2,1,0:T(8,128)(2,1)S(1)}, u32[]{:S(2)}, u32[]{:S(2)}) collective-permute-start(bf16[2,128,128]{2,1,0:T(8,128)(2,1)S(1)} %solve_blocks.1.refs_1_.refs_0_), channel_id=1, source_target_pairs={{0,1},{1,0},{2,3},{3,2},{4,5},{5,4},{6,7},{7,6},{8,9},{9,8},{10,11... | collective-permute-start | bytes 196616 | tf_op jit(solution)/shard_map/ppermute | solution.py:337
  17.4 7.4 %collective-permute-start.10 = (bf16[2,128,128]{2,1,0:T(8,128)(2,1)S(1)}, bf16[2,128,128]{2,1,0:T(8,128)(2,1)S(1)}, u32[]{:S(2)}, u32[]{:S(2)}) collective-permute-start(bf16[2,128,128]{2,1,0:T(8,128)(2,1)S(1)} %get-tuple-element.39), channel_id=1, source_target_pairs={{4,0},{12,1},{16,2},{24,3},{1,4},{9,5},{21,6},{29,7},{6,8},{14,9},... | collective-permute-start | bytes 196616 | tf_op jit(solution)/shard_map/ppermute | solution.py:355
  18.8 6.1 %collective-permute-start.5 = (bf16[2,128,128]{2,1,0:T(8,128)(2,1)S(1)}, bf16[2,128,128]{2,1,0:T(8,128)(2,1)S(1)}, u32[]{:S(2)}, u32[]{:S(2)}) collective-permute-start(bf16[2,128,128]{2,1,0:T(8,128)(2,1)S(1)} %collective-permute-done.4.refs_4_.refs_2_.refs_3_), channel_id=1, source_target_pairs={{0,1},{1,0},{2,3},{3,2},{4,5},{5,4},{6,7},{7,6},{8,9},{9,8},{10,11... | collective-permute-start | bytes 196616 | tf_op jit(solution)/shard_map/ppermute | solution.py:337
  19.7 5.2 %collective-permute-start.7 = (bf16[2,128,128]{2,1,0:T(8,128)(2,1)S(1)}, bf16[2,128,128]{2,1,0:T(8,128)(2,1)S(1)}, u32[]{:S(2)}, u32[]{:S(2)}) collective-permute-start(bf16[2,128,128]{2,1,0:T(8,128)(2,1)S(1)} %collective-permute-done.6.refs_6_.refs_4_.refs_5_), channel_id=1, source_target_pairs={{0,1},{1,0},{2,3},{3,2},{4,5},{5,4},{6,7},{7,6},{8,9},{9,8},{10,11... | collective-permute-start | bytes 196616 | tf_op jit(solution)/shard_map/ppermute | solution.py:337
  21.7 4.3 %collective-permute-start.9 = (bf16[2,128,128]{2,1,0:T(8,128)(2,1)S(1)}, bf16[2,128,128]{2,1,0:T(8,128)(2,1)S(1)}, u32[]{:S(2)}, u32[]{:S(2)}) collective-permute-start(bf16[2,128,128]{2,1,0:T(8,128)(2,1)S(1)} %collective-permute-done.8.refs_8_.refs_6_.refs_7_), channel_id=1, source_target_pairs={{0,1},{1,0},{2,3},{3,2},{4,5},{5,4},{6,7},{7,6},{8,9},{9,8},{10,11... | collective-permute-start | bytes 196616 | tf_op jit(solution)/shard_map/ppermute | solution.py:337
  24.8 8.7 %copy-start = (bf16[16,1,128,128]{3,2,1,0:T(8,128)(2,1)S(1)}, bf16[16,1,128,128]{3,2,1,0:T(8,128)(2,1)}, u32[]{:S(2)}) copy-start(bf16[16,1,128,128]{3,2,1,0:T(8,128)(2,1)} %refs_2_.5) | copy-start | bytes 1572868
  26.7 5.4 %collective-permute-start.11 = (bf16[4,128,128]{2,1,0:T(8,128)(2,1)S(1)}, bf16[4,128,128]{2,1,0:T(8,128)(2,1)S(1)}, u32[]{:S(2)}, u32[]{:S(2)}) collective-permute-start(bf16[4,128,128]{2,1,0:T(8,128)(2,1)S(1)} %block_sums.9), channel_id=1, source_target_pairs={{0,16},{1,17},{2,18},{3,19},{4,20},{5,21},{6,22},{7,23},{8,24},{9,... | collective-permute-start | bytes 393224 | tf_op jit(solution)/shard_map/ppermute | solution.py:300
  32.1 1.4 %collective-permute-start.12 = (bf16[4,128,128]{2,1,0:T(8,128)(2,1)S(1)}, bf16[4,128,128]{2,1,0:T(8,128)(2,1)S(1)}, u32[]{:S(2)}, u32[]{:S(2)}) collective-permute-start(bf16[4,128,128]{2,1,0:T(8,128)(2,1)S(1)} %add.125.refs_0_), channel_id=1, source_target_pairs={{0,8},{1,9},{2,10},{3,11},{4,12},{5,13},{6,14},{7,15},{8,0},{9,1},... | collective-permute-start | bytes 393224 | tf_op jit(solution)/shard_map/ppermute | solution.py:300
  33.7 9.5 %collective-permute-start.13 = (bf16[4,128,128]{2,1,0:T(8,128)(2,1)S(1)}, bf16[4,128,128]{2,1,0:T(8,128)(2,1)S(1)}, u32[]{:S(2)}, u32[]{:S(2)}) collective-permute-start(bf16[4,128,128]{2,1,0:T(8,128)(2,1)S(1)} %sum_and_solve.5.refs_2_), channel_id=1, source_target_pairs={{0,2},{1,10},{2,18},{3,26},{4,6},{5,14},{6,22},{7,30},{8,3},{9,11}... | collective-permute-start | bytes 393224 | tf_op jit(solution)/shard_map/ppermute | solution.py:285
  34.9 8.8 %collective-permute-start.14 = (bf16[4,128,128]{2,1,0:T(8,128)(2,1)S(1)}, bf16[4,128,128]{2,1,0:T(8,128)(2,1)S(1)}, u32[]{:S(2)}, u32[]{:S(2)}) collective-permute-start(bf16[4,128,128]{2,1,0:T(8,128)(2,1)S(1)} %sum_and_solve.5.refs_2_), channel_id=1, source_target_pairs={{0,7},{1,15},{2,21},{3,29},{4,1},{5,9},{6,19},{7,27},{8,6},{9,14},... | collective-permute-start | bytes 393224 | tf_op jit(solution)/shard_map/ppermute | solution.py:285
  44.0 4.5 %collective-permute-start.15 = (bf16[2,128,128]{2,1,0:T(8,128)(2,1)S(1)}, bf16[2,128,128]{2,1,0:T(8,128)(2,1)S(1)}, u32[]{:S(2)}, u32[]{:S(2)}) collective-permute-start(bf16[2,128,128]{2,1,0:T(8,128)(2,1)S(1)} %block_sums.11), channel_id=1, source_target_pairs={{0,16},{1,17},{2,18},{3,19},{4,20},{5,21},{6,22},{7,23},{8,24},{9,... | collective-permute-start | bytes 196616 | tf_op jit(solution)/shard_map/ppermute | solution.py:300
  48.6 1.3 %collective-permute-start.16 = (bf16[2,128,128]{2,1,0:T(8,128)(2,1)S(1)}, bf16[2,128,128]{2,1,0:T(8,128)(2,1)S(1)}, u32[]{:S(2)}, u32[]{:S(2)}) collective-permute-start(bf16[2,128,128]{2,1,0:T(8,128)(2,1)S(1)} %add.126.refs_0_), channel_id=1, source_target_pairs={{0,8},{1,9},{2,10},{3,11},{4,12},{5,13},{6,14},{7,15},{8,0},{9,1},... | collective-permute-start | bytes 196616 | tf_op jit(solution)/shard_map/ppermute | solution.py:300
  50.0 7.1 %collective-permute-start.17 = (bf16[2,128,128]{2,1,0:T(8,128)(2,1)S(1)}, bf16[2,128,128]{2,1,0:T(8,128)(2,1)S(1)}, u32[]{:S(2)}, u32[]{:S(2)}) collective-permute-start(bf16[2,128,128]{2,1,0:T(8,128)(2,1)S(1)} %sum_and_solve.6.refs_1_.refs_2_), channel_id=1, source_target_pairs={{0,2},{1,10},{2,18},{3,26},{4,6},{5,14},{6,22},{7,30},{8,3},{9,11}... | collective-permute-start | bytes 196616 | tf_op jit(solution)/shard_map/ppermute | solution.py:285
  51.5 5.6 %collective-permute-start.18 = (bf16[2,128,128]{2,1,0:T(8,128)(2,1)S(1)}, bf16[2,128,128]{2,1,0:T(8,128)(2,1)S(1)}, u32[]{:S(2)}, u32[]{:S(2)}) collective-permute-start(bf16[2,128,128]{2,1,0:T(8,128)(2,1)S(1)} %sum_and_solve.6.refs_1_.refs_2_), channel_id=1, source_target_pairs={{0,7},{1,15},{2,21},{3,29},{4,1},{5,9},{6,19},{7,27},{8,6},{9,14},... | collective-permute-start | bytes 196616 | tf_op jit(solution)/shard_map/ppermute | solution.py:285
  56.8 7.1 %copy-start.1 = (bf16[16,1,128,128]{3,2,1,0:T(8,128)(2,1)S(1)}, bf16[16,1,128,128]{3,2,1,0:T(8,128)(2,1)}, u32[]{:S(2)}) copy-start(bf16[16,1,128,128]{3,2,1,0:T(8,128)(2,1)} %refs_3_.5) | copy-start | bytes 1572868
  57.4 5.2 %collective-permute-start.19 = (bf16[2,128,128]{2,1,0:T(8,128)(2,1)S(1)}, bf16[2,128,128]{2,1,0:T(8,128)(2,1)S(1)}, u32[]{:S(2)}, u32[]{:S(2)}) collective-permute-start(bf16[2,128,128]{2,1,0:T(8,128)(2,1)S(1)} %block_sums.13), channel_id=1, source_target_pairs={{0,16},{1,17},{2,18},{3,19},{4,20},{5,21},{6,22},{7,23},{8,24},{9,... | collective-permute-start | bytes 196616 | tf_op jit(solution)/shard_map/ppermute | solution.py:300
  62.6 1.3 %collective-permute-start.20 = (bf16[2,128,128]{2,1,0:T(8,128)(2,1)S(1)}, bf16[2,128,128]{2,1,0:T(8,128)(2,1)S(1)}, u32[]{:S(2)}, u32[]{:S(2)}) collective-permute-start(bf16[2,128,128]{2,1,0:T(8,128)(2,1)S(1)} %add.127.refs_0_), channel_id=1, source_target_pairs={{0,8},{1,9},{2,10},{3,11},{4,12},{5,13},{6,14},{7,15},{8,0},{9,1},... | collective-permute-start | bytes 196616 | tf_op jit(solution)/shard_map/ppermute | solution.py:300
  64.2 6.8 %collective-permute-start.21 = (bf16[2,128,128]{2,1,0:T(8,128)(2,1)S(1)}, bf16[2,128,128]{2,1,0:T(8,128)(2,1)S(1)}, u32[]{:S(2)}, u32[]{:S(2)}) collective-permute-start(bf16[2,128,128]{2,1,0:T(8,128)(2,1)S(1)} %sum_and_solve.7.refs_1_), channel_id=1, source_target_pairs={{0,2},{1,10},{2,18},{3,26},{4,6},{5,14},{6,22},{7,30},{8,3},{9,11}... | collective-permute-start | bytes 196616 | tf_op jit(solution)/shard_map/ppermute | solution.py:285
  64.9 6.1 %collective-permute-start.22 = (bf16[2,128,128]{2,1,0:T(8,128)(2,1)S(1)}, bf16[2,128,128]{2,1,0:T(8,128)(2,1)S(1)}, u32[]{:S(2)}, u32[]{:S(2)}) collective-permute-start(bf16[2,128,128]{2,1,0:T(8,128)(2,1)S(1)} %sum_and_solve.7.refs_1_), channel_id=1, source_target_pairs={{0,7},{1,15},{2,21},{3,29},{4,1},{5,9},{6,19},{7,27},{8,6},{9,14},... | collective-permute-start | bytes 196616 | tf_op jit(solution)/shard_map/ppermute | solution.py:285
  71.2 4.9 %collective-permute-start.23 = (bf16[2,128,128]{2,1,0:T(8,128)(2,1)S(1)}, bf16[2,128,128]{2,1,0:T(8,128)(2,1)S(1)}, u32[]{:S(2)}, u32[]{:S(2)}) collective-permute-start(bf16[2,128,128]{2,1,0:T(8,128)(2,1)S(1)} %block_sums.14), channel_id=1, source_target_pairs={{0,16},{1,17},{2,18},{3,19},{4,20},{5,21},{6,22},{7,23},{8,24},{9,... | collective-permute-start | bytes 196616 | tf_op jit(solution)/shard_map/ppermute | solution.py:300
  76.2 1.3 %collective-permute-start.24 = (bf16[2,128,128]{2,1,0:T(8,128)(2,1)S(1)}, bf16[2,128,128]{2,1,0:T(8,128)(2,1)S(1)}, u32[]{:S(2)}, u32[]{:S(2)}) collective-permute-start(bf16[2,128,128]{2,1,0:T(8,128)(2,1)S(1)} %add.128.refs_0_), channel_id=1, source_target_pairs={{0,8},{1,9},{2,10},{3,11},{4,12},{5,13},{6,14},{7,15},{8,0},{9,1},... | collective-permute-start | bytes 196616 | tf_op jit(solution)/shard_map/ppermute | solution.py:300
  77.6 4.9 %collective-permute-start.25 = (bf16[2,128,128]{2,1,0:T(8,128)(2,1)S(1)}, bf16[2,128,128]{2,1,0:T(8,128)(2,1)S(1)}, u32[]{:S(2)}, u32[]{:S(2)}) collective-permute-start(bf16[2,128,128]{2,1,0:T(8,128)(2,1)S(1)} %sum_and_solve.8.refs_1_), channel_id=1, source_target_pairs={{0,2},{1,10},{2,18},{3,26},{4,6},{5,14},{6,22},{7,30},{8,3},{9,11}... | collective-permute-start | bytes 196616 | tf_op jit(solution)/shard_map/ppermute | solution.py:285
  78.8 5.3 %collective-permute-start.26 = (bf16[2,128,128]{2,1,0:T(8,128)(2,1)S(1)}, bf16[2,128,128]{2,1,0:T(8,128)(2,1)S(1)}, u32[]{:S(2)}, u32[]{:S(2)}) collective-permute-start(bf16[2,128,128]{2,1,0:T(8,128)(2,1)S(1)} %sum_and_solve.8.refs_1_), channel_id=1, source_target_pairs={{0,7},{1,15},{2,21},{3,29},{4,1},{5,9},{6,19},{7,27},{8,6},{9,14},... | collective-permute-start | bytes 196616 | tf_op jit(solution)/shard_map/ppermute | solution.py:285
  84.4 5.0 %collective-permute-start.27 = (bf16[4,128,128]{2,1,0:T(8,128)(2,1)S(1)}, bf16[4,128,128]{2,1,0:T(8,128)(2,1)S(1)}, u32[]{:S(2)}, u32[]{:S(2)}) collective-permute-start(bf16[4,128,128]{2,1,0:T(8,128)(2,1)S(1)} %block_sums.16), channel_id=1, source_target_pairs={{0,16},{1,17},{2,18},{3,19},{4,20},{5,21},{6,22},{7,23},{8,24},{9,... | collective-permute-start | bytes 393224 | tf_op jit(solution)/shard_map/ppermute | solution.py:300
  89.5 2.4 %collective-permute-start.28 = (bf16[4,128,128]{2,1,0:T(8,128)(2,1)S(1)}, bf16[4,128,128]{2,1,0:T(8,128)(2,1)S(1)}, u32[]{:S(2)}, u32[]{:S(2)}) collective-permute-start(bf16[4,128,128]{2,1,0:T(8,128)(2,1)S(1)} %add.129.refs_0_), channel_id=1, source_target_pairs={{0,8},{1,9},{2,10},{3,11},{4,12},{5,13},{6,14},{7,15},{8,0},{9,1},... | collective-permute-start | bytes 393224 | tf_op jit(solution)/shard_map/ppermute | solution.py:300
  92.1 7.8 %collective-permute-start.29 = (bf16[4,128,128]{2,1,0:T(8,128)(2,1)S(1)}, bf16[4,128,128]{2,1,0:T(8,128)(2,1)S(1)}, u32[]{:S(2)}, u32[]{:S(2)}) collective-permute-start(bf16[4,128,128]{2,1,0:T(8,128)(2,1)S(1)} %sum_and_solve.9), channel_id=1, source_target_pairs={{0,2},{1,10},{2,18},{3,26},{4,6},{5,14},{6,22},{7,30},{8,3},{9,11}... | collective-permute-start | bytes 393224 | tf_op jit(solution)/shard_map/ppermute | solution.py:285
  94.8 8.7 %collective-permute-start.30 = (bf16[4,128,128]{2,1,0:T(8,128)(2,1)S(1)}, bf16[4,128,128]{2,1,0:T(8,128)(2,1)S(1)}, u32[]{:S(2)}, u32[]{:S(2)}) collective-permute-start(bf16[4,128,128]{2,1,0:T(8,128)(2,1)S(1)} %sum_and_solve.9), channel_id=1, source_target_pairs={{0,7},{1,15},{2,21},{3,29},{4,1},{5,9},{6,19},{7,27},{8,6},{9,14},... | collective-permute-start | bytes 393224 | tf_op jit(solution)/shard_map/ppermute | solution.py:285
  104.3 2.3 %collective-permute-start.31 = (bf16[4,128,128]{2,1,0:T(8,128)(2,1)S(1)}, bf16[4,128,128]{2,1,0:T(8,128)(2,1)S(1)}, u32[]{:S(2)}, u32[]{:S(2)}) collective-permute-start(bf16[4,128,128]{2,1,0:T(8,128)(2,1)S(1)} %get-tuple-element.28), channel_id=1, source_target_pairs={{0,8},{8,0},{1,9},{9,1},{2,10},{10,2},{3,11},{11,3},{4,12},{12,4},... | collective-permute-start | bytes 393224 | tf_op jit(solution)/shard_map/ppermute | solution.py:410
  106.6 5.8 %collective-permute-start.32 = (bf16[4,128,128]{2,1,0:T(8,128)(2,1)S(1)}, bf16[4,128,128]{2,1,0:T(8,128)(2,1)S(1)}, u32[]{:S(2)}, u32[]{:S(2)}) collective-permute-start(bf16[4,128,128]{2,1,0:T(8,128)(2,1)S(1)} %get-tuple-element.29), channel_id=1, source_target_pairs={{0,16},{16,0},{1,17},{17,1},{2,18},{18,2},{3,19},{19,3},{4,20},{20... | collective-permute-start | bytes 393224 | tf_op jit(solution)/shard_map/ppermute | solution.py:411
  112.7 4.5 %collective-permute-start.33 = (bf16[128,128]{1,0:T(8,128)(2,1)S(1)}, bf16[128,128]{1,0:T(8,128)(2,1)S(1)}, u32[]{:S(2)}, u32[]{:S(2)}) collective-permute-start(bf16[128,128]{1,0:T(8,128)(2,1)S(1)} %get-tuple-element.38), channel_id=1, source_target_pairs={{0,2},{1,3},{2,0},{3,1},{4,6},{5,7},{6,4},{7,5},{8,10},{9,11},{10,... | collective-permute-start | bytes 98312 | tf_op jit(solution)/shard_map/ppermute | solution.py:425
  113.5 4.8 %collective-permute-start.34 = (bf16[128,128]{1,0:T(8,128)(2,1)S(1)}, bf16[128,128]{1,0:T(8,128)(2,1)S(1)}, u32[]{:S(2)}, u32[]{:S(2)}) collective-permute-start(bf16[128,128]{1,0:T(8,128)(2,1)S(1)} %get-tuple-element.37), channel_id=1, source_target_pairs={{0,4},{1,5},{2,6},{3,7},{4,0},{5,1},{6,2},{7,3},{8,12},{9,13},{10,... | collective-permute-start | bytes 98312 | tf_op jit(solution)/shard_map/ppermute | solution.py:425
  114.5 5.7 %collective-permute-start.35 = (bf16[128,128]{1,0:T(8,128)(2,1)S(1)}, bf16[128,128]{1,0:T(8,128)(2,1)S(1)}, u32[]{:S(2)}, u32[]{:S(2)}) collective-permute-start(bf16[128,128]{1,0:T(8,128)(2,1)S(1)} %get-tuple-element.36), channel_id=1, source_target_pairs={{0,6},{1,7},{2,4},{3,5},{4,2},{5,3},{6,0},{7,1},{8,14},{9,15},{10,... | collective-permute-start | bytes 98312 | tf_op jit(solution)/shard_map/ppermute | solution.py:425
  120.2 4.3 %collective-permute-start.36 = (bf16[2,128,128]{2,1,0:T(8,128)(2,1)S(1)}, bf16[2,128,128]{2,1,0:T(8,128)(2,1)S(1)}, u32[]{:S(2)}, u32[]{:S(2)}) collective-permute-start(bf16[2,128,128]{2,1,0:T(8,128)(2,1)S(1)} %pad_maximum_fusion.1), channel_id=1, source_target_pairs={{0,1},{1,0},{2,3},{3,2},{4,5},{5,4},{6,7},{7,6},{8,9},{9,8},{10,11... | collective-permute-start | bytes 196616 | tf_op jit(solution)/shard_map/ppermute | solution.py:425

commit v9 on v7

--- a/solution.py
+++ b/solution.py
@@ -421,8 +421,8 @@
         def crossed(values, t):
             return lax.ppermute(values, ALL_AXES, [(device(r, c), device(r, c ^ t)) for r, c in everyone])
 
-        received = [crossed(pick(rows, upper_id ^ t), 2 * t) for t in range(per - 1, 0, -1)]
-        received = jnp.stack([pick(rows, upper_id)] + received[::-1])
+        received = [crossed(pick(rows, upper_id ^ t), 2 * t) for t in range(1, per)]
+        received = jnp.stack([pick(rows, upper_id)] + received)
         kept, sent = [
             jnp.stack([pick(received, upper_id ^ (per // 2 * p + i)) for i in range(per // 2)])
             for p in (last_id, 1 - last_id)

time: 126 us -> 126 us (level)
  no operation moved by 1% of the time
where the time goes in v9:
time: 126 us; the launch traced here: 125 us
  starting transfers between devices  51.4 us (41%)
  waiting for transfers between devices  50.7 us (40%)
  Pallas kernels  19.2 us (15%)
  local copies, waits for them, and re-layouts  2.71 us (2%)
    ppermute x10, waiting for transfers between devices, summands(): other = lax.ppermute(partial, ALL_AXES, pairs)  25.4 us
    ppermute x10, starting transfers between devices, spread(): lax.ppermute(values, ALL_AXES, [(device(r, c), device(*route(t, r, c))) f...  19.7 us
    pallas_call x5, Pallas kernels, lay_out(): pl.pallas_call(kernel, grid_spec=pltpu.PrefetchScalarGridSpec(num_scalar_...  12.7 us
    ppermute x10, starting transfers between devices, summands(): other = lax.ppermute(partial, ALL_AXES, pairs)  8.29 us
    ppermute x7, starting transfers between devices, exchange(): lax.ppermute(values, ALL_AXES, [(device(r, c), device(r, c ^ t)) for r, c...  8.03 us
    ppermute x10, waiting for transfers between devices, spread(): lax.ppermute(values, ALL_AXES, [(device(r, c), device(*route(t, r, c))) f...  7.9 us
    ppermute x4, waiting for transfers between devices, crossed(): lax.ppermute(values, ALL_AXES, [(device(r, c), device(r, c ^ t)) for r, c...  5.99 us
    ppermute x1, waiting for transfers between devices, on_device(): other = lax.ppermute(own.astype(jnp.bfloat16), 'hi', [(0, 1), (1, 0)])  5.58 us
  transfers between devices with their start and end apart: 37, of which 24 were waited for; matrix products, arithmetic and copies ran while one was open for 1% of the time, Pallas kernels for 12%

profile of v9, /device:TPU:0, one launch (start us, length us, event | category | flops | bytes accessed | tf_op | source)
XLA Modules:
  0.0 125.1 jit_solution(10969707101842600513)
XLA Ops:
  0.0 0.9 constant_dynamic-slice_fusion.6
  0.9 3.0 %collective-permute-start.1 = (bf16[2,128,128]{2,1,0:T(8,128)(2,1)S(1)}, bf16[2,128,128]{2,1,0:T(8,128)(2,1)S(1)}, u32[]{:S(2)}, u32[]{:S(2)}) collective-permute-start(bf16[2,128,128]{2,1,0:T(8,128)(2,1)S(1)} %get-tuple-element.44), channel_id=1, source_target_pairs={{0,16},{16,0},{1,17},{17,1},{2,18},{18,2},{3,19},{19,3},{4,20},{20... | collective-permute-start | bytes 196616 | tf_op jit(solution)/shard_map/ppermute | solution.py:344
  3.9 1.0 slice.15
  4.9 2.6 %collective-permute-start = (bf16[2,128,128]{2,1,0:T(8,128)(2,1)S(1)}, bf16[2,128,128]{2,1,0:T(8,128)(2,1)S(1)}, u32[]{:S(2)}, u32[]{:S(2)}) collective-permute-start(bf16[2,128,128]{2,1,0:T(8,128)(2,1)S(1)} %dynamic-slice_bitcast_fusion.2.refs_1_), channel_id=1, source_target_pairs={{0,4},{1,12},{2,16},{3,24},{4,1},{5,9},{6,21},{7,29},{8,6},{9,14},... | collective-permute-start | bytes 196616 | tf_op jit(solution)/shard_map/ppermute | solution.py:340
  7.6 1.2 collective-permute-start.2
  8.9 2.5 %lay_out.5.refs_0_ = bf16[8,4,2,128,128]{4,3,2,1,0:T(8,128)(2,1)S(1)} custom-call(s32[3]{0:T(128)S(1)} %pad_add_fusion.scal, s32[16,32]{1,0:T(8,128)} %bitcast.45, bf16[16,4,8,128,128]{4,3,2,1,0:T(8,128)(2,1)} %bitcast.38, bf16[2,128,128]{2,1,0:T(8,128)(2,1)S(1)} %dynamic-slice_bitcast_fusion.2.refs_1_), custom_call_target="tpu_custom_call" | custom-call | bytes 8388608 | tf_op jit(solution)/shard_map/lay_out/pallas_call | solution.py:64
  12.0 3.1 %collective-permute-start.6 = (bf16[2,128,128]{2,1,0:T(8,128)(2,1)S(1)}, bf16[2,128,128]{2,1,0:T(8,128)(2,1)S(1)}, u32[]{:S(2)}, u32[]{:S(2)}) collective-permute-start(bf16[2,128,128]{2,1,0:T(8,128)(2,1)S(1)} %solve_blocks.1.refs_1_.refs_0_), channel_id=1, source_target_pairs={{0,4},{1,5},{2,6},{3,7},{4,0},{5,1},{6,2},{7,3},{8,12},{9,13},{10,... | collective-permute-start | bytes 196616 | tf_op jit(solution)/shard_map/ppermute | solution.py:337
  15.1 0.9 collective-permute-start.8
  16.0 1.3 %collective-permute-start.3 = (bf16[2,128,128]{2,1,0:T(8,128)(2,1)S(1)}, bf16[2,128,128]{2,1,0:T(8,128)(2,1)S(1)}, u32[]{:S(2)}, u32[]{:S(2)}) collective-permute-start(bf16[2,128,128]{2,1,0:T(8,128)(2,1)S(1)} %solve_blocks.1.refs_1_.refs_0_), channel_id=1, source_target_pairs={{0,1},{1,0},{2,3},{3,2},{4,5},{5,4},{6,7},{7,6},{8,9},{9,8},{10,11... | collective-permute-start | bytes 196616 | tf_op jit(solution)/shard_map/ppermute | solution.py:337
  17.4 1.4 %collective-permute-start.10 = (bf16[2,128,128]{2,1,0:T(8,128)(2,1)S(1)}, bf16[2,128,128]{2,1,0:T(8,128)(2,1)S(1)}, u32[]{:S(2)}, u32[]{:S(2)}) collective-permute-start(bf16[2,128,128]{2,1,0:T(8,128)(2,1)S(1)} %get-tuple-element.39), channel_id=1, source_target_pairs={{4,0},{12,1},{16,2},{24,3},{1,4},{9,5},{21,6},{29,7},{6,8},{14,9},... | collective-permute-start | bytes 196616 | tf_op jit(solution)/shard_map/ppermute | solution.py:354
  19.9 0.9 collective-permute-start.7
  20.8 0.9 collective-permute-done.8.refs_7_.refs_6_
  22.5 1.7 %collective-permute-done.10 = bf16[2,128,128]{2,1,0:T(8,128)(2,1)S(1)} collective-permute-done((bf16[2,128,128]{2,1,0:T(8,128)(2,1)S(1)}, bf16[2,128,128]{2,1,0:T(8,128)(2,1)S(1)}, u32[]{:S(2)}, u32[]{:S(2)}) %collective-permute-start.10) | collective-permute-done | bytes 65568 | tf_op jit(solution)/shard_map/ppermute | solution.py:354
  24.7 1.4 %collective-permute-done.9.refs_8_.refs_7_ = bf16[2,128,128]{2,1,0:T(8,128)(2,1)S(1)} collective-permute-done((bf16[2,128,128]{2,1,0:T(8,128)(2,1)S(1)}, bf16[2,128,128]{2,1,0:T(8,128)(2,1)S(1)}, u32[]{:S(2)}, u32[]{:S(2)}) %collective-permute-start.9) | collective-permute-done | bytes 65568 | tf_op jit(solution)/shard_map/ppermute | solution.py:337
  26.8 1.6 %collective-permute-start.11 = (bf16[4,128,128]{2,1,0:T(8,128)(2,1)S(1)}, bf16[4,128,128]{2,1,0:T(8,128)(2,1)S(1)}, u32[]{:S(2)}, u32[]{:S(2)}) collective-permute-start(bf16[4,128,128]{2,1,0:T(8,128)(2,1)S(1)} %block_sums.9), channel_id=1, source_target_pairs={{0,16},{1,17},{2,18},{3,19},{4,20},{5,21},{6,22},{7,23},{8,24},{9,... | collective-permute-start | bytes 393224 | tf_op jit(solution)/shard_map/ppermute | solution.py:300
  28.4 4.0 %collective-permute-done.11 = bf16[4,128,128]{2,1,0:T(8,128)(2,1)S(1)} collective-permute-done((bf16[4,128,128]{2,1,0:T(8,128)(2,1)S(1)}, bf16[4,128,128]{2,1,0:T(8,128)(2,1)S(1)}, u32[]{:S(2)}, u32[]{:S(2)}) %collective-permute-start.11) | collective-permute-done | bytes 131104 | tf_op jit(solution)/shard_map/ppermute | solution.py:300
  32.5 1.3 %collective-permute-done.12.refs_1_ = bf16[4,128,128]{2,1,0:T(8,128)(2,1)S(1)} collective-permute-done((bf16[4,128,128]{2,1,0:T(8,128)(2,1)S(1)}, bf16[4,128,128]{2,1,0:T(8,128)(2,1)S(1)}, u32[]{:S(2)}, u32[]{:S(2)}) %collective-permute-start.12) | collective-permute-done | bytes 131104 | tf_op jit(solution)/shard_map/ppermute | solution.py:300
  34.0 1.2 collective-permute-start.13
  35.2 3.5 %collective-permute-start.14 = (bf16[4,128,128]{2,1,0:T(8,128)(2,1)S(1)}, bf16[4,128,128]{2,1,0:T(8,128)(2,1)S(1)}, u32[]{:S(2)}, u32[]{:S(2)}) collective-permute-start(bf16[4,128,128]{2,1,0:T(8,128)(2,1)S(1)} %sum_and_solve.5.refs_2_), channel_id=1, source_target_pairs={{0,7},{1,15},{2,21},{3,29},{4,1},{5,9},{6,19},{7,27},{8,6},{9,14},... | collective-permute-start | bytes 393224 | tf_op jit(solution)/shard_map/ppermute | solution.py:285
  39.5 2.7 %lay_out.6 = (bf16[8,4,2,128,128]{4,3,2,1,0:T(8,128)(2,1)S(1)}, bf16[4,2,2,128,128]{4,3,2,1,0:T(8,128)(2,1)S(1)}) custom-call(s32[3]{0:T(128)S(1)} %pad_add_fusion.scal, s32[16,32]{1,0:T(8,128)} %bitcast.46, bf16[16,16,2,128,128]{4,3,2,1,0:T(8,128)(2,1)} %bitcast.39, bf16[16,4,8,128,128]{4,3,2,1,0:T(8,128)(2,1)} %bitcast.40, ...), custom_call_target="tpu_custom_call" | custom-call | bytes 10485760 | tf_op jit(solution)/shard_map/lay_out/pallas_call | solution.py:64
  42.9 0.8 collective-permute-done.14.refs_2_
  44.0 2.2 %collective-permute-start.15 = (bf16[2,128,128]{2,1,0:T(8,128)(2,1)S(1)}, bf16[2,128,128]{2,1,0:T(8,128)(2,1)S(1)}, u32[]{:S(2)}, u32[]{:S(2)}) collective-permute-start(bf16[2,128,128]{2,1,0:T(8,128)(2,1)S(1)} %block_sums.11), channel_id=1, source_target_pairs={{0,16},{1,17},{2,18},{3,19},{4,20},{5,21},{6,22},{7,23},{8,24},{9,... | collective-permute-start | bytes 196616 | tf_op jit(solution)/shard_map/ppermute | solution.py:300
  46.2 2.3 %collective-permute-done.15 = bf16[2,128,128]{2,1,0:T(8,128)(2,1)S(1)} collective-permute-done((bf16[2,128,128]{2,1,0:T(8,128)(2,1)S(1)}, bf16[2,128,128]{2,1,0:T(8,128)(2,1)S(1)}, u32[]{:S(2)}, u32[]{:S(2)}) %collective-permute-start.15) | collective-permute-done | bytes 65568 | tf_op jit(solution)/shard_map/ppermute | solution.py:300
  48.6 1.2 collective-permute-done.16.refs_1_
  50.0 1.9 %collective-permute-start.17 = (bf16[2,128,128]{2,1,0:T(8,128)(2,1)S(1)}, bf16[2,128,128]{2,1,0:T(8,128)(2,1)S(1)}, u32[]{:S(2)}, u32[]{:S(2)}) collective-permute-start(bf16[2,128,128]{2,1,0:T(8,128)(2,1)S(1)} %sum_and_solve.6.refs_1_.refs_2_), channel_id=1, source_target_pairs={{0,2},{1,10},{2,18},{3,26},{4,6},{5,14},{6,22},{7,30},{8,3},{9,11}... | collective-permute-start | bytes 196616 | tf_op jit(solution)/shard_map/ppermute | solution.py:285
  51.8 2.7 %collective-permute-start.18 = (bf16[2,128,128]{2,1,0:T(8,128)(2,1)S(1)}, bf16[2,128,128]{2,1,0:T(8,128)(2,1)S(1)}, u32[]{:S(2)}, u32[]{:S(2)}) collective-permute-start(bf16[2,128,128]{2,1,0:T(8,128)(2,1)S(1)} %sum_and_solve.6.refs_1_.refs_2_), channel_id=1, source_target_pairs={{0,7},{1,15},{2,21},{3,29},{4,1},{5,9},{6,19},{7,27},{8,6},{9,14},... | collective-permute-start | bytes 196616 | tf_op jit(solution)/shard_map/ppermute | solution.py:285
  54.5 2.1 %lay_out.7 = (bf16[4,2,2,128,128]{4,3,2,1,0:T(8,128)(2,1)S(1)}, bf16[2,2,2,128,128]{4,3,2,1,0:T(8,128)(2,1)S(1)}) custom-call(s32[3]{0:T(128)S(1)} %pad_add_fusion.scal, s32[16,32]{1,0:T(8,128)} %bitcast.47, bf16[16,16,2,128,128]{4,3,2,1,0:T(8,128)(2,1)} %bitcast.41, bf16[2,128,128]{2,1,0:T(8,128)(2,1)S(1)} %sum_and_solve.6.refs_1_.refs_2_), custom_call_target="tpu_custom_call" | custom-call | bytes 3145728 | tf_op jit(solution)/shard_map/lay_out/pallas_call | solution.py:64
  57.1 3.2 %collective-permute-start.19 = (bf16[2,128,128]{2,1,0:T(8,128)(2,1)S(1)}, bf16[2,128,128]{2,1,0:T(8,128)(2,1)S(1)}, u32[]{:S(2)}, u32[]{:S(2)}) collective-permute-start(bf16[2,128,128]{2,1,0:T(8,128)(2,1)S(1)} %block_sums.13), channel_id=1, source_target_pairs={{0,16},{1,17},{2,18},{3,19},{4,20},{5,21},{6,22},{7,23},{8,24},{9,... | collective-permute-start | bytes 196616 | tf_op jit(solution)/shard_map/ppermute | solution.py:300
  60.3 2.5 %collective-permute-done.19 = bf16[2,128,128]{2,1,0:T(8,128)(2,1)S(1)} collective-permute-done((bf16[2,128,128]{2,1,0:T(8,128)(2,1)S(1)}, bf16[2,128,128]{2,1,0:T(8,128)(2,1)S(1)}, u32[]{:S(2)}, u32[]{:S(2)}) %collective-permute-start.19) | collective-permute-done | bytes 65568 | tf_op jit(solution)/shard_map/ppermute | solution.py:300
  63.0 1.2 collective-permute-done.20.refs_1_
  65.0 4.3 %collective-permute-start.22 = (bf16[2,128,128]{2,1,0:T(8,128)(2,1)S(1)}, bf16[2,128,128]{2,1,0:T(8,128)(2,1)S(1)}, u32[]{:S(2)}, u32[]{:S(2)}) collective-permute-start(bf16[2,128,128]{2,1,0:T(8,128)(2,1)S(1)} %sum_and_solve.7.refs_1_), channel_id=1, source_target_pairs={{0,7},{1,15},{2,21},{3,29},{4,1},{5,9},{6,19},{7,27},{8,6},{9,14},... | collective-permute-start | bytes 196616 | tf_op jit(solution)/shard_map/ppermute | solution.py:285
  69.3 2.6 %lay_out.8 = (bf16[2,2,2,128,128]{4,3,2,1,0:T(8,128)(2,1)S(1)}, bf16[2,4,2,128,128]{4,3,2,1,0:T(8,128)(2,1)S(1)}, bf16[2,4,2,128,128]{4,3,2,1,0:T(8,128)(2,1)S(1)}, bf16[2,8,2,128,128]{4,3,2,1,0:T(8,128)(2,1)S(1)}) custom-call(s32[3]{0:T(128)S(1)} %pad_add_fusion.scal, s32[16,32]{1,0:T(8,128)} %bitcast.48, bf16[16,16,2,128,128]{4,3,2,1,0:T(8,128)(2,1)} %bitcast.42, ...), custom_call_target="tpu_custom_call" | custom-call | bytes 9437184 | tf_op jit(solution)/shard_map/lay_out/pallas_call | solution.py:64
  72.9 4.2 %collective-permute-done.23 = bf16[2,128,128]{2,1,0:T(8,128)(2,1)S(1)} collective-permute-done((bf16[2,128,128]{2,1,0:T(8,128)(2,1)S(1)}, bf16[2,128,128]{2,1,0:T(8,128)(2,1)S(1)}, u32[]{:S(2)}, u32[]{:S(2)}) %collective-permute-start.23) | collective-permute-done | bytes 65568 | tf_op jit(solution)/shard_map/ppermute | solution.py:300
  77.4 1.1 collective-permute-done.24.refs_1_
  79.2 3.3 %collective-permute-start.26 = (bf16[2,128,128]{2,1,0:T(8,128)(2,1)S(1)}, bf16[2,128,128]{2,1,0:T(8,128)(2,1)S(1)}, u32[]{:S(2)}, u32[]{:S(2)}) collective-permute-start(bf16[2,128,128]{2,1,0:T(8,128)(2,1)S(1)} %sum_and_solve.8.refs_1_), channel_id=1, source_target_pairs={{0,7},{1,15},{2,21},{3,29},{4,1},{5,9},{6,19},{7,27},{8,6},{9,14},... | collective-permute-start | bytes 196616 | tf_op jit(solution)/shard_map/ppermute | solution.py:285
  83.0 3.4 %collective-permute-done.26.refs_2_.refs_5_ = bf16[2,128,128]{2,1,0:T(8,128)(2,1)S(1)} collective-permute-done((bf16[2,128,128]{2,1,0:T(8,128)(2,1)S(1)}, bf16[2,128,128]{2,1,0:T(8,128)(2,1)S(1)}, u32[]{:S(2)}, u32[]{:S(2)}) %collective-permute-start.26) | collective-permute-done | bytes 65568 | tf_op jit(solution)/shard_map/ppermute | solution.py:285
  86.8 6.1 %collective-permute-done.27 = bf16[4,128,128]{2,1,0:T(8,128)(2,1)S(1)} collective-permute-done((bf16[4,128,128]{2,1,0:T(8,128)(2,1)S(1)}, bf16[4,128,128]{2,1,0:T(8,128)(2,1)S(1)}, u32[]{:S(2)}, u32[]{:S(2)}) %collective-permute-start.27) | collective-permute-done | bytes 131104 | tf_op jit(solution)/shard_map/ppermute | solution.py:300
  93.0 1.3 %collective-permute-done.28.refs_1_ = bf16[4,128,128]{2,1,0:T(8,128)(2,1)S(1)} collective-permute-done((bf16[4,128,128]{2,1,0:T(8,128)(2,1)S(1)}, bf16[4,128,128]{2,1,0:T(8,128)(2,1)S(1)}, u32[]{:S(2)}, u32[]{:S(2)}) %collective-permute-start.28) | collective-permute-done | bytes 131104 | tf_op jit(solution)/shard_map/ppermute | solution.py:300
  94.6 1.9 %collective-permute-start.30 = (bf16[4,128,128]{2,1,0:T(8,128)(2,1)S(1)}, bf16[4,128,128]{2,1,0:T(8,128)(2,1)S(1)}, u32[]{:S(2)}, u32[]{:S(2)}) collective-permute-start(bf16[4,128,128]{2,1,0:T(8,128)(2,1)S(1)} %sum_and_solve.9), channel_id=1, source_target_pairs={{0,7},{1,15},{2,21},{3,29},{4,1},{5,9},{6,19},{7,27},{8,6},{9,14},... | collective-permute-start | bytes 393224 | tf_op jit(solution)/shard_map/ppermute | solution.py:285
  96.5 2.9 %lay_out.9 = (bf16[2,8,2,128,128]{4,3,2,1,0:T(8,128)(2,1)S(1)}, bf16[4,8,2,128,128]{4,3,2,1,0:T(8,128)(2,1)S(1)}) custom-call(s32[3]{0:T(128)S(1)} %pad_add_fusion.scal, s32[16,32]{1,0:T(8,128)} %bitcast.49, bf16[16,16,2,128,128]{4,3,2,1,0:T(8,128)(2,1)} %bitcast.43, bf16[2,128,128]{2,1,0:T(8,128)(2,1)S(1)} %sum_and_solve.8.refs_1_), custom_call_target="tpu_custom_call" | custom-call | bytes 12582912 | tf_op jit(solution)/shard_map/lay_out/pallas_call | solution.py:64
  100.1 3.4 %collective-permute-done.30.refs_1_ = bf16[4,128,128]{2,1,0:T(8,128)(2,1)S(1)} collective-permute-done((bf16[4,128,128]{2,1,0:T(8,128)(2,1)S(1)}, bf16[4,128,128]{2,1,0:T(8,128)(2,1)S(1)}, u32[]{:S(2)}, u32[]{:S(2)}) %collective-permute-start.30) | collective-permute-done | bytes 131104 | tf_op jit(solution)/shard_map/ppermute | solution.py:285
  104.2 2.1 %collective-permute-start.31 = (bf16[4,128,128]{2,1,0:T(8,128)(2,1)S(1)}, bf16[4,128,128]{2,1,0:T(8,128)(2,1)S(1)}, u32[]{:S(2)}, u32[]{:S(2)}) collective-permute-start(bf16[4,128,128]{2,1,0:T(8,128)(2,1)S(1)} %get-tuple-element.28), channel_id=1, source_target_pairs={{0,8},{8,0},{1,9},{9,1},{2,10},{10,2},{3,11},{11,3},{4,12},{12,4},... | collective-permute-start | bytes 393224 | tf_op jit(solution)/shard_map/ppermute | solution.py:407
  106.3 1.0 collective-permute-done.31
  107.6 5.6 %collective-permute-done.32.other_ref = bf16[4,128,128]{2,1,0:T(8,128)(2,1)S(1)} collective-permute-done((bf16[4,128,128]{2,1,0:T(8,128)(2,1)S(1)}, bf16[4,128,128]{2,1,0:T(8,128)(2,1)S(1)}, u32[]{:S(2)}, u32[]{:S(2)}) %collective-permute-start.32) | collective-permute-done | bytes 131104 | tf_op jit(solution)/shard_map/ppermute | solution.py:408
  114.3 3.5 %collective-permute-start.35 = (bf16[128,128]{1,0:T(8,128)(2,1)S(1)}, bf16[128,128]{1,0:T(8,128)(2,1)S(1)}, u32[]{:S(2)}, u32[]{:S(2)}) collective-permute-start(bf16[128,128]{1,0:T(8,128)(2,1)S(1)} %get-tuple-element.36), channel_id=1, source_target_pairs={{0,6},{1,7},{2,4},{3,5},{4,2},{5,3},{6,0},{7,1},{8,14},{9,15},{10,... | collective-permute-start | bytes 98312 | tf_op jit(solution)/shard_map/ppermute | solution.py:422
  117.8 0.9 collective-permute-done.34
  118.7 1.4 %collective-permute-done.35 = bf16[128,128]{1,0:T(8,128)(2,1)S(1)} collective-permute-done((bf16[128,128]{1,0:T(8,128)(2,1)S(1)}, bf16[128,128]{1,0:T(8,128)(2,1)S(1)}, u32[]{:S(2)}, u32[]{:S(2)}) %collective-permute-start.35) | collective-permute-done | bytes 32800 | tf_op jit(solution)/shard_map/ppermute | solution.py:422
  120.7 3.8 %collective-permute-done.36 = bf16[2,128,128]{2,1,0:T(8,128)(2,1)S(1)} collective-permute-done((bf16[2,128,128]{2,1,0:T(8,128)(2,1)S(1)}, bf16[2,128,128]{2,1,0:T(8,128)(2,1)S(1)}, u32[]{:S(2)}, u32[]{:S(2)}) %collective-permute-start.36) | collective-permute-done | bytes 65568 | tf_op jit(solution)/shard_map/ppermute | solution.py:422
  (81 shorter events, 14.7 us)
Async XLA Ops:
  0.9 6.7 %collective-permute-start.1 = (bf16[2,128,128]{2,1,0:T(8,128)(2,1)S(1)}, bf16[2,128,128]{2,1,0:T(8,128)(2,1)S(1)}, u32[]{:S(2)}, u32[]{:S(2)}) collective-permute-start(bf16[2,128,128]{2,1,0:T(8,128)(2,1)S(1)} %get-tuple-element.44), channel_id=1, source_target_pairs={{0,16},{16,0},{1,17},{17,1},{2,18},{18,2},{3,19},{19,3},{4,20},{20... | collective-permute-start | bytes 196616 | tf_op jit(solution)/shard_map/ppermute | solution.py:344
  4.9 6.5 %collective-permute-start = (bf16[2,128,128]{2,1,0:T(8,128)(2,1)S(1)}, bf16[2,128,128]{2,1,0:T(8,128)(2,1)S(1)}, u32[]{:S(2)}, u32[]{:S(2)}) collective-permute-start(bf16[2,128,128]{2,1,0:T(8,128)(2,1)S(1)} %dynamic-slice_bitcast_fusion.2.refs_1_), channel_id=1, source_target_pairs={{0,4},{1,12},{2,16},{3,24},{4,1},{5,9},{6,21},{7,29},{8,6},{9,14},... | collective-permute-start | bytes 196616 | tf_op jit(solution)/shard_map/ppermute | solution.py:340
  7.6 3.8 %collective-permute-start.2 = (bf16[2,128,128]{2,1,0:T(8,128)(2,1)S(1)}, bf16[2,128,128]{2,1,0:T(8,128)(2,1)S(1)}, u32[]{:S(2)}, u32[]{:S(2)}) collective-permute-start(bf16[2,128,128]{2,1,0:T(8,128)(2,1)S(1)} %get-tuple-element.42), channel_id=1, source_target_pairs={{0,8},{8,0},{1,9},{9,1},{2,10},{10,2},{3,11},{11,3},{4,12},{12,4},... | collective-permute-start | bytes 196616 | tf_op jit(solution)/shard_map/ppermute | solution.py:344
  11.6 22.2 %copy-start = (bf16[16,1,128,128]{3,2,1,0:T(8,128)(2,1)S(1)}, bf16[16,1,128,128]{3,2,1,0:T(8,128)(2,1)}, u32[]{:S(2)}) copy-start(bf16[16,1,128,128]{3,2,1,0:T(8,128)(2,1)} %refs_2_.5) | copy-start | bytes 1572868
  11.6 7.2 %collective-permute-start.4 = (bf16[2,128,128]{2,1,0:T(8,128)(2,1)S(1)}, bf16[2,128,128]{2,1,0:T(8,128)(2,1)S(1)}, u32[]{:S(2)}, u32[]{:S(2)}) collective-permute-start(bf16[2,128,128]{2,1,0:T(8,128)(2,1)S(1)} %solve_blocks.1.refs_1_.refs_0_), channel_id=1, source_target_pairs={{0,2},{1,3},{2,0},{3,1},{4,6},{5,7},{6,4},{7,5},{8,10},{9,11},{10,... | collective-permute-start | bytes 196616 | tf_op jit(solution)/shard_map/ppermute | solution.py:337
  12.0 7.9 %collective-permute-start.6 = (bf16[2,128,128]{2,1,0:T(8,128)(2,1)S(1)}, bf16[2,128,128]{2,1,0:T(8,128)(2,1)S(1)}, u32[]{:S(2)}, u32[]{:S(2)}) collective-permute-start(bf16[2,128,128]{2,1,0:T(8,128)(2,1)S(1)} %solve_blocks.1.refs_1_.refs_0_), channel_id=1, source_target_pairs={{0,4},{1,5},{2,6},{3,7},{4,0},{5,1},{6,2},{7,3},{8,12},{9,13},{10,... | collective-permute-start | bytes 196616 | tf_op jit(solution)/shard_map/ppermute | solution.py:337
  15.1 6.6 %collective-permute-start.8 = (bf16[2,128,128]{2,1,0:T(8,128)(2,1)S(1)}, bf16[2,128,128]{2,1,0:T(8,128)(2,1)S(1)}, u32[]{:S(2)}, u32[]{:S(2)}) collective-permute-start(bf16[2,128,128]{2,1,0:T(8,128)(2,1)S(1)} %solve_blocks.1.refs_1_.refs_0_), channel_id=1, source_target_pairs={{0,6},{1,7},{2,4},{3,5},{4,2},{5,3},{6,0},{7,1},{8,14},{9,15},{10,... | collective-permute-start | bytes 196616 | tf_op jit(solution)/shard_map/ppermute | solution.py:337
  16.0 8.3 %collective-permute-start.3 = (bf16[2,128,128]{2,1,0:T(8,128)(2,1)S(1)}, bf16[2,128,128]{2,1,0:T(8,128)(2,1)S(1)}, u32[]{:S(2)}, u32[]{:S(2)}) collective-permute-start(bf16[2,128,128]{2,1,0:T(8,128)(2,1)S(1)} %solve_blocks.1.refs_1_.refs_0_), channel_id=1, source_target_pairs={{0,1},{1,0},{2,3},{3,2},{4,5},{5,4},{6,7},{7,6},{8,9},{9,8},{10,11... | collective-permute-start | bytes 196616 | tf_op jit(solution)/shard_map/ppermute | solution.py:337
  17.4 6.8 %collective-permute-start.10 = (bf16[2,128,128]{2,1,0:T(8,128)(2,1)S(1)}, bf16[2,128,128]{2,1,0:T(8,128)(2,1)S(1)}, u32[]{:S(2)}, u32[]{:S(2)}) collective-permute-start(bf16[2,128,128]{2,1,0:T(8,128)(2,1)S(1)} %get-tuple-element.39), channel_id=1, source_target_pairs={{4,0},{12,1},{16,2},{24,3},{1,4},{9,5},{21,6},{29,7},{6,8},{14,9},... | collective-permute-start | bytes 196616 | tf_op jit(solution)/shard_map/ppermute | solution.py:354
  18.8 5.5 %collective-permute-start.5 = (bf16[2,128,128]{2,1,0:T(8,128)(2,1)S(1)}, bf16[2,128,128]{2,1,0:T(8,128)(2,1)S(1)}, u32[]{:S(2)}, u32[]{:S(2)}) collective-permute-start(bf16[2,128,128]{2,1,0:T(8,128)(2,1)S(1)} %collective-permute-done.4.refs_3_.refs_2_), channel_id=1, source_target_pairs={{0,1},{1,0},{2,3},{3,2},{4,5},{5,4},{6,7},{7,6},{8,9},{9,8},{10,11... | collective-permute-start | bytes 196616 | tf_op jit(solution)/shard_map/ppermute | solution.py:337
  19.9 4.7 %collective-permute-start.7 = (bf16[2,128,128]{2,1,0:T(8,128)(2,1)S(1)}, bf16[2,128,128]{2,1,0:T(8,128)(2,1)S(1)}, u32[]{:S(2)}, u32[]{:S(2)}) collective-permute-start(bf16[2,128,128]{2,1,0:T(8,128)(2,1)S(1)} %collective-permute-done.6.refs_5_.refs_4_), channel_id=1, source_target_pairs={{0,1},{1,0},{2,3},{3,2},{4,5},{5,4},{6,7},{7,6},{8,9},{9,8},{10,11... | collective-permute-start | bytes 196616 | tf_op jit(solution)/shard_map/ppermute | solution.py:337
  21.7 4.4 %collective-permute-start.9 = (bf16[2,128,128]{2,1,0:T(8,128)(2,1)S(1)}, bf16[2,128,128]{2,1,0:T(8,128)(2,1)S(1)}, u32[]{:S(2)}, u32[]{:S(2)}) collective-permute-start(bf16[2,128,128]{2,1,0:T(8,128)(2,1)S(1)} %collective-permute-done.8.refs_7_.refs_6_), channel_id=1, source_target_pairs={{0,1},{1,0},{2,3},{3,2},{4,5},{5,4},{6,7},{7,6},{8,9},{9,8},{10,11... | collective-permute-start | bytes 196616 | tf_op jit(solution)/shard_map/ppermute | solution.py:337
  26.8 5.6 %collective-permute-start.11 = (bf16[4,128,128]{2,1,0:T(8,128)(2,1)S(1)}, bf16[4,128,128]{2,1,0:T(8,128)(2,1)S(1)}, u32[]{:S(2)}, u32[]{:S(2)}) collective-permute-start(bf16[4,128,128]{2,1,0:T(8,128)(2,1)S(1)} %block_sums.9), channel_id=1, source_target_pairs={{0,16},{1,17},{2,18},{3,19},{4,20},{5,21},{6,22},{7,23},{8,24},{9,... | collective-permute-start | bytes 393224 | tf_op jit(solution)/shard_map/ppermute | solution.py:300
  32.4 1.4 %collective-permute-start.12 = (bf16[4,128,128]{2,1,0:T(8,128)(2,1)S(1)}, bf16[4,128,128]{2,1,0:T(8,128)(2,1)S(1)}, u32[]{:S(2)}, u32[]{:S(2)}) collective-permute-start(bf16[4,128,128]{2,1,0:T(8,128)(2,1)S(1)} %add.125.refs_0_), channel_id=1, source_target_pairs={{0,8},{1,9},{2,10},{3,11},{4,12},{5,13},{6,14},{7,15},{8,0},{9,1},... | collective-permute-start | bytes 393224 | tf_op jit(solution)/shard_map/ppermute | solution.py:300
  34.0 8.9 %collective-permute-start.13 = (bf16[4,128,128]{2,1,0:T(8,128)(2,1)S(1)}, bf16[4,128,128]{2,1,0:T(8,128)(2,1)S(1)}, u32[]{:S(2)}, u32[]{:S(2)}) collective-permute-start(bf16[4,128,128]{2,1,0:T(8,128)(2,1)S(1)} %sum_and_solve.5.refs_2_), channel_id=1, source_target_pairs={{0,2},{1,10},{2,18},{3,26},{4,6},{5,14},{6,22},{7,30},{8,3},{9,11}... | collective-permute-start | bytes 393224 | tf_op jit(solution)/shard_map/ppermute | solution.py:285
  35.2 8.5 %collective-permute-start.14 = (bf16[4,128,128]{2,1,0:T(8,128)(2,1)S(1)}, bf16[4,128,128]{2,1,0:T(8,128)(2,1)S(1)}, u32[]{:S(2)}, u32[]{:S(2)}) collective-permute-start(bf16[4,128,128]{2,1,0:T(8,128)(2,1)S(1)} %sum_and_solve.5.refs_2_), channel_id=1, source_target_pairs={{0,7},{1,15},{2,21},{3,29},{4,1},{5,9},{6,19},{7,27},{8,6},{9,14},... | collective-permute-start | bytes 393224 | tf_op jit(solution)/shard_map/ppermute | solution.py:285
  44.0 4.5 %collective-permute-start.15 = (bf16[2,128,128]{2,1,0:T(8,128)(2,1)S(1)}, bf16[2,128,128]{2,1,0:T(8,128)(2,1)S(1)}, u32[]{:S(2)}, u32[]{:S(2)}) collective-permute-start(bf16[2,128,128]{2,1,0:T(8,128)(2,1)S(1)} %block_sums.11), channel_id=1, source_target_pairs={{0,16},{1,17},{2,18},{3,19},{4,20},{5,21},{6,22},{7,23},{8,24},{9,... | collective-permute-start | bytes 196616 | tf_op jit(solution)/shard_map/ppermute | solution.py:300
  48.5 1.3 %collective-permute-start.16 = (bf16[2,128,128]{2,1,0:T(8,128)(2,1)S(1)}, bf16[2,128,128]{2,1,0:T(8,128)(2,1)S(1)}, u32[]{:S(2)}, u32[]{:S(2)}) collective-permute-start(bf16[2,128,128]{2,1,0:T(8,128)(2,1)S(1)} %add.126.refs_0_), channel_id=1, source_target_pairs={{0,8},{1,9},{2,10},{3,11},{4,12},{5,13},{6,14},{7,15},{8,0},{9,1},... | collective-permute-start | bytes 196616 | tf_op jit(solution)/shard_map/ppermute | solution.py:300
  50.0 6.9 %collective-permute-start.17 = (bf16[2,128,128]{2,1,0:T(8,128)(2,1)S(1)}, bf16[2,128,128]{2,1,0:T(8,128)(2,1)S(1)}, u32[]{:S(2)}, u32[]{:S(2)}) collective-permute-start(bf16[2,128,128]{2,1,0:T(8,128)(2,1)S(1)} %sum_and_solve.6.refs_1_.refs_2_), channel_id=1, source_target_pairs={{0,2},{1,10},{2,18},{3,26},{4,6},{5,14},{6,22},{7,30},{8,3},{9,11}... | collective-permute-start | bytes 196616 | tf_op jit(solution)/shard_map/ppermute | solution.py:285
  51.8 5.1 %collective-permute-start.18 = (bf16[2,128,128]{2,1,0:T(8,128)(2,1)S(1)}, bf16[2,128,128]{2,1,0:T(8,128)(2,1)S(1)}, u32[]{:S(2)}, u32[]{:S(2)}) collective-permute-start(bf16[2,128,128]{2,1,0:T(8,128)(2,1)S(1)} %sum_and_solve.6.refs_1_.refs_2_), channel_id=1, source_target_pairs={{0,7},{1,15},{2,21},{3,29},{4,1},{5,9},{6,19},{7,27},{8,6},{9,14},... | collective-permute-start | bytes 196616 | tf_op jit(solution)/shard_map/ppermute | solution.py:285
  56.6 7.6 %copy-start.1 = (bf16[16,1,128,128]{3,2,1,0:T(8,128)(2,1)S(1)}, bf16[16,1,128,128]{3,2,1,0:T(8,128)(2,1)}, u32[]{:S(2)}) copy-start(bf16[16,1,128,128]{3,2,1,0:T(8,128)(2,1)} %refs_3_.5) | copy-start | bytes 1572868
  57.1 5.7 %collective-permute-start.19 = (bf16[2,128,128]{2,1,0:T(8,128)(2,1)S(1)}, bf16[2,128,128]{2,1,0:T(8,128)(2,1)S(1)}, u32[]{:S(2)}, u32[]{:S(2)}) collective-permute-start(bf16[2,128,128]{2,1,0:T(8,128)(2,1)S(1)} %block_sums.13), channel_id=1, source_target_pairs={{0,16},{1,17},{2,18},{3,19},{4,20},{5,21},{6,22},{7,23},{8,24},{9,... | collective-permute-start | bytes 196616 | tf_op jit(solution)/shard_map/ppermute | solution.py:300
  62.9 1.3 %collective-permute-start.20 = (bf16[2,128,128]{2,1,0:T(8,128)(2,1)S(1)}, bf16[2,128,128]{2,1,0:T(8,128)(2,1)S(1)}, u32[]{:S(2)}, u32[]{:S(2)}) collective-permute-start(bf16[2,128,128]{2,1,0:T(8,128)(2,1)S(1)} %add.127.refs_0_), channel_id=1, source_target_pairs={{0,8},{1,9},{2,10},{3,11},{4,12},{5,13},{6,14},{7,15},{8,0},{9,1},... | collective-permute-start | bytes 196616 | tf_op jit(solution)/shard_map/ppermute | solution.py:300
  64.5 7.4 %collective-permute-start.21 = (bf16[2,128,128]{2,1,0:T(8,128)(2,1)S(1)}, bf16[2,128,128]{2,1,0:T(8,128)(2,1)S(1)}, u32[]{:S(2)}, u32[]{:S(2)}) collective-permute-start(bf16[2,128,128]{2,1,0:T(8,128)(2,1)S(1)} %sum_and_solve.7.refs_1_), channel_id=1, source_target_pairs={{0,2},{1,10},{2,18},{3,26},{4,6},{5,14},{6,22},{7,30},{8,3},{9,11}... | collective-permute-start | bytes 196616 | tf_op jit(solution)/shard_map/ppermute | solution.py:285
  65.0 7.0 %collective-permute-start.22 = (bf16[2,128,128]{2,1,0:T(8,128)(2,1)S(1)}, bf16[2,128,128]{2,1,0:T(8,128)(2,1)S(1)}, u32[]{:S(2)}, u32[]{:S(2)}) collective-permute-start(bf16[2,128,128]{2,1,0:T(8,128)(2,1)S(1)} %sum_and_solve.7.refs_1_), channel_id=1, source_target_pairs={{0,7},{1,15},{2,21},{3,29},{4,1},{5,9},{6,19},{7,27},{8,6},{9,14},... | collective-permute-start | bytes 196616 | tf_op jit(solution)/shard_map/ppermute | solution.py:285
  72.2 5.0 %collective-permute-start.23 = (bf16[2,128,128]{2,1,0:T(8,128)(2,1)S(1)}, bf16[2,128,128]{2,1,0:T(8,128)(2,1)S(1)}, u32[]{:S(2)}, u32[]{:S(2)}) collective-permute-start(bf16[2,128,128]{2,1,0:T(8,128)(2,1)S(1)} %block_sums.14), channel_id=1, source_target_pairs={{0,16},{1,17},{2,18},{3,19},{4,20},{5,21},{6,22},{7,23},{8,24},{9,... | collective-permute-start | bytes 196616 | tf_op jit(solution)/shard_map/ppermute | solution.py:300
  77.2 1.3 %collective-permute-start.24 = (bf16[2,128,128]{2,1,0:T(8,128)(2,1)S(1)}, bf16[2,128,128]{2,1,0:T(8,128)(2,1)S(1)}, u32[]{:S(2)}, u32[]{:S(2)}) collective-permute-start(bf16[2,128,128]{2,1,0:T(8,128)(2,1)S(1)} %add.128.refs_0_), channel_id=1, source_target_pairs={{0,8},{1,9},{2,10},{3,11},{4,12},{5,13},{6,14},{7,15},{8,0},{9,1},... | collective-permute-start | bytes 196616 | tf_op jit(solution)/shard_map/ppermute | solution.py:300
  78.7 4.3 %collective-permute-start.25 = (bf16[2,128,128]{2,1,0:T(8,128)(2,1)S(1)}, bf16[2,128,128]{2,1,0:T(8,128)(2,1)S(1)}, u32[]{:S(2)}, u32[]{:S(2)}) collective-permute-start(bf16[2,128,128]{2,1,0:T(8,128)(2,1)S(1)} %sum_and_solve.8.refs_1_), channel_id=1, source_target_pairs={{0,2},{1,10},{2,18},{3,26},{4,6},{5,14},{6,22},{7,30},{8,3},{9,11}... | collective-permute-start | bytes 196616 | tf_op jit(solution)/shard_map/ppermute | solution.py:285
  79.2 7.3 %collective-permute-start.26 = (bf16[2,128,128]{2,1,0:T(8,128)(2,1)S(1)}, bf16[2,128,128]{2,1,0:T(8,128)(2,1)S(1)}, u32[]{:S(2)}, u32[]{:S(2)}) collective-permute-start(bf16[2,128,128]{2,1,0:T(8,128)(2,1)S(1)} %sum_and_solve.8.refs_1_), channel_id=1, source_target_pairs={{0,7},{1,15},{2,21},{3,29},{4,1},{5,9},{6,19},{7,27},{8,6},{9,14},... | collective-permute-start | bytes 196616 | tf_op jit(solution)/shard_map/ppermute | solution.py:285
  86.7 6.2 %collective-permute-start.27 = (bf16[4,128,128]{2,1,0:T(8,128)(2,1)S(1)}, bf16[4,128,128]{2,1,0:T(8,128)(2,1)S(1)}, u32[]{:S(2)}, u32[]{:S(2)}) collective-permute-start(bf16[4,128,128]{2,1,0:T(8,128)(2,1)S(1)} %block_sums.16), channel_id=1, source_target_pairs={{0,16},{1,17},{2,18},{3,19},{4,20},{5,21},{6,22},{7,23},{8,24},{9,... | collective-permute-start | bytes 393224 | tf_op jit(solution)/shard_map/ppermute | solution.py:300
  93.0 1.4 %collective-permute-start.28 = (bf16[4,128,128]{2,1,0:T(8,128)(2,1)S(1)}, bf16[4,128,128]{2,1,0:T(8,128)(2,1)S(1)}, u32[]{:S(2)}, u32[]{:S(2)}) collective-permute-start(bf16[4,128,128]{2,1,0:T(8,128)(2,1)S(1)} %add.129.refs_0_), channel_id=1, source_target_pairs={{0,8},{1,9},{2,10},{3,11},{4,12},{5,13},{6,14},{7,15},{8,0},{9,1},... | collective-permute-start | bytes 393224 | tf_op jit(solution)/shard_map/ppermute | solution.py:300
  94.6 5.6 %collective-permute-start.29 = (bf16[4,128,128]{2,1,0:T(8,128)(2,1)S(1)}, bf16[4,128,128]{2,1,0:T(8,128)(2,1)S(1)}, u32[]{:S(2)}, u32[]{:S(2)}) collective-permute-start(bf16[4,128,128]{2,1,0:T(8,128)(2,1)S(1)} %sum_and_solve.9), channel_id=1, source_target_pairs={{0,2},{1,10},{2,18},{3,26},{4,6},{5,14},{6,22},{7,30},{8,3},{9,11}... | collective-permute-start | bytes 393224 | tf_op jit(solution)/shard_map/ppermute | solution.py:285
  94.6 8.8 %collective-permute-start.30 = (bf16[4,128,128]{2,1,0:T(8,128)(2,1)S(1)}, bf16[4,128,128]{2,1,0:T(8,128)(2,1)S(1)}, u32[]{:S(2)}, u32[]{:S(2)}) collective-permute-start(bf16[4,128,128]{2,1,0:T(8,128)(2,1)S(1)} %sum_and_solve.9), channel_id=1, source_target_pairs={{0,7},{1,15},{2,21},{3,29},{4,1},{5,9},{6,19},{7,27},{8,6},{9,14},... | collective-permute-start | bytes 393224 | tf_op jit(solution)/shard_map/ppermute | solution.py:285
  104.2 3.1 %collective-permute-start.31 = (bf16[4,128,128]{2,1,0:T(8,128)(2,1)S(1)}, bf16[4,128,128]{2,1,0:T(8,128)(2,1)S(1)}, u32[]{:S(2)}, u32[]{:S(2)}) collective-permute-start(bf16[4,128,128]{2,1,0:T(8,128)(2,1)S(1)} %get-tuple-element.28), channel_id=1, source_target_pairs={{0,8},{8,0},{1,9},{9,1},{2,10},{10,2},{3,11},{11,3},{4,12},{12,4},... | collective-permute-start | bytes 393224 | tf_op jit(solution)/shard_map/ppermute | solution.py:407
  107.3 5.8 %collective-permute-start.32 = (bf16[4,128,128]{2,1,0:T(8,128)(2,1)S(1)}, bf16[4,128,128]{2,1,0:T(8,128)(2,1)S(1)}, u32[]{:S(2)}, u32[]{:S(2)}) collective-permute-start(bf16[4,128,128]{2,1,0:T(8,128)(2,1)S(1)} %get-tuple-element.29), channel_id=1, source_target_pairs={{0,16},{16,0},{1,17},{17,1},{2,18},{18,2},{3,19},{19,3},{4,20},{20... | collective-permute-start | bytes 393224 | tf_op jit(solution)/shard_map/ppermute | solution.py:408
  113.4 4.5 %collective-permute-start.33 = (bf16[128,128]{1,0:T(8,128)(2,1)S(1)}, bf16[128,128]{1,0:T(8,128)(2,1)S(1)}, u32[]{:S(2)}, u32[]{:S(2)}) collective-permute-start(bf16[128,128]{1,0:T(8,128)(2,1)S(1)} %get-tuple-element.38), channel_id=1, source_target_pairs={{0,2},{1,3},{2,0},{3,1},{4,6},{5,7},{6,4},{7,5},{8,10},{9,11},{10,... | collective-permute-start | bytes 98312 | tf_op jit(solution)/shard_map/ppermute | solution.py:422
  113.8 4.9 %collective-permute-start.34 = (bf16[128,128]{1,0:T(8,128)(2,1)S(1)}, bf16[128,128]{1,0:T(8,128)(2,1)S(1)}, u32[]{:S(2)}, u32[]{:S(2)}) collective-permute-start(bf16[128,128]{1,0:T(8,128)(2,1)S(1)} %get-tuple-element.37), channel_id=1, source_target_pairs={{0,4},{1,5},{2,6},{3,7},{4,0},{5,1},{6,2},{7,3},{8,12},{9,13},{10,... | collective-permute-start | bytes 98312 | tf_op jit(solution)/shard_map/ppermute | solution.py:422
  114.3 5.8 %collective-permute-start.35 = (bf16[128,128]{1,0:T(8,128)(2,1)S(1)}, bf16[128,128]{1,0:T(8,128)(2,1)S(1)}, u32[]{:S(2)}, u32[]{:S(2)}) collective-permute-start(bf16[128,128]{1,0:T(8,128)(2,1)S(1)} %get-tuple-element.36), channel_id=1, source_target_pairs={{0,6},{1,7},{2,4},{3,5},{4,2},{5,3},{6,0},{7,1},{8,14},{9,15},{10,... | collective-permute-start | bytes 98312 | tf_op jit(solution)/shard_map/ppermute | solution.py:422
  120.1 4.3 %collective-permute-start.36 = (bf16[2,128,128]{2,1,0:T(8,128)(2,1)S(1)}, bf16[2,128,128]{2,1,0:T(8,128)(2,1)S(1)}, u32[]{:S(2)}, u32[]{:S(2)}) collective-permute-start(bf16[2,128,128]{2,1,0:T(8,128)(2,1)S(1)} %pad_maximum_fusion.1), channel_id=1, source_target_pairs={{0,1},{1,0},{2,3},{3,2},{4,5},{5,4},{6,7},{7,6},{8,9},{9,8},{10,11... | collective-permute-start | bytes 196616 | tf_op jit(solution)/shard_map/ppermute | solution.py:422
